TPU v7x, 32 devices: a whole 2x2x4 slice. The times are simulated.
32 devices in a mesh: ctx: 2 (over x), exp: 16 (over z, y, core).
Axes of the slice: x: 2, y: 2, z: 4, core: 2. Of those that a mesh axis runs over, the one named last changes fastest.
Arguments:
- hidden: bfloat16 [16, 16, 5120], P('exp', 'ctx'), may hold values from -6 to 6
- queries: bfloat16 [256, 36864], P('ctx', 'exp'), may hold values from -50 to 50
- latents: bfloat16 [256, 576], P('ctx'), may hold values from -6.5 to 6.5
- expert_ids: int32 [16, 16, 6], P('exp', 'ctx'), may hold values from 0 to 15, all different within a row; in each aligned block of 8 rows (0 to 7, 8 to 15, ..., all dimensions but the last counted through in order) at most 4 rows name the same one
- route_weight: float32 [16, 16, 6], P('exp', 'ctx'), may hold values from 0.1 to 1
- w_gate: bfloat16 [16, 1536, 5120], P('exp', 'ctx'), may hold values from -0.078125 to 0.078125
- w_up: bfloat16 [16, 1536, 5120], P('exp', 'ctx'), may hold values from -0.078125 to 0.078125
- w_down: bfloat16 [16, 5120, 1536], P('exp', 'ctx'), may hold values from -0.15625 to 0.15625
Outputs:
- attended: bfloat16 [256, 32768], P('ctx', 'exp')
- moe_out: bfloat16 [16, 16, 5120], P('exp', 'ctx')
Inputs may be any that keep to these rules, and one draw needn't show every extreme that they name: `expert_ids`: each token names 6 different experts. Within the 8 rows of one device (aligned blocks of rows of one group) no expert is named by more than 4 rows, a bound that some block reaches.
All inputs are finite; a program needn't handle non-finite values.
Results may differ from a plain program's by a relative error of at most 0.0057.
Values may be sent and summed in bfloat16 or wider, within the bound.
No kernel may reach another device: no remote copies, remote signals or barrier semaphores. Data moves between devices by JAX's collectives and lax.ppermute only.
A program may use at most 64 MiB of HBM per device.

v0:
```python
import jax
import jax.numpy as jnp
from jax import lax
from jax.sharding import PartitionSpec as P

LATENT = 512
ROPE = 64


SCALE = 0.07216878364870322


def shifted(block, axis, distance):
    devices = range(lax.axis_size(axis))
    route = [(i - distance, i) for i in devices if i - distance in devices]
    return lax.ppermute(block, axis, route)


def place_picks(picks, experts, capacity):
    flat = picks.reshape(-1)
    onehot = (flat[:, None] == jnp.arange(experts, dtype=jnp.int32)[None, :]).astype(jnp.int32)
    earlier = jnp.cumsum(onehot, axis=0) - onehot
    rank = jnp.sum(earlier * onehot, axis=1)
    target = flat * capacity + rank
    return (target[:, None] == jnp.arange(experts * capacity, dtype=jnp.int32)[None, :]).astype(
        jnp.float32
    )


def token_table(tok_count, topk):
    owner = jnp.arange(tok_count * topk, dtype=jnp.int32) // topk
    return (owner[:, None] == jnp.arange(tok_count, dtype=jnp.int32)[None, :]).astype(jnp.float32)


def times_rows(left, right):
    return lax.dot_general(
        left, right, (((1,), (1,)), ((), ())), preferred_element_type=jnp.float32
    )


def on_device(hidden, queries, latents, expert_ids, route_weight, w_gate, w_up, w_down):
    tok_att = latents.shape[0]
    heads_dev = queries.shape[1] // (LATENT + ROPE)
    tok_dev = hidden.shape[1]
    width = hidden.shape[2]
    topk = expert_ids.shape[2]
    experts = lax.axis_size("exp")
    groups = lax.axis_size("ctx")
    capacity = min(tok_dev, max(2, 3 * topk * tok_dev // (2 * experts)))
    slots = experts * capacity
    earlier_kv = shifted(latents, "ctx", 1)
    keys = jnp.concatenate([earlier_kv, latents], axis=0)
    query_rows = queries.reshape(tok_att, heads_dev, LATENT + ROPE)
    scores = jnp.einsum("thc,kc->htk", query_rows, keys, preferred_element_type=jnp.float32) * SCALE
    row_pos = jnp.arange(tok_att, dtype=jnp.int32)
    key_pos = jnp.arange(2 * tok_att, dtype=jnp.int32)
    seen_own = (key_pos[None, :] >= tok_att) & (key_pos[None, :] - tok_att <= row_pos[:, None])
    seen_prev = (key_pos[None, :] < tok_att) & (lax.axis_index("ctx") > 0)
    scores = jnp.where((seen_own | seen_prev)[None, :, :], scores, jnp.float32(-1e30))
    top = jnp.max(scores, axis=-1, keepdims=True)
    expo = jnp.exp(scores - top)
    probs = (expo / jnp.sum(expo, axis=-1, keepdims=True)).astype(jnp.bfloat16)
    mixed_heads = jnp.einsum(
        "htk,kc->thc", probs, keys[:, :LATENT], preferred_element_type=jnp.float32
    )
    attended = mixed_heads.astype(jnp.bfloat16).reshape(tok_att, heads_dev * LATENT)
    tokens = hidden[0]
    picks = expert_ids[0]
    pick_weight = route_weight[0].reshape(-1)
    tok_hot = token_table(tok_dev, topk)
    slot_hot = place_picks(picks, experts, capacity)
    gate_w = w_gate[0]
    up_w = w_up[0]
    down_w = w_down[0]
    send_matrix = jnp.dot(slot_hot.T, tok_hot).astype(jnp.bfloat16)
    outgoing = jnp.dot(send_matrix, tokens, preferred_element_type=jnp.float32).astype(jnp.bfloat16)
    outgoing = outgoing.reshape(experts, capacity, width)
    arrived = lax.all_to_all(outgoing, "exp", split_axis=0, concat_axis=0, tiled=True)
    piece = lax.all_gather(arrived.reshape(slots, width), "ctx", axis=0, tiled=True)
    gate = times_rows(piece, gate_w)
    upper = times_rows(piece, up_w)
    hidden_units = (jax.nn.silu(gate) * upper).astype(jnp.bfloat16)
    projected = times_rows(lax.all_gather(hidden_units, "ctx", axis=1, tiled=True), down_w)
    columns = projected.astype(jnp.bfloat16).reshape(groups, experts, capacity, down_w.shape[0])
    by_block = lax.all_to_all(columns, "ctx", split_axis=0, concat_axis=3, tiled=True)
    returned = lax.all_to_all(by_block, "exp", split_axis=1, concat_axis=1, tiled=True)
    combine_matrix = jnp.dot(
        slot_hot.T, tok_hot * pick_weight[:, None], precision=lax.Precision.HIGHEST
    )
    back_rows = returned.reshape(slots, width).astype(jnp.float32)
    mixed = jnp.dot(combine_matrix.T, back_rows, precision=lax.Precision.HIGHEST).astype(
        jnp.bfloat16
    )
    return (attended, mixed[None])


def solution(mesh):
    placed = (
        P("exp", "ctx", None),
        P("ctx", "exp"),
        P("ctx", None),
        P("exp", "ctx", None),
        P("exp", "ctx", None),
        P("exp", "ctx", None),
        P("exp", "ctx", None),
        P("exp", "ctx", None),
    )
    return jax.shard_map(
        on_device,
        mesh=mesh,
        in_specs=placed,
        out_specs=(P("ctx", "exp"), P("exp", "ctx", None)),
        check_vma=False,
    )
```

profile of v0, /device:TPU:0, one launch (start us, length us, event | category | flops | bytes accessed | tf_op | source)
XLA Modules:
  0.0 127.1 jit_solution(9977341146433380835)
XLA Ops:
  7.2 0.8 copy.30
  8.0 0.1 reshape_squeeze.3
  8.2 0.2 select_reduce_fusion
  8.4 0.6 convolution_convert_fusion
  9.1 0.2 reshape.116
  9.3 25.4 %all_to_all.28 = bf16[16,4,5120]{2,1,0:T(4,128)(2,1)S(1)} all-to-all(bf16[16,4,5120]{2,1,0:T(4,128)(2,1)S(1)} %reshape.116), channel_id=1, replica_groups=mesh['ctx'=2,'exp'=16] {'exp'}, dimensions={0} | all-to-all | bytes 1310720 | tf_op jit(solution)/shard_map/all_to_all | solution.py:78
  34.7 1.0 reshape.117
  35.8 23.0 %all-gather.2.cloned.1.call-done = bf16[128,5120]{1,0:T(8,128)(2,1)} async-done(((bf16[64,5120]{1,0:T(8,128)(2,1)}), bf16[128,5120]{1,0:T(8,128)(2,1)}) %all-gather.2.cloned.1.call-update) | async-done | bytes 1310736 | tf_op jit(solution)/shard_map/all_gather | solution.py:79
  58.7 6.5 %fusion.5 = f32[128,768]{1,0:T(8,128)S(1)} fusion(bf16[128,5120]{1,0:T(8,128)(2,1)} %all-gather.2.cloned.1.call-done, bf16[1,768,5120]{2,1,0:T(8,128)(2,1)} %param.13), kind=kOutput, calls=%fused_computation.5 | convolution fusion | flops 1006632960 | bytes 9568256 | tf_op jit(solution)/shard_map/dot_general | solution.py:36
  65.2 6.2 %fusion.18 = bf16[128,768]{1,0:T(8,128)(2,1)S(1)} fusion(bf16[128,5120]{1,0:T(8,128)(2,1)S(1)} %copy-done.1, bf16[1,768,5120]{2,1,0:T(8,128)(2,1)} %param.14, f32[128,768]{1,0:T(8,128)S(1)} %fusion.5), kind=kOutput, calls=%fused_computation.18 | convolution fusion | flops 1007222784 | bytes 9764864 | tf_op jit(solution)/shard_map/dot_general | solution.py:36
  71.4 7.5 %all_gather.7 = bf16[128,1536]{1,0:T(8,128)(2,1)S(1)} all-gather(bf16[128,768]{1,0:T(8,128)(2,1)S(1)} %fusion.18), channel_id=1, replica_groups=mesh['ctx'=2,'exp'=16] {'ctx'}, dimensions={1}, use_global_device_ids=true | all-gather | bytes 589824 | tf_op jit(solution)/shard_map/all_gather | solution.py:83
  78.9 2.6 %fusion.8 = bf16[128,2560]{1,0:T(8,128)(2,1)S(1)} fusion(bf16[128,1536]{1,0:T(8,128)(2,1)S(1)} %all_gather.7, bf16[1,2560,1536]{2,1,0:T(8,128)(2,1)S(1)} %bitcast.48), kind=kOutput, calls=%fused_computation.10 | convolution fusion | flops 1006960640 | bytes 8912896 | tf_op jit(solution)/shard_map/dot_general | solution.py:36
  81.5 0.2 reshape.118
  81.7 1.0 copy.32
  82.7 3.5 %all-to-all-start.1 = ((bf16[2,16,4,2560]{3,1,2,0:T(8,128)(2,1)}), bf16[2,16,4,2560]{3,1,2,0:T(8,128)(2,1)S(1)}, u32[]{:S(2)}, u32[]{:S(2)}) async-start(bf16[2,16,4,2560]{3,1,2,0:T(8,128)(2,1)} %copy.32), calls=%async_computation.1 | async-start | bytes 1310720 | tf_op jit(solution)/shard_map/all_to_all | solution.py:85
  86.2 3.9 %collective-permute-start = (bf16[128,576]{0,1:T(8,128)(2,1)S(1)}, bf16[128,576]{0,1:T(8,128)(2,1)S(1)}, u32[]{:S(2)}, u32[]{:S(2)}) collective-permute-start(bf16[128,576]{0,1:T(8,128)(2,1)S(1)} %copy-done.3), channel_id=1, source_target_pairs={{0,16},{1,17},{2,18},{3,19},{4,20},{5,21},{6,22},{7,23},{8,24},{9,... | collective-permute-start | bytes 442376 | tf_op jit(solution)/shard_map/ppermute | solution.py:16
  90.1 0.1 copy.31
  90.2 0.1 mul.45
  90.3 0.3 copy.28
  90.6 4.3 %all-to-all-done.1 = bf16[2,16,4,2560]{3,1,2,0:T(8,128)(2,1)S(1)} async-done(((bf16[2,16,4,2560]{3,1,2,0:T(8,128)(2,1)}), bf16[2,16,4,2560]{3,1,2,0:T(8,128)(2,1)S(1)}, u32[]{:S(2)}, u32[]{:S(2)}) %all-to-all-start.1) | async-done | bytes 655392 | tf_op jit(solution)/shard_map/all_to_all | solution.py:85
  95.0 0.7 copy.37
  95.6 1.3 reshape.122
  96.9 5.6 %all-to-all-start.2 = ((bf16[1,16,4,5120]{3,2,0,1:T(4,128)(2,1)}), bf16[1,16,4,5120]{3,2,0,1:T(4,128)(2,1)S(1)}, u32[]{:S(2)}, u32[]{:S(2)}) async-start(bf16[1,16,4,5120]{3,2,0,1:T(4,128)(2,1)} %reshape.122), calls=%async_computation.2 | async-start | bytes 1310720 | tf_op jit(solution)/shard_map/all_to_all | solution.py:86
  102.5 0.2 fusion.24
  102.7 0.3 fusion.26
  103.0 0.4 fusion.14
  103.5 0.1 fusion.39
  103.6 0.4 convolution_convert_fusion.2
  104.0 1.0 copy.35
  105.0 14.1 %all-to-all-done.2 = bf16[1,16,4,5120]{3,2,0,1:T(4,128)(2,1)S(1)} async-done(((bf16[1,16,4,5120]{3,2,0,1:T(4,128)(2,1)}), bf16[1,16,4,5120]{3,2,0,1:T(4,128)(2,1)S(1)}, u32[]{:S(2)}, u32[]{:S(2)}) %all-to-all-start.2) | async-done | bytes 655392 | tf_op jit(solution)/shard_map/all_to_all | solution.py:86
  119.1 0.1 reshape.119
  119.3 1.0 fusion.7
  (25 shorter events, 0.3 us)
Async XLA Ops:
  7.2 1.3 copy-start
  7.2 51.6 %all-gather.2.cloned.1.call-start = ((), (), s32[]{:S(2)}) async-start(), calls=%async_computation.3 | async-start | bytes 1966080 | tf_op jit(solution)/shard_map/all_gather | solution.py:79
  58.7 6.5 %copy-start.1 = (bf16[128,5120]{1,0:T(8,128)(2,1)S(1)}, bf16[128,5120]{1,0:T(8,128)(2,1)}, u32[]{:S(2)}) copy-start(bf16[128,5120]{1,0:T(8,128)(2,1)} %all-gather.2.cloned.1.call-done) | copy-start | bytes 3932164
  58.7 20.2 %slice-start = ((s8[7864320]{0:T(1024)(128)(4,1)}), s8[4194304]{0:T(1024)(128)(4,1)S(1)}, s32[]{:S(2)}) async-start(s8[7864320]{0:T(1024)(128)(4,1)} %bitcast.47), calls=%async_computation.4 | async-start | bytes 8388608
  65.2 13.7 %slice-start.1 = ((s8[7864320]{0:T(1024)(128)(4,1)}), s8[3670016]{0:T(1024)(128)(4,1)S(1)}, s32[]{:S(2)}) async-start(s8[7864320]{0:T(1024)(128)(4,1)} %bitcast.47), calls=%async_computation.5 | async-start | bytes 7340032
  71.4 14.8 %copy-start.3 = (bf16[128,576]{0,1:T(8,128)(2,1)S(1)}, bf16[128,576]{0,1:T(8,128)(2,1)}, u32[]{:S(2)}) copy-start(bf16[128,576]{0,1:T(8,128)(2,1)} %param.10) | copy-start | bytes 442372
  71.4 18.7 %copy-start.4 = (f32[1,8,6]{1,0,2:T(1,128)S(1)}, f32[1,8,6]{1,0,2:T(1,128)}, u32[]{:S(2)}) copy-start(f32[1,8,6]{1,0,2:T(1,128)} %param.12) | copy-start | bytes 580
  71.4 18.8 %copy-start.2 = (bf16[128,2304]{1,0:T(8,128)(2,1)S(1)}, bf16[128,2304]{1,0:T(8,128)(2,1)}, u32[]{:S(2)}) copy-start(bf16[128,2304]{1,0:T(8,128)(2,1)} %param.9) | copy-start | bytes 1769476
  82.7 12.3 %all-to-all-start.1 = ((bf16[2,16,4,2560]{3,1,2,0:T(8,128)(2,1)}), bf16[2,16,4,2560]{3,1,2,0:T(8,128)(2,1)S(1)}, u32[]{:S(2)}, u32[]{:S(2)}) async-start(bf16[2,16,4,2560]{3,1,2,0:T(8,128)(2,1)} %copy.32), calls=%async_computation.1 | async-start | bytes 1310720 | tf_op jit(solution)/shard_map/all_to_all | solution.py:85
  86.2 16.8 %collective-permute-start = (bf16[128,576]{0,1:T(8,128)(2,1)S(1)}, bf16[128,576]{0,1:T(8,128)(2,1)S(1)}, u32[]{:S(2)}, u32[]{:S(2)}) collective-permute-start(bf16[128,576]{0,1:T(8,128)(2,1)S(1)} %copy-done.3), channel_id=1, source_target_pairs={{0,16},{1,17},{2,18},{3,19},{4,20},{5,21},{6,22},{7,23},{8,24},{9,... | collective-permute-start | bytes 442376 | tf_op jit(solution)/shard_map/ppermute | solution.py:16
  96.9 22.2 %all-to-all-start.2 = ((bf16[1,16,4,5120]{3,2,0,1:T(4,128)(2,1)}), bf16[1,16,4,5120]{3,2,0,1:T(4,128)(2,1)S(1)}, u32[]{:S(2)}, u32[]{:S(2)}) async-start(bf16[1,16,4,5120]{3,2,0,1:T(4,128)(2,1)} %reshape.122), calls=%async_computation.2 | async-start | bytes 1310720 | tf_op jit(solution)/shard_map/all_to_all | solution.py:86
Sparse Core Ops, SparseCore 0:
  35.9 22.8 all-gather.1
where the time goes:
time: 128 us; the launch traced here: 127 us
  waiting for transfers between devices  41.4 us (32%)
  blocking collectives  32.9 us (26%)
  matrix products  17.9 us (14%)
  between operations  14.2 us (11%)
  starting transfers between devices  13.1 us (10%)
  local copies, waits for them, and re-layouts  6.9 us (5%)
    all_to_all x1, blocking collectives, on_device(): lax.all_to_all(outgoing, 'exp', split_axis=0, concat_axis=0, tiled=True)  25.4 us
    all_gather x1, waiting for transfers between devices, on_device(): lax.all_gather(arrived.reshape(slots, width), 'ctx', axis=0, tiled=True)  23 us
    dot_general x3, matrix products, times_rows(): lax.dot_general(left, right, (((1,), (1,)), ((), ())), preferred_element_...  15.3 us
    all_to_all x1, waiting for transfers between devices, on_device(): lax.all_to_all(by_block, 'exp', split_axis=1, concat_axis=1, tiled=True)  14.1 us
    all_gather x1, blocking collectives, on_device(): lax.all_gather(hidden_units, 'ctx', axis=1, tiled=True)  7.45 us
    all_to_all x1, starting transfers between devices, on_device(): lax.all_to_all(by_block, 'exp', split_axis=1, concat_axis=1, tiled=True)  5.62 us
    all_to_all x1, waiting for transfers between devices, on_device(): lax.all_to_all(columns, 'ctx', split_axis=0, concat_axis=3, tiled=True)  4.34 us
    ppermute x1, starting transfers between devices, shifted(): return lax.ppermute(block, axis, route)  3.9 us
  transfers between devices with their start and end apart: 4, of which 3 were waited for; matrix products, arithmetic and copies ran while one was open for 4% of the time, Pallas kernels for 0%

commit v1 on v0

--- a/solution.py
+++ b/solution.py
@@ -38,7 +38,115 @@
     )
 
 
-def on_device(hidden, queries, latents, expert_ids, route_weight, w_gate, w_up, w_down):
+def swapped(block, axis, bit):
+    return lax.ppermute(block, axis, [(i, i ^ bit) for i in range(lax.axis_size(axis))])
+
+
+def moved(block, steps):
+    count = lax.axis_size("exp")
+    return lax.ppermute(block, "exp", [(i, (i + 4 * steps) % count) for i in range(count)])
+
+
+def attention(queries, latents, earlier_kv):
+    tok_att = latents.shape[0]
+    heads_dev = queries.shape[1] // (LATENT + ROPE)
+    keys = jnp.concatenate([earlier_kv, latents], axis=0)
+    query_rows = queries.reshape(tok_att, heads_dev, LATENT + ROPE)
+    scores = jnp.einsum("thc,kc->htk", query_rows, keys, preferred_element_type=jnp.float32) * SCALE
+    row_pos = jnp.arange(tok_att, dtype=jnp.int32)
+    key_pos = jnp.arange(2 * tok_att, dtype=jnp.int32)
+    seen_own = (key_pos[None, :] >= tok_att) & (key_pos[None, :] - tok_att <= row_pos[:, None])
+    seen_prev = (key_pos[None, :] < tok_att) & (lax.axis_index("ctx") > 0)
+    scores = jnp.where((seen_own | seen_prev)[None, :, :], scores, jnp.float32(-1e30))
+    top = jnp.max(scores, axis=-1, keepdims=True)
+    expo = jnp.exp(scores - top)
+    probs = (expo / jnp.sum(expo, axis=-1, keepdims=True)).astype(jnp.bfloat16)
+    mixed_heads = jnp.einsum(
+        "htk,kc->thc", probs, keys[:, :LATENT], preferred_element_type=jnp.float32
+    )
+    return mixed_heads.astype(jnp.bfloat16).reshape(tok_att, heads_dev * LATENT)
+
+
+def on_device_gathered(
+    hidden, queries, latents, expert_ids, route_weight, w_gate, w_up, w_down
+):
+    tok_dev = hidden.shape[1]
+    width = hidden.shape[2]
+    topk = expert_ids.shape[2]
+    experts = lax.axis_size("exp")
+    line = experts // 4
+    capacity = min(tok_dev, max(2, 3 * topk * tok_dev // (2 * experts)))
+    half = width // 2
+    unit = line * tok_dev
+    bf16, f32 = jnp.bfloat16, jnp.float32
+    first = lax.axis_index("ctx") == 0
+    earlier_kv = shifted(latents, "ctx", 1)
+
+    weight = route_weight[0]
+    high = weight.astype(bf16)
+    low = (weight - high.astype(f32)).astype(bf16)
+    notes = jnp.concatenate([expert_ids[0].astype(bf16), high, low], axis=1)
+    notes = jnp.pad(notes, ((0, 0), (0, 128 - notes.shape[1])))
+    rows = jnp.concatenate([hidden[0], notes], axis=1)
+
+    along = jnp.concatenate([rows] + [moved(rows, d) for d in range(1, line)], axis=0)
+    left, right = along[:, :half], along[:, half:]
+    left_y = swapped(left, "exp", 2)
+    right_x = swapped(right, "ctx", 1)
+    left_2 = jnp.concatenate([left, left_y], axis=0)
+    right_2 = jnp.concatenate([right, right_x], axis=0)
+    left_x = swapped(left_2, "ctx", 1)
+    right_y = swapped(right_2, "exp", 2)
+    left_4 = jnp.concatenate([left_2, left_x], axis=0)
+    right_4 = jnp.concatenate([right, right_y[:unit], right_x, right_y[unit:]], axis=0)
+    chip = jnp.concatenate([left_4, right_4], axis=1)
+    every = jnp.concatenate([chip, swapped(chip, "exp", 1)], axis=0)
+
+    count = every.shape[0]
+    names = every[:, width : width + topk].astype(f32)
+    weights = every[:, width + topk : width + 2 * topk].astype(f32) + every[
+        :, width + 2 * topk : width + 3 * topk
+    ].astype(f32)
+    mine = names == lax.axis_index("exp").astype(f32)
+    coef = jnp.sum(jnp.where(mine, weights, 0.0), axis=1)
+    hit = jnp.any(mine, axis=1)
+    by_block = hit.reshape(count // tok_dev, tok_dev).astype(jnp.int32)
+    rank = jnp.cumsum(by_block, axis=1) - by_block
+    slot = (jnp.arange(count // tok_dev, dtype=jnp.int32)[:, None] * capacity + rank).reshape(-1)
+    slots = count // tok_dev * capacity
+    pick = ((jnp.arange(slots, dtype=jnp.int32)[:, None] == slot[None, :]) & hit[None, :]).astype(bf16)
+
+    tokens = every[:, :width]
+    gate = times_rows(tokens, w_gate[0])
+    upper = times_rows(tokens, w_up[0])
+    act = (jax.nn.silu(gate) * upper).astype(bf16)
+    packed = jnp.dot(pick, act, preferred_element_type=f32).astype(bf16)
+    other = swapped(packed, "ctx", 1)
+    other = other.reshape(2, 2, slots // 4, other.shape[1])[:, ::-1].reshape(packed.shape)
+    other = jnp.dot(pick.T, other, preferred_element_type=f32).astype(bf16)
+    units = jnp.concatenate(
+        [jnp.where(first, act, other), jnp.where(first, other, act)], axis=1
+    )
+    projected = times_rows(units, w_down[0])
+    share = (projected * coef[:, None]).astype(bf16).reshape(2, count // 2, -1)
+
+    columns = share.shape[2]
+    total = share[0].astype(f32) + swapped(share[1], "exp", 1).astype(f32)
+    total = total.reshape(2, 2, unit, columns)
+    total = total[:, 0] + swapped(total[:, 1].astype(bf16), "exp", 2).astype(f32)
+    total = total.reshape(2, line, tok_dev, columns)
+    parts = [moved(total[:, d].astype(bf16), line - d) for d in range(1, line)]
+    total = total[:, 0] + sum(part.astype(f32) for part in parts)
+    total = total.astype(bf16)
+    far = swapped(total[1], "ctx", 1)
+    near = total[0]
+    mixed = jnp.concatenate(
+        [jnp.where(first, near, far), jnp.where(first, far, near)], axis=1
+    )
+    return (attention(queries, latents, earlier_kv), mixed[None])
+
+
+def on_device_slots(hidden, queries, latents, expert_ids, route_weight, w_gate, w_up, w_down):
     tok_att = latents.shape[0]
     heads_dev = queries.shape[1] // (LATENT + ROPE)
     tok_dev = hidden.shape[1]
@@ -95,6 +203,9 @@
 
 
 def solution(mesh):
+    experts, groups = mesh.shape["exp"], mesh.shape["ctx"]
+    whole = groups == 2 and experts % 4 == 0 and experts <= 16
+    on_device = on_device_gathered if whole else on_device_slots
     placed = (
         P("exp", "ctx", None),
         P("ctx", "exp"),

time: 128 us -> 92.5 us (0.72)
  blocking collectives: 32.9 us -> 0 us
  between operations: 14.2 us -> 0.93 us
  starting transfers between devices: 13.1 us -> 23 us
  other arithmetic: 0.67 us -> 7.42 us
  matrix products: 17.9 us -> 14.7 us
  local copies, waits for them, and re-layouts: 6.9 us -> 4.17 us
    ppermute x0 -> x15, waiting for transfers between devices: none -> 39.6 us  [the longest x9 26.8 us: swapped(): lax.ppermute(block, axis, [(i, i ^ bit) for i in range(lax.axis_size(axis...]
    all_to_all x1 -> x0, blocking collectives: 25.4 us -> none  [on_device(): lax.all_to_all(outgoing, 'exp', split_axis=0, concat_axis=0, tiled=True)]
    all_gather x1 -> x0, waiting for transfers between devices: 23 us -> none  [on_device(): lax.all_gather(arrived.reshape(slots, width), 'ctx', axis=0, tiled=True)]
    ppermute x0 -> x15, starting transfers between devices: none -> 19.8 us  [the longest x9 10.5 us: swapped(): lax.ppermute(block, axis, [(i, i ^ bit) for i in range(lax.axis_size(axis...]
    all_to_all x2 -> x0, waiting for transfers between devices: 18.4 us -> none  [the longest x1 14.1 us: on_device(): lax.all_to_all(by_block, 'exp', split_axis=1, concat_axis=1, tiled=True)]
    all_to_all x2 -> x0, starting transfers between devices: 9.13 us -> none  [the longest x1 5.62 us: on_device(): lax.all_to_all(by_block, 'exp', split_axis=1, concat_axis=1, tiled=True)]
    all_gather x1 -> x0, blocking collectives: 7.45 us -> none  [on_device(): lax.all_gather(hidden_units, 'ctx', axis=1, tiled=True)]
    concatenate x0 -> x7, other arithmetic: none -> 4.89 us  [the longest x1 1.88 us: on_device_gathered(): every = jnp.concatenate([chip, swapped(chip, 'exp', 1)], axis=0)]
  transfers between devices with their start and end apart: 4 -> 16, of which waited for: 3 -> 14; matrix products, arithmetic and copies ran while one was open for 4% -> 5% of each run, Pallas kernels for 0% -> 0%
where the time goes in v1:
time: 92.5 us; the launch traced here: 92.2 us
  waiting for transfers between devices  42 us (45%)
  starting transfers between devices  23 us (25%)
  matrix products  14.7 us (16%)
  other arithmetic  7.42 us (8%)
  local copies, waits for them, and re-layouts  4.17 us (5%)
  between operations  0.93 us (1%)
    ppermute x9, waiting for transfers between devices, swapped(): lax.ppermute(block, axis, [(i, i ^ bit) for i in range(lax.axis_size(axis...  26.8 us
    dot_general x3, matrix products, times_rows(): lax.dot_general(left, right, (((1,), (1,)), ((), ())), preferred_element_...  13.4 us
    ppermute x6, waiting for transfers between devices, moved(): lax.ppermute(block, 'exp', [(i, (i + 4 * steps) % count) for i in range(c...  12.7 us
    ppermute x9, starting transfers between devices, swapped(): lax.ppermute(block, axis, [(i, i ^ bit) for i in range(lax.axis_size(axis...  10.5 us
    ppermute x6, starting transfers between devices, moved(): lax.ppermute(block, 'exp', [(i, (i + 4 * steps) % count) for i in range(c...  9.33 us
    unnamed x15, local copies, waits for them, and re-layouts  3.65 us
    ppermute x1, starting transfers between devices, shifted(): return lax.ppermute(block, axis, route)  3.17 us
    ppermute x1, waiting for transfers between devices, shifted(): return lax.ppermute(block, axis, route)  2.45 us
  transfers between devices with their start and end apart: 16, of which 14 were waited for; matrix products, arithmetic and copies ran while one was open for 5% of the time, Pallas kernels for 0%

profile of v1, /device:TPU:0, one launch (start us, length us, event | category | flops | bytes accessed | tf_op | source)
XLA Modules:
  0.0 92.2 jit_solution(5685175030082645149)
XLA Ops:
  2.2 0.9 pad_maximum_fusion.8
  3.1 5.0 %collective-permute-start.3 = (bf16[8,5248]{1,0:T(8,128)(2,1)S(1)}, bf16[8,5248]{1,0:T(8,128)(2,1)S(1)}, u32[]{:S(2)}, u32[]{:S(2)}) collective-permute-start(bf16[8,5248]{1,0:T(8,128)(2,1)S(1)} %pad_maximum_fusion.8), channel_id=1, source_target_pairs={{0,12},{1,13},{2,14},{3,15},{4,0},{5,1},{6,2},{7,3},{8,4},{9,5},{1... | collective-permute-start | bytes 251912 | tf_op jit(solution)/shard_map/ppermute | solution.py:47
  8.2 1.0 %collective-permute-start.1 = (bf16[8,5248]{1,0:T(8,128)(2,1)S(1)}, bf16[8,5248]{1,0:T(8,128)(2,1)S(1)}, u32[]{:S(2)}, u32[]{:S(2)}) collective-permute-start(bf16[8,5248]{1,0:T(8,128)(2,1)S(1)} %pad_maximum_fusion.8), channel_id=1, source_target_pairs={{0,4},{1,5},{2,6},{3,7},{4,8},{5,9},{6,10},{7,11},{8,12},{9,13},{1... | collective-permute-start | bytes 251912 | tf_op jit(solution)/shard_map/ppermute | solution.py:47
  9.2 1.9 %collective-permute-done.3 = bf16[8,5248]{1,0:T(8,128)(2,1)S(1)} collective-permute-done((bf16[8,5248]{1,0:T(8,128)(2,1)S(1)}, bf16[8,5248]{1,0:T(8,128)(2,1)S(1)}, u32[]{:S(2)}, u32[]{:S(2)}) %collective-permute-start.3) | collective-permute-done | bytes 84000 | tf_op jit(solution)/shard_map/ppermute | solution.py:47
  11.1 4.8 %collective-permute-done.2 = bf16[8,5248]{1,0:T(8,128)(2,1)S(1)} collective-permute-done((bf16[8,5248]{1,0:T(8,128)(2,1)S(1)}, bf16[8,5248]{1,0:T(8,128)(2,1)S(1)}, u32[]{:S(2)}, u32[]{:S(2)}) %collective-permute-start.2) | collective-permute-done | bytes 84000 | tf_op jit(solution)/shard_map/ppermute | solution.py:47
  15.9 0.8 pad_maximum_fusion.3
  16.7 1.6 %collective-permute-start.6 = (bf16[32,2688]{1,0:T(8,128)(2,1)S(1)}, bf16[32,2688]{1,0:T(8,128)(2,1)S(1)}, u32[]{:S(2)}, u32[]{:S(2)}) collective-permute-start(bf16[32,2688]{1,0:T(8,128)(2,1)S(1)} %pad_maximum_fusion.3), channel_id=1, source_target_pairs={{0,16},{16,0},{1,17},{17,1},{2,18},{18,2},{3,19},{19,3},{4,20},{20... | collective-permute-start | bytes 516104 | tf_op jit(solution)/shard_map/ppermute | solution.py:42
  19.0 1.6 %collective-permute-start.4 = (bf16[32,2560]{1,0:T(8,128)(2,1)S(1)}, bf16[32,2560]{1,0:T(8,128)(2,1)S(1)}, u32[]{:S(2)}, u32[]{:S(2)}) collective-permute-start(bf16[32,2560]{1,0:T(8,128)(2,1)S(1)} %pad_maximum_fusion.7), channel_id=1, source_target_pairs={{0,2},{1,3},{2,0},{3,1},{4,6},{5,7},{6,4},{7,5},{8,10},{9,11},{10,... | collective-permute-start | bytes 491528 | tf_op jit(solution)/shard_map/ppermute | solution.py:42
  20.6 2.1 %collective-permute-done.6 = bf16[32,2688]{1,0:T(8,128)(2,1)S(1)} collective-permute-done((bf16[32,2688]{1,0:T(8,128)(2,1)S(1)}, bf16[32,2688]{1,0:T(8,128)(2,1)S(1)}, u32[]{:S(2)}, u32[]{:S(2)}) %collective-permute-start.6) | collective-permute-done | bytes 172064 | tf_op jit(solution)/shard_map/ppermute | solution.py:42
  22.7 1.6 %collective-permute-start.7 = (bf16[64,2688]{1,0:T(8,128)(2,1)S(1)}, bf16[64,2688]{1,0:T(8,128)(2,1)S(1)}, u32[]{:S(2)}, u32[]{:S(2)}) collective-permute-start(bf16[64,2688]{1,0:T(8,128)(2,1)S(1)} %pad_maximum_fusion.1), channel_id=1, source_target_pairs={{0,2},{1,3},{2,0},{3,1},{4,6},{5,7},{6,4},{7,5},{8,10},{9,11},{10,... | collective-permute-start | bytes 1032200 | tf_op jit(solution)/shard_map/ppermute | solution.py:42
  25.0 0.9 %collective-permute-start.5 = (bf16[64,2560]{1,0:T(8,128)(2,1)S(1)}, bf16[64,2560]{1,0:T(8,128)(2,1)S(1)}, u32[]{:S(2)}, u32[]{:S(2)}) collective-permute-start(bf16[64,2560]{1,0:T(8,128)(2,1)S(1)} %pad_maximum_fusion.2), channel_id=1, source_target_pairs={{0,16},{16,0},{1,17},{17,1},{2,18},{18,2},{3,19},{19,3},{4,20},{20... | collective-permute-start | bytes 983048 | tf_op jit(solution)/shard_map/ppermute | solution.py:42
  25.9 6.1 %collective-permute-done.7 = bf16[64,2688]{1,0:T(8,128)(2,1)S(1)} collective-permute-done((bf16[64,2688]{1,0:T(8,128)(2,1)S(1)}, bf16[64,2688]{1,0:T(8,128)(2,1)S(1)}, u32[]{:S(2)}, u32[]{:S(2)}) %collective-permute-start.7) | collective-permute-done | bytes 344096 | tf_op jit(solution)/shard_map/ppermute | solution.py:42
  32.8 1.2 %maximum_maximum_fusion = bf16[128,5248]{1,0:T(8,128)(2,1)} fusion(bf16[32,2688]{1,0:T(8,128)(2,1)S(1)} %get-tuple-element.13, bf16[32,2688]{1,0:T(8,128)(2,1)S(1)} %collective-permute-done.6, bf16[32,2688]{1,0:T(8,128)(2,1)S(1)} %get-tuple-element.12, bf16[32,2688]{1,0:T(8,128)(2,1)S(1)} %pad_maximum_fusion.3, ...), kind=kLoop, calls=%fused_computation.12 | loop fusion | flops 9404416 | bytes 2686976 | tf_op jit(solution)/shard_map/concatenate | solution.py:102
  34.1 3.1 %collective-permute-done.8 = bf16[128,5248]{1,0:T(8,128)(2,1)S(1)} collective-permute-done((bf16[128,5248]{1,0:T(8,128)(2,1)}, bf16[128,5248]{1,0:T(8,128)(2,1)S(1)}, u32[]{:S(2)}, u32[]{:S(2)}) %collective-permute-start.8) | collective-permute-done | bytes 1343520 | tf_op jit(solution)/shard_map/ppermute | solution.py:42
  37.8 1.9 %pad_maximum_fusion = bf16[256,5248]{1,0:T(8,128)(2,1)S(1)} fusion(bf16[128,5248]{1,0:T(8,128)(2,1)S(1)} %collective-permute-done.8, bf16[32,2688]{1,0:T(8,128)(2,1)S(1)} %get-tuple-element.13, bf16[32,2688]{1,0:T(8,128)(2,1)S(1)} %collective-permute-done.6, bf16[32,2688]{1,0:T(8,128)(2,1)S(1)} %get-tuple-element.12, ...), kind=kLoop, calls=%fused_computation.9 | loop fusion | flops 21495808 | bytes 5373952 | tf_op jit(solution)/shard_map/concatenate | solution.py:103
  39.7 5.6 %fusion.5 = f32[256,768]{1,0:T(8,128)S(1)} fusion(bf16[1,768,5120]{2,1,0:T(8,128)(2,1)} %param.13, bf16[256,5248]{1,0:T(8,128)(2,1)S(1)} %pad_maximum_fusion), kind=kOutput, calls=%fused_computation.5 | convolution fusion | flops 2013265920 | bytes 11272192 | tf_op jit(solution)/shard_map/dot_general | solution.py:36
  45.3 2.2 %multiply_convert_fusion = bf16[256,768]{1,0:T(8,128)(2,1)S(1)} fusion(f32[256,768]{1,0:T(8,128)S(1)} %fusion.5, bf16[1,768,5120]{2,1,0:T(8,128)(2,1)S(1)} %bitcast.96, bf16[256,5248]{1,0:T(8,128)(2,1)S(1)} %pad_maximum_fusion), kind=kOutput, calls=%fused_computation.25 | convolution fusion | flops 2014445568 | bytes 11665408 | tf_op jit(solution)/shard_map/dot_general | solution.py:36
  47.8 1.3 %collective-permute-start.9 = (bf16[128,768]{1,0:T(8,128)(2,1)S(1)}, bf16[128,768]{1,0:T(8,128)(2,1)S(1)}, u32[]{:S(2)}, u32[]{:S(2)}) collective-permute-start(bf16[128,768]{1,0:T(8,128)(2,1)S(1)} %convolution_convert_fusion.2), channel_id=1, source_target_pairs={{0,16},{16,0},{1,17},{17,1},{2,18},{18,2},{3,19},{19,3},{4,20},{20... | collective-permute-start | bytes 589832 | tf_op jit(solution)/shard_map/ppermute | solution.py:42
  49.3 5.5 %collective-permute-done.9 = bf16[128,768]{1,0:T(8,128)(2,1)S(1)} collective-permute-done((bf16[128,768]{1,0:T(8,128)(2,1)S(1)}, bf16[128,768]{1,0:T(8,128)(2,1)S(1)}, u32[]{:S(2)}, u32[]{:S(2)}) %collective-permute-start.9) | collective-permute-done | bytes 196640 | tf_op jit(solution)/shard_map/ppermute | solution.py:42
  55.1 5.5 %fusion.10 = bf16[256,2560]{1,0:T(8,128)(2,1)S(1)} fusion(bf16[1,2560,1536]{2,1,0:T(8,128)(2,1)} %param.15, f32[256]{0:T(256)S(1)} %select_reduce_fusion, bf16[256,768]{1,0:T(8,128)(2,1)S(1)} %get-tuple-element.11, bf16[256,768]{1,0:T(8,128)(2,1)S(1)} %get-tuple-element.10), kind=kOutput, calls=%fused_computation.8 | convolution fusion | flops 2016149504 | bytes 9962496 | tf_op jit(solution)/shard_map/dot_general | solution.py:36
  60.8 3.2 %collective-permute-start = (bf16[128,576]{0,1:T(8,128)(2,1)S(1)}, bf16[128,576]{0,1:T(8,128)(2,1)S(1)}, u32[]{:S(2)}, u32[]{:S(2)}) collective-permute-start(bf16[128,576]{0,1:T(8,128)(2,1)S(1)} %copy-done.2), channel_id=1, source_target_pairs={{0,16},{1,17},{2,18},{3,19},{4,20},{5,21},{6,22},{7,23},{8,24},{9,... | collective-permute-start | bytes 442376 | tf_op jit(solution)/shard_map/ppermute | solution.py:16
  64.0 1.1 %copy.16 = bf16[128,2304]{0,1:T(8,128)(2,1)} copy(bf16[128,2304]{1,0:T(8,128)(2,1)S(1)} %copy-done) | data formatting | bytes 1179648 | tf_op args[1]
  65.2 2.5 %collective-permute-done = bf16[128,576]{0,1:T(8,128)(2,1)S(1)} collective-permute-done((bf16[128,576]{0,1:T(8,128)(2,1)S(1)}, bf16[128,576]{0,1:T(8,128)(2,1)S(1)}, u32[]{:S(2)}, u32[]{:S(2)}) %collective-permute-start) | collective-permute-done | bytes 147488 | tf_op jit(solution)/shard_map/ppermute | solution.py:16
  67.9 0.9 collective-permute-start.11
  69.3 8.0 %collective-permute-done.11 = bf16[2,32,2560]{2,1,0:T(8,128)(2,1)S(1)} collective-permute-done((bf16[2,32,2560]{2,1,0:T(8,128)(2,1)S(1)}, bf16[2,32,2560]{2,1,0:T(8,128)(2,1)S(1)}, u32[]{:S(2)}, u32[]{:S(2)}) %collective-permute-start.11) | collective-permute-done | bytes 327712 | tf_op jit(solution)/shard_map/ppermute | solution.py:42
  77.4 2.0 %collective-permute-start.12 = (bf16[2,8,2560]{2,1,0:T(8,128)(2,1)S(1)}, bf16[2,8,2560]{2,1,0:T(8,128)(2,1)S(1)}, u32[]{:S(2)}, u32[]{:S(2)}) collective-permute-start(bf16[2,8,2560]{2,1,0:T(8,128)(2,1)S(1)} %get-tuple-element.14), channel_id=1, source_target_pairs={{0,12},{1,13},{2,14},{3,15},{4,0},{5,1},{6,2},{7,3},{8,4},{9,5},{1... | collective-permute-start | bytes 245768 | tf_op jit(solution)/shard_map/ppermute | solution.py:47
  79.5 1.2 %collective-permute-start.13 = (bf16[2,8,2560]{2,1,0:T(8,128)(2,1)S(1)}, bf16[2,8,2560]{2,1,0:T(8,128)(2,1)S(1)}, u32[]{:S(2)}, u32[]{:S(2)}) collective-permute-start(bf16[2,8,2560]{2,1,0:T(8,128)(2,1)S(1)} %get-tuple-element.16), channel_id=1, source_target_pairs={{0,8},{1,9},{2,10},{3,11},{4,12},{5,13},{6,14},{7,15},{8,0},{9,1},... | collective-permute-start | bytes 245768 | tf_op jit(solution)/shard_map/ppermute | solution.py:47
  80.8 2.8 %collective-permute-done.12 = bf16[2,8,2560]{2,1,0:T(8,128)(2,1)S(1)} collective-permute-done((bf16[2,8,2560]{2,1,0:T(8,128)(2,1)S(1)}, bf16[2,8,2560]{2,1,0:T(8,128)(2,1)S(1)}, u32[]{:S(2)}, u32[]{:S(2)}) %collective-permute-start.12) | collective-permute-done | bytes 81952 | tf_op jit(solution)/shard_map/ppermute | solution.py:47
  83.7 2.0 %collective-permute-done.14 = bf16[2,8,2560]{2,1,0:T(8,128)(2,1)S(1)} collective-permute-done((bf16[2,8,2560]{2,1,0:T(8,128)(2,1)S(1)}, bf16[2,8,2560]{2,1,0:T(8,128)(2,1)S(1)}, u32[]{:S(2)}, u32[]{:S(2)}) %collective-permute-start.14) | collective-permute-done | bytes 81952 | tf_op jit(solution)/shard_map/ppermute | solution.py:47
  85.7 1.3 %collective-permute-done.13 = bf16[2,8,2560]{2,1,0:T(8,128)(2,1)S(1)} collective-permute-done((bf16[2,8,2560]{2,1,0:T(8,128)(2,1)S(1)}, bf16[2,8,2560]{2,1,0:T(8,128)(2,1)S(1)}, u32[]{:S(2)}, u32[]{:S(2)}) %collective-permute-start.13) | collective-permute-done | bytes 81952 | tf_op jit(solution)/shard_map/ppermute | solution.py:47
  87.0 2.5 %collective-permute-start.15 = (bf16[8,2560]{1,0:T(8,128)(2,1)S(1)}, bf16[8,2560]{1,0:T(8,128)(2,1)S(1)}, u32[]{:S(2)}, u32[]{:S(2)}) collective-permute-start(bf16[8,2560]{1,0:T(8,128)(2,1)S(1)} %slice_bitcast_fusion.6), channel_id=1, source_target_pairs={{0,16},{16,0},{1,17},{17,1},{2,18},{18,2},{3,19},{19,3},{4,20},{20... | collective-permute-start | bytes 122888 | tf_op jit(solution)/shard_map/ppermute | solution.py:42
  89.9 1.0 %copy.25 = bf16[128,2048]{1,0:T(8,128)(2,1)} copy(bf16[128,2048]{0,1:T(8,128)(2,1)S(1)} %bitcast.93) | data formatting | bytes 1048576
  (59 shorter events, 8.2 us)
Async XLA Ops:
  3.1 7.9 %collective-permute-start.3 = (bf16[8,5248]{1,0:T(8,128)(2,1)S(1)}, bf16[8,5248]{1,0:T(8,128)(2,1)S(1)}, u32[]{:S(2)}, u32[]{:S(2)}) collective-permute-start(bf16[8,5248]{1,0:T(8,128)(2,1)S(1)} %pad_maximum_fusion.8), channel_id=1, source_target_pairs={{0,12},{1,13},{2,14},{3,15},{4,0},{5,1},{6,2},{7,3},{8,4},{9,5},{1... | collective-permute-start | bytes 251912 | tf_op jit(solution)/shard_map/ppermute | solution.py:47
  8.2 7.7 %collective-permute-start.2 = (bf16[8,5248]{1,0:T(8,128)(2,1)S(1)}, bf16[8,5248]{1,0:T(8,128)(2,1)S(1)}, u32[]{:S(2)}, u32[]{:S(2)}) collective-permute-start(bf16[8,5248]{1,0:T(8,128)(2,1)S(1)} %pad_maximum_fusion.8), channel_id=1, source_target_pairs={{0,8},{1,9},{2,10},{3,11},{4,12},{5,13},{6,14},{7,15},{8,0},{9,1},... | collective-permute-start | bytes 251912 | tf_op jit(solution)/shard_map/ppermute | solution.py:47
  8.2 7.7 %collective-permute-start.1 = (bf16[8,5248]{1,0:T(8,128)(2,1)S(1)}, bf16[8,5248]{1,0:T(8,128)(2,1)S(1)}, u32[]{:S(2)}, u32[]{:S(2)}) collective-permute-start(bf16[8,5248]{1,0:T(8,128)(2,1)S(1)} %pad_maximum_fusion.8), channel_id=1, source_target_pairs={{0,4},{1,5},{2,6},{3,7},{4,8},{5,9},{6,10},{7,11},{8,12},{9,13},{1... | collective-permute-start | bytes 251912 | tf_op jit(solution)/shard_map/ppermute | solution.py:47
  16.7 6.0 %collective-permute-start.6 = (bf16[32,2688]{1,0:T(8,128)(2,1)S(1)}, bf16[32,2688]{1,0:T(8,128)(2,1)S(1)}, u32[]{:S(2)}, u32[]{:S(2)}) collective-permute-start(bf16[32,2688]{1,0:T(8,128)(2,1)S(1)} %pad_maximum_fusion.3), channel_id=1, source_target_pairs={{0,16},{16,0},{1,17},{17,1},{2,18},{18,2},{3,19},{19,3},{4,20},{20... | collective-permute-start | bytes 516104 | tf_op jit(solution)/shard_map/ppermute | solution.py:42
  19.0 5.9 %collective-permute-start.4 = (bf16[32,2560]{1,0:T(8,128)(2,1)S(1)}, bf16[32,2560]{1,0:T(8,128)(2,1)S(1)}, u32[]{:S(2)}, u32[]{:S(2)}) collective-permute-start(bf16[32,2560]{1,0:T(8,128)(2,1)S(1)} %pad_maximum_fusion.7), channel_id=1, source_target_pairs={{0,2},{1,3},{2,0},{3,1},{4,6},{5,7},{6,4},{7,5},{8,10},{9,11},{10,... | collective-permute-start | bytes 491528 | tf_op jit(solution)/shard_map/ppermute | solution.py:42
  22.7 9.2 %collective-permute-start.7 = (bf16[64,2688]{1,0:T(8,128)(2,1)S(1)}, bf16[64,2688]{1,0:T(8,128)(2,1)S(1)}, u32[]{:S(2)}, u32[]{:S(2)}) collective-permute-start(bf16[64,2688]{1,0:T(8,128)(2,1)S(1)} %pad_maximum_fusion.1), channel_id=1, source_target_pairs={{0,2},{1,3},{2,0},{3,1},{4,6},{5,7},{6,4},{7,5},{8,10},{9,11},{10,... | collective-permute-start | bytes 1032200 | tf_op jit(solution)/shard_map/ppermute | solution.py:42
  25.0 7.8 %collective-permute-start.5 = (bf16[64,2560]{1,0:T(8,128)(2,1)S(1)}, bf16[64,2560]{1,0:T(8,128)(2,1)S(1)}, u32[]{:S(2)}, u32[]{:S(2)}) collective-permute-start(bf16[64,2560]{1,0:T(8,128)(2,1)S(1)} %pad_maximum_fusion.2), channel_id=1, source_target_pairs={{0,16},{16,0},{1,17},{17,1},{2,18},{18,2},{3,19},{19,3},{4,20},{20... | collective-permute-start | bytes 983048 | tf_op jit(solution)/shard_map/ppermute | solution.py:42
  34.0 3.3 %collective-permute-start.8 = (bf16[128,5248]{1,0:T(8,128)(2,1)}, bf16[128,5248]{1,0:T(8,128)(2,1)S(1)}, u32[]{:S(2)}, u32[]{:S(2)}) collective-permute-start(bf16[128,5248]{1,0:T(8,128)(2,1)} %maximum_maximum_fusion), channel_id=1, source_target_pairs={{0,1},{1,0},{2,3},{3,2},{4,5},{5,4},{6,7},{7,6},{8,9},{9,8},{10,11... | collective-permute-start | bytes 4030472 | tf_op jit(solution)/shard_map/ppermute | solution.py:42
  37.7 7.5 %slice-start = ((s8[7864320]{0:T(1024)(128)(4,1)}), s8[4194304]{0:T(1024)(128)(4,1)S(1)}, s32[]{:S(2)}) async-start(s8[7864320]{0:T(1024)(128)(4,1)} %bitcast.95), calls=%async_computation | async-start | bytes 8388608
  39.6 5.6 %slice-start.1 = ((s8[7864320]{0:T(1024)(128)(4,1)}), s8[3670016]{0:T(1024)(128)(4,1)S(1)}, s32[]{:S(2)}) async-start(s8[7864320]{0:T(1024)(128)(4,1)} %bitcast.95), calls=%async_computation.1 | async-start | bytes 7340032
  47.8 7.0 %collective-permute-start.9 = (bf16[128,768]{1,0:T(8,128)(2,1)S(1)}, bf16[128,768]{1,0:T(8,128)(2,1)S(1)}, u32[]{:S(2)}, u32[]{:S(2)}) collective-permute-start(bf16[128,768]{1,0:T(8,128)(2,1)S(1)} %convolution_convert_fusion.2), channel_id=1, source_target_pairs={{0,16},{16,0},{1,17},{17,1},{2,18},{18,2},{3,19},{19,3},{4,20},{20... | collective-permute-start | bytes 589832 | tf_op jit(solution)/shard_map/ppermute | solution.py:42
  55.1 5.7 %copy-start.2 = (bf16[128,576]{0,1:T(8,128)(2,1)S(1)}, bf16[128,576]{0,1:T(8,128)(2,1)}, u32[]{:S(2)}) copy-start(bf16[128,576]{0,1:T(8,128)(2,1)} %param.10) | copy-start | bytes 442372
  55.1 8.9 %copy-start = (bf16[128,2304]{1,0:T(8,128)(2,1)S(1)}, bf16[128,2304]{1,0:T(8,128)(2,1)}, u32[]{:S(2)}) copy-start(bf16[128,2304]{1,0:T(8,128)(2,1)} %param.9) | copy-start | bytes 1769476
  60.7 7.0 %collective-permute-start.10 = (bf16[128,2560]{1,0:T(8,128)(2,1)S(1)}, bf16[128,2560]{1,0:T(8,128)(2,1)S(1)}, u32[]{:S(2)}, u32[]{:S(2)}) collective-permute-start(bf16[128,2560]{1,0:T(8,128)(2,1)S(1)} %slice.87), channel_id=1, source_target_pairs={{0,1},{1,0},{2,3},{3,2},{4,5},{5,4},{6,7},{7,6},{8,9},{9,8},{10,11... | collective-permute-start | bytes 1966088 | tf_op jit(solution)/shard_map/ppermute | solution.py:42
  60.8 6.9 %collective-permute-start = (bf16[128,576]{0,1:T(8,128)(2,1)S(1)}, bf16[128,576]{0,1:T(8,128)(2,1)S(1)}, u32[]{:S(2)}, u32[]{:S(2)}) collective-permute-start(bf16[128,576]{0,1:T(8,128)(2,1)S(1)} %copy-done.2), channel_id=1, source_target_pairs={{0,16},{1,17},{2,18},{3,19},{4,20},{5,21},{6,22},{7,23},{8,24},{9,... | collective-permute-start | bytes 442376 | tf_op jit(solution)/shard_map/ppermute | solution.py:16
  65.0 3.8 %copy-start.1 = (bf16[128,2304]{0,1:T(8,128)(2,1)S(1)}, bf16[128,2304]{0,1:T(8,128)(2,1)}, u32[]{:S(2)}) copy-start(bf16[128,2304]{0,1:T(8,128)(2,1)} %copy.16) | copy-start | bytes 1769476
  67.9 9.4 %collective-permute-start.11 = (bf16[2,32,2560]{2,1,0:T(8,128)(2,1)S(1)}, bf16[2,32,2560]{2,1,0:T(8,128)(2,1)S(1)}, u32[]{:S(2)}, u32[]{:S(2)}) collective-permute-start(bf16[2,32,2560]{2,1,0:T(8,128)(2,1)S(1)} %fusion.24), channel_id=1, source_target_pairs={{0,2},{1,3},{2,0},{3,1},{4,6},{5,7},{6,4},{7,5},{8,10},{9,11},{10,... | collective-permute-start | bytes 983048 | tf_op jit(solution)/shard_map/ppermute | solution.py:42
  77.4 6.2 %collective-permute-start.12 = (bf16[2,8,2560]{2,1,0:T(8,128)(2,1)S(1)}, bf16[2,8,2560]{2,1,0:T(8,128)(2,1)S(1)}, u32[]{:S(2)}, u32[]{:S(2)}) collective-permute-start(bf16[2,8,2560]{2,1,0:T(8,128)(2,1)S(1)} %get-tuple-element.14), channel_id=1, source_target_pairs={{0,12},{1,13},{2,14},{3,15},{4,0},{5,1},{6,2},{7,3},{8,4},{9,5},{1... | collective-permute-start | bytes 245768 | tf_op jit(solution)/shard_map/ppermute | solution.py:47
  79.4 6.2 %collective-permute-start.14 = (bf16[2,8,2560]{2,1,0:T(8,128)(2,1)S(1)}, bf16[2,8,2560]{2,1,0:T(8,128)(2,1)S(1)}, u32[]{:S(2)}, u32[]{:S(2)}) collective-permute-start(bf16[2,8,2560]{2,1,0:T(8,128)(2,1)S(1)} %get-tuple-element.15), channel_id=1, source_target_pairs={{0,4},{1,5},{2,6},{3,7},{4,8},{5,9},{6,10},{7,11},{8,12},{9,13},{1... | collective-permute-start | bytes 245768 | tf_op jit(solution)/shard_map/ppermute | solution.py:47
  79.5 7.4 %collective-permute-start.13 = (bf16[2,8,2560]{2,1,0:T(8,128)(2,1)S(1)}, bf16[2,8,2560]{2,1,0:T(8,128)(2,1)S(1)}, u32[]{:S(2)}, u32[]{:S(2)}) collective-permute-start(bf16[2,8,2560]{2,1,0:T(8,128)(2,1)S(1)} %get-tuple-element.16), channel_id=1, source_target_pairs={{0,8},{1,9},{2,10},{3,11},{4,12},{5,13},{6,14},{7,15},{8,0},{9,1},... | collective-permute-start | bytes 245768 | tf_op jit(solution)/shard_map/ppermute | solution.py:47
  87.0 4.5 %collective-permute-start.15 = (bf16[8,2560]{1,0:T(8,128)(2,1)S(1)}, bf16[8,2560]{1,0:T(8,128)(2,1)S(1)}, u32[]{:S(2)}, u32[]{:S(2)}) collective-permute-start(bf16[8,2560]{1,0:T(8,128)(2,1)S(1)} %slice_bitcast_fusion.6), channel_id=1, source_target_pairs={{0,16},{16,0},{1,17},{17,1},{2,18},{18,2},{3,19},{19,3},{4,20},{20... | collective-permute-start | bytes 122888 | tf_op jit(solution)/shard_map/ppermute | solution.py:42

commit v2 on v0

--- a/solution.py
+++ b/solution.py
@@ -1,6 +1,8 @@
 import jax
 import jax.numpy as jnp
 from jax import lax
+from jax.experimental import pallas as pl
+from jax.experimental.pallas import tpu as pltpu
 from jax.sharding import PartitionSpec as P
 
 LATENT = 512
@@ -38,7 +40,444 @@
     )
 
 
-def on_device(hidden, queries, latents, expert_ids, route_weight, w_gate, w_up, w_down):
+def swapped(block, axis, bit):
+    return lax.ppermute(block, axis, [(i, i ^ bit) for i in range(lax.axis_size(axis))])
+
+
+def moved(block, steps):
+    count = lax.axis_size("exp")
+    return lax.ppermute(block, "exp", [(i, (i + 4 * steps) % count) for i in range(count)])
+
+
+def paired(block, partner):
+    count = lax.axis_size("exp")
+    both = lax.axis_size("ctx") * count
+    route = []
+    for i in range(both):
+        ctx, exp = partner(i // count, i % count)
+        route.append((i, ctx * count + exp))
+    return lax.ppermute(block, ("ctx", "exp"), route)
+
+
+def over_y(ctx, exp):
+    return ctx, exp ^ 2
+
+
+def over_x(ctx, exp):
+    return 1 - ctx, exp
+
+
+def y_then_x(ctx, exp):
+    return over_x(ctx, exp) if exp % 2 else over_y(ctx, exp)
+
+
+def x_then_y(ctx, exp):
+    return over_y(ctx, exp) if exp % 2 else over_x(ctx, exp)
+
+
+def times_rows_in(left, right):
+    return lax.dot_general(
+        left, right, (((1,), (1,)), ((), ())), preferred_element_type=jnp.float32
+    )
+
+
+def in_vmem(array):
+    return pltpu.with_memory_space_constraint(array, pltpu.VMEM)
+
+
+def in_hbm(array):
+    return pltpu.with_memory_space_constraint(array, pltpu.HBM)
+
+
+def local_kernel(body, ins, outs, scratch, name, cost=None):
+    kinds = {"vmem": pltpu.VMEM, "hbm": pl.ANY}
+    place = {"vmem": in_vmem, "hbm": in_hbm}
+    made = [
+        pltpu.VMEM(shape, dtype) if kind == "vmem" else jax.ShapeDtypeStruct(shape, dtype)
+        for shape, dtype, kind in outs
+    ]
+    return pl.pallas_call(
+        body,
+        in_specs=[pl.BlockSpec(memory_space=kinds[kind]) for _, kind in ins],
+        out_specs=[pl.BlockSpec(memory_space=kinds[kind]) for _, _, kind in outs],
+        out_shape=made,
+        scratch_shapes=scratch,
+        compiler_params=pltpu.CompilerParams(vmem_limit_bytes=20 * 1024 * 1024),
+        cost_estimate=cost,
+        name=name,
+    )(*[place[kind](array) for array, kind in ins])
+
+
+def start_copies(pairs, sems, pieces):
+    copies = []
+    for number, (source, target) in enumerate(pairs):
+        step = target.shape[0] // pieces
+        for piece in range(pieces):
+            span = pl.ds(piece * step, step)
+            copy = pltpu.make_async_copy(
+                source.at[span, :], target.at[span, :], sems.at[number * pieces + piece]
+            )
+            copy.start()
+            copies.append(copy)
+    return copies
+
+
+PIECES = 4
+
+
+def rows_kernel(tokens_in, names_in, weights_in, out, tokens, names, weights, sems, *, half, topk):
+    copies = [
+        pltpu.make_async_copy(source, target, sems.at[number])
+        for number, (source, target) in enumerate(
+            ((tokens_in, tokens), (names_in, names), (weights_in, weights))
+        )
+    ]
+    for copy in copies:
+        copy.start()
+    for copy in copies:
+        copy.wait()
+    count = tokens.shape[0]
+    width = tokens.shape[1]
+    out[:, :half] = tokens[:, :half]
+    out[:, half + 128 :] = tokens[:, half:width]
+    lane = lax.broadcasted_iota(jnp.int32, (count, 128), 1)
+    same = lax.broadcasted_iota(jnp.int32, (count, count), 0) == lax.broadcasted_iota(
+        jnp.int32, (count, count), 1
+    )
+
+    def column(row):
+        return jnp.sum(
+            jnp.where(same, jnp.broadcast_to(row, same.shape), 0.0), axis=1, keepdims=True
+        )
+
+    note = jnp.zeros((count, 128), jnp.float32)
+    for k in range(topk):
+        name = column(names[k].astype(jnp.float32))
+        weight = column(weights[k])
+        low = weight - weight.astype(jnp.bfloat16).astype(jnp.float32)
+        for value, at in ((name, k), (weight, topk + k), (low, 2 * topk + k)):
+            note = jnp.where(lane == at, value, note)
+    out[:, half : half + 128] = note.astype(jnp.bfloat16)
+
+
+def fetch_kernel(after, gate_w, up_w, gate_out, up_out, sems):
+    half = gate_out.shape[1]
+    pairs = [(gate_w.at[:, :half], gate_out), (up_w.at[:, :half], up_out)]
+    for copy in start_copies(pairs, sems, PIECES):
+        copy.wait()
+
+
+def stack_kernel(*refs, cuts):
+    ins, outs = refs[: len(refs) - len(cuts)], refs[len(refs) - len(cuts) :]
+    for out, (low, high) in zip(outs, cuts):
+        if ins[0].shape[0] % 16 == 0:
+            at = 0
+            for ref in ins:
+                out[at : at + ref.shape[0], :] = ref[:, low:high]
+                at += ref.shape[0]
+        else:
+            rows = [ref[:, low:high].astype(jnp.float32) for ref in ins]
+            out[...] = jnp.concatenate(rows, axis=0).astype(out.dtype)
+
+
+def attention_kernel(
+    after, earlier, queries_in, latents_in, gate_all, up_all,
+    attended, gate_next, up_next, queries, latents, even, odd, mixed, sems, copy_sems,
+):
+    width, rows = latents.shape
+    half = gate_next.shape[1]
+    pad = even.shape[0] - width
+    loads = [
+        pltpu.make_async_copy(queries_in, queries, sems.at[0]),
+        pltpu.make_async_copy(latents_in, latents, sems.at[1]),
+    ]
+    for copy in loads:
+        copy.start()
+    pairs = [(gate_all.at[:, half:], gate_next), (up_all.at[:, half:], up_next)]
+    copies = start_copies(pairs, copy_sems, PIECES)
+    for copy in loads:
+        copy.wait()
+    even[width:, :] = jnp.zeros((pad, 2 * rows), jnp.bfloat16)
+    odd[:pad, :] = jnp.zeros((pad, 2 * rows), jnp.bfloat16)
+    even[:width, :rows] = earlier[...]
+    even[:width, rows:] = latents[...]
+    odd[pad:, :rows] = earlier[...]
+    odd[pad:, rows:] = latents[...]
+    row = lax.broadcasted_iota(jnp.int32, (rows, 2 * rows), 0)
+    key = lax.broadcasted_iota(jnp.int32, (rows, 2 * rows), 1)
+    nearest = jnp.where(lax.axis_index("ctx") > 0, 0, rows)
+    seen = (key >= nearest) & (key <= row + rows)
+    heads = attended.shape[1] // LATENT
+    writes = []
+    for head in range(heads):
+        start = head * width
+        keys, start = (even, start) if start % 128 == 0 else (odd, start - pad)
+        scores = jnp.dot(
+            queries[:, start : start + width + pad], keys[...], preferred_element_type=jnp.float32
+        )
+        scores = jnp.where(seen, scores * SCALE, jnp.float32(-1e30))
+        expo = jnp.exp(scores - jnp.max(scores, axis=-1, keepdims=True))
+        probs = (expo / jnp.sum(expo, axis=-1, keepdims=True)).astype(jnp.bfloat16)
+        span = slice(head * LATENT, (head + 1) * LATENT)
+        mixed[:, span] = times_rows_in(probs, even[:LATENT, :]).astype(jnp.bfloat16)
+        write = pltpu.make_async_copy(mixed.at[:, span], attended.at[:, span], sems.at[2 + head])
+        write.start()
+        writes.append(write)
+    for copy in writes + copies:
+        copy.wait()
+
+
+def assemble(place, core, two_ref, far_ref, two_other_ref, far_other_ref, unit, start=0):
+    span = slice(start, start + place.shape[1])
+    for lane, two, far in ((0, two_ref, far_ref), (1, two_other_ref, far_other_ref)):
+        went_x = core if lane == 0 else 1 - core
+        base = lane * 4 * unit
+        near = pl.multiple_of(base + (2 - went_x) * unit, unit)
+        next_ = pl.multiple_of(base + (1 + went_x) * unit, unit)
+        place[base : base + unit, :] = two[:unit, span]
+        place[pl.ds(near, unit), :] = two[unit:, span]
+        place[pl.ds(next_, unit), :] = far[:unit, span]
+        place[base + 3 * unit : base + 4 * unit, :] = far[unit:, span]
+
+
+def first_kernel(
+    two, far, two_other, far_other, gate_w, up_w,
+    gate_out, up_out, pick_out, pick_far_out, coef_out,
+    tokens, notes, *, unit, tok_dev, capacity, topk,
+):
+    width = tokens.shape[1]
+    rows = tokens.shape[0]
+    slots = pick_out.shape[1]
+    expert = lax.axis_index("exp")
+    assemble(tokens, expert % 2, two, far, two_other, far_other, unit)
+    gate_out[...] = times_rows_in(tokens[...], gate_w[...])
+    up_out[...] = times_rows_in(tokens[...], up_w[...])
+
+    assemble(notes, expert % 2, two, far, two_other, far_other, unit, width)
+    note = notes[...].astype(jnp.float32)
+    lane = lax.broadcasted_iota(jnp.int32, note.shape, 1)
+    mine = (note == expert.astype(jnp.float32)) & (lane < topk)
+    weight = pltpu.roll(note, 128 - topk, 1) + pltpu.roll(note, 128 - 2 * topk, 1)
+    coef = jnp.sum(jnp.where(mine, weight, 0.0), axis=1, keepdims=True)
+    hit = jnp.sum(mine.astype(jnp.float32), axis=1, keepdims=True)
+    shift = tok_dev.bit_length() - 1
+    at = lax.broadcasted_iota(jnp.int32, (rows, rows), 0)
+    before = lax.broadcasted_iota(jnp.int32, (rows, rows), 1)
+    earlier = ((at >> shift) == (before >> shift)) & (before < at)
+    hits = jnp.broadcast_to(hit, (rows, slots))
+    rank = jnp.dot(
+        earlier.astype(jnp.float32).astype(jnp.bfloat16),
+        hits.astype(jnp.bfloat16),
+        preferred_element_type=jnp.float32,
+    ).astype(jnp.int32)
+    row = lax.broadcasted_iota(jnp.int32, (rows, slots), 0)
+    slot = (row >> shift) * capacity + rank
+    group = unit // tok_dev * capacity
+    away = ((row >> (unit.bit_length() - 1)) & 1) == 0
+    slot_far = slot + jnp.where(away, group, -group)
+    column = lax.broadcasted_iota(jnp.int32, (rows, slots), 1)
+    pick_out[...] = jnp.where(slot == column, hits, 0.0).astype(jnp.bfloat16)
+    pick_far_out[...] = jnp.where(slot_far == column, hits, 0.0).astype(jnp.bfloat16)
+    coef_out[...] = jnp.broadcast_to(coef, coef_out.shape)
+
+
+def second_kernel(
+    two, far, two_other, far_other, gate_w, up_w, gate_in, up_in, pick,
+    act_out, packed_out, tokens, *, unit, wide,
+):
+    units = act_out.shape[1]
+    assemble(tokens, lax.axis_index("exp") % 2, two, far, two_other, far_other, unit)
+    for n in range(0, units, wide):
+        span = slice(n, n + wide)
+        gate = gate_in[:, span] + times_rows_in(tokens[...], gate_w[span, :])
+        upper = up_in[:, span] + times_rows_in(tokens[...], up_w[span, :])
+        act = (gate / (1.0 + jnp.exp(-gate)) * upper).astype(jnp.bfloat16)
+        act_out[:, span] = act
+        packed_out[:, span] = lax.dot_general(
+            pick[...], act, (((0,), (0,)), ((), ())), preferred_element_type=jnp.float32
+        ).astype(jnp.bfloat16)
+
+
+def own_kernel(act, down_w, out, down_other, down_own, sems):
+    units = act.shape[1]
+    ctx = lax.axis_index("ctx")
+    own_at = pl.multiple_of(ctx * units, 128)
+    other_at = pl.multiple_of((1 - ctx) * units, 128)
+    pairs = [
+        (down_w.at[:, pl.ds(own_at, units)], down_own),
+        (down_w.at[:, pl.ds(other_at, units)], down_other),
+    ]
+    copies = start_copies(pairs, sems, PIECES)
+    tall = out.shape[1] // PIECES
+    for piece in range(PIECES):
+        copies[piece].wait()
+        span = slice(piece * tall, (piece + 1) * tall)
+        out[:, span] = times_rows_in(act[...], down_own[span, :])
+    for copy in copies[PIECES:]:
+        copy.wait()
+
+
+def other_kernel(packed, pick, coef, down_w, own, keep, give, act, *, tall, start):
+    act[...] = jnp.dot(pick[...], packed[...], preferred_element_type=jnp.float32).astype(
+        jnp.bfloat16
+    )
+    half = keep.shape[0]
+    for n in range(0, keep.shape[1], tall):
+        span = slice(start + n, start + n + tall)
+        projected = own[:, span] + times_rows_in(act[...], down_w[span, :])
+        projected = projected * coef[:, :1]
+        keep[:, n : n + tall] = projected[:half].astype(jnp.bfloat16)
+        give[:, n : n + tall] = projected[half:].astype(jnp.bfloat16)
+
+
+def on_device_gathered(
+    hidden, queries, latents, expert_ids, route_weight, w_gate, w_up, w_down
+):
+    tok_dev = hidden.shape[1]
+    width = hidden.shape[2]
+    topk = expert_ids.shape[2]
+    units = w_gate.shape[1]
+    columns = w_down.shape[1]
+    tok_att, key_width = latents.shape
+    heads_dev = queries.shape[1] // key_width
+    experts = lax.axis_size("exp")
+    line = experts // 4
+    capacity = min(tok_dev, max(2, 3 * topk * tok_dev // (2 * experts)))
+    half = width // 2
+    unit = line * tok_dev
+    count = 8 * unit
+    slots = count // tok_dev * capacity
+    bf16, f32 = jnp.bfloat16, jnp.float32
+    first = lax.axis_index("ctx") == 0
+    copy_sems = pltpu.SemaphoreType.DMA((2 * PIECES,))
+
+    (rows,) = local_kernel(
+        lambda *refs: rows_kernel(*refs, half=half, topk=topk),
+        [
+            (hidden[0], "hbm"),
+            (jnp.transpose(expert_ids, (2, 0, 1)), "hbm"),
+            (jnp.transpose(route_weight, (2, 0, 1)), "hbm"),
+        ],
+        [((tok_dev, width + 128), bf16, "vmem")],
+        [
+            pltpu.VMEM((tok_dev, width), bf16),
+            pltpu.VMEM((topk, 1, tok_dev), jnp.int32),
+            pltpu.VMEM((topk, 1, tok_dev), f32),
+            pltpu.SemaphoreType.DMA((3,)),
+        ],
+        "rows",
+    )
+    along = [rows] + [moved(rows, d) for d in range(1, line)]
+    earlier_kv = swapped(latents.T, "ctx", 1)
+    gate_1, up_1 = local_kernel(
+        fetch_kernel,
+        [(rows, "vmem"), (w_gate[0], "hbm"), (w_up[0], "hbm")],
+        [((units, half), bf16, "vmem")] * 2,
+        [copy_sems],
+        "fetch",
+    )
+    *along, earlier_kv, gate_1, up_1 = lax.optimization_barrier((*along, earlier_kv, gate_1, up_1))
+    cuts = ((0, half + 128), (half + 128, width + 128))
+    nears = local_kernel(
+        lambda *refs: stack_kernel(*refs, cuts=cuts),
+        [(row, "vmem") for row in along],
+        [((unit, high - low), bf16, "vmem") for low, high in cuts],
+        [],
+        "stack_line",
+    )
+    pad = -key_width % 128
+    attended, gate_2, up_2 = local_kernel(
+        attention_kernel,
+        [
+            (nears[1], "vmem"), (earlier_kv, "vmem"), (queries, "hbm"), (latents.T, "hbm"),
+            (w_gate[0], "hbm"), (w_up[0], "hbm"),
+        ],
+        [((tok_att, heads_dev * LATENT), bf16, "hbm")] + [((units, half), bf16, "vmem")] * 2,
+        [
+            pltpu.VMEM((tok_att, heads_dev * key_width), bf16),
+            pltpu.VMEM((key_width, tok_att), bf16),
+            pltpu.VMEM((key_width + pad, 2 * tok_att), bf16),
+            pltpu.VMEM((key_width + pad, 2 * tok_att), bf16),
+            pltpu.VMEM((tok_att, heads_dev * LATENT), bf16),
+            pltpu.SemaphoreType.DMA((2 + heads_dev,)),
+            copy_sems,
+        ],
+        "attention",
+    )
+    passed = [paired(near, y_then_x) for near in nears]
+    passed[0], gate_2, up_2 = lax.optimization_barrier((passed[0], gate_2, up_2))
+    pieces = []
+    for near, got in zip(nears, passed):
+        shape = (2 * unit, near.shape[1])
+        (two,) = local_kernel(
+            lambda *refs, cut=near.shape[1]: stack_kernel(*refs, cuts=((0, cut),)),
+            [(near, "vmem"), (got, "vmem")],
+            [(shape, bf16, "vmem")],
+            [],
+            "stack_two",
+        )
+        far = paired(two, x_then_y)
+        group = (two, far, swapped(two, "exp", 1), swapped(far, "exp", 1))
+        pieces.append([(piece, "vmem") for piece in group])
+
+    gate, up, pick, pick_far, coef = local_kernel(
+        lambda *refs: first_kernel(
+            *refs, unit=unit, tok_dev=tok_dev, capacity=capacity, topk=topk
+        ),
+        [*pieces[0], (gate_1, "vmem"), (up_1, "vmem")],
+        [((count, units), f32, "vmem")] * 2
+        + [((count, slots), bf16, "vmem")] * 2
+        + [((count, 128), f32, "vmem")],
+        [pltpu.VMEM((count, half), bf16), pltpu.VMEM((count, 128), bf16)],
+        "gate_up_first",
+    )
+    act, packed = local_kernel(
+        lambda *refs: second_kernel(*refs, unit=unit, wide=256),
+        [
+            *pieces[1], (gate_2, "vmem"), (up_2, "vmem"),
+            (gate, "vmem"), (up, "vmem"), (pick, "vmem"),
+        ],
+        [((count, units), bf16, "vmem"), ((slots, units), bf16, "vmem")],
+        [pltpu.VMEM((count, half), bf16)],
+        "gate_up_second",
+    )
+    other = swapped(packed, "ctx", 1)
+    own, down_other = local_kernel(
+        own_kernel,
+        [(act, "vmem"), (w_down[0], "hbm")],
+        [((count, columns), f32, "vmem"), ((columns, units), bf16, "vmem")],
+        [pltpu.VMEM((columns, units), bf16), copy_sems],
+        "down_own",
+    )
+    sums = []
+    part = columns // 2
+    for start in (0, part):
+        keep, give = local_kernel(
+            lambda *refs, start=start: other_kernel(*refs, tall=256, start=start),
+            [
+                (other, "vmem"), (pick_far, "vmem"), (coef, "vmem"),
+                (down_other, "vmem"), (own, "vmem"),
+            ],
+            [((count // 2, part), bf16, "vmem")] * 2,
+            [pltpu.VMEM((count, units), bf16)],
+            "down_other",
+        )
+        total = keep.astype(f32) + swapped(give, "exp", 1).astype(f32)
+        total = total[: 2 * unit] + swapped(total[2 * unit :].astype(bf16), "exp", 2).astype(f32)
+        sums.append(total)
+    total = jnp.concatenate(sums, axis=1).reshape(2, line, tok_dev, columns)
+    parts = [moved(total[:, d].astype(bf16), line - d) for d in range(1, line)]
+    total = total[:, 0] + sum(part.astype(f32) for part in parts)
+    total = total.astype(bf16)
+    far = swapped(total[1], "ctx", 1)
+    near = total[0]
+    mixed = jnp.concatenate(
+        [jnp.where(first, near, far), jnp.where(first, far, near)], axis=1
+    )
+    return (attended, mixed[None])
+
+
+def on_device_slots(hidden, queries, latents, expert_ids, route_weight, w_gate, w_up, w_down):
     tok_att = latents.shape[0]
     heads_dev = queries.shape[1] // (LATENT + ROPE)
     tok_dev = hidden.shape[1]
@@ -95,6 +534,9 @@
 
 
 def solution(mesh):
+    experts, groups = mesh.shape["exp"], mesh.shape["ctx"]
+    whole = groups == 2 and experts % 4 == 0 and experts <= 16
+    on_device = on_device_gathered if whole else on_device_slots
     placed = (
         P("exp", "ctx", None),
         P("ctx", "exp"),

time: 128 us -> 73.6 us (0.57)
  blocking collectives: 32.9 us -> 0 us
  Pallas kernels: 0 us -> 20.3 us
  matrix products: 17.9 us -> 0 us
  between operations: 14.2 us -> 0.83 us
  waiting for transfers between devices: 41.4 us -> 30.1 us
  starting transfers between devices: 13.1 us -> 21.3 us
  local copies, waits for them, and re-layouts: 6.9 us -> 0.07 us
    ppermute x1 -> x21, waiting for transfers between devices: 0.01 us -> 30.1 us  [the longest x11 14.2 us: swapped(): lax.ppermute(block, axis, [(i, i ^ bit) for i in range(lax.axis_size(axis...]
    all_to_all x1 -> x0, blocking collectives: 25.4 us -> none  [on_device(): lax.all_to_all(outgoing, 'exp', split_axis=0, concat_axis=0, tiled=True)]
    all_gather x1 -> x0, waiting for transfers between devices: 23 us -> none  [on_device(): lax.all_gather(arrived.reshape(slots, width), 'ctx', axis=0, tiled=True)]
    pallas_call x0 -> x11, Pallas kernels: none -> 20.3 us  [local_kernel(): pl.pallas_call(body, in_specs=[pl.BlockSpec(memory_space=kinds[kind]) for...]
    all_to_all x2 -> x0, waiting for transfers between devices: 18.4 us -> none  [the longest x1 14.1 us: on_device(): lax.all_to_all(by_block, 'exp', split_axis=1, concat_axis=1, tiled=True)]
    dot_general x8 -> x0, matrix products: 17.9 us -> none  [the longest x3 15.3 us: times_rows(): lax.dot_general(left, right, (((1,), (1,)), ((), ())), preferred_element_...]
    ppermute x1 -> x21, starting transfers between devices: 3.9 us -> 21.3 us  [the longest x6 9.37 us: moved(): lax.ppermute(block, 'exp', [(i, (i + 4 * steps) % count) for i in range(c...]
    all_to_all x2 -> x0, starting transfers between devices: 9.13 us -> none  [the longest x1 5.62 us: on_device(): lax.all_to_all(by_block, 'exp', split_axis=1, concat_axis=1, tiled=True)]
  transfers between devices with their start and end apart: 4 -> 21, of which waited for: 3 -> 10; matrix products, arithmetic and copies ran while one was open for 4% -> 0% of each run, Pallas kernels for 0% -> 23%
where the time goes in v2:
time: 73.6 us; the launch traced here: 73.4 us
  waiting for transfers between devices  30.1 us (41%)
  starting transfers between devices  21.3 us (29%)
  Pallas kernels  20.3 us (28%)
  other arithmetic  0.93 us (1%)
  between operations  0.83 us (1%)
    pallas_call x11, Pallas kernels, local_kernel(): pl.pallas_call(body, in_specs=[pl.BlockSpec(memory_space=kinds[kind]) for...  20.3 us
    ppermute x11, waiting for transfers between devices, swapped(): lax.ppermute(block, axis, [(i, i ^ bit) for i in range(lax.axis_size(axis...  14.2 us
    ppermute x6, starting transfers between devices, moved(): lax.ppermute(block, 'exp', [(i, (i + 4 * steps) % count) for i in range(c...  9.37 us
    ppermute x4, waiting for transfers between devices, paired(): return lax.ppermute(block, ('ctx', 'exp'), route)  8.13 us
    ppermute x6, waiting for transfers between devices, moved(): lax.ppermute(block, 'exp', [(i, (i + 4 * steps) % count) for i in range(c...  7.76 us
    ppermute x11, starting transfers between devices, swapped(): lax.ppermute(block, axis, [(i, i ^ bit) for i in range(lax.axis_size(axis...  7.66 us
    ppermute x4, starting transfers between devices, paired(): return lax.ppermute(block, ('ctx', 'exp'), route)  4.25 us
  transfers between devices with their start and end apart: 21, of which 10 were waited for; matrix products, arithmetic and copies ran while one was open for 0% of the time, Pallas kernels for 23%

profile of v2, /device:TPU:0, one launch (start us, length us, event | category | flops | bytes accessed | tf_op | source)
XLA Modules:
  0.0 73.4 jit_solution(10003476577635822970)
XLA Ops:
  0.6 3.0 %collective-permute-start.3 = (bf16[576,128]{1,0:T(8,128)(2,1)}, bf16[576,128]{1,0:T(8,128)(2,1)S(1)}, u32[]{:S(2)}, u32[]{:S(2)}) collective-permute-start(bf16[576,128]{1,0:T(8,128)(2,1)} %bitcast.37), channel_id=1, source_target_pairs={{0,16},{16,0},{1,17},{17,1},{2,18},{18,2},{3,19},{19,3},{4,20},{20... | collective-permute-start | bytes 442376 | tf_op jit(solution)/shard_map/ppermute | solution.py:44
  3.6 1.0 %rows.1.after.refs_0_ = bf16[8,5248]{1,0:T(8,128)(2,1)S(1)} custom-call(bf16[8,5120]{1,0:T(8,128)(2,1)} %bitcast.39, s32[6,1,8]{2,1,0:T(1,128)} %bitcast.40, f32[6,1,8]{2,1,0:T(1,128)} %bitcast.41), custom_call_target="tpu_custom_call" | custom-call | tf_op jit(solution)/shard_map/rows/pallas_call | solution.py:99
  4.7 1.6 %collective-permute-start = (bf16[8,5248]{1,0:T(8,128)(2,1)S(1)}, bf16[8,5248]{1,0:T(8,128)(2,1)S(1)}, u32[]{:S(2)}, u32[]{:S(2)}) collective-permute-start(bf16[8,5248]{1,0:T(8,128)(2,1)S(1)} %rows.1.after.refs_0_), channel_id=1, source_target_pairs={{0,4},{1,5},{2,6},{3,7},{4,8},{5,9},{6,10},{7,11},{8,12},{9,13},{1... | collective-permute-start | bytes 251912 | tf_op jit(solution)/shard_map/ppermute | solution.py:49
  6.3 2.6 %collective-permute-start.1 = (bf16[8,5248]{1,0:T(8,128)(2,1)S(1)}, bf16[8,5248]{1,0:T(8,128)(2,1)S(1)}, u32[]{:S(2)}, u32[]{:S(2)}) collective-permute-start(bf16[8,5248]{1,0:T(8,128)(2,1)S(1)} %rows.1.after.refs_0_), channel_id=1, source_target_pairs={{0,8},{1,9},{2,10},{3,11},{4,12},{5,13},{6,14},{7,15},{8,0},{9,1},... | collective-permute-start | bytes 251912 | tf_op jit(solution)/shard_map/ppermute | solution.py:49
  8.9 1.3 %collective-permute-start.2 = (bf16[8,5248]{1,0:T(8,128)(2,1)S(1)}, bf16[8,5248]{1,0:T(8,128)(2,1)S(1)}, u32[]{:S(2)}, u32[]{:S(2)}) collective-permute-start(bf16[8,5248]{1,0:T(8,128)(2,1)S(1)} %rows.1.after.refs_0_), channel_id=1, source_target_pairs={{0,12},{1,13},{2,14},{3,15},{4,0},{5,1},{6,2},{7,3},{8,4},{9,5},{1... | collective-permute-start | bytes 251912 | tf_op jit(solution)/shard_map/ppermute | solution.py:49
  10.2 3.3 %fetch.1 = (bf16[768,2560]{1,0:T(8,128)(2,1)S(1)}, bf16[768,2560]{1,0:T(8,128)(2,1)S(1)}) custom-call(bf16[8,5248]{1,0:T(8,128)(2,1)S(1)} %rows.1.after.refs_0_, bf16[768,5120]{1,0:T(8,128)(2,1)} %bitcast.30, bf16[768,5120]{1,0:T(8,128)(2,1)} %bitcast.32), custom_call_target="tpu_custom_call" | custom-call | tf_op jit(solution)/shard_map/fetch/pallas_call | solution.py:99
  13.6 1.1 %collective-permute-done.1.refs_2_ = bf16[8,5248]{1,0:T(8,128)(2,1)S(1)} collective-permute-done((bf16[8,5248]{1,0:T(8,128)(2,1)S(1)}, bf16[8,5248]{1,0:T(8,128)(2,1)S(1)}, u32[]{:S(2)}, u32[]{:S(2)}) %collective-permute-start.1) | collective-permute-done | bytes 84000 | tf_op jit(solution)/shard_map/ppermute | solution.py:49
  14.7 1.6 %collective-permute-start.8 = (bf16[32,2688]{1,0:T(8,128)(2,1)S(1)}, bf16[32,2688]{1,0:T(8,128)(2,1)S(1)}, u32[]{:S(2)}, u32[]{:S(2)}) collective-permute-start(bf16[32,2688]{1,0:T(8,128)(2,1)S(1)} %get-tuple-element.41.refs_0_), channel_id=1, source_target_pairs={{0,2},{1,17},{2,0},{3,19},{4,6},{5,21},{6,4},{7,23},{8,10},{9,25},... | collective-permute-start | bytes 516104 | tf_op jit(solution)/shard_map/ppermute | solution.py:59
  16.2 0.5 collective-permute-start.4
  16.8 5.5 %attention.1 = (bf16[128,2048]{1,0:T(8,128)(2,1)}, bf16[768,2560]{1,0:T(8,128)(2,1)S(1)}, bf16[768,2560]{1,0:T(8,128)(2,1)S(1)}) custom-call(bf16[32,2560]{1,0:T(8,128)(2,1)S(1)} %get-tuple-element.38.after.refs_0_, bf16[576,128]{1,0:T(8,128)(2,1)S(1)} %collective-permute-done.3.earlier, bf16[128,2304]{1,0:T(8,128)(2,1)} %queries_in.1, ...), custom_call_target="tpu_custom_call" | custom-call | tf_op jit(solution)/shard_map/attention/pallas_call | solution.py:99
  22.7 1.8 %collective-permute-start.5 = (bf16[64,2560]{1,0:T(8,128)(2,1)S(1)}, bf16[64,2560]{1,0:T(8,128)(2,1)S(1)}, u32[]{:S(2)}, u32[]{:S(2)}) collective-permute-start(bf16[64,2560]{1,0:T(8,128)(2,1)S(1)} %stack_two.2.refs_0_), channel_id=1, source_target_pairs={{0,16},{1,3},{2,18},{3,1},{4,20},{5,7},{6,22},{7,5},{8,24},{9,11},... | collective-permute-start | bytes 983048 | tf_op jit(solution)/shard_map/ppermute | solution.py:59
  24.4 5.1 %collective-permute-done.9.refs_1_ = bf16[64,2688]{1,0:T(8,128)(2,1)S(1)} collective-permute-done((bf16[64,2688]{1,0:T(8,128)(2,1)S(1)}, bf16[64,2688]{1,0:T(8,128)(2,1)S(1)}, u32[]{:S(2)}, u32[]{:S(2)}) %collective-permute-start.9) | collective-permute-done | bytes 344096 | tf_op jit(solution)/shard_map/ppermute | solution.py:59
  29.6 0.5 collective-permute-start.6
  30.1 3.0 %collective-permute-done.5.refs_1_ = bf16[64,2560]{1,0:T(8,128)(2,1)S(1)} collective-permute-done((bf16[64,2560]{1,0:T(8,128)(2,1)S(1)}, bf16[64,2560]{1,0:T(8,128)(2,1)S(1)}, u32[]{:S(2)}, u32[]{:S(2)}) %collective-permute-start.5) | collective-permute-done | bytes 327712 | tf_op jit(solution)/shard_map/ppermute | solution.py:59
  33.1 2.3 %gate_up_first.1 = (f32[256,768]{1,0:T(8,128)S(1)}, f32[256,768]{1,0:T(8,128)S(1)}, bf16[256,128]{1,0:T(8,128)(2,1)S(1)}, bf16[256,128]{1,0:T(8,128)(2,1)S(1)}, f32[256,128]{1,0:T(8,128)S(1)}) custom-call(bf16[64,2688]{1,0:T(8,128)(2,1)S(1)} %stack_two.3.refs_0_, bf16[64,2688]{1,0:T(8,128)(2,1)S(1)} %collective-permute-done.9.refs_1_, ...), custom_call_target="tpu_custom_call" | custom-call | tf_op jit(solution)/shard_map/gate_up_first/pallas_call | solution.py:99
  35.4 2.8 %gate_up_second.1 = (bf16[256,768]{1,0:T(8,128)(2,1)S(1)}, bf16[128,768]{1,0:T(8,128)(2,1)S(1)}) custom-call(bf16[64,2560]{1,0:T(8,128)(2,1)S(1)} %stack_two.2.refs_0_, bf16[64,2560]{1,0:T(8,128)(2,1)S(1)} %collective-permute-done.5.refs_1_, bf16[64,2560]{1,0:T(8,128)(2,1)S(1)} %collective-permute-done.6.refs_2_, ...), custom_call_target="tpu_custom_call" | custom-call | tf_op jit(solution)/shard_map/gate_up_second/pallas_call | solution.py:99
  38.6 3.7 %down_own.1 = (f32[256,2560]{1,0:T(8,128)S(1)}, bf16[2560,768]{1,0:T(8,128)(2,1)S(1)}) custom-call(bf16[256,768]{1,0:T(8,128)(2,1)S(1)} %get-tuple-element.55.act, bf16[2560,1536]{1,0:T(8,128)(2,1)} %bitcast.34), custom_call_target="tpu_custom_call" | custom-call | tf_op jit(solution)/shard_map/down_own/pallas_call | solution.py:99
  42.3 3.3 %collective-permute-done.12.refs_0_ = bf16[128,768]{1,0:T(8,128)(2,1)S(1)} collective-permute-done((bf16[128,768]{1,0:T(8,128)(2,1)S(1)}, bf16[128,768]{1,0:T(8,128)(2,1)S(1)}, u32[]{:S(2)}, u32[]{:S(2)}) %collective-permute-start.12) | collective-permute-done | bytes 196640 | tf_op jit(solution)/shard_map/ppermute | solution.py:44
  45.6 0.8 %down_other.2 = (bf16[128,1280]{1,0:T(8,128)(2,1)S(1)}, bf16[128,1280]{1,0:T(8,128)(2,1)S(1)}) custom-call(bf16[128,768]{1,0:T(8,128)(2,1)S(1)} %collective-permute-done.12.refs_0_, bf16[256,128]{1,0:T(8,128)(2,1)S(1)} %get-tuple-element.53.refs_1_, f32[256,128]{1,0:T(8,128)S(1)} %get-tuple-element.54.refs_2_, ...), custom_call_target="tpu_custom_call" | custom-call | tf_op jit(solution)/shard_map/down_other/pallas_call | solution.py:99
  46.5 0.8 %down_other.3 = (bf16[128,1280]{1,0:T(8,128)(2,1)S(1)}, bf16[128,1280]{1,0:T(8,128)(2,1)S(1)}) custom-call(bf16[128,768]{1,0:T(8,128)(2,1)S(1)} %collective-permute-done.12.refs_0_, bf16[256,128]{1,0:T(8,128)(2,1)S(1)} %get-tuple-element.53.refs_1_, f32[256,128]{1,0:T(8,128)S(1)} %get-tuple-element.54.refs_2_, ...), custom_call_target="tpu_custom_call" | custom-call | tf_op jit(solution)/shard_map/down_other/pallas_call | solution.py:99
  47.3 0.6 collective-permute-start.15
  48.2 1.6 %collective-permute-start.14 = (bf16[64,1280]{1,0:T(8,128)(2,1)S(1)}, bf16[64,1280]{1,0:T(8,128)(2,1)S(1)}, u32[]{:S(2)}, u32[]{:S(2)}) collective-permute-start(bf16[64,1280]{1,0:T(8,128)(2,1)S(1)} %slice.74), channel_id=1, source_target_pairs={{0,2},{1,3},{2,0},{3,1},{4,6},{5,7},{6,4},{7,5},{8,10},{9,11},{10,... | collective-permute-start | bytes 491528 | tf_op jit(solution)/shard_map/ppermute | solution.py:44
  49.9 0.9 %collective-permute-start.16 = (bf16[64,1280]{1,0:T(8,128)(2,1)S(1)}, bf16[64,1280]{1,0:T(8,128)(2,1)S(1)}, u32[]{:S(2)}, u32[]{:S(2)}) collective-permute-start(bf16[64,1280]{1,0:T(8,128)(2,1)S(1)} %slice.73), channel_id=1, source_target_pairs={{0,2},{1,3},{2,0},{3,1},{4,6},{5,7},{6,4},{7,5},{8,10},{9,11},{10,... | collective-permute-start | bytes 491528 | tf_op jit(solution)/shard_map/ppermute | solution.py:44
  50.8 4.5 %collective-permute-done.14 = bf16[64,1280]{1,0:T(8,128)(2,1)S(1)} collective-permute-done((bf16[64,1280]{1,0:T(8,128)(2,1)S(1)}, bf16[64,1280]{1,0:T(8,128)(2,1)S(1)}, u32[]{:S(2)}, u32[]{:S(2)}) %collective-permute-start.14) | collective-permute-done | bytes 163872 | tf_op jit(solution)/shard_map/ppermute | solution.py:44
  55.3 2.7 %collective-permute-done.16 = bf16[64,1280]{1,0:T(8,128)(2,1)S(1)} collective-permute-done((bf16[64,1280]{1,0:T(8,128)(2,1)S(1)}, bf16[64,1280]{1,0:T(8,128)(2,1)S(1)}, u32[]{:S(2)}, u32[]{:S(2)}) %collective-permute-start.16) | collective-permute-done | bytes 163872 | tf_op jit(solution)/shard_map/ppermute | solution.py:44
  58.1 3.2 %collective-permute-start.17 = (bf16[2,8,2560]{2,1,0:T(8,128)(2,1)S(1)}, bf16[2,8,2560]{2,1,0:T(8,128)(2,1)S(1)}, u32[]{:S(2)}, u32[]{:S(2)}) collective-permute-start(bf16[2,8,2560]{2,1,0:T(8,128)(2,1)S(1)} %get-tuple-element.62), channel_id=1, source_target_pairs={{0,12},{1,13},{2,14},{3,15},{4,0},{5,1},{6,2},{7,3},{8,4},{9,5},{1... | collective-permute-start | bytes 245768 | tf_op jit(solution)/shard_map/ppermute | solution.py:49
  61.5 0.4 collective-permute-start.19
  61.9 2.3 %collective-permute-done.17 = bf16[2,8,2560]{2,1,0:T(8,128)(2,1)S(1)} collective-permute-done((bf16[2,8,2560]{2,1,0:T(8,128)(2,1)S(1)}, bf16[2,8,2560]{2,1,0:T(8,128)(2,1)S(1)}, u32[]{:S(2)}, u32[]{:S(2)}) %collective-permute-start.17) | collective-permute-done | bytes 81952 | tf_op jit(solution)/shard_map/ppermute | solution.py:49
  64.2 4.4 %collective-permute-done.18 = bf16[2,8,2560]{2,1,0:T(8,128)(2,1)S(1)} collective-permute-done((bf16[2,8,2560]{2,1,0:T(8,128)(2,1)S(1)}, bf16[2,8,2560]{2,1,0:T(8,128)(2,1)S(1)}, u32[]{:S(2)}, u32[]{:S(2)}) %collective-permute-start.18) | collective-permute-done | bytes 81952 | tf_op jit(solution)/shard_map/ppermute | solution.py:49
  68.7 0.6 collective-permute-start.20
  69.3 3.5 %collective-permute-done.20 = bf16[8,2560]{1,0:T(8,128)(2,1)S(1)} collective-permute-done((bf16[8,2560]{1,0:T(8,128)(2,1)S(1)}, bf16[8,2560]{1,0:T(8,128)(2,1)S(1)}, u32[]{:S(2)}, u32[]{:S(2)}) %collective-permute-start.20) | collective-permute-done | bytes 40992 | tf_op jit(solution)/shard_map/ppermute | solution.py:44
  72.8 0.6 maximum_bitcast_fusion
  (33 shorter events, 1.8 us)
Async XLA Ops:
  0.6 14.0 %collective-permute-start.3 = (bf16[576,128]{1,0:T(8,128)(2,1)}, bf16[576,128]{1,0:T(8,128)(2,1)S(1)}, u32[]{:S(2)}, u32[]{:S(2)}) collective-permute-start(bf16[576,128]{1,0:T(8,128)(2,1)} %bitcast.37), channel_id=1, source_target_pairs={{0,16},{16,0},{1,17},{17,1},{2,18},{18,2},{3,19},{19,3},{4,20},{20... | collective-permute-start | bytes 442376 | tf_op jit(solution)/shard_map/ppermute | solution.py:44
  4.7 8.9 %collective-permute-start = (bf16[8,5248]{1,0:T(8,128)(2,1)S(1)}, bf16[8,5248]{1,0:T(8,128)(2,1)S(1)}, u32[]{:S(2)}, u32[]{:S(2)}) collective-permute-start(bf16[8,5248]{1,0:T(8,128)(2,1)S(1)} %rows.1.after.refs_0_), channel_id=1, source_target_pairs={{0,4},{1,5},{2,6},{3,7},{4,8},{5,9},{6,10},{7,11},{8,12},{9,13},{1... | collective-permute-start | bytes 251912 | tf_op jit(solution)/shard_map/ppermute | solution.py:49
  6.3 8.3 %collective-permute-start.1 = (bf16[8,5248]{1,0:T(8,128)(2,1)S(1)}, bf16[8,5248]{1,0:T(8,128)(2,1)S(1)}, u32[]{:S(2)}, u32[]{:S(2)}) collective-permute-start(bf16[8,5248]{1,0:T(8,128)(2,1)S(1)} %rows.1.after.refs_0_), channel_id=1, source_target_pairs={{0,8},{1,9},{2,10},{3,11},{4,12},{5,13},{6,14},{7,15},{8,0},{9,1},... | collective-permute-start | bytes 251912 | tf_op jit(solution)/shard_map/ppermute | solution.py:49
  8.9 5.8 %collective-permute-start.2 = (bf16[8,5248]{1,0:T(8,128)(2,1)S(1)}, bf16[8,5248]{1,0:T(8,128)(2,1)S(1)}, u32[]{:S(2)}, u32[]{:S(2)}) collective-permute-start(bf16[8,5248]{1,0:T(8,128)(2,1)S(1)} %rows.1.after.refs_0_), channel_id=1, source_target_pairs={{0,12},{1,13},{2,14},{3,15},{4,0},{5,1},{6,2},{7,3},{8,4},{9,5},{1... | collective-permute-start | bytes 251912 | tf_op jit(solution)/shard_map/ppermute | solution.py:49
  14.7 7.6 %collective-permute-start.8 = (bf16[32,2688]{1,0:T(8,128)(2,1)S(1)}, bf16[32,2688]{1,0:T(8,128)(2,1)S(1)}, u32[]{:S(2)}, u32[]{:S(2)}) collective-permute-start(bf16[32,2688]{1,0:T(8,128)(2,1)S(1)} %get-tuple-element.41.refs_0_), channel_id=1, source_target_pairs={{0,2},{1,17},{2,0},{3,19},{4,6},{5,21},{6,4},{7,23},{8,10},{9,25},... | collective-permute-start | bytes 516104 | tf_op jit(solution)/shard_map/ppermute | solution.py:59
  16.2 6.4 %collective-permute-start.4 = (bf16[32,2560]{1,0:T(8,128)(2,1)S(1)}, bf16[32,2560]{1,0:T(8,128)(2,1)S(1)}, u32[]{:S(2)}, u32[]{:S(2)}) collective-permute-start(bf16[32,2560]{1,0:T(8,128)(2,1)S(1)} %get-tuple-element.38.after.refs_0_), channel_id=1, source_target_pairs={{0,2},{1,17},{2,0},{3,19},{4,6},{5,21},{6,4},{7,23},{8,10},{9,25},... | collective-permute-start | bytes 491528 | tf_op jit(solution)/shard_map/ppermute | solution.py:59
  22.3 7.3 %collective-permute-start.9 = (bf16[64,2688]{1,0:T(8,128)(2,1)S(1)}, bf16[64,2688]{1,0:T(8,128)(2,1)S(1)}, u32[]{:S(2)}, u32[]{:S(2)}) collective-permute-start(bf16[64,2688]{1,0:T(8,128)(2,1)S(1)} %stack_two.3.refs_0_), channel_id=1, source_target_pairs={{0,16},{1,3},{2,18},{3,1},{4,20},{5,7},{6,22},{7,5},{8,24},{9,11},... | collective-permute-start | bytes 1032200 | tf_op jit(solution)/shard_map/ppermute | solution.py:59
  22.7 10.4 %collective-permute-start.5 = (bf16[64,2560]{1,0:T(8,128)(2,1)S(1)}, bf16[64,2560]{1,0:T(8,128)(2,1)S(1)}, u32[]{:S(2)}, u32[]{:S(2)}) collective-permute-start(bf16[64,2560]{1,0:T(8,128)(2,1)S(1)} %stack_two.2.refs_0_), channel_id=1, source_target_pairs={{0,16},{1,3},{2,18},{3,1},{4,20},{5,7},{6,22},{7,5},{8,24},{9,11},... | collective-permute-start | bytes 983048 | tf_op jit(solution)/shard_map/ppermute | solution.py:59
  24.4 8.6 %collective-permute-start.10 = (bf16[64,2688]{1,0:T(8,128)(2,1)S(1)}, bf16[64,2688]{1,0:T(8,128)(2,1)S(1)}, u32[]{:S(2)}, u32[]{:S(2)}) collective-permute-start(bf16[64,2688]{1,0:T(8,128)(2,1)S(1)} %stack_two.3.refs_0_), channel_id=1, source_target_pairs={{0,1},{1,0},{2,3},{3,2},{4,5},{5,4},{6,7},{7,6},{8,9},{9,8},{10,11... | collective-permute-start | bytes 1032200 | tf_op jit(solution)/shard_map/ppermute | solution.py:44
  29.6 3.5 %collective-permute-start.11 = (bf16[64,2688]{1,0:T(8,128)(2,1)S(1)}, bf16[64,2688]{1,0:T(8,128)(2,1)S(1)}, u32[]{:S(2)}, u32[]{:S(2)}) collective-permute-start(bf16[64,2688]{1,0:T(8,128)(2,1)S(1)} %collective-permute-done.9.refs_1_), channel_id=1, source_target_pairs={{0,1},{1,0},{2,3},{3,2},{4,5},{5,4},{6,7},{7,6},{8,9},{9,8},{10,11... | collective-permute-start | bytes 1032200 | tf_op jit(solution)/shard_map/ppermute | solution.py:44
  29.6 5.8 %collective-permute-start.6 = (bf16[64,2560]{1,0:T(8,128)(2,1)S(1)}, bf16[64,2560]{1,0:T(8,128)(2,1)S(1)}, u32[]{:S(2)}, u32[]{:S(2)}) collective-permute-start(bf16[64,2560]{1,0:T(8,128)(2,1)S(1)} %stack_two.2.refs_0_), channel_id=1, source_target_pairs={{0,1},{1,0},{2,3},{3,2},{4,5},{5,4},{6,7},{7,6},{8,9},{9,8},{10,11... | collective-permute-start | bytes 983048 | tf_op jit(solution)/shard_map/ppermute | solution.py:44
  33.1 2.3 %collective-permute-start.7 = (bf16[64,2560]{1,0:T(8,128)(2,1)S(1)}, bf16[64,2560]{1,0:T(8,128)(2,1)S(1)}, u32[]{:S(2)}, u32[]{:S(2)}) collective-permute-start(bf16[64,2560]{1,0:T(8,128)(2,1)S(1)} %collective-permute-done.5.refs_1_), channel_id=1, source_target_pairs={{0,1},{1,0},{2,3},{3,2},{4,5},{5,4},{6,7},{7,6},{8,9},{9,8},{10,11... | collective-permute-start | bytes 983048 | tf_op jit(solution)/shard_map/ppermute | solution.py:44
  38.2 7.4 %collective-permute-start.12 = (bf16[128,768]{1,0:T(8,128)(2,1)S(1)}, bf16[128,768]{1,0:T(8,128)(2,1)S(1)}, u32[]{:S(2)}, u32[]{:S(2)}) collective-permute-start(bf16[128,768]{1,0:T(8,128)(2,1)S(1)} %get-tuple-element.52), channel_id=1, source_target_pairs={{0,16},{16,0},{1,17},{17,1},{2,18},{18,2},{3,19},{19,3},{4,20},{20... | collective-permute-start | bytes 589832 | tf_op jit(solution)/shard_map/ppermute | solution.py:44
  46.4 1.7 %collective-permute-start.13 = (bf16[128,1280]{1,0:T(8,128)(2,1)S(1)}, bf16[128,1280]{1,0:T(8,128)(2,1)S(1)}, u32[]{:S(2)}, u32[]{:S(2)}) collective-permute-start(bf16[128,1280]{1,0:T(8,128)(2,1)S(1)} %get-tuple-element.59), channel_id=1, source_target_pairs={{0,1},{1,0},{2,3},{3,2},{4,5},{5,4},{6,7},{7,6},{8,9},{9,8},{10,11... | collective-permute-start | bytes 983048 | tf_op jit(solution)/shard_map/ppermute | solution.py:44
  47.3 2.5 %collective-permute-start.15 = (bf16[128,1280]{1,0:T(8,128)(2,1)S(1)}, bf16[128,1280]{1,0:T(8,128)(2,1)S(1)}, u32[]{:S(2)}, u32[]{:S(2)}) collective-permute-start(bf16[128,1280]{1,0:T(8,128)(2,1)S(1)} %get-tuple-element.61), channel_id=1, source_target_pairs={{0,1},{1,0},{2,3},{3,2},{4,5},{5,4},{6,7},{7,6},{8,9},{9,8},{10,11... | collective-permute-start | bytes 983048 | tf_op jit(solution)/shard_map/ppermute | solution.py:44
  48.2 7.1 %collective-permute-start.14 = (bf16[64,1280]{1,0:T(8,128)(2,1)S(1)}, bf16[64,1280]{1,0:T(8,128)(2,1)S(1)}, u32[]{:S(2)}, u32[]{:S(2)}) collective-permute-start(bf16[64,1280]{1,0:T(8,128)(2,1)S(1)} %slice.74), channel_id=1, source_target_pairs={{0,2},{1,3},{2,0},{3,1},{4,6},{5,7},{6,4},{7,5},{8,10},{9,11},{10,... | collective-permute-start | bytes 491528 | tf_op jit(solution)/shard_map/ppermute | solution.py:44
  49.9 8.1 %collective-permute-start.16 = (bf16[64,1280]{1,0:T(8,128)(2,1)S(1)}, bf16[64,1280]{1,0:T(8,128)(2,1)S(1)}, u32[]{:S(2)}, u32[]{:S(2)}) collective-permute-start(bf16[64,1280]{1,0:T(8,128)(2,1)S(1)} %slice.73), channel_id=1, source_target_pairs={{0,2},{1,3},{2,0},{3,1},{4,6},{5,7},{6,4},{7,5},{8,10},{9,11},{10,... | collective-permute-start | bytes 491528 | tf_op jit(solution)/shard_map/ppermute | solution.py:44
  58.1 6.1 %collective-permute-start.17 = (bf16[2,8,2560]{2,1,0:T(8,128)(2,1)S(1)}, bf16[2,8,2560]{2,1,0:T(8,128)(2,1)S(1)}, u32[]{:S(2)}, u32[]{:S(2)}) collective-permute-start(bf16[2,8,2560]{2,1,0:T(8,128)(2,1)S(1)} %get-tuple-element.62), channel_id=1, source_target_pairs={{0,12},{1,13},{2,14},{3,15},{4,0},{5,1},{6,2},{7,3},{8,4},{9,5},{1... | collective-permute-start | bytes 245768 | tf_op jit(solution)/shard_map/ppermute | solution.py:49
  61.3 7.3 %collective-permute-start.18 = (bf16[2,8,2560]{2,1,0:T(8,128)(2,1)S(1)}, bf16[2,8,2560]{2,1,0:T(8,128)(2,1)S(1)}, u32[]{:S(2)}, u32[]{:S(2)}) collective-permute-start(bf16[2,8,2560]{2,1,0:T(8,128)(2,1)S(1)} %get-tuple-element.64), channel_id=1, source_target_pairs={{0,8},{1,9},{2,10},{3,11},{4,12},{5,13},{6,14},{7,15},{8,0},{9,1},... | collective-permute-start | bytes 245768 | tf_op jit(solution)/shard_map/ppermute | solution.py:49
  61.5 7.1 %collective-permute-start.19 = (bf16[2,8,2560]{2,1,0:T(8,128)(2,1)S(1)}, bf16[2,8,2560]{2,1,0:T(8,128)(2,1)S(1)}, u32[]{:S(2)}, u32[]{:S(2)}) collective-permute-start(bf16[2,8,2560]{2,1,0:T(8,128)(2,1)S(1)} %get-tuple-element.63), channel_id=1, source_target_pairs={{0,4},{1,5},{2,6},{3,7},{4,8},{5,9},{6,10},{7,11},{8,12},{9,13},{1... | collective-permute-start | bytes 245768 | tf_op jit(solution)/shard_map/ppermute | solution.py:49
  68.7 4.1 %collective-permute-start.20 = (bf16[8,2560]{1,0:T(8,128)(2,1)S(1)}, bf16[8,2560]{1,0:T(8,128)(2,1)S(1)}, u32[]{:S(2)}, u32[]{:S(2)}) collective-permute-start(bf16[8,2560]{1,0:T(8,128)(2,1)S(1)} %slice_bitcast_fusion.4), channel_id=1, source_target_pairs={{0,16},{16,0},{1,17},{17,1},{2,18},{18,2},{3,19},{19,3},{4,20},{20... | collective-permute-start | bytes 122888 | tf_op jit(solution)/shard_map/ppermute | solution.py:44

commit v3 on v2

--- a/solution.py
+++ b/solution.py
@@ -44,9 +44,10 @@
     return lax.ppermute(block, axis, [(i, i ^ bit) for i in range(lax.axis_size(axis))])
 
 
-def moved(block, steps):
-    count = lax.axis_size("exp")
-    return lax.ppermute(block, "exp", [(i, (i + 4 * steps) % count) for i in range(count)])
+def along_line(block, steps):
+    return lax.ppermute(
+        block, "exp", [(i, i ^ (4 * steps)) for i in range(lax.axis_size("exp"))]
+    )
 
 
 def paired(block, partner):
@@ -89,8 +90,8 @@
     return pltpu.with_memory_space_constraint(array, pltpu.HBM)
 
 
-def local_kernel(body, ins, outs, scratch, name, cost=None):
-    kinds = {"vmem": pltpu.VMEM, "hbm": pl.ANY}
+def local_kernel(body, ins, outs, scratch, name):
+    kinds = {"vmem": pltpu.VMEM, "hbm": pl.ANY, "result": pltpu.VMEM}
     place = {"vmem": in_vmem, "hbm": in_hbm}
     made = [
         pltpu.VMEM(shape, dtype) if kind == "vmem" else jax.ShapeDtypeStruct(shape, dtype)
@@ -103,7 +104,7 @@
         out_shape=made,
         scratch_shapes=scratch,
         compiler_params=pltpu.CompilerParams(vmem_limit_bytes=20 * 1024 * 1024),
-        cost_estimate=cost,
+        cost_estimate=pl.CostEstimate(flops=0, bytes_accessed=0, transcendentals=0),
         name=name,
     )(*[place[kind](array) for array, kind in ins])
 
@@ -160,9 +161,14 @@
     out[:, half : half + 128] = note.astype(jnp.bfloat16)
 
 
-def fetch_kernel(after, gate_w, up_w, gate_out, up_out, sems):
-    half = gate_out.shape[1]
-    pairs = [(gate_w.at[:, :half], gate_out), (up_w.at[:, :half], up_out)]
+def fetch_kernel(after, *refs, start):
+    count = len(refs) // 2
+    ins, outs, sems = refs[:count], refs[count:-1], refs[-1]
+    pairs = [(a.at[:, start : start + b.shape[1]], b) for a, b in zip(ins[:2], outs[:2])]
+    if count > 2:
+        width = outs[2].shape[1]
+        own_at = pl.multiple_of(lax.axis_index("ctx") * width, 128)
+        pairs.append((ins[2].at[:, pl.ds(own_at, width)], outs[2]))
     for copy in start_copies(pairs, sems, PIECES):
         copy.wait()
 
@@ -181,11 +187,9 @@
 
 
 def attention_kernel(
-    after, earlier, queries_in, latents_in, gate_all, up_all,
-    attended, gate_next, up_next, queries, latents, even, odd, mixed, sems, copy_sems,
+    after, earlier, queries_in, latents_in, attended, queries, latents, even, odd, mixed, sems
 ):
     width, rows = latents.shape
-    half = gate_next.shape[1]
     pad = even.shape[0] - width
     loads = [
         pltpu.make_async_copy(queries_in, queries, sems.at[0]),
@@ -193,8 +197,6 @@
     ]
     for copy in loads:
         copy.start()
-    pairs = [(gate_all.at[:, half:], gate_next), (up_all.at[:, half:], up_next)]
-    copies = start_copies(pairs, copy_sems, PIECES)
     for copy in loads:
         copy.wait()
     even[width:, :] = jnp.zeros((pad, 2 * rows), jnp.bfloat16)
@@ -223,7 +225,7 @@
         write = pltpu.make_async_copy(mixed.at[:, span], attended.at[:, span], sems.at[2 + head])
         write.start()
         writes.append(write)
-    for copy in writes + copies:
+    for copy in writes:
         copy.wait()
 
 
@@ -281,53 +283,120 @@
     coef_out[...] = jnp.broadcast_to(coef, coef_out.shape)
 
 
+def finish_units(tokens, gate_w, up_w, gate_in, up_in, pick, act_out, packed_out, start):
+    span = slice(start, start + act_out.shape[1])
+    gate = gate_in[:, span] + times_rows_in(tokens[...], gate_w[span, :])
+    upper = up_in[:, span] + times_rows_in(tokens[...], up_w[span, :])
+    act = (gate / (1.0 + jnp.exp(-gate)) * upper).astype(jnp.bfloat16)
+    act_out[...] = act
+    packed_out[...] = lax.dot_general(
+        pick[...], act, (((0,), (0,)), ((), ())), preferred_element_type=jnp.float32
+    ).astype(jnp.bfloat16)
+
+
 def second_kernel(
     two, far, two_other, far_other, gate_w, up_w, gate_in, up_in, pick,
-    act_out, packed_out, tokens, *, unit, wide,
+    act_out, packed_out, tokens, *, unit,
 ):
-    units = act_out.shape[1]
     assemble(tokens, lax.axis_index("exp") % 2, two, far, two_other, far_other, unit)
-    for n in range(0, units, wide):
-        span = slice(n, n + wide)
-        gate = gate_in[:, span] + times_rows_in(tokens[...], gate_w[span, :])
-        upper = up_in[:, span] + times_rows_in(tokens[...], up_w[span, :])
-        act = (gate / (1.0 + jnp.exp(-gate)) * upper).astype(jnp.bfloat16)
-        act_out[:, span] = act
-        packed_out[:, span] = lax.dot_general(
-            pick[...], act, (((0,), (0,)), ((), ())), preferred_element_type=jnp.float32
+    finish_units(tokens, gate_w, up_w, gate_in, up_in, pick, act_out, packed_out, 0)
+
+
+def third_kernel(tokens, gate_w, up_w, gate_in, up_in, pick, act_out, packed_out, *, start):
+    finish_units(tokens, gate_w, up_w, gate_in, up_in, pick, act_out, packed_out, start)
+
+
+def own_kernel(act_a, act_b, down_own, down_w, out, down_other, sems):
+    units = down_own.shape[1]
+    few = act_a.shape[1]
+    other_at = pl.multiple_of((1 - lax.axis_index("ctx")) * units, 128)
+    copies = start_copies([(down_w.at[:, pl.ds(other_at, units)], down_other)], sems, PIECES)
+    tall = out.shape[1] // 5 if out.shape[1] % 640 == 0 else out.shape[1]
+    for n in range(0, out.shape[1], tall):
+        span = slice(n, n + tall)
+        out[:, span] = times_rows_in(act_a[...], down_own[span, :few]) + times_rows_in(
+            act_b[...], down_own[span, few:]
+        )
+    for copy in copies:
+        copy.wait()
+
+
+def other_kernel(packed_a, packed_b, pick, coef, down_w, own, keep, give, act, *, start):
+    few = packed_a.shape[1]
+    for packed, span in ((packed_a, slice(0, few)), (packed_b, slice(few, act.shape[1]))):
+        act[:, span] = jnp.dot(
+            pick[...], packed[...], preferred_element_type=jnp.float32
         ).astype(jnp.bfloat16)
-
-
-def own_kernel(act, down_w, out, down_other, down_own, sems):
-    units = act.shape[1]
-    ctx = lax.axis_index("ctx")
-    own_at = pl.multiple_of(ctx * units, 128)
-    other_at = pl.multiple_of((1 - ctx) * units, 128)
-    pairs = [
-        (down_w.at[:, pl.ds(own_at, units)], down_own),
-        (down_w.at[:, pl.ds(other_at, units)], down_other),
-    ]
-    copies = start_copies(pairs, sems, PIECES)
-    tall = out.shape[1] // PIECES
-    for piece in range(PIECES):
-        copies[piece].wait()
-        span = slice(piece * tall, (piece + 1) * tall)
-        out[:, span] = times_rows_in(act[...], down_own[span, :])
-    for copy in copies[PIECES:]:
-        copy.wait()
-
-
-def other_kernel(packed, pick, coef, down_w, own, keep, give, act, *, tall, start):
-    act[...] = jnp.dot(pick[...], packed[...], preferred_element_type=jnp.float32).astype(
-        jnp.bfloat16
-    )
-    half = keep.shape[0]
-    for n in range(0, keep.shape[1], tall):
+    half, part = keep.shape
+    tall = part // 5 if part % 5 == 0 else part
+    for n in range(0, part, tall):
         span = slice(start + n, start + n + tall)
         projected = own[:, span] + times_rows_in(act[...], down_w[span, :])
         projected = projected * coef[:, :1]
         keep[:, n : n + tall] = projected[:half].astype(jnp.bfloat16)
         give[:, n : n + tall] = projected[half:].astype(jnp.bfloat16)
+
+
+def spread_kernel(keep, got, send, stay):
+    core = lax.axis_index("exp") % 2
+    unit = keep.shape[0] // 4
+
+    def total(block):
+        span = slice(block * unit, (block + 1) * unit)
+        return keep[span, :].astype(jnp.float32) + got[span, :].astype(jnp.float32)
+
+    for this, (stays, sends) in enumerate((((0, 1), (2, 3)), ((0, 2), (1, 3)))):
+
+        @pl.when(core == this)
+        def _():
+            for number in range(2):
+                span = slice(number * unit, (number + 1) * unit)
+                stay[span, :] = total(stays[number])
+                send[span, :] = total(sends[number]).astype(jnp.bfloat16)
+
+
+def cross_kernel(stay, got, send, left):
+    core = lax.axis_index("exp") % 2
+    unit, part = send.shape[0], send.shape[1] // 2
+
+    @pl.when(core == 0)
+    def _():
+        left[:, :part] = stay[:unit, :] + got[:unit, :].astype(jnp.float32)
+        left[:, part:] = jnp.zeros((unit, part), jnp.float32)
+        send[:, :part] = (stay[unit:, :] + got[unit:, :].astype(jnp.float32)).astype(jnp.bfloat16)
+        send[:, part:] = jnp.zeros((unit, part), jnp.bfloat16)
+
+    @pl.when(core == 1)
+    def _():
+        left[:, :part] = stay[:unit, :]
+        left[:, part:] = got[:unit, :].astype(jnp.float32)
+        send[:, :part] = stay[unit:, :].astype(jnp.bfloat16)
+        send[:, part:] = got[unit:, :]
+
+
+def line_kernel(*refs, line):
+    ins, outs = refs[:4], refs[4:]
+    core = lax.axis_index("exp") % 2
+    ctx = lax.axis_index("ctx")
+    count = outs[0].shape[0]
+    part = ins[0].shape[1] // 2
+    for number in range(2):
+        left, got = ins[2 * number], ins[2 * number + 1]
+        arrived = got[...].astype(jnp.float32)
+        own = left[:, :part] + jnp.where(core == 1, arrived[:, :part], 0.0)
+        other = left[:, part:] + jnp.where(core == 1, arrived[:, part:], arrived[:, :part])
+        for value, side in ((own, ctx), (other, 1 - ctx)):
+            at = pl.multiple_of(side * 2 * part + number * part, 128)
+            for place, out in enumerate(outs):
+                rows = value[place * count : (place + 1) * count]
+                out[:, pl.ds(at, part)] = rows.astype(out.dtype)
+
+
+def sum_kernel(first, *refs):
+    total = first[...]
+    for ref in refs[:-1]:
+        total = total + ref[...].astype(jnp.float32)
+    refs[-1][...] = total.astype(refs[-1].dtype)
 
 
 def on_device_gathered(
@@ -348,7 +417,6 @@
     count = 8 * unit
     slots = count // tok_dev * capacity
     bf16, f32 = jnp.bfloat16, jnp.float32
-    first = lax.axis_index("ctx") == 0
     copy_sems = pltpu.SemaphoreType.DMA((2 * PIECES,))
 
     (rows,) = local_kernel(
@@ -367,10 +435,12 @@
         ],
         "rows",
     )
-    along = [rows] + [moved(rows, d) for d in range(1, line)]
-    earlier_kv = swapped(latents.T, "ctx", 1)
+    places = range(line - 1, 0, -1)
+    along = [rows] + [along_line(rows, d) for d in places]
+    latents_t, _ = lax.optimization_barrier((latents.T, rows))
+    earlier_kv = swapped(latents_t, "ctx", 1)
     gate_1, up_1 = local_kernel(
-        fetch_kernel,
+        lambda *refs: fetch_kernel(*refs, start=0),
         [(rows, "vmem"), (w_gate[0], "hbm"), (w_up[0], "hbm")],
         [((units, half), bf16, "vmem")] * 2,
         [copy_sems],
@@ -385,40 +455,30 @@
         [],
         "stack_line",
     )
-    pad = -key_width % 128
-    attended, gate_2, up_2 = local_kernel(
-        attention_kernel,
-        [
-            (nears[1], "vmem"), (earlier_kv, "vmem"), (queries, "hbm"), (latents.T, "hbm"),
-            (w_gate[0], "hbm"), (w_up[0], "hbm"),
-        ],
-        [((tok_att, heads_dev * LATENT), bf16, "hbm")] + [((units, half), bf16, "vmem")] * 2,
-        [
-            pltpu.VMEM((tok_att, heads_dev * key_width), bf16),
-            pltpu.VMEM((key_width, tok_att), bf16),
-            pltpu.VMEM((key_width + pad, 2 * tok_att), bf16),
-            pltpu.VMEM((key_width + pad, 2 * tok_att), bf16),
-            pltpu.VMEM((tok_att, heads_dev * LATENT), bf16),
-            pltpu.SemaphoreType.DMA((2 + heads_dev,)),
-            copy_sems,
-        ],
-        "attention",
-    )
-    passed = [paired(near, y_then_x) for near in nears]
-    passed[0], gate_2, up_2 = lax.optimization_barrier((passed[0], gate_2, up_2))
     pieces = []
-    for near, got in zip(nears, passed):
-        shape = (2 * unit, near.shape[1])
+    for near in nears:
+        got = paired(near, y_then_x)
         (two,) = local_kernel(
             lambda *refs, cut=near.shape[1]: stack_kernel(*refs, cuts=((0, cut),)),
             [(near, "vmem"), (got, "vmem")],
-            [(shape, bf16, "vmem")],
+            [((2 * unit, near.shape[1]), bf16, "vmem")],
             [],
             "stack_two",
         )
-        far = paired(two, x_then_y)
+        pieces.append([two, paired(two, x_then_y)])
+    gate_2, up_2, down_mine = local_kernel(
+        lambda *refs: fetch_kernel(*refs, start=half),
+        [(pieces[1][0], "vmem"), (w_gate[0], "hbm"), (w_up[0], "hbm"), (w_down[0], "hbm")],
+        [((units, half), bf16, "vmem")] * 2 + [((columns, units), bf16, "vmem")],
+        [pltpu.SemaphoreType.DMA((3 * PIECES,))],
+        "fetch",
+    )
+    pieces[0][1], gate_2, up_2, down_mine = lax.optimization_barrier(
+        (pieces[0][1], gate_2, up_2, down_mine)
+    )
+    for number, (two, far) in enumerate(pieces):
         group = (two, far, swapped(two, "exp", 1), swapped(far, "exp", 1))
-        pieces.append([(piece, "vmem") for piece in group])
+        pieces[number] = [(piece, "vmem") for piece in group]
 
     gate, up, pick, pick_far, coef = local_kernel(
         lambda *refs: first_kernel(
@@ -431,48 +491,97 @@
         [pltpu.VMEM((count, half), bf16), pltpu.VMEM((count, 128), bf16)],
         "gate_up_first",
     )
-    act, packed = local_kernel(
-        lambda *refs: second_kernel(*refs, unit=unit, wide=256),
+    few = 2 * units // 3 if units % 384 == 0 else units // 2
+    sums_in = [(gate_2, "vmem"), (up_2, "vmem"), (gate, "vmem"), (up, "vmem"), (pick, "vmem")]
+    act_a, packed_a, tokens = local_kernel(
+        lambda *refs: second_kernel(*refs, unit=unit),
+        [*pieces[1], *sums_in],
         [
-            *pieces[1], (gate_2, "vmem"), (up_2, "vmem"),
-            (gate, "vmem"), (up, "vmem"), (pick, "vmem"),
+            ((count, few), bf16, "vmem"),
+            ((slots, few), bf16, "vmem"),
+            ((count, half), bf16, "vmem"),
         ],
-        [((count, units), bf16, "vmem"), ((slots, units), bf16, "vmem")],
-        [pltpu.VMEM((count, half), bf16)],
+        [],
         "gate_up_second",
     )
-    other = swapped(packed, "ctx", 1)
+    other_a = swapped(packed_a, "ctx", 1)
+    act_b, packed_b = local_kernel(
+        lambda *refs: third_kernel(*refs, start=few),
+        [(tokens, "vmem"), *sums_in],
+        [((count, units - few), bf16, "vmem"), ((slots, units - few), bf16, "vmem")],
+        [],
+        "gate_up_third",
+    )
+    other_b = swapped(packed_b, "ctx", 1)
     own, down_other = local_kernel(
         own_kernel,
-        [(act, "vmem"), (w_down[0], "hbm")],
+        [(act_a, "vmem"), (act_b, "vmem"), (down_mine, "vmem"), (w_down[0], "hbm")],
         [((count, columns), f32, "vmem"), ((columns, units), bf16, "vmem")],
-        [pltpu.VMEM((columns, units), bf16), copy_sems],
+        [pltpu.SemaphoreType.DMA((PIECES,))],
         "down_own",
     )
-    sums = []
     part = columns // 2
+    crossing = []
     for start in (0, part):
         keep, give = local_kernel(
-            lambda *refs, start=start: other_kernel(*refs, tall=256, start=start),
+            lambda *refs, start=start: other_kernel(*refs, start=start),
             [
-                (other, "vmem"), (pick_far, "vmem"), (coef, "vmem"),
+                (other_a, "vmem"), (other_b, "vmem"), (pick_far, "vmem"), (coef, "vmem"),
                 (down_other, "vmem"), (own, "vmem"),
             ],
             [((count // 2, part), bf16, "vmem")] * 2,
             [pltpu.VMEM((count, units), bf16)],
             "down_other",
         )
-        total = keep.astype(f32) + swapped(give, "exp", 1).astype(f32)
-        total = total[: 2 * unit] + swapped(total[2 * unit :].astype(bf16), "exp", 2).astype(f32)
-        sums.append(total)
-    total = jnp.concatenate(sums, axis=1).reshape(2, line, tok_dev, columns)
-    parts = [moved(total[:, d].astype(bf16), line - d) for d in range(1, line)]
-    total = total[:, 0] + sum(part.astype(f32) for part in parts)
-    total = total.astype(bf16)
-    far = swapped(total[1], "ctx", 1)
-    near = total[0]
-    mixed = jnp.concatenate(
-        [jnp.where(first, near, far), jnp.where(first, far, near)], axis=1
+        send, stay = local_kernel(
+            spread_kernel,
+            [(keep, "vmem"), (swapped(give, "exp", 1), "vmem")],
+            [((2 * unit, part), bf16, "vmem"), ((2 * unit, part), f32, "vmem")],
+            [],
+            "spread",
+        )
+        crossing.append((stay, paired(send, y_then_x)))
+    lines = []
+    for stay, got in crossing:
+        send, left = local_kernel(
+            cross_kernel,
+            [(stay, "vmem"), (got, "vmem")],
+            [((unit, 2 * part), bf16, "vmem"), ((unit, 2 * part), f32, "vmem")],
+            [],
+            "cross",
+        )
+        lines += [left, paired(send, x_then_y)]
+    pad = -key_width % 128
+    (attended,) = local_kernel(
+        attention_kernel,
+        [(send, "vmem"), (earlier_kv, "vmem"), (queries, "hbm"), (latents.T, "hbm")],
+        [((tok_att, heads_dev * LATENT), bf16, "hbm")],
+        [
+            pltpu.VMEM((tok_att, heads_dev * key_width), bf16),
+            pltpu.VMEM((key_width, tok_att), bf16),
+            pltpu.VMEM((key_width + pad, 2 * tok_att), bf16),
+            pltpu.VMEM((key_width + pad, 2 * tok_att), bf16),
+            pltpu.VMEM((tok_att, heads_dev * LATENT), bf16),
+            pltpu.SemaphoreType.DMA((2 + heads_dev,)),
+        ],
+        "attention",
+    )
+    lines[1], attended = lax.optimization_barrier((lines[1], attended))
+    keep, *sends = local_kernel(
+        lambda *refs: line_kernel(*refs, line=line),
+        [(block, "vmem") for block in lines],
+        [((tok_dev, 2 * columns), f32, "vmem")]
+        + [((tok_dev, 2 * columns), bf16, "vmem")] * (line - 1),
+        [],
+        "line",
+    )
+    got = [along_line(block, d) for block, d in zip(sends, places)]
+    (mixed,) = local_kernel(
+        sum_kernel,
+        [(block, "vmem") for block in (keep, *got)],
+        [((tok_dev, 2 * columns), bf16, "result")],
+        [],
+        "sum",
     )
     return (attended, mixed[None])
 
@@ -535,7 +644,7 @@
 
 def solution(mesh):
     experts, groups = mesh.shape["exp"], mesh.shape["ctx"]
-    whole = groups == 2 and experts % 4 == 0 and experts <= 16
+    whole = groups == 2 and experts == 16
     on_device = on_device_gathered if whole else on_device_slots
     placed = (
         P("exp", "ctx", None),

time: 73.6 us -> 68.1 us (0.925)
  waiting for transfers between devices: 30.1 us -> 21.6 us
  Pallas kernels: 20.3 us -> 23 us
  starting transfers between devices: 21.3 us -> 22.5 us
  other arithmetic: 0.93 us -> 0 us
    ppermute x11 -> x9, waiting for transfers between devices: 14.2 us -> 1.29 us  [swapped(): lax.ppermute(block, axis, [(i, i ^ bit) for i in range(lax.axis_size(axis...]
    ppermute x4 -> x8, waiting for transfers between devices: 8.13 us -> 12.9 us  [paired(): return lax.ppermute(block, ('ctx', 'exp'), route)]
    ppermute x4 -> x8, starting transfers between devices: 4.25 us -> 7.24 us  [paired(): return lax.ppermute(block, ('ctx', 'exp'), route)]
    pallas_call x11 -> x19, Pallas kernels: 20.3 us -> 23 us  [local_kernel(): pl.pallas_call(body, in_specs=[pl.BlockSpec(memory_space=kinds[kind]) for...]
    ppermute x11 -> x9, starting transfers between devices: 7.66 us -> 6.41 us  [swapped(): lax.ppermute(block, axis, [(i, i ^ bit) for i in range(lax.axis_size(axis...]
  transfers between devices with their start and end apart: 21 -> 23, of which waited for: 10 -> 11; matrix products, arithmetic and copies ran while one was open for 0% -> 0% of each run, Pallas kernels for 23% -> 28%
where the time goes in v3:
time: 68.1 us; the launch traced here: 67.9 us
  Pallas kernels  23 us (34%)
  starting transfers between devices  22.5 us (33%)
  waiting for transfers between devices  21.6 us (32%)
  between operations  0.82 us (1%)
    pallas_call x19, Pallas kernels, local_kernel(): pl.pallas_call(body, in_specs=[pl.BlockSpec(memory_space=kinds[kind]) for...  23 us
    ppermute x8, waiting for transfers between devices, paired(): return lax.ppermute(block, ('ctx', 'exp'), route)  12.9 us
    ppermute x6, starting transfers between devices, along_line(): lax.ppermute(block, 'exp', [(i, i ^ 4 * steps) for i in range(lax.axis_si...  8.84 us
    ppermute x6, waiting for transfers between devices, along_line(): lax.ppermute(block, 'exp', [(i, i ^ 4 * steps) for i in range(lax.axis_si...  7.36 us
    ppermute x8, starting transfers between devices, paired(): return lax.ppermute(block, ('ctx', 'exp'), route)  7.24 us
    ppermute x9, starting transfers between devices, swapped(): lax.ppermute(block, axis, [(i, i ^ bit) for i in range(lax.axis_size(axis...  6.41 us
  transfers between devices with their start and end apart: 23, of which 11 were waited for; matrix products, arithmetic and copies ran while one was open for 0% of the time, Pallas kernels for 28%

profile of v3, /device:TPU:0, one launch (start us, length us, event | category | flops | bytes accessed | tf_op | source)
XLA Modules:
  0.0 67.9 jit_solution(13131904648054877438)
XLA Ops:
  0.6 1.0 %rows.1.refs_0_ = bf16[8,5248]{1,0:T(8,128)(2,1)S(1)} custom-call(bf16[8,5120]{1,0:T(8,128)(2,1)} %bitcast.16, s32[6,1,8]{2,1,0:T(1,128)} %bitcast.18, f32[6,1,8]{2,1,0:T(1,128)} %bitcast.19), custom_call_target="tpu_custom_call" | custom-call | tf_op jit(solution)/shard_map/rows/pallas_call | solution.py:100
  1.7 3.0 %collective-permute-start.3 = (bf16[576,128]{1,0:T(8,128)(2,1)}, bf16[576,128]{1,0:T(8,128)(2,1)S(1)}, u32[]{:S(2)}, u32[]{:S(2)}) collective-permute-start(bf16[576,128]{1,0:T(8,128)(2,1)} %bitcast.14), channel_id=1, source_target_pairs={{0,16},{16,0},{1,17},{17,1},{2,18},{18,2},{3,19},{19,3},{4,20},{20... | collective-permute-start | bytes 442376 | tf_op jit(solution)/shard_map/ppermute | solution.py:44
  4.7 3.6 %collective-permute-start = (bf16[8,5248]{1,0:T(8,128)(2,1)S(1)}, bf16[8,5248]{1,0:T(8,128)(2,1)S(1)}, u32[]{:S(2)}, u32[]{:S(2)}) collective-permute-start(bf16[8,5248]{1,0:T(8,128)(2,1)S(1)} %rows.1.refs_0_), channel_id=1, source_target_pairs={{0,12},{1,13},{2,14},{3,15},{4,8},{5,9},{6,10},{7,11},{8,4},{9,5},... | collective-permute-start | bytes 251912 | tf_op jit(solution)/shard_map/ppermute | solution.py:48
  8.3 0.8 %collective-permute-start.2 = (bf16[8,5248]{1,0:T(8,128)(2,1)S(1)}, bf16[8,5248]{1,0:T(8,128)(2,1)S(1)}, u32[]{:S(2)}, u32[]{:S(2)}) collective-permute-start(bf16[8,5248]{1,0:T(8,128)(2,1)S(1)} %rows.1.refs_0_), channel_id=1, source_target_pairs={{0,4},{1,5},{2,6},{3,7},{4,0},{5,1},{6,2},{7,3},{8,12},{9,13},{10,... | collective-permute-start | bytes 251912 | tf_op jit(solution)/shard_map/ppermute | solution.py:48
  9.0 3.3 %fetch.2 = (bf16[768,2560]{1,0:T(8,128)(2,1)S(1)}, bf16[768,2560]{1,0:T(8,128)(2,1)S(1)}) custom-call(bf16[8,5248]{1,0:T(8,128)(2,1)S(1)} %rows.1.refs_0_, bf16[768,5120]{1,0:T(8,128)(2,1)} %bitcast.8, bf16[768,5120]{1,0:T(8,128)(2,1)} %bitcast.10), custom_call_target="tpu_custom_call" | custom-call | tf_op jit(solution)/shard_map/fetch/pallas_call | solution.py:100
  12.4 2.6 %collective-permute-done.1.refs_2_ = bf16[8,5248]{1,0:T(8,128)(2,1)S(1)} collective-permute-done((bf16[8,5248]{1,0:T(8,128)(2,1)S(1)}, bf16[8,5248]{1,0:T(8,128)(2,1)S(1)}, u32[]{:S(2)}, u32[]{:S(2)}) %collective-permute-start.1) | collective-permute-done | bytes 84000 | tf_op jit(solution)/shard_map/ppermute | solution.py:48
  15.0 1.6 %collective-permute-start.8 = (bf16[32,2688]{1,0:T(8,128)(2,1)S(1)}, bf16[32,2688]{1,0:T(8,128)(2,1)S(1)}, u32[]{:S(2)}, u32[]{:S(2)}) collective-permute-start(bf16[32,2688]{1,0:T(8,128)(2,1)S(1)} %get-tuple-element.59.refs_0_), channel_id=1, source_target_pairs={{0,2},{1,17},{2,0},{3,19},{4,6},{5,21},{6,4},{7,23},{8,10},{9,25},... | collective-permute-start | bytes 516104 | tf_op jit(solution)/shard_map/ppermute | solution.py:60
  17.1 3.4 %collective-permute-done.8.refs_1_ = bf16[32,2688]{1,0:T(8,128)(2,1)S(1)} collective-permute-done((bf16[32,2688]{1,0:T(8,128)(2,1)S(1)}, bf16[32,2688]{1,0:T(8,128)(2,1)S(1)}, u32[]{:S(2)}, u32[]{:S(2)}) %collective-permute-start.8) | collective-permute-done | bytes 172064 | tf_op jit(solution)/shard_map/ppermute | solution.py:60
  21.1 1.3 %collective-permute-done.4.refs_1_ = bf16[32,2560]{1,0:T(8,128)(2,1)S(1)} collective-permute-done((bf16[32,2560]{1,0:T(8,128)(2,1)S(1)}, bf16[32,2560]{1,0:T(8,128)(2,1)S(1)}, u32[]{:S(2)}, u32[]{:S(2)}) %collective-permute-start.4) | collective-permute-done | bytes 163872 | tf_op jit(solution)/shard_map/ppermute | solution.py:60
  22.4 0.8 %collective-permute-start.5 = (bf16[64,2560]{1,0:T(8,128)(2,1)S(1)}, bf16[64,2560]{1,0:T(8,128)(2,1)S(1)}, u32[]{:S(2)}, u32[]{:S(2)}) collective-permute-start(bf16[64,2560]{1,0:T(8,128)(2,1)S(1)} %stack_two.2.refs_0_), channel_id=1, source_target_pairs={{0,16},{1,3},{2,18},{3,1},{4,20},{5,7},{6,22},{7,5},{8,24},{9,11},... | collective-permute-start | bytes 983048 | tf_op jit(solution)/shard_map/ppermute | solution.py:60
  23.3 4.5 %fetch.3 = (bf16[768,2560]{1,0:T(8,128)(2,1)S(1)}, bf16[768,2560]{1,0:T(8,128)(2,1)S(1)}, bf16[2560,768]{1,0:T(8,128)(2,1)S(1)}) custom-call(bf16[64,2560]{1,0:T(8,128)(2,1)S(1)} %stack_two.2.refs_0_, bf16[768,5120]{1,0:T(8,128)(2,1)} %bitcast.9, bf16[768,5120]{1,0:T(8,128)(2,1)} %bitcast.11, bf16[2560,1536]{1,0:T(8,128)(2,1)} %bitcast.12), custom_call_target="tpu_custom_call" | custom-call | tf_op jit(solution)/shard_map/fetch/pallas_call | solution.py:100
  28.4 3.0 %collective-permute-done.5.refs_1_ = bf16[64,2560]{1,0:T(8,128)(2,1)S(1)} collective-permute-done((bf16[64,2560]{1,0:T(8,128)(2,1)S(1)}, bf16[64,2560]{1,0:T(8,128)(2,1)S(1)}, u32[]{:S(2)}, u32[]{:S(2)}) %collective-permute-start.5) | collective-permute-done | bytes 327712 | tf_op jit(solution)/shard_map/ppermute | solution.py:60
  31.4 2.3 %gate_up_first.1 = (f32[256,768]{1,0:T(8,128)S(1)}, f32[256,768]{1,0:T(8,128)S(1)}, bf16[256,128]{1,0:T(8,128)(2,1)S(1)}, bf16[256,128]{1,0:T(8,128)(2,1)S(1)}, f32[256,128]{1,0:T(8,128)S(1)}) custom-call(bf16[64,2688]{1,0:T(8,128)(2,1)S(1)} %stack_two.3.refs_0_, bf16[64,2688]{1,0:T(8,128)(2,1)S(1)} %collective-permute-done.9.refs_1_, ...), custom_call_target="tpu_custom_call" | custom-call | tf_op jit(solution)/shard_map/gate_up_first/pallas_call | solution.py:100
  33.7 1.7 %gate_up_second.1 = (bf16[256,512]{1,0:T(8,128)(2,1)S(1)}, bf16[128,512]{1,0:T(8,128)(2,1)S(1)}, bf16[256,2560]{1,0:T(8,128)(2,1)S(1)}) custom-call(bf16[64,2560]{1,0:T(8,128)(2,1)S(1)} %stack_two.2.refs_0_, bf16[64,2560]{1,0:T(8,128)(2,1)S(1)} %collective-permute-done.5.refs_1_, bf16[64,2560]{1,0:T(8,128)(2,1)S(1)} %collective-permute-done.6.refs_2_, ...), custom_call_target="tpu_custom_call" | custom-call | tf_op jit(solution)/shard_map/gate_up_second/pallas_call | solution.py:100
  36.0 1.0 %gate_up_third.1 = (bf16[256,256]{1,0:T(8,128)(2,1)S(1)}, bf16[128,256]{1,0:T(8,128)(2,1)S(1)}) custom-call(bf16[256,2560]{1,0:T(8,128)(2,1)S(1)} %get-tuple-element.72.refs_0_, bf16[768,2560]{1,0:T(8,128)(2,1)S(1)} %get-tuple-element.63.refs_4_.refs_1_, bf16[768,2560]{1,0:T(8,128)(2,1)S(1)} %get-tuple-element.64.refs_5_.refs_2_, ...), custom_call_target="tpu_custom_call" | custom-call | tf_op jit(solution)/shard_map/gate_up_third/pallas_call | solution.py:100
  37.1 1.6 %collective-permute-start.13 = (bf16[128,256]{1,0:T(8,128)(2,1)S(1)}, bf16[128,256]{1,0:T(8,128)(2,1)S(1)}, u32[]{:S(2)}, u32[]{:S(2)}) collective-permute-start(bf16[128,256]{1,0:T(8,128)(2,1)S(1)} %get-tuple-element.73), channel_id=1, source_target_pairs={{0,16},{16,0},{1,17},{17,1},{2,18},{18,2},{3,19},{19,3},{4,20},{20... | collective-permute-start | bytes 196616 | tf_op jit(solution)/shard_map/ppermute | solution.py:44
  38.6 3.1 %down_own.1 = (f32[256,2560]{1,0:T(8,128)S(1)}, bf16[2560,768]{1,0:T(8,128)(2,1)S(1)}) custom-call(bf16[256,512]{1,0:T(8,128)(2,1)S(1)} %get-tuple-element.76.act_a, bf16[256,256]{1,0:T(8,128)(2,1)S(1)} %get-tuple-element.77.act_b, bf16[2560,768]{1,0:T(8,128)(2,1)S(1)} %get-tuple-element.78.down_own, bf16[2560,1536]{1,0:T(8,128)(2,1)} %bitcast.13), custom_call_target="tpu_custom_call" | custom-call | tf_op jit(solution)/shard_map/down_own/pallas_call | solution.py:100
  41.8 1.0 %collective-permute-done.13.refs_1_ = bf16[128,256]{1,0:T(8,128)(2,1)S(1)} collective-permute-done((bf16[128,256]{1,0:T(8,128)(2,1)S(1)}, bf16[128,256]{1,0:T(8,128)(2,1)S(1)}, u32[]{:S(2)}, u32[]{:S(2)}) %collective-permute-start.13) | collective-permute-done | bytes 65568 | tf_op jit(solution)/shard_map/ppermute | solution.py:44
  42.8 0.8 %down_other.2 = (bf16[128,1280]{1,0:T(8,128)(2,1)S(1)}, bf16[128,1280]{1,0:T(8,128)(2,1)S(1)}) custom-call(bf16[128,512]{1,0:T(8,128)(2,1)S(1)} %collective-permute-done.12.refs_0_, bf16[128,256]{1,0:T(8,128)(2,1)S(1)} %collective-permute-done.13.refs_1_, bf16[256,128]{1,0:T(8,128)(2,1)S(1)} %get-tuple-element.74.refs_2_, ...), custom_call_target="tpu_custom_call" | custom-call | tf_op jit(solution)/shard_map/down_other/pallas_call | solution.py:100
  43.7 0.8 %down_other.3 = (bf16[128,1280]{1,0:T(8,128)(2,1)S(1)}, bf16[128,1280]{1,0:T(8,128)(2,1)S(1)}) custom-call(bf16[128,512]{1,0:T(8,128)(2,1)S(1)} %collective-permute-done.12.refs_0_, bf16[128,256]{1,0:T(8,128)(2,1)S(1)} %collective-permute-done.13.refs_1_, bf16[256,128]{1,0:T(8,128)(2,1)S(1)} %get-tuple-element.74.refs_2_, ...), custom_call_target="tpu_custom_call" | custom-call | tf_op jit(solution)/shard_map/down_other/pallas_call | solution.py:100
  45.4 1.6 %collective-permute-start.15 = (bf16[64,1280]{1,0:T(8,128)(2,1)S(1)}, bf16[64,1280]{1,0:T(8,128)(2,1)S(1)}, u32[]{:S(2)}, u32[]{:S(2)}) collective-permute-start(bf16[64,1280]{1,0:T(8,128)(2,1)S(1)} %get-tuple-element.84), channel_id=1, source_target_pairs={{0,2},{1,17},{2,0},{3,19},{4,6},{5,21},{6,4},{7,23},{8,10},{9,25},... | collective-permute-start | bytes 491528 | tf_op jit(solution)/shard_map/ppermute | solution.py:60
  47.1 0.9 %collective-permute-start.18 = (bf16[64,1280]{1,0:T(8,128)(2,1)S(1)}, bf16[64,1280]{1,0:T(8,128)(2,1)S(1)}, u32[]{:S(2)}, u32[]{:S(2)}) collective-permute-start(bf16[64,1280]{1,0:T(8,128)(2,1)S(1)} %get-tuple-element.89), channel_id=1, source_target_pairs={{0,2},{1,17},{2,0},{3,19},{4,6},{5,21},{6,4},{7,23},{8,10},{9,25},... | collective-permute-start | bytes 491528 | tf_op jit(solution)/shard_map/ppermute | solution.py:60
  48.0 2.8 %collective-permute-done.15.got = bf16[64,1280]{1,0:T(8,128)(2,1)S(1)} collective-permute-done((bf16[64,1280]{1,0:T(8,128)(2,1)S(1)}, bf16[64,1280]{1,0:T(8,128)(2,1)S(1)}, u32[]{:S(2)}, u32[]{:S(2)}) %collective-permute-start.15) | collective-permute-done | bytes 163872 | tf_op jit(solution)/shard_map/ppermute | solution.py:60
  50.8 0.6 collective-permute-start.16
  51.4 1.1 %collective-permute-done.18.got = bf16[64,1280]{1,0:T(8,128)(2,1)S(1)} collective-permute-done((bf16[64,1280]{1,0:T(8,128)(2,1)S(1)}, bf16[64,1280]{1,0:T(8,128)(2,1)S(1)}, u32[]{:S(2)}, u32[]{:S(2)}) %collective-permute-start.18) | collective-permute-done | bytes 163872 | tf_op jit(solution)/shard_map/ppermute | solution.py:60
  53.2 3.3 %attention.1 = bf16[128,2048]{1,0:T(8,128)(2,1)} custom-call(bf16[32,2560]{1,0:T(8,128)(2,1)S(1)} %get-tuple-element.90.after, bf16[576,128]{1,0:T(8,128)(2,1)S(1)} %collective-permute-done.3.earlier, bf16[128,2304]{1,0:T(8,128)(2,1)} %queries_in.1, bf16[576,128]{1,0:T(8,128)(2,1)} %bitcast.15), custom_call_target="tpu_custom_call" | custom-call | tf_op jit(solution)/shard_map/attention/pallas_call | solution.py:100
  56.5 1.4 %collective-permute-done.19.refs_3_ = bf16[32,2560]{1,0:T(8,128)(2,1)S(1)} collective-permute-done((bf16[32,2560]{1,0:T(8,128)(2,1)S(1)}, bf16[32,2560]{1,0:T(8,128)(2,1)S(1)}, u32[]{:S(2)}, u32[]{:S(2)}) %collective-permute-start.19) | collective-permute-done | bytes 163872 | tf_op jit(solution)/shard_map/ppermute | solution.py:60
  58.1 3.1 %collective-permute-start.20 = (bf16[8,5120]{1,0:T(8,128)(2,1)S(1)}, bf16[8,5120]{1,0:T(8,128)(2,1)S(1)}, u32[]{:S(2)}, u32[]{:S(2)}) collective-permute-start(bf16[8,5120]{1,0:T(8,128)(2,1)S(1)} %get-tuple-element.97), channel_id=1, source_target_pairs={{0,12},{1,13},{2,14},{3,15},{4,8},{5,9},{6,10},{7,11},{8,4},{9,5},... | collective-permute-start | bytes 245768 | tf_op jit(solution)/shard_map/ppermute | solution.py:48
  61.1 1.4 %collective-permute-start.22 = (bf16[8,5120]{1,0:T(8,128)(2,1)S(1)}, bf16[8,5120]{1,0:T(8,128)(2,1)S(1)}, u32[]{:S(2)}, u32[]{:S(2)}) collective-permute-start(bf16[8,5120]{1,0:T(8,128)(2,1)S(1)} %get-tuple-element.99), channel_id=1, source_target_pairs={{0,4},{1,5},{2,6},{3,7},{4,0},{5,1},{6,2},{7,3},{8,12},{9,13},{10,... | collective-permute-start | bytes 245768 | tf_op jit(solution)/shard_map/ppermute | solution.py:48
  62.5 2.2 %collective-permute-done.20.refs_0_ = bf16[8,5120]{1,0:T(8,128)(2,1)S(1)} collective-permute-done((bf16[8,5120]{1,0:T(8,128)(2,1)S(1)}, bf16[8,5120]{1,0:T(8,128)(2,1)S(1)}, u32[]{:S(2)}, u32[]{:S(2)}) %collective-permute-start.20) | collective-permute-done | bytes 81952 | tf_op jit(solution)/shard_map/ppermute | solution.py:48
  64.7 2.6 %collective-permute-done.21.refs_1_ = bf16[8,5120]{1,0:T(8,128)(2,1)S(1)} collective-permute-done((bf16[8,5120]{1,0:T(8,128)(2,1)S(1)}, bf16[8,5120]{1,0:T(8,128)(2,1)S(1)}, u32[]{:S(2)}, u32[]{:S(2)}) %collective-permute-start.21) | collective-permute-done | bytes 81952 | tf_op jit(solution)/shard_map/ppermute | solution.py:48
  67.2 0.7 sum.1
  (33 shorter events, 4.2 us)
Async XLA Ops:
  1.7 13.4 %collective-permute-start.3 = (bf16[576,128]{1,0:T(8,128)(2,1)}, bf16[576,128]{1,0:T(8,128)(2,1)S(1)}, u32[]{:S(2)}, u32[]{:S(2)}) collective-permute-start(bf16[576,128]{1,0:T(8,128)(2,1)} %bitcast.14), channel_id=1, source_target_pairs={{0,16},{16,0},{1,17},{17,1},{2,18},{18,2},{3,19},{19,3},{4,20},{20... | collective-permute-start | bytes 442376 | tf_op jit(solution)/shard_map/ppermute | solution.py:44
  4.7 7.7 %collective-permute-start = (bf16[8,5248]{1,0:T(8,128)(2,1)S(1)}, bf16[8,5248]{1,0:T(8,128)(2,1)S(1)}, u32[]{:S(2)}, u32[]{:S(2)}) collective-permute-start(bf16[8,5248]{1,0:T(8,128)(2,1)S(1)} %rows.1.refs_0_), channel_id=1, source_target_pairs={{0,12},{1,13},{2,14},{3,15},{4,8},{5,9},{6,10},{7,11},{8,4},{9,5},... | collective-permute-start | bytes 251912 | tf_op jit(solution)/shard_map/ppermute | solution.py:48
  8.3 6.8 %collective-permute-start.1 = (bf16[8,5248]{1,0:T(8,128)(2,1)S(1)}, bf16[8,5248]{1,0:T(8,128)(2,1)S(1)}, u32[]{:S(2)}, u32[]{:S(2)}) collective-permute-start(bf16[8,5248]{1,0:T(8,128)(2,1)S(1)} %rows.1.refs_0_), channel_id=1, source_target_pairs={{0,8},{1,9},{2,10},{3,11},{4,12},{5,13},{6,14},{7,15},{8,0},{9,1},... | collective-permute-start | bytes 251912 | tf_op jit(solution)/shard_map/ppermute | solution.py:48
  8.3 6.8 %collective-permute-start.2 = (bf16[8,5248]{1,0:T(8,128)(2,1)S(1)}, bf16[8,5248]{1,0:T(8,128)(2,1)S(1)}, u32[]{:S(2)}, u32[]{:S(2)}) collective-permute-start(bf16[8,5248]{1,0:T(8,128)(2,1)S(1)} %rows.1.refs_0_), channel_id=1, source_target_pairs={{0,4},{1,5},{2,6},{3,7},{4,0},{5,1},{6,2},{7,3},{8,12},{9,13},{10,... | collective-permute-start | bytes 251912 | tf_op jit(solution)/shard_map/ppermute | solution.py:48
  15.0 5.5 %collective-permute-start.8 = (bf16[32,2688]{1,0:T(8,128)(2,1)S(1)}, bf16[32,2688]{1,0:T(8,128)(2,1)S(1)}, u32[]{:S(2)}, u32[]{:S(2)}) collective-permute-start(bf16[32,2688]{1,0:T(8,128)(2,1)S(1)} %get-tuple-element.59.refs_0_), channel_id=1, source_target_pairs={{0,2},{1,17},{2,0},{3,19},{4,6},{5,21},{6,4},{7,23},{8,10},{9,25},... | collective-permute-start | bytes 516104 | tf_op jit(solution)/shard_map/ppermute | solution.py:60
  16.6 5.8 %collective-permute-start.4 = (bf16[32,2560]{1,0:T(8,128)(2,1)S(1)}, bf16[32,2560]{1,0:T(8,128)(2,1)S(1)}, u32[]{:S(2)}, u32[]{:S(2)}) collective-permute-start(bf16[32,2560]{1,0:T(8,128)(2,1)S(1)} %get-tuple-element.58.refs_0_), channel_id=1, source_target_pairs={{0,2},{1,17},{2,0},{3,19},{4,6},{5,21},{6,4},{7,23},{8,10},{9,25},... | collective-permute-start | bytes 491528 | tf_op jit(solution)/shard_map/ppermute | solution.py:60
  20.5 7.3 %collective-permute-start.9 = (bf16[64,2688]{1,0:T(8,128)(2,1)S(1)}, bf16[64,2688]{1,0:T(8,128)(2,1)S(1)}, u32[]{:S(2)}, u32[]{:S(2)}) collective-permute-start(bf16[64,2688]{1,0:T(8,128)(2,1)S(1)} %stack_two.3.refs_0_), channel_id=1, source_target_pairs={{0,16},{1,3},{2,18},{3,1},{4,20},{5,7},{6,22},{7,5},{8,24},{9,11},... | collective-permute-start | bytes 1032200 | tf_op jit(solution)/shard_map/ppermute | solution.py:60
  22.4 8.9 %collective-permute-start.5 = (bf16[64,2560]{1,0:T(8,128)(2,1)S(1)}, bf16[64,2560]{1,0:T(8,128)(2,1)S(1)}, u32[]{:S(2)}, u32[]{:S(2)}) collective-permute-start(bf16[64,2560]{1,0:T(8,128)(2,1)S(1)} %stack_two.2.refs_0_), channel_id=1, source_target_pairs={{0,16},{1,3},{2,18},{3,1},{4,20},{5,7},{6,22},{7,5},{8,24},{9,11},... | collective-permute-start | bytes 983048 | tf_op jit(solution)/shard_map/ppermute | solution.py:60
  27.7 3.6 %collective-permute-start.10 = (bf16[64,2688]{1,0:T(8,128)(2,1)S(1)}, bf16[64,2688]{1,0:T(8,128)(2,1)S(1)}, u32[]{:S(2)}, u32[]{:S(2)}) collective-permute-start(bf16[64,2688]{1,0:T(8,128)(2,1)S(1)} %stack_two.3.refs_0_), channel_id=1, source_target_pairs={{0,1},{1,0},{2,3},{3,2},{4,5},{5,4},{6,7},{7,6},{8,9},{9,8},{10,11... | collective-permute-start | bytes 1032200 | tf_op jit(solution)/shard_map/ppermute | solution.py:44
  27.9 3.5 %collective-permute-start.11 = (bf16[64,2688]{1,0:T(8,128)(2,1)S(1)}, bf16[64,2688]{1,0:T(8,128)(2,1)S(1)}, u32[]{:S(2)}, u32[]{:S(2)}) collective-permute-start(bf16[64,2688]{1,0:T(8,128)(2,1)S(1)} %collective-permute-done.9.refs_1_), channel_id=1, source_target_pairs={{0,1},{1,0},{2,3},{3,2},{4,5},{5,4},{6,7},{7,6},{8,9},{9,8},{10,11... | collective-permute-start | bytes 1032200 | tf_op jit(solution)/shard_map/ppermute | solution.py:44
  28.3 5.4 %collective-permute-start.6 = (bf16[64,2560]{1,0:T(8,128)(2,1)S(1)}, bf16[64,2560]{1,0:T(8,128)(2,1)S(1)}, u32[]{:S(2)}, u32[]{:S(2)}) collective-permute-start(bf16[64,2560]{1,0:T(8,128)(2,1)S(1)} %stack_two.2.refs_0_), channel_id=1, source_target_pairs={{0,1},{1,0},{2,3},{3,2},{4,5},{5,4},{6,7},{7,6},{8,9},{9,8},{10,11... | collective-permute-start | bytes 983048 | tf_op jit(solution)/shard_map/ppermute | solution.py:44
  31.4 2.3 %collective-permute-start.7 = (bf16[64,2560]{1,0:T(8,128)(2,1)S(1)}, bf16[64,2560]{1,0:T(8,128)(2,1)S(1)}, u32[]{:S(2)}, u32[]{:S(2)}) collective-permute-start(bf16[64,2560]{1,0:T(8,128)(2,1)S(1)} %collective-permute-done.5.refs_1_), channel_id=1, source_target_pairs={{0,1},{1,0},{2,3},{3,2},{4,5},{5,4},{6,7},{7,6},{8,9},{9,8},{10,11... | collective-permute-start | bytes 983048 | tf_op jit(solution)/shard_map/ppermute | solution.py:44
  35.4 7.4 %collective-permute-start.12 = (bf16[128,512]{1,0:T(8,128)(2,1)S(1)}, bf16[128,512]{1,0:T(8,128)(2,1)S(1)}, u32[]{:S(2)}, u32[]{:S(2)}) collective-permute-start(bf16[128,512]{1,0:T(8,128)(2,1)S(1)} %get-tuple-element.71), channel_id=1, source_target_pairs={{0,16},{16,0},{1,17},{17,1},{2,18},{18,2},{3,19},{19,3},{4,20},{20... | collective-permute-start | bytes 393224 | tf_op jit(solution)/shard_map/ppermute | solution.py:44
  37.1 5.7 %collective-permute-start.13 = (bf16[128,256]{1,0:T(8,128)(2,1)S(1)}, bf16[128,256]{1,0:T(8,128)(2,1)S(1)}, u32[]{:S(2)}, u32[]{:S(2)}) collective-permute-start(bf16[128,256]{1,0:T(8,128)(2,1)S(1)} %get-tuple-element.73), channel_id=1, source_target_pairs={{0,16},{16,0},{1,17},{17,1},{2,18},{18,2},{3,19},{19,3},{4,20},{20... | collective-permute-start | bytes 196616 | tf_op jit(solution)/shard_map/ppermute | solution.py:44
  43.6 1.7 %collective-permute-start.14 = (bf16[128,1280]{1,0:T(8,128)(2,1)S(1)}, bf16[128,1280]{1,0:T(8,128)(2,1)S(1)}, u32[]{:S(2)}, u32[]{:S(2)}) collective-permute-start(bf16[128,1280]{1,0:T(8,128)(2,1)S(1)} %get-tuple-element.82), channel_id=1, source_target_pairs={{0,1},{1,0},{2,3},{3,2},{4,5},{5,4},{6,7},{7,6},{8,9},{9,8},{10,11... | collective-permute-start | bytes 983048 | tf_op jit(solution)/shard_map/ppermute | solution.py:44
  44.5 2.5 %collective-permute-start.17 = (bf16[128,1280]{1,0:T(8,128)(2,1)S(1)}, bf16[128,1280]{1,0:T(8,128)(2,1)S(1)}, u32[]{:S(2)}, u32[]{:S(2)}) collective-permute-start(bf16[128,1280]{1,0:T(8,128)(2,1)S(1)} %get-tuple-element.87), channel_id=1, source_target_pairs={{0,1},{1,0},{2,3},{3,2},{4,5},{5,4},{6,7},{7,6},{8,9},{9,8},{10,11... | collective-permute-start | bytes 983048 | tf_op jit(solution)/shard_map/ppermute | solution.py:44
  45.4 5.4 %collective-permute-start.15 = (bf16[64,1280]{1,0:T(8,128)(2,1)S(1)}, bf16[64,1280]{1,0:T(8,128)(2,1)S(1)}, u32[]{:S(2)}, u32[]{:S(2)}) collective-permute-start(bf16[64,1280]{1,0:T(8,128)(2,1)S(1)} %get-tuple-element.84), channel_id=1, source_target_pairs={{0,2},{1,17},{2,0},{3,19},{4,6},{5,21},{6,4},{7,23},{8,10},{9,25},... | collective-permute-start | bytes 491528 | tf_op jit(solution)/shard_map/ppermute | solution.py:60
  47.1 5.5 %collective-permute-start.18 = (bf16[64,1280]{1,0:T(8,128)(2,1)S(1)}, bf16[64,1280]{1,0:T(8,128)(2,1)S(1)}, u32[]{:S(2)}, u32[]{:S(2)}) collective-permute-start(bf16[64,1280]{1,0:T(8,128)(2,1)S(1)} %get-tuple-element.89), channel_id=1, source_target_pairs={{0,2},{1,17},{2,0},{3,19},{4,6},{5,21},{6,4},{7,23},{8,10},{9,25},... | collective-permute-start | bytes 491528 | tf_op jit(solution)/shard_map/ppermute | solution.py:60
  50.8 5.7 %collective-permute-start.16 = (bf16[32,2560]{1,0:T(8,128)(2,1)S(1)}, bf16[32,2560]{1,0:T(8,128)(2,1)S(1)}, u32[]{:S(2)}, u32[]{:S(2)}) collective-permute-start(bf16[32,2560]{1,0:T(8,128)(2,1)S(1)} %get-tuple-element.85), channel_id=1, source_target_pairs={{0,16},{1,3},{2,18},{3,1},{4,20},{5,7},{6,22},{7,5},{8,24},{9,11},... | collective-permute-start | bytes 491528 | tf_op jit(solution)/shard_map/ppermute | solution.py:60
  52.6 5.4 %collective-permute-start.19 = (bf16[32,2560]{1,0:T(8,128)(2,1)S(1)}, bf16[32,2560]{1,0:T(8,128)(2,1)S(1)}, u32[]{:S(2)}, u32[]{:S(2)}) collective-permute-start(bf16[32,2560]{1,0:T(8,128)(2,1)S(1)} %get-tuple-element.90.after), channel_id=1, source_target_pairs={{0,16},{1,3},{2,18},{3,1},{4,20},{5,7},{6,22},{7,5},{8,24},{9,11},... | collective-permute-start | bytes 491528 | tf_op jit(solution)/shard_map/ppermute | solution.py:60
  58.1 6.6 %collective-permute-start.20 = (bf16[8,5120]{1,0:T(8,128)(2,1)S(1)}, bf16[8,5120]{1,0:T(8,128)(2,1)S(1)}, u32[]{:S(2)}, u32[]{:S(2)}) collective-permute-start(bf16[8,5120]{1,0:T(8,128)(2,1)S(1)} %get-tuple-element.97), channel_id=1, source_target_pairs={{0,12},{1,13},{2,14},{3,15},{4,8},{5,9},{6,10},{7,11},{8,4},{9,5},... | collective-permute-start | bytes 245768 | tf_op jit(solution)/shard_map/ppermute | solution.py:48
  61.1 6.1 %collective-permute-start.21 = (bf16[8,5120]{1,0:T(8,128)(2,1)S(1)}, bf16[8,5120]{1,0:T(8,128)(2,1)S(1)}, u32[]{:S(2)}, u32[]{:S(2)}) collective-permute-start(bf16[8,5120]{1,0:T(8,128)(2,1)S(1)} %get-tuple-element.98), channel_id=1, source_target_pairs={{0,8},{1,9},{2,10},{3,11},{4,12},{5,13},{6,14},{7,15},{8,0},{9,1},... | collective-permute-start | bytes 245768 | tf_op jit(solution)/shard_map/ppermute | solution.py:48
  61.1 6.1 %collective-permute-start.22 = (bf16[8,5120]{1,0:T(8,128)(2,1)S(1)}, bf16[8,5120]{1,0:T(8,128)(2,1)S(1)}, u32[]{:S(2)}, u32[]{:S(2)}) collective-permute-start(bf16[8,5120]{1,0:T(8,128)(2,1)S(1)} %get-tuple-element.99), channel_id=1, source_target_pairs={{0,4},{1,5},{2,6},{3,7},{4,0},{5,1},{6,2},{7,3},{8,12},{9,13},{10,... | collective-permute-start | bytes 245768 | tf_op jit(solution)/shard_map/ppermute | solution.py:48

commit v4 on v3

--- a/solution.py
+++ b/solution.py
@@ -66,14 +66,6 @@
 
 def over_x(ctx, exp):
     return 1 - ctx, exp
-
-
-def y_then_x(ctx, exp):
-    return over_x(ctx, exp) if exp % 2 else over_y(ctx, exp)
-
-
-def x_then_y(ctx, exp):
-    return over_y(ctx, exp) if exp % 2 else over_x(ctx, exp)
 
 
 def times_rows_in(left, right):
@@ -229,17 +221,15 @@
         copy.wait()
 
 
-def assemble(place, core, two_ref, far_ref, two_other_ref, far_other_ref, unit, start=0):
+def assemble(place, two_ref, far_ref, two_other_ref, far_other_ref, unit, y_first, start=0):
     span = slice(start, start + place.shape[1])
+    order = (0, 2, 1, 3) if y_first else (0, 1, 2, 3)
     for lane, two, far in ((0, two_ref, far_ref), (1, two_other_ref, far_other_ref)):
-        went_x = core if lane == 0 else 1 - core
-        base = lane * 4 * unit
-        near = pl.multiple_of(base + (2 - went_x) * unit, unit)
-        next_ = pl.multiple_of(base + (1 + went_x) * unit, unit)
-        place[base : base + unit, :] = two[:unit, span]
-        place[pl.ds(near, unit), :] = two[unit:, span]
-        place[pl.ds(next_, unit), :] = far[:unit, span]
-        place[base + 3 * unit : base + 4 * unit, :] = far[unit:, span]
+        for number, block in enumerate(order):
+            ref = (two, far)[number // 2]
+            rows = slice(number % 2 * unit, (number % 2 + 1) * unit)
+            base = (lane * 4 + block) * unit
+            place[base : base + unit, :] = ref[rows, span]
 
 
 def first_kernel(
@@ -251,11 +241,11 @@
     rows = tokens.shape[0]
     slots = pick_out.shape[1]
     expert = lax.axis_index("exp")
-    assemble(tokens, expert % 2, two, far, two_other, far_other, unit)
+    assemble(tokens, two, far, two_other, far_other, unit, True)
     gate_out[...] = times_rows_in(tokens[...], gate_w[...])
     up_out[...] = times_rows_in(tokens[...], up_w[...])
 
-    assemble(notes, expert % 2, two, far, two_other, far_other, unit, width)
+    assemble(notes, two, far, two_other, far_other, unit, True, width)
     note = notes[...].astype(jnp.float32)
     lane = lax.broadcasted_iota(jnp.int32, note.shape, 1)
     mine = (note == expert.astype(jnp.float32)) & (lane < topk)
@@ -298,7 +288,7 @@
     two, far, two_other, far_other, gate_w, up_w, gate_in, up_in, pick,
     act_out, packed_out, tokens, *, unit,
 ):
-    assemble(tokens, lax.axis_index("exp") % 2, two, far, two_other, far_other, unit)
+    assemble(tokens, two, far, two_other, far_other, unit, False)
     finish_units(tokens, gate_w, up_w, gate_in, up_in, pick, act_out, packed_out, 0)
 
 
@@ -337,59 +327,43 @@
         give[:, n : n + tall] = projected[half:].astype(jnp.bfloat16)
 
 
-def spread_kernel(keep, got, send, stay):
-    core = lax.axis_index("exp") % 2
+def spread_kernel(keep, got, send, stay, *, y_first):
     unit = keep.shape[0] // 4
-
-    def total(block):
-        span = slice(block * unit, (block + 1) * unit)
-        return keep[span, :].astype(jnp.float32) + got[span, :].astype(jnp.float32)
-
-    for this, (stays, sends) in enumerate((((0, 1), (2, 3)), ((0, 2), (1, 3)))):
-
-        @pl.when(core == this)
-        def _():
-            for number in range(2):
-                span = slice(number * unit, (number + 1) * unit)
-                stay[span, :] = total(stays[number])
-                send[span, :] = total(sends[number]).astype(jnp.bfloat16)
-
-
-def cross_kernel(stay, got, send, left):
-    core = lax.axis_index("exp") % 2
-    unit, part = send.shape[0], send.shape[1] // 2
-
-    @pl.when(core == 0)
-    def _():
-        left[:, :part] = stay[:unit, :] + got[:unit, :].astype(jnp.float32)
-        left[:, part:] = jnp.zeros((unit, part), jnp.float32)
-        send[:, :part] = (stay[unit:, :] + got[unit:, :].astype(jnp.float32)).astype(jnp.bfloat16)
-        send[:, part:] = jnp.zeros((unit, part), jnp.bfloat16)
-
-    @pl.when(core == 1)
-    def _():
+    stays, sends = ((0, 1), (2, 3)) if y_first else ((0, 2), (1, 3))
+    for out, blocks in ((stay, stays), (send, sends)):
+        for number, block in enumerate(blocks):
+            span = slice(block * unit, (block + 1) * unit)
+            total = keep[span, :].astype(jnp.float32) + got[span, :].astype(jnp.float32)
+            out[number * unit : (number + 1) * unit, :] = total.astype(out.dtype)
+
+
+def cross_kernel(stay, got, send, left, *, y_first):
+    unit, part = send.shape[0], stay.shape[1]
+    if y_first:
+        left[...] = stay[:unit, :] + got[:unit, :].astype(jnp.float32)
+        send[...] = (stay[unit:, :] + got[unit:, :].astype(jnp.float32)).astype(jnp.bfloat16)
+    else:
         left[:, :part] = stay[:unit, :]
         left[:, part:] = got[:unit, :].astype(jnp.float32)
         send[:, :part] = stay[unit:, :].astype(jnp.bfloat16)
         send[:, part:] = got[unit:, :]
 
 
-def line_kernel(*refs, line):
-    ins, outs = refs[:4], refs[4:]
-    core = lax.axis_index("exp") % 2
+def line_kernel(left_y, got_x, left_x, got_y, *outs):
     ctx = lax.axis_index("ctx")
-    count = outs[0].shape[0]
-    part = ins[0].shape[1] // 2
-    for number in range(2):
-        left, got = ins[2 * number], ins[2 * number + 1]
-        arrived = got[...].astype(jnp.float32)
-        own = left[:, :part] + jnp.where(core == 1, arrived[:, :part], 0.0)
-        other = left[:, part:] + jnp.where(core == 1, arrived[:, part:], arrived[:, :part])
-        for value, side in ((own, ctx), (other, 1 - ctx)):
-            at = pl.multiple_of(side * 2 * part + number * part, 128)
-            for place, out in enumerate(outs):
-                rows = value[place * count : (place + 1) * count]
-                out[:, pl.ds(at, part)] = rows.astype(out.dtype)
+    count, part = outs[0].shape[0], left_y.shape[1]
+    whole = left_x[...] + got_y[...].astype(jnp.float32)
+    blocks = (
+        (left_y[...], ctx, 0),
+        (got_x[...].astype(jnp.float32), 1 - ctx, 0),
+        (whole[:, :part], ctx, 1),
+        (whole[:, part:], 1 - ctx, 1),
+    )
+    for value, side, number in blocks:
+        at = pl.multiple_of(side * 2 * part + number * part, 128)
+        for place, out in enumerate(outs):
+            rows = value[place * count : (place + 1) * count]
+            out[:, pl.ds(at, part)] = rows.astype(out.dtype)
 
 
 def sum_kernel(first, *refs):
@@ -456,8 +430,8 @@
         "stack_line",
     )
     pieces = []
-    for near in nears:
-        got = paired(near, y_then_x)
+    for near, first, then in zip(nears, (over_y, over_x), (over_x, over_y)):
+        got = paired(near, first)
         (two,) = local_kernel(
             lambda *refs, cut=near.shape[1]: stack_kernel(*refs, cuts=((0, cut),)),
             [(near, "vmem"), (got, "vmem")],
@@ -465,7 +439,7 @@
             [],
             "stack_two",
         )
-        pieces.append([two, paired(two, x_then_y)])
+        pieces.append([two, paired(two, then)])
     gate_2, up_2, down_mine = local_kernel(
         lambda *refs: fetch_kernel(*refs, start=half),
         [(pieces[1][0], "vmem"), (w_gate[0], "hbm"), (w_up[0], "hbm"), (w_down[0], "hbm")],
@@ -522,7 +496,7 @@
     )
     part = columns // 2
     crossing = []
-    for start in (0, part):
+    for start, y_first in ((0, True), (part, False)):
         keep, give = local_kernel(
             lambda *refs, start=start: other_kernel(*refs, start=start),
             [
@@ -534,23 +508,24 @@
             "down_other",
         )
         send, stay = local_kernel(
-            spread_kernel,
+            lambda *refs, y_first=y_first: spread_kernel(*refs, y_first=y_first),
             [(keep, "vmem"), (swapped(give, "exp", 1), "vmem")],
             [((2 * unit, part), bf16, "vmem"), ((2 * unit, part), f32, "vmem")],
             [],
             "spread",
         )
-        crossing.append((stay, paired(send, y_then_x)))
+        crossing.append((y_first, stay, paired(send, over_y if y_first else over_x)))
     lines = []
-    for stay, got in crossing:
+    for y_first, stay, got in crossing:
+        wide = part if y_first else 2 * part
         send, left = local_kernel(
-            cross_kernel,
+            lambda *refs, y_first=y_first: cross_kernel(*refs, y_first=y_first),
             [(stay, "vmem"), (got, "vmem")],
-            [((unit, 2 * part), bf16, "vmem"), ((unit, 2 * part), f32, "vmem")],
+            [((unit, wide), bf16, "vmem"), ((unit, wide), f32, "vmem")],
             [],
             "cross",
         )
-        lines += [left, paired(send, x_then_y)]
+        lines += [left, paired(send, over_x if y_first else over_y)]
     pad = -key_width % 128
     (attended,) = local_kernel(
         attention_kernel,
@@ -568,7 +543,7 @@
     )
     lines[1], attended = lax.optimization_barrier((lines[1], attended))
     keep, *sends = local_kernel(
-        lambda *refs: line_kernel(*refs, line=line),
+        line_kernel,
         [(block, "vmem") for block in lines],
         [((tok_dev, 2 * columns), f32, "vmem")]
         + [((tok_dev, 2 * columns), bf16, "vmem")] * (line - 1),

time: 68.1 us -> 67.6 us (level)
  waiting for transfers between devices: 21.6 us -> 20.6 us
  starting transfers between devices: 22.5 us -> 23.2 us
    ppermute x8, waiting for transfers between devices: 12.9 us -> 10.9 us  [paired(): return lax.ppermute(block, ('ctx', 'exp'), route)]
    ppermute x9, waiting for transfers between devices: 1.29 us -> 2.48 us  [swapped(): lax.ppermute(block, axis, [(i, i ^ bit) for i in range(lax.axis_size(axis...]
    ppermute x8, starting transfers between devices: 7.24 us -> 7.94 us  [paired(): return lax.ppermute(block, ('ctx', 'exp'), route)]
  transfers between devices with their start and end apart: 23 -> 23, of which waited for: 11 -> 12; matrix products, arithmetic and copies ran while one was open for 0% -> 0% of each run, Pallas kernels for 28% -> 28%
where the time goes in v4:
time: 67.6 us; the launch traced here: 67.5 us
  starting transfers between devices  23.2 us (34%)
  Pallas kernels  23 us (34%)
  waiting for transfers between devices  20.6 us (30%)
  between operations  0.8 us (1%)
    pallas_call x19, Pallas kernels, local_kernel(): pl.pallas_call(body, in_specs=[pl.BlockSpec(memory_space=kinds[kind]) for...  23 us
    ppermute x8, waiting for transfers between devices, paired(): return lax.ppermute(block, ('ctx', 'exp'), route)  10.9 us
    ppermute x6, starting transfers between devices, along_line(): lax.ppermute(block, 'exp', [(i, i ^ 4 * steps) for i in range(lax.axis_si...  8.84 us
    ppermute x8, starting transfers between devices, paired(): return lax.ppermute(block, ('ctx', 'exp'), route)  7.94 us
    ppermute x6, waiting for transfers between devices, along_line(): lax.ppermute(block, 'exp', [(i, i ^ 4 * steps) for i in range(lax.axis_si...  7.12 us
    ppermute x9, starting transfers between devices, swapped(): lax.ppermute(block, axis, [(i, i ^ bit) for i in range(lax.axis_size(axis...  6.38 us
    ppermute x9, waiting for transfers between devices, swapped(): lax.ppermute(block, axis, [(i, i ^ bit) for i in range(lax.axis_size(axis...  2.48 us
  transfers between devices with their start and end apart: 23, of which 12 were waited for; matrix products, arithmetic and copies ran while one was open for 0% of the time, Pallas kernels for 28%

profile of v4, /device:TPU:0, one launch (start us, length us, event | category | flops | bytes accessed | tf_op | source)
XLA Modules:
  0.0 67.5 jit_solution(10048238385388970201)
XLA Ops:
  0.6 1.0 %rows.1.refs_0_ = bf16[8,5248]{1,0:T(8,128)(2,1)S(1)} custom-call(bf16[8,5120]{1,0:T(8,128)(2,1)} %bitcast.16, s32[6,1,8]{2,1,0:T(1,128)} %bitcast.18, f32[6,1,8]{2,1,0:T(1,128)} %bitcast.19), custom_call_target="tpu_custom_call" | custom-call | tf_op jit(solution)/shard_map/rows/pallas_call | solution.py:92
  1.7 3.0 %collective-permute-start.3 = (bf16[576,128]{1,0:T(8,128)(2,1)}, bf16[576,128]{1,0:T(8,128)(2,1)S(1)}, u32[]{:S(2)}, u32[]{:S(2)}) collective-permute-start(bf16[576,128]{1,0:T(8,128)(2,1)} %bitcast.14), channel_id=1, source_target_pairs={{0,16},{16,0},{1,17},{17,1},{2,18},{18,2},{3,19},{19,3},{4,20},{20... | collective-permute-start | bytes 442376 | tf_op jit(solution)/shard_map/ppermute | solution.py:44
  4.7 3.6 %collective-permute-start = (bf16[8,5248]{1,0:T(8,128)(2,1)S(1)}, bf16[8,5248]{1,0:T(8,128)(2,1)S(1)}, u32[]{:S(2)}, u32[]{:S(2)}) collective-permute-start(bf16[8,5248]{1,0:T(8,128)(2,1)S(1)} %rows.1.refs_0_), channel_id=1, source_target_pairs={{0,12},{1,13},{2,14},{3,15},{4,8},{5,9},{6,10},{7,11},{8,4},{9,5},... | collective-permute-start | bytes 251912 | tf_op jit(solution)/shard_map/ppermute | solution.py:48
  8.3 0.8 %collective-permute-start.2 = (bf16[8,5248]{1,0:T(8,128)(2,1)S(1)}, bf16[8,5248]{1,0:T(8,128)(2,1)S(1)}, u32[]{:S(2)}, u32[]{:S(2)}) collective-permute-start(bf16[8,5248]{1,0:T(8,128)(2,1)S(1)} %rows.1.refs_0_), channel_id=1, source_target_pairs={{0,4},{1,5},{2,6},{3,7},{4,0},{5,1},{6,2},{7,3},{8,12},{9,13},{10,... | collective-permute-start | bytes 251912 | tf_op jit(solution)/shard_map/ppermute | solution.py:48
  9.0 3.3 %fetch.2 = (bf16[768,2560]{1,0:T(8,128)(2,1)S(1)}, bf16[768,2560]{1,0:T(8,128)(2,1)S(1)}) custom-call(bf16[8,5248]{1,0:T(8,128)(2,1)S(1)} %rows.1.refs_0_, bf16[768,5120]{1,0:T(8,128)(2,1)} %bitcast.8, bf16[768,5120]{1,0:T(8,128)(2,1)} %bitcast.10), custom_call_target="tpu_custom_call" | custom-call | tf_op jit(solution)/shard_map/fetch/pallas_call | solution.py:92
  12.4 2.6 %collective-permute-done.1.refs_2_ = bf16[8,5248]{1,0:T(8,128)(2,1)S(1)} collective-permute-done((bf16[8,5248]{1,0:T(8,128)(2,1)S(1)}, bf16[8,5248]{1,0:T(8,128)(2,1)S(1)}, u32[]{:S(2)}, u32[]{:S(2)}) %collective-permute-start.1) | collective-permute-done | bytes 84000 | tf_op jit(solution)/shard_map/ppermute | solution.py:48
  15.0 1.6 %collective-permute-start.8 = (bf16[32,2688]{1,0:T(8,128)(2,1)S(1)}, bf16[32,2688]{1,0:T(8,128)(2,1)S(1)}, u32[]{:S(2)}, u32[]{:S(2)}) collective-permute-start(bf16[32,2688]{1,0:T(8,128)(2,1)S(1)} %get-tuple-element.59.refs_0_), channel_id=1, source_target_pairs={{0,2},{1,3},{2,0},{3,1},{4,6},{5,7},{6,4},{7,5},{8,10},{9,11},{10,... | collective-permute-start | bytes 516104 | tf_op jit(solution)/shard_map/ppermute | solution.py:60
  17.2 4.0 %collective-permute-done.8.refs_1_ = bf16[32,2688]{1,0:T(8,128)(2,1)S(1)} collective-permute-done((bf16[32,2688]{1,0:T(8,128)(2,1)S(1)}, bf16[32,2688]{1,0:T(8,128)(2,1)S(1)}, u32[]{:S(2)}, u32[]{:S(2)}) %collective-permute-start.8) | collective-permute-done | bytes 172064 | tf_op jit(solution)/shard_map/ppermute | solution.py:60
  21.5 0.7 collective-permute-done.4.refs_1_
  22.2 1.2 %collective-permute-start.5 = (bf16[64,2560]{1,0:T(8,128)(2,1)S(1)}, bf16[64,2560]{1,0:T(8,128)(2,1)S(1)}, u32[]{:S(2)}, u32[]{:S(2)}) collective-permute-start(bf16[64,2560]{1,0:T(8,128)(2,1)S(1)} %stack_two.2.refs_0_), channel_id=1, source_target_pairs={{0,2},{1,3},{2,0},{3,1},{4,6},{5,7},{6,4},{7,5},{8,10},{9,11},{10,... | collective-permute-start | bytes 983048 | tf_op jit(solution)/shard_map/ppermute | solution.py:60
  23.4 4.5 %fetch.3 = (bf16[768,2560]{1,0:T(8,128)(2,1)S(1)}, bf16[768,2560]{1,0:T(8,128)(2,1)S(1)}, bf16[2560,768]{1,0:T(8,128)(2,1)S(1)}) custom-call(bf16[64,2560]{1,0:T(8,128)(2,1)S(1)} %stack_two.2.refs_0_, bf16[768,5120]{1,0:T(8,128)(2,1)} %bitcast.9, bf16[768,5120]{1,0:T(8,128)(2,1)} %bitcast.11, bf16[2560,1536]{1,0:T(8,128)(2,1)} %bitcast.12), custom_call_target="tpu_custom_call" | custom-call | tf_op jit(solution)/shard_map/fetch/pallas_call | solution.py:92
  27.9 2.1 %collective-permute-done.9.refs_1_ = bf16[64,2688]{1,0:T(8,128)(2,1)S(1)} collective-permute-done((bf16[64,2688]{1,0:T(8,128)(2,1)S(1)}, bf16[64,2688]{1,0:T(8,128)(2,1)S(1)}, u32[]{:S(2)}, u32[]{:S(2)}) %collective-permute-start.9) | collective-permute-done | bytes 344096 | tf_op jit(solution)/shard_map/ppermute | solution.py:60
  30.5 1.1 %collective-permute-done.11.refs_3_ = bf16[64,2688]{1,0:T(8,128)(2,1)S(1)} collective-permute-done((bf16[64,2688]{1,0:T(8,128)(2,1)S(1)}, bf16[64,2688]{1,0:T(8,128)(2,1)S(1)}, u32[]{:S(2)}, u32[]{:S(2)}) %collective-permute-start.11) | collective-permute-done | bytes 344096 | tf_op jit(solution)/shard_map/ppermute | solution.py:44
  31.7 2.3 %gate_up_first.1 = (f32[256,768]{1,0:T(8,128)S(1)}, f32[256,768]{1,0:T(8,128)S(1)}, bf16[256,128]{1,0:T(8,128)(2,1)S(1)}, bf16[256,128]{1,0:T(8,128)(2,1)S(1)}, f32[256,128]{1,0:T(8,128)S(1)}) custom-call(bf16[64,2688]{1,0:T(8,128)(2,1)S(1)} %stack_two.3.refs_0_, bf16[64,2688]{1,0:T(8,128)(2,1)S(1)} %collective-permute-done.9.refs_1_, ...), custom_call_target="tpu_custom_call" | custom-call | tf_op jit(solution)/shard_map/gate_up_first/pallas_call | solution.py:92
  34.0 1.7 %gate_up_second.1 = (bf16[256,512]{1,0:T(8,128)(2,1)S(1)}, bf16[128,512]{1,0:T(8,128)(2,1)S(1)}, bf16[256,2560]{1,0:T(8,128)(2,1)S(1)}) custom-call(bf16[64,2560]{1,0:T(8,128)(2,1)S(1)} %stack_two.2.refs_0_, bf16[64,2560]{1,0:T(8,128)(2,1)S(1)} %collective-permute-done.5.refs_1_, bf16[64,2560]{1,0:T(8,128)(2,1)S(1)} %collective-permute-done.6.refs_2_, ...), custom_call_target="tpu_custom_call" | custom-call | tf_op jit(solution)/shard_map/gate_up_second/pallas_call | solution.py:92
  36.1 1.0 %gate_up_third.1 = (bf16[256,256]{1,0:T(8,128)(2,1)S(1)}, bf16[128,256]{1,0:T(8,128)(2,1)S(1)}) custom-call(bf16[256,2560]{1,0:T(8,128)(2,1)S(1)} %get-tuple-element.72.refs_0_, bf16[768,2560]{1,0:T(8,128)(2,1)S(1)} %get-tuple-element.63.refs_4_.refs_1_, bf16[768,2560]{1,0:T(8,128)(2,1)S(1)} %get-tuple-element.64.refs_5_.refs_2_, ...), custom_call_target="tpu_custom_call" | custom-call | tf_op jit(solution)/shard_map/gate_up_third/pallas_call | solution.py:92
  37.1 1.8 %collective-permute-start.13 = (bf16[128,256]{1,0:T(8,128)(2,1)S(1)}, bf16[128,256]{1,0:T(8,128)(2,1)S(1)}, u32[]{:S(2)}, u32[]{:S(2)}) collective-permute-start(bf16[128,256]{1,0:T(8,128)(2,1)S(1)} %get-tuple-element.73), channel_id=1, source_target_pairs={{0,16},{16,0},{1,17},{17,1},{2,18},{18,2},{3,19},{19,3},{4,20},{20... | collective-permute-start | bytes 196616 | tf_op jit(solution)/shard_map/ppermute | solution.py:44
  38.9 3.1 %down_own.1 = (f32[256,2560]{1,0:T(8,128)S(1)}, bf16[2560,768]{1,0:T(8,128)(2,1)S(1)}) custom-call(bf16[256,512]{1,0:T(8,128)(2,1)S(1)} %get-tuple-element.76.act_a, bf16[256,256]{1,0:T(8,128)(2,1)S(1)} %get-tuple-element.77.act_b, bf16[2560,768]{1,0:T(8,128)(2,1)S(1)} %get-tuple-element.78.down_own, bf16[2560,1536]{1,0:T(8,128)(2,1)} %bitcast.13), custom_call_target="tpu_custom_call" | custom-call | tf_op jit(solution)/shard_map/down_own/pallas_call | solution.py:92
  42.0 0.7 collective-permute-done.13.refs_1_
  42.7 0.8 %down_other.3 = (bf16[128,1280]{1,0:T(8,128)(2,1)S(1)}, bf16[128,1280]{1,0:T(8,128)(2,1)S(1)}) custom-call(bf16[128,512]{1,0:T(8,128)(2,1)S(1)} %collective-permute-done.12.refs_0_, bf16[128,256]{1,0:T(8,128)(2,1)S(1)} %collective-permute-done.13.refs_1_, bf16[256,128]{1,0:T(8,128)(2,1)S(1)} %get-tuple-element.74.refs_2_, ...), custom_call_target="tpu_custom_call" | custom-call | tf_op jit(solution)/shard_map/down_other/pallas_call | solution.py:92
  43.6 0.8 %down_other.2 = (bf16[128,1280]{1,0:T(8,128)(2,1)S(1)}, bf16[128,1280]{1,0:T(8,128)(2,1)S(1)}) custom-call(bf16[128,512]{1,0:T(8,128)(2,1)S(1)} %collective-permute-done.12.refs_0_, bf16[128,256]{1,0:T(8,128)(2,1)S(1)} %collective-permute-done.13.refs_1_, bf16[256,128]{1,0:T(8,128)(2,1)S(1)} %get-tuple-element.74.refs_2_, ...), custom_call_target="tpu_custom_call" | custom-call | tf_op jit(solution)/shard_map/down_other/pallas_call | solution.py:92
  46.3 1.6 %collective-permute-start.15 = (bf16[64,1280]{1,0:T(8,128)(2,1)S(1)}, bf16[64,1280]{1,0:T(8,128)(2,1)S(1)}, u32[]{:S(2)}, u32[]{:S(2)}) collective-permute-start(bf16[64,1280]{1,0:T(8,128)(2,1)S(1)} %get-tuple-element.84), channel_id=1, source_target_pairs={{0,2},{1,3},{2,0},{3,1},{4,6},{5,7},{6,4},{7,5},{8,10},{9,11},{10,... | collective-permute-start | bytes 491528 | tf_op jit(solution)/shard_map/ppermute | solution.py:60
  47.9 3.7 %collective-permute-done.18.refs_1_ = bf16[64,1280]{1,0:T(8,128)(2,1)S(1)} collective-permute-done((bf16[64,1280]{1,0:T(8,128)(2,1)S(1)}, bf16[64,1280]{1,0:T(8,128)(2,1)S(1)}, u32[]{:S(2)}, u32[]{:S(2)}) %collective-permute-start.18) | collective-permute-done | bytes 163872 | tf_op jit(solution)/shard_map/ppermute | solution.py:60
  51.7 1.6 %collective-permute-start.19 = (bf16[32,2560]{1,0:T(8,128)(2,1)S(1)}, bf16[32,2560]{1,0:T(8,128)(2,1)S(1)}, u32[]{:S(2)}, u32[]{:S(2)}) collective-permute-start(bf16[32,2560]{1,0:T(8,128)(2,1)S(1)} %get-tuple-element.90.after), channel_id=1, source_target_pairs={{0,2},{1,3},{2,0},{3,1},{4,6},{5,7},{6,4},{7,5},{8,10},{9,11},{10,... | collective-permute-start | bytes 491528 | tf_op jit(solution)/shard_map/ppermute | solution.py:60
  53.3 0.6 collective-permute-start.16
  53.9 3.3 %attention.1 = bf16[128,2048]{1,0:T(8,128)(2,1)} custom-call(bf16[32,2560]{1,0:T(8,128)(2,1)S(1)} %get-tuple-element.90.after, bf16[576,128]{1,0:T(8,128)(2,1)S(1)} %collective-permute-done.3.earlier, bf16[128,2304]{1,0:T(8,128)(2,1)} %queries_in.1, bf16[576,128]{1,0:T(8,128)(2,1)} %bitcast.15), custom_call_target="tpu_custom_call" | custom-call | tf_op jit(solution)/shard_map/attention/pallas_call | solution.py:92
  57.2 0.6 collective-permute-done.16.got_x
  57.8 2.0 %collective-permute-start.20 = (bf16[8,5120]{1,0:T(8,128)(2,1)S(1)}, bf16[8,5120]{1,0:T(8,128)(2,1)S(1)}, u32[]{:S(2)}, u32[]{:S(2)}) collective-permute-start(bf16[8,5120]{1,0:T(8,128)(2,1)S(1)} %get-tuple-element.97), channel_id=1, source_target_pairs={{0,12},{1,13},{2,14},{3,15},{4,8},{5,9},{6,10},{7,11},{8,4},{9,5},... | collective-permute-start | bytes 245768 | tf_op jit(solution)/shard_map/ppermute | solution.py:48
  59.8 2.5 %collective-permute-start.22 = (bf16[8,5120]{1,0:T(8,128)(2,1)S(1)}, bf16[8,5120]{1,0:T(8,128)(2,1)S(1)}, u32[]{:S(2)}, u32[]{:S(2)}) collective-permute-start(bf16[8,5120]{1,0:T(8,128)(2,1)S(1)} %get-tuple-element.99), channel_id=1, source_target_pairs={{0,4},{1,5},{2,6},{3,7},{4,0},{5,1},{6,2},{7,3},{8,12},{9,13},{10,... | collective-permute-start | bytes 245768 | tf_op jit(solution)/shard_map/ppermute | solution.py:48
  62.3 2.3 %collective-permute-done.20.refs_0_ = bf16[8,5120]{1,0:T(8,128)(2,1)S(1)} collective-permute-done((bf16[8,5120]{1,0:T(8,128)(2,1)S(1)}, bf16[8,5120]{1,0:T(8,128)(2,1)S(1)}, u32[]{:S(2)}, u32[]{:S(2)}) %collective-permute-start.20) | collective-permute-done | bytes 81952 | tf_op jit(solution)/shard_map/ppermute | solution.py:48
  64.6 2.2 %collective-permute-done.21.refs_1_ = bf16[8,5120]{1,0:T(8,128)(2,1)S(1)} collective-permute-done((bf16[8,5120]{1,0:T(8,128)(2,1)S(1)}, bf16[8,5120]{1,0:T(8,128)(2,1)S(1)}, u32[]{:S(2)}, u32[]{:S(2)}) %collective-permute-start.21) | collective-permute-done | bytes 81952 | tf_op jit(solution)/shard_map/ppermute | solution.py:48
  66.8 0.7 %sum.1 = bf16[8,5120]{1,0:T(8,128)(2,1)} custom-call(f32[8,5120]{1,0:T(8,128)S(1)} %get-tuple-element.96.first, bf16[8,5120]{1,0:T(8,128)(2,1)S(1)} %collective-permute-done.20.refs_0_, bf16[8,5120]{1,0:T(8,128)(2,1)S(1)} %collective-permute-done.21.refs_1_, bf16[8,5120]{1,0:T(8,128)(2,1)S(1)} %collective-permute-done.22.refs_2_), custom_call_target="tpu_custom_call" | custom-call | tf_op jit(solution)/shard_map/sum/pallas_call | solution.py:92
  (33 shorter events, 4.0 us)
Async XLA Ops:
  1.7 13.4 %collective-permute-start.3 = (bf16[576,128]{1,0:T(8,128)(2,1)}, bf16[576,128]{1,0:T(8,128)(2,1)S(1)}, u32[]{:S(2)}, u32[]{:S(2)}) collective-permute-start(bf16[576,128]{1,0:T(8,128)(2,1)} %bitcast.14), channel_id=1, source_target_pairs={{0,16},{16,0},{1,17},{17,1},{2,18},{18,2},{3,19},{19,3},{4,20},{20... | collective-permute-start | bytes 442376 | tf_op jit(solution)/shard_map/ppermute | solution.py:44
  4.7 7.7 %collective-permute-start = (bf16[8,5248]{1,0:T(8,128)(2,1)S(1)}, bf16[8,5248]{1,0:T(8,128)(2,1)S(1)}, u32[]{:S(2)}, u32[]{:S(2)}) collective-permute-start(bf16[8,5248]{1,0:T(8,128)(2,1)S(1)} %rows.1.refs_0_), channel_id=1, source_target_pairs={{0,12},{1,13},{2,14},{3,15},{4,8},{5,9},{6,10},{7,11},{8,4},{9,5},... | collective-permute-start | bytes 251912 | tf_op jit(solution)/shard_map/ppermute | solution.py:48
  8.3 6.8 %collective-permute-start.1 = (bf16[8,5248]{1,0:T(8,128)(2,1)S(1)}, bf16[8,5248]{1,0:T(8,128)(2,1)S(1)}, u32[]{:S(2)}, u32[]{:S(2)}) collective-permute-start(bf16[8,5248]{1,0:T(8,128)(2,1)S(1)} %rows.1.refs_0_), channel_id=1, source_target_pairs={{0,8},{1,9},{2,10},{3,11},{4,12},{5,13},{6,14},{7,15},{8,0},{9,1},... | collective-permute-start | bytes 251912 | tf_op jit(solution)/shard_map/ppermute | solution.py:48
  8.3 6.8 %collective-permute-start.2 = (bf16[8,5248]{1,0:T(8,128)(2,1)S(1)}, bf16[8,5248]{1,0:T(8,128)(2,1)S(1)}, u32[]{:S(2)}, u32[]{:S(2)}) collective-permute-start(bf16[8,5248]{1,0:T(8,128)(2,1)S(1)} %rows.1.refs_0_), channel_id=1, source_target_pairs={{0,4},{1,5},{2,6},{3,7},{4,0},{5,1},{6,2},{7,3},{8,12},{9,13},{10,... | collective-permute-start | bytes 251912 | tf_op jit(solution)/shard_map/ppermute | solution.py:48
  15.0 6.1 %collective-permute-start.8 = (bf16[32,2688]{1,0:T(8,128)(2,1)S(1)}, bf16[32,2688]{1,0:T(8,128)(2,1)S(1)}, u32[]{:S(2)}, u32[]{:S(2)}) collective-permute-start(bf16[32,2688]{1,0:T(8,128)(2,1)S(1)} %get-tuple-element.59.refs_0_), channel_id=1, source_target_pairs={{0,2},{1,3},{2,0},{3,1},{4,6},{5,7},{6,4},{7,5},{8,10},{9,11},{10,... | collective-permute-start | bytes 516104 | tf_op jit(solution)/shard_map/ppermute | solution.py:60
  16.6 5.6 %collective-permute-start.4 = (bf16[32,2560]{1,0:T(8,128)(2,1)S(1)}, bf16[32,2560]{1,0:T(8,128)(2,1)S(1)}, u32[]{:S(2)}, u32[]{:S(2)}) collective-permute-start(bf16[32,2560]{1,0:T(8,128)(2,1)S(1)} %get-tuple-element.58.refs_0_), channel_id=1, source_target_pairs={{0,16},{1,17},{2,18},{3,19},{4,20},{5,21},{6,22},{7,23},{8,24},{9,... | collective-permute-start | bytes 491528 | tf_op jit(solution)/shard_map/ppermute | solution.py:60
  21.1 8.9 %collective-permute-start.9 = (bf16[64,2688]{1,0:T(8,128)(2,1)S(1)}, bf16[64,2688]{1,0:T(8,128)(2,1)S(1)}, u32[]{:S(2)}, u32[]{:S(2)}) collective-permute-start(bf16[64,2688]{1,0:T(8,128)(2,1)S(1)} %stack_two.3.refs_0_), channel_id=1, source_target_pairs={{0,16},{1,17},{2,18},{3,19},{4,20},{5,21},{6,22},{7,23},{8,24},{9,... | collective-permute-start | bytes 1032200 | tf_op jit(solution)/shard_map/ppermute | solution.py:60
  22.2 8.3 %collective-permute-start.5 = (bf16[64,2560]{1,0:T(8,128)(2,1)S(1)}, bf16[64,2560]{1,0:T(8,128)(2,1)S(1)}, u32[]{:S(2)}, u32[]{:S(2)}) collective-permute-start(bf16[64,2560]{1,0:T(8,128)(2,1)S(1)} %stack_two.2.refs_0_), channel_id=1, source_target_pairs={{0,2},{1,3},{2,0},{3,1},{4,6},{5,7},{6,4},{7,5},{8,10},{9,11},{10,... | collective-permute-start | bytes 983048 | tf_op jit(solution)/shard_map/ppermute | solution.py:60
  27.9 2.7 %collective-permute-start.10 = (bf16[64,2688]{1,0:T(8,128)(2,1)S(1)}, bf16[64,2688]{1,0:T(8,128)(2,1)S(1)}, u32[]{:S(2)}, u32[]{:S(2)}) collective-permute-start(bf16[64,2688]{1,0:T(8,128)(2,1)S(1)} %stack_two.3.refs_0_), channel_id=1, source_target_pairs={{0,1},{1,0},{2,3},{3,2},{4,5},{5,4},{6,7},{7,6},{8,9},{9,8},{10,11... | collective-permute-start | bytes 1032200 | tf_op jit(solution)/shard_map/ppermute | solution.py:44
  30.0 1.7 %collective-permute-start.11 = (bf16[64,2688]{1,0:T(8,128)(2,1)S(1)}, bf16[64,2688]{1,0:T(8,128)(2,1)S(1)}, u32[]{:S(2)}, u32[]{:S(2)}) collective-permute-start(bf16[64,2688]{1,0:T(8,128)(2,1)S(1)} %collective-permute-done.9.refs_1_), channel_id=1, source_target_pairs={{0,1},{1,0},{2,3},{3,2},{4,5},{5,4},{6,7},{7,6},{8,9},{9,8},{10,11... | collective-permute-start | bytes 1032200 | tf_op jit(solution)/shard_map/ppermute | solution.py:44
  30.0 3.9 %collective-permute-start.6 = (bf16[64,2560]{1,0:T(8,128)(2,1)S(1)}, bf16[64,2560]{1,0:T(8,128)(2,1)S(1)}, u32[]{:S(2)}, u32[]{:S(2)}) collective-permute-start(bf16[64,2560]{1,0:T(8,128)(2,1)S(1)} %stack_two.2.refs_0_), channel_id=1, source_target_pairs={{0,1},{1,0},{2,3},{3,2},{4,5},{5,4},{6,7},{7,6},{8,9},{9,8},{10,11... | collective-permute-start | bytes 983048 | tf_op jit(solution)/shard_map/ppermute | solution.py:44
  30.5 3.4 %collective-permute-start.7 = (bf16[64,2560]{1,0:T(8,128)(2,1)S(1)}, bf16[64,2560]{1,0:T(8,128)(2,1)S(1)}, u32[]{:S(2)}, u32[]{:S(2)}) collective-permute-start(bf16[64,2560]{1,0:T(8,128)(2,1)S(1)} %collective-permute-done.5.refs_1_), channel_id=1, source_target_pairs={{0,1},{1,0},{2,3},{3,2},{4,5},{5,4},{6,7},{7,6},{8,9},{9,8},{10,11... | collective-permute-start | bytes 983048 | tf_op jit(solution)/shard_map/ppermute | solution.py:44
  35.7 7.0 %collective-permute-start.12 = (bf16[128,512]{1,0:T(8,128)(2,1)S(1)}, bf16[128,512]{1,0:T(8,128)(2,1)S(1)}, u32[]{:S(2)}, u32[]{:S(2)}) collective-permute-start(bf16[128,512]{1,0:T(8,128)(2,1)S(1)} %get-tuple-element.71), channel_id=1, source_target_pairs={{0,16},{16,0},{1,17},{17,1},{2,18},{18,2},{3,19},{19,3},{4,20},{20... | collective-permute-start | bytes 393224 | tf_op jit(solution)/shard_map/ppermute | solution.py:44
  37.1 5.6 %collective-permute-start.13 = (bf16[128,256]{1,0:T(8,128)(2,1)S(1)}, bf16[128,256]{1,0:T(8,128)(2,1)S(1)}, u32[]{:S(2)}, u32[]{:S(2)}) collective-permute-start(bf16[128,256]{1,0:T(8,128)(2,1)S(1)} %get-tuple-element.73), channel_id=1, source_target_pairs={{0,16},{16,0},{1,17},{17,1},{2,18},{18,2},{3,19},{19,3},{4,20},{20... | collective-permute-start | bytes 196616 | tf_op jit(solution)/shard_map/ppermute | solution.py:44
  43.5 1.7 %collective-permute-start.17 = (bf16[128,1280]{1,0:T(8,128)(2,1)S(1)}, bf16[128,1280]{1,0:T(8,128)(2,1)S(1)}, u32[]{:S(2)}, u32[]{:S(2)}) collective-permute-start(bf16[128,1280]{1,0:T(8,128)(2,1)S(1)} %get-tuple-element.87), channel_id=1, source_target_pairs={{0,1},{1,0},{2,3},{3,2},{4,5},{5,4},{6,7},{7,6},{8,9},{9,8},{10,11... | collective-permute-start | bytes 983048 | tf_op jit(solution)/shard_map/ppermute | solution.py:44
  44.4 1.8 %collective-permute-start.14 = (bf16[128,1280]{1,0:T(8,128)(2,1)S(1)}, bf16[128,1280]{1,0:T(8,128)(2,1)S(1)}, u32[]{:S(2)}, u32[]{:S(2)}) collective-permute-start(bf16[128,1280]{1,0:T(8,128)(2,1)S(1)} %get-tuple-element.82), channel_id=1, source_target_pairs={{0,1},{1,0},{2,3},{3,2},{4,5},{5,4},{6,7},{7,6},{8,9},{9,8},{10,11... | collective-permute-start | bytes 983048 | tf_op jit(solution)/shard_map/ppermute | solution.py:44
  45.3 6.3 %collective-permute-start.18 = (bf16[64,1280]{1,0:T(8,128)(2,1)S(1)}, bf16[64,1280]{1,0:T(8,128)(2,1)S(1)}, u32[]{:S(2)}, u32[]{:S(2)}) collective-permute-start(bf16[64,1280]{1,0:T(8,128)(2,1)S(1)} %get-tuple-element.89), channel_id=1, source_target_pairs={{0,16},{1,17},{2,18},{3,19},{4,20},{5,21},{6,22},{7,23},{8,24},{9,... | collective-permute-start | bytes 491528 | tf_op jit(solution)/shard_map/ppermute | solution.py:60
  46.3 6.9 %collective-permute-start.15 = (bf16[64,1280]{1,0:T(8,128)(2,1)S(1)}, bf16[64,1280]{1,0:T(8,128)(2,1)S(1)}, u32[]{:S(2)}, u32[]{:S(2)}) collective-permute-start(bf16[64,1280]{1,0:T(8,128)(2,1)S(1)} %get-tuple-element.84), channel_id=1, source_target_pairs={{0,2},{1,3},{2,0},{3,1},{4,6},{5,7},{6,4},{7,5},{8,10},{9,11},{10,... | collective-permute-start | bytes 491528 | tf_op jit(solution)/shard_map/ppermute | solution.py:60
  51.7 6.1 %collective-permute-start.19 = (bf16[32,2560]{1,0:T(8,128)(2,1)S(1)}, bf16[32,2560]{1,0:T(8,128)(2,1)S(1)}, u32[]{:S(2)}, u32[]{:S(2)}) collective-permute-start(bf16[32,2560]{1,0:T(8,128)(2,1)S(1)} %get-tuple-element.90.after), channel_id=1, source_target_pairs={{0,2},{1,3},{2,0},{3,1},{4,6},{5,7},{6,4},{7,5},{8,10},{9,11},{10,... | collective-permute-start | bytes 491528 | tf_op jit(solution)/shard_map/ppermute | solution.py:60
  53.3 4.5 %collective-permute-start.16 = (bf16[32,1280]{1,0:T(8,128)(2,1)S(1)}, bf16[32,1280]{1,0:T(8,128)(2,1)S(1)}, u32[]{:S(2)}, u32[]{:S(2)}) collective-permute-start(bf16[32,1280]{1,0:T(8,128)(2,1)S(1)} %get-tuple-element.85), channel_id=1, source_target_pairs={{0,16},{1,17},{2,18},{3,19},{4,20},{5,21},{6,22},{7,23},{8,24},{9,... | collective-permute-start | bytes 245768 | tf_op jit(solution)/shard_map/ppermute | solution.py:60
  57.8 6.8 %collective-permute-start.20 = (bf16[8,5120]{1,0:T(8,128)(2,1)S(1)}, bf16[8,5120]{1,0:T(8,128)(2,1)S(1)}, u32[]{:S(2)}, u32[]{:S(2)}) collective-permute-start(bf16[8,5120]{1,0:T(8,128)(2,1)S(1)} %get-tuple-element.97), channel_id=1, source_target_pairs={{0,12},{1,13},{2,14},{3,15},{4,8},{5,9},{6,10},{7,11},{8,4},{9,5},... | collective-permute-start | bytes 245768 | tf_op jit(solution)/shard_map/ppermute | solution.py:48
  59.8 6.9 %collective-permute-start.21 = (bf16[8,5120]{1,0:T(8,128)(2,1)S(1)}, bf16[8,5120]{1,0:T(8,128)(2,1)S(1)}, u32[]{:S(2)}, u32[]{:S(2)}) collective-permute-start(bf16[8,5120]{1,0:T(8,128)(2,1)S(1)} %get-tuple-element.98), channel_id=1, source_target_pairs={{0,8},{1,9},{2,10},{3,11},{4,12},{5,13},{6,14},{7,15},{8,0},{9,1},... | collective-permute-start | bytes 245768 | tf_op jit(solution)/shard_map/ppermute | solution.py:48
  59.8 6.9 %collective-permute-start.22 = (bf16[8,5120]{1,0:T(8,128)(2,1)S(1)}, bf16[8,5120]{1,0:T(8,128)(2,1)S(1)}, u32[]{:S(2)}, u32[]{:S(2)}) collective-permute-start(bf16[8,5120]{1,0:T(8,128)(2,1)S(1)} %get-tuple-element.99), channel_id=1, source_target_pairs={{0,4},{1,5},{2,6},{3,7},{4,0},{5,1},{6,2},{7,3},{8,12},{9,13},{10,... | collective-permute-start | bytes 245768 | tf_op jit(solution)/shard_map/ppermute | solution.py:48

commit v5 on v4

--- a/solution.py
+++ b/solution.py
@@ -118,11 +118,20 @@
 PIECES = 4
 
 
-def rows_kernel(tokens_in, names_in, weights_in, out, tokens, names, weights, sems, *, half, topk):
+def rows_kernel(
+    tokens_in, names_in, weights_in, latents_in, out, latents, tokens, names, weights, sems, *, half, topk
+):
+    share = latents.shape[0]
+    at = pl.multiple_of(lax.axis_index("exp") % 2 * share, 16)
     copies = [
         pltpu.make_async_copy(source, target, sems.at[number])
         for number, (source, target) in enumerate(
-            ((tokens_in, tokens), (names_in, names), (weights_in, weights))
+            (
+                (tokens_in, tokens),
+                (names_in, names),
+                (weights_in, weights),
+                (latents_in.at[pl.ds(at, share), :], latents),
+            )
         )
     ]
     for copy in copies:
@@ -157,10 +166,12 @@
     count = len(refs) // 2
     ins, outs, sems = refs[:count], refs[count:-1], refs[-1]
     pairs = [(a.at[:, start : start + b.shape[1]], b) for a, b in zip(ins[:2], outs[:2])]
-    if count > 2:
-        width = outs[2].shape[1]
-        own_at = pl.multiple_of(lax.axis_index("ctx") * width, 128)
-        pairs.append((ins[2].at[:, pl.ds(own_at, width)], outs[2]))
+    for source, target in zip(ins[2:], outs[2:]):
+        width = target.shape[1]
+        if source.shape[1] != width:
+            own_at = pl.multiple_of(lax.axis_index("ctx") * width, 128)
+            source = source.at[:, pl.ds(own_at, width)]
+        pairs.append((source, target))
     for copy in start_copies(pairs, sems, PIECES):
         copy.wait()
 
@@ -179,23 +190,18 @@
 
 
 def attention_kernel(
-    after, earlier, queries_in, latents_in, attended, queries, latents, even, odd, mixed, sems
+    after, earlier, earlier_other, queries, latents, attended, even, odd, mixed, sems
 ):
     width, rows = latents.shape
     pad = even.shape[0] - width
-    loads = [
-        pltpu.make_async_copy(queries_in, queries, sems.at[0]),
-        pltpu.make_async_copy(latents_in, latents, sems.at[1]),
-    ]
-    for copy in loads:
-        copy.start()
-    for copy in loads:
-        copy.wait()
     even[width:, :] = jnp.zeros((pad, 2 * rows), jnp.bfloat16)
     odd[:pad, :] = jnp.zeros((pad, 2 * rows), jnp.bfloat16)
-    even[:width, :rows] = earlier[...]
+    share = width // 2
+    core = lax.axis_index("exp") % 2
+    for side, ref in ((core, earlier), (1 - core, earlier_other)):
+        even[pl.ds(pl.multiple_of(side * share, 16), share), :rows] = ref[...]
+        odd[pl.ds(pl.multiple_of(side * share + pad, 16), share), :rows] = ref[...]
     even[:width, rows:] = latents[...]
-    odd[pad:, :rows] = earlier[...]
     odd[pad:, rows:] = latents[...]
     row = lax.broadcasted_iota(jnp.int32, (rows, 2 * rows), 0)
     key = lax.broadcasted_iota(jnp.int32, (rows, 2 * rows), 1)
@@ -214,7 +220,7 @@
         probs = (expo / jnp.sum(expo, axis=-1, keepdims=True)).astype(jnp.bfloat16)
         span = slice(head * LATENT, (head + 1) * LATENT)
         mixed[:, span] = times_rows_in(probs, even[:LATENT, :]).astype(jnp.bfloat16)
-        write = pltpu.make_async_copy(mixed.at[:, span], attended.at[:, span], sems.at[2 + head])
+        write = pltpu.make_async_copy(mixed.at[:, span], attended.at[:, span], sems.at[head])
         write.start()
         writes.append(write)
     for copy in writes:
@@ -391,33 +397,36 @@
     count = 8 * unit
     slots = count // tok_dev * capacity
     bf16, f32 = jnp.bfloat16, jnp.float32
-    copy_sems = pltpu.SemaphoreType.DMA((2 * PIECES,))
-
-    (rows,) = local_kernel(
+
+    rows, latents_half = local_kernel(
         lambda *refs: rows_kernel(*refs, half=half, topk=topk),
         [
             (hidden[0], "hbm"),
             (jnp.transpose(expert_ids, (2, 0, 1)), "hbm"),
             (jnp.transpose(route_weight, (2, 0, 1)), "hbm"),
+            (latents.T, "hbm"),
         ],
-        [((tok_dev, width + 128), bf16, "vmem")],
+        [((tok_dev, width + 128), bf16, "vmem"), ((key_width // 2, tok_att), bf16, "vmem")],
         [
             pltpu.VMEM((tok_dev, width), bf16),
             pltpu.VMEM((topk, 1, tok_dev), jnp.int32),
             pltpu.VMEM((topk, 1, tok_dev), f32),
-            pltpu.SemaphoreType.DMA((3,)),
+            pltpu.SemaphoreType.DMA((4,)),
         ],
         "rows",
     )
-    places = range(line - 1, 0, -1)
+    places = (3, 2, 1)
     along = [rows] + [along_line(rows, d) for d in places]
-    latents_t, _ = lax.optimization_barrier((latents.T, rows))
-    earlier_kv = swapped(latents_t, "ctx", 1)
-    gate_1, up_1 = local_kernel(
+    earlier_kv = swapped(latents_half, "ctx", 1)
+    gate_1, up_1, queries_here, latents_here = local_kernel(
         lambda *refs: fetch_kernel(*refs, start=0),
-        [(rows, "vmem"), (w_gate[0], "hbm"), (w_up[0], "hbm")],
-        [((units, half), bf16, "vmem")] * 2,
-        [copy_sems],
+        [
+            (rows, "vmem"), (w_gate[0], "hbm"), (w_up[0], "hbm"),
+            (queries, "hbm"), (latents.T, "hbm"),
+        ],
+        [((units, half), bf16, "vmem")] * 2
+        + [(queries.shape, bf16, "vmem"), ((key_width, tok_att), bf16, "vmem")],
+        [pltpu.SemaphoreType.DMA((4 * PIECES,))],
         "fetch",
     )
     *along, earlier_kv, gate_1, up_1 = lax.optimization_barrier((*along, earlier_kv, gate_1, up_1))
@@ -447,8 +456,9 @@
         [pltpu.SemaphoreType.DMA((3 * PIECES,))],
         "fetch",
     )
-    pieces[0][1], gate_2, up_2, down_mine = lax.optimization_barrier(
-        (pieces[0][1], gate_2, up_2, down_mine)
+    earlier_other = swapped(earlier_kv, "exp", 1)
+    pieces[0][1], gate_2, up_2, down_mine, earlier_other = lax.optimization_barrier(
+        (pieces[0][1], gate_2, up_2, down_mine, earlier_other)
     )
     for number, (two, far) in enumerate(pieces):
         group = (two, far, swapped(two, "exp", 1), swapped(far, "exp", 1))
@@ -526,22 +536,6 @@
             "cross",
         )
         lines += [left, paired(send, over_x if y_first else over_y)]
-    pad = -key_width % 128
-    (attended,) = local_kernel(
-        attention_kernel,
-        [(send, "vmem"), (earlier_kv, "vmem"), (queries, "hbm"), (latents.T, "hbm")],
-        [((tok_att, heads_dev * LATENT), bf16, "hbm")],
-        [
-            pltpu.VMEM((tok_att, heads_dev * key_width), bf16),
-            pltpu.VMEM((key_width, tok_att), bf16),
-            pltpu.VMEM((key_width + pad, 2 * tok_att), bf16),
-            pltpu.VMEM((key_width + pad, 2 * tok_att), bf16),
-            pltpu.VMEM((tok_att, heads_dev * LATENT), bf16),
-            pltpu.SemaphoreType.DMA((2 + heads_dev,)),
-        ],
-        "attention",
-    )
-    lines[1], attended = lax.optimization_barrier((lines[1], attended))
     keep, *sends = local_kernel(
         line_kernel,
         [(block, "vmem") for block in lines],
@@ -550,7 +544,22 @@
         [],
         "line",
     )
-    got = [along_line(block, d) for block, d in zip(sends, places)]
+    pad = -key_width % 128
+    (attended,) = local_kernel(
+        attention_kernel,
+        [(sends[0], "vmem"), (earlier_kv, "vmem"), (earlier_other, "vmem"), (queries_here, "vmem"), (latents_here, "vmem")],
+        [((tok_att, heads_dev * LATENT), bf16, "hbm")],
+        [
+            pltpu.VMEM((key_width + pad, 2 * tok_att), bf16),
+            pltpu.VMEM((key_width + pad, 2 * tok_att), bf16),
+            pltpu.VMEM((tok_att, heads_dev * LATENT), bf16),
+            pltpu.SemaphoreType.DMA((heads_dev,)),
+        ],
+        "attention",
+    )
+    sends = dict(zip(places, sends))
+    got = [along_line(sends[d], d) for d in (3, 1, 2)]
+    got[-1], attended = lax.optimization_barrier((got[-1], attended))
     (mixed,) = local_kernel(
         sum_kernel,
         [(block, "vmem") for block in (keep, *got)],

time: 67.6 us -> 65.4 us (0.967)
  waiting for transfers between devices: 20.6 us -> 15.1 us
  starting transfers between devices: 23.2 us -> 27.2 us
  Pallas kernels: 23 us -> 22.1 us
    ppermute x8, starting transfers between devices: 7.94 us -> 12.4 us  [paired(): return lax.ppermute(block, ('ctx', 'exp'), route)]
    ppermute x6, waiting for transfers between devices: 7.12 us -> 4 us  [along_line(): lax.ppermute(block, 'exp', [(i, i ^ 4 * steps) for i in range(lax.axis_si...]
    ppermute x8, waiting for transfers between devices: 10.9 us -> 9.37 us  [paired(): return lax.ppermute(block, ('ctx', 'exp'), route)]
    ppermute x9 -> x10, starting transfers between devices: 6.38 us -> 5.51 us  [swapped(): lax.ppermute(block, axis, [(i, i ^ bit) for i in range(lax.axis_size(axis...]
    pallas_call x19, Pallas kernels: 23 us -> 22.1 us  [local_kernel(): pl.pallas_call(body, in_specs=[pl.BlockSpec(memory_space=kinds[kind]) for...]
    ppermute x9 -> x10, waiting for transfers between devices: 2.48 us -> 1.71 us  [swapped(): lax.ppermute(block, axis, [(i, i ^ bit) for i in range(lax.axis_size(axis...]
  transfers between devices with their start and end apart: 23 -> 24, of which waited for: 12 -> 12; matrix products, arithmetic and copies ran while one was open for 0% -> 0% of each run, Pallas kernels for 28% -> 27%
where the time goes in v5:
time: 65.4 us; the launch traced here: 65.3 us
  starting transfers between devices  27.2 us (42%)
  Pallas kernels  22.1 us (34%)
  waiting for transfers between devices  15.1 us (23%)
  between operations  0.8 us (1%)
    pallas_call x19, Pallas kernels, local_kernel(): pl.pallas_call(body, in_specs=[pl.BlockSpec(memory_space=kinds[kind]) for...  22.1 us
    ppermute x8, starting transfers between devices, paired(): return lax.ppermute(block, ('ctx', 'exp'), route)  12.4 us
    ppermute x8, waiting for transfers between devices, paired(): return lax.ppermute(block, ('ctx', 'exp'), route)  9.37 us
    ppermute x6, starting transfers between devices, along_line(): lax.ppermute(block, 'exp', [(i, i ^ 4 * steps) for i in range(lax.axis_si...  9.31 us
    ppermute x10, starting transfers between devices, swapped(): lax.ppermute(block, axis, [(i, i ^ bit) for i in range(lax.axis_size(axis...  5.51 us
    ppermute x6, waiting for transfers between devices, along_line(): lax.ppermute(block, 'exp', [(i, i ^ 4 * steps) for i in range(lax.axis_si...  4 us
    ppermute x10, waiting for transfers between devices, swapped(): lax.ppermute(block, axis, [(i, i ^ bit) for i in range(lax.axis_size(axis...  1.71 us
  transfers between devices with their start and end apart: 24, of which 12 were waited for; matrix products, arithmetic and copies ran while one was open for 0% of the time, Pallas kernels for 27%

profile of v5, /device:TPU:0, one launch (start us, length us, event | category | flops | bytes accessed | tf_op | source)
XLA Modules:
  0.0 65.3 jit_solution(17950089067417135925)
XLA Ops:
  0.6 1.1 %rows.1 = (bf16[8,5248]{1,0:T(8,128)(2,1)S(1)}, bf16[288,128]{1,0:T(8,128)(2,1)S(1)}) custom-call(bf16[8,5120]{1,0:T(8,128)(2,1)} %bitcast.16, s32[6,1,8]{2,1,0:T(1,128)} %bitcast.18, f32[6,1,8]{2,1,0:T(1,128)} %bitcast.19, bf16[576,128]{1,0:T(8,128)(2,1)} %bitcast.14), custom_call_target="tpu_custom_call" | custom-call | tf_op jit(solution)/shard_map/rows/pallas_call | solution.py:92
  1.7 5.1 %collective-permute-start = (bf16[8,5248]{1,0:T(8,128)(2,1)S(1)}, bf16[8,5248]{1,0:T(8,128)(2,1)S(1)}, u32[]{:S(2)}, u32[]{:S(2)}) collective-permute-start(bf16[8,5248]{1,0:T(8,128)(2,1)S(1)} %get-tuple-element.59.refs_0_), channel_id=1, source_target_pairs={{0,12},{1,13},{2,14},{3,15},{4,8},{5,9},{6,10},{7,11},{8,4},{9,5},... | collective-permute-start | bytes 251912 | tf_op jit(solution)/shard_map/ppermute | solution.py:48
  7.5 1.6 %collective-permute-start.3 = (bf16[288,128]{1,0:T(8,128)(2,1)S(1)}, bf16[288,128]{1,0:T(8,128)(2,1)S(1)}, u32[]{:S(2)}, u32[]{:S(2)}) collective-permute-start(bf16[288,128]{1,0:T(8,128)(2,1)S(1)} %get-tuple-element.56), channel_id=1, source_target_pairs={{0,16},{16,0},{1,17},{17,1},{2,18},{18,2},{3,19},{19,3},{4,20},{20... | collective-permute-start | bytes 221192 | tf_op jit(solution)/shard_map/ppermute | solution.py:44
  9.1 3.5 %fetch.2 = (bf16[768,2560]{1,0:T(8,128)(2,1)S(1)}, bf16[768,2560]{1,0:T(8,128)(2,1)S(1)}, bf16[128,2304]{1,0:T(8,128)(2,1)S(1)}, bf16[576,128]{1,0:T(8,128)(2,1)S(1)}) custom-call(bf16[8,5248]{1,0:T(8,128)(2,1)S(1)} %get-tuple-element.59.refs_0_, bf16[768,5120]{1,0:T(8,128)(2,1)} %bitcast.8, bf16[768,5120]{1,0:T(8,128)(2,1)} %bitcast.10, ...), custom_call_target="tpu_custom_call" | custom-call | tf_op jit(solution)/shard_map/fetch/pallas_call | solution.py:92
  12.7 1.2 %collective-permute-done.1.refs_2_ = bf16[8,5248]{1,0:T(8,128)(2,1)S(1)} collective-permute-done((bf16[8,5248]{1,0:T(8,128)(2,1)S(1)}, bf16[8,5248]{1,0:T(8,128)(2,1)S(1)}, u32[]{:S(2)}, u32[]{:S(2)}) %collective-permute-start.1) | collective-permute-done | bytes 84000 | tf_op jit(solution)/shard_map/ppermute | solution.py:48
  13.9 1.6 %collective-permute-start.8 = (bf16[32,2688]{1,0:T(8,128)(2,1)S(1)}, bf16[32,2688]{1,0:T(8,128)(2,1)S(1)}, u32[]{:S(2)}, u32[]{:S(2)}) collective-permute-start(bf16[32,2688]{1,0:T(8,128)(2,1)S(1)} %get-tuple-element.64.refs_0_), channel_id=1, source_target_pairs={{0,2},{1,3},{2,0},{3,1},{4,6},{5,7},{6,4},{7,5},{8,10},{9,11},{10,... | collective-permute-start | bytes 516104 | tf_op jit(solution)/shard_map/ppermute | solution.py:60
  15.5 1.5 %collective-permute-start.4 = (bf16[32,2560]{1,0:T(8,128)(2,1)S(1)}, bf16[32,2560]{1,0:T(8,128)(2,1)S(1)}, u32[]{:S(2)}, u32[]{:S(2)}) collective-permute-start(bf16[32,2560]{1,0:T(8,128)(2,1)S(1)} %get-tuple-element.63.refs_0_), channel_id=1, source_target_pairs={{0,16},{1,17},{2,18},{3,19},{4,20},{5,21},{6,22},{7,23},{8,24},{9,... | collective-permute-start | bytes 491528 | tf_op jit(solution)/shard_map/ppermute | solution.py:60
  17.0 2.5 %collective-permute-done.8.refs_1_ = bf16[32,2688]{1,0:T(8,128)(2,1)S(1)} collective-permute-done((bf16[32,2688]{1,0:T(8,128)(2,1)S(1)}, bf16[32,2688]{1,0:T(8,128)(2,1)S(1)}, u32[]{:S(2)}, u32[]{:S(2)}) %collective-permute-start.8) | collective-permute-done | bytes 172064 | tf_op jit(solution)/shard_map/ppermute | solution.py:60
  19.5 1.7 %collective-permute-start.9 = (bf16[64,2688]{1,0:T(8,128)(2,1)S(1)}, bf16[64,2688]{1,0:T(8,128)(2,1)S(1)}, u32[]{:S(2)}, u32[]{:S(2)}) collective-permute-start(bf16[64,2688]{1,0:T(8,128)(2,1)S(1)} %stack_two.3.refs_0_), channel_id=1, source_target_pairs={{0,16},{1,17},{2,18},{3,19},{4,20},{5,21},{6,22},{7,23},{8,24},{9,... | collective-permute-start | bytes 1032200 | tf_op jit(solution)/shard_map/ppermute | solution.py:60
  21.3 1.6 %collective-permute-start.5 = (bf16[64,2560]{1,0:T(8,128)(2,1)S(1)}, bf16[64,2560]{1,0:T(8,128)(2,1)S(1)}, u32[]{:S(2)}, u32[]{:S(2)}) collective-permute-start(bf16[64,2560]{1,0:T(8,128)(2,1)S(1)} %stack_two.2.refs_0_), channel_id=1, source_target_pairs={{0,2},{1,3},{2,0},{3,1},{4,6},{5,7},{6,4},{7,5},{8,10},{9,11},{10,... | collective-permute-start | bytes 983048 | tf_op jit(solution)/shard_map/ppermute | solution.py:60
  22.8 4.5 %fetch.3 = (bf16[768,2560]{1,0:T(8,128)(2,1)S(1)}, bf16[768,2560]{1,0:T(8,128)(2,1)S(1)}, bf16[2560,768]{1,0:T(8,128)(2,1)S(1)}) custom-call(bf16[64,2560]{1,0:T(8,128)(2,1)S(1)} %stack_two.2.refs_0_, bf16[768,5120]{1,0:T(8,128)(2,1)} %bitcast.9, bf16[768,5120]{1,0:T(8,128)(2,1)} %bitcast.11, bf16[2560,1536]{1,0:T(8,128)(2,1)} %bitcast.12), custom_call_target="tpu_custom_call" | custom-call | tf_op jit(solution)/shard_map/fetch/pallas_call | solution.py:92
  29.2 0.6 collective-permute-done.12.refs_3_
  29.8 2.3 %gate_up_first.1 = (f32[256,768]{1,0:T(8,128)S(1)}, f32[256,768]{1,0:T(8,128)S(1)}, bf16[256,128]{1,0:T(8,128)(2,1)S(1)}, bf16[256,128]{1,0:T(8,128)(2,1)S(1)}, f32[256,128]{1,0:T(8,128)S(1)}) custom-call(bf16[64,2688]{1,0:T(8,128)(2,1)S(1)} %stack_two.3.refs_0_, bf16[64,2688]{1,0:T(8,128)(2,1)S(1)} %collective-permute-done.9.refs_1_, ...), custom_call_target="tpu_custom_call" | custom-call | tf_op jit(solution)/shard_map/gate_up_first/pallas_call | solution.py:92
  32.2 1.7 %gate_up_second.1 = (bf16[256,512]{1,0:T(8,128)(2,1)S(1)}, bf16[128,512]{1,0:T(8,128)(2,1)S(1)}, bf16[256,2560]{1,0:T(8,128)(2,1)S(1)}) custom-call(bf16[64,2560]{1,0:T(8,128)(2,1)S(1)} %stack_two.2.refs_0_, bf16[64,2560]{1,0:T(8,128)(2,1)S(1)} %collective-permute-done.5.refs_1_, bf16[64,2560]{1,0:T(8,128)(2,1)S(1)} %collective-permute-done.6.refs_2_, ...), custom_call_target="tpu_custom_call" | custom-call | tf_op jit(solution)/shard_map/gate_up_second/pallas_call | solution.py:92
  33.9 1.6 %collective-permute-start.13 = (bf16[128,512]{1,0:T(8,128)(2,1)S(1)}, bf16[128,512]{1,0:T(8,128)(2,1)S(1)}, u32[]{:S(2)}, u32[]{:S(2)}) collective-permute-start(bf16[128,512]{1,0:T(8,128)(2,1)S(1)} %get-tuple-element.77), channel_id=1, source_target_pairs={{0,16},{16,0},{1,17},{17,1},{2,18},{18,2},{3,19},{19,3},{4,20},{20... | collective-permute-start | bytes 393224 | tf_op jit(solution)/shard_map/ppermute | solution.py:44
  35.4 1.0 %gate_up_third.1 = (bf16[256,256]{1,0:T(8,128)(2,1)S(1)}, bf16[128,256]{1,0:T(8,128)(2,1)S(1)}) custom-call(bf16[256,2560]{1,0:T(8,128)(2,1)S(1)} %get-tuple-element.78.refs_0_, bf16[768,2560]{1,0:T(8,128)(2,1)S(1)} %get-tuple-element.69.refs_4_.refs_1_, bf16[768,2560]{1,0:T(8,128)(2,1)S(1)} %get-tuple-element.70.refs_5_.refs_2_, ...), custom_call_target="tpu_custom_call" | custom-call | tf_op jit(solution)/shard_map/gate_up_third/pallas_call | solution.py:92
  37.1 3.1 %down_own.1 = (f32[256,2560]{1,0:T(8,128)S(1)}, bf16[2560,768]{1,0:T(8,128)(2,1)S(1)}) custom-call(bf16[256,512]{1,0:T(8,128)(2,1)S(1)} %get-tuple-element.82.act_a, bf16[256,256]{1,0:T(8,128)(2,1)S(1)} %get-tuple-element.83.act_b, bf16[2560,768]{1,0:T(8,128)(2,1)S(1)} %get-tuple-element.84.down_own, bf16[2560,1536]{1,0:T(8,128)(2,1)} %bitcast.13), custom_call_target="tpu_custom_call" | custom-call | tf_op jit(solution)/shard_map/down_own/pallas_call | solution.py:92
  40.2 0.7 %collective-permute-done.14.refs_1_ = bf16[128,256]{1,0:T(8,128)(2,1)S(1)} collective-permute-done((bf16[128,256]{1,0:T(8,128)(2,1)S(1)}, bf16[128,256]{1,0:T(8,128)(2,1)S(1)}, u32[]{:S(2)}, u32[]{:S(2)}) %collective-permute-start.14) | collective-permute-done | bytes 65568 | tf_op jit(solution)/shard_map/ppermute | solution.py:44
  41.0 0.8 %down_other.3 = (bf16[128,1280]{1,0:T(8,128)(2,1)S(1)}, bf16[128,1280]{1,0:T(8,128)(2,1)S(1)}) custom-call(bf16[128,512]{1,0:T(8,128)(2,1)S(1)} %collective-permute-done.13.refs_0_, bf16[128,256]{1,0:T(8,128)(2,1)S(1)} %collective-permute-done.14.refs_1_, bf16[256,128]{1,0:T(8,128)(2,1)S(1)} %get-tuple-element.80.refs_2_, ...), custom_call_target="tpu_custom_call" | custom-call | tf_op jit(solution)/shard_map/down_other/pallas_call | solution.py:92
  41.9 0.8 %down_other.2 = (bf16[128,1280]{1,0:T(8,128)(2,1)S(1)}, bf16[128,1280]{1,0:T(8,128)(2,1)S(1)}) custom-call(bf16[128,512]{1,0:T(8,128)(2,1)S(1)} %collective-permute-done.13.refs_0_, bf16[128,256]{1,0:T(8,128)(2,1)S(1)} %collective-permute-done.14.refs_1_, bf16[256,128]{1,0:T(8,128)(2,1)S(1)} %get-tuple-element.80.refs_2_, ...), custom_call_target="tpu_custom_call" | custom-call | tf_op jit(solution)/shard_map/down_other/pallas_call | solution.py:92
  43.6 1.5 %collective-permute-start.19 = (bf16[64,1280]{1,0:T(8,128)(2,1)S(1)}, bf16[64,1280]{1,0:T(8,128)(2,1)S(1)}, u32[]{:S(2)}, u32[]{:S(2)}) collective-permute-start(bf16[64,1280]{1,0:T(8,128)(2,1)S(1)} %get-tuple-element.96), channel_id=1, source_target_pairs={{0,16},{1,17},{2,18},{3,19},{4,20},{5,21},{6,22},{7,23},{8,24},{9,... | collective-permute-start | bytes 491528 | tf_op jit(solution)/shard_map/ppermute | solution.py:60
  45.1 1.6 %collective-permute-start.16 = (bf16[64,1280]{1,0:T(8,128)(2,1)S(1)}, bf16[64,1280]{1,0:T(8,128)(2,1)S(1)}, u32[]{:S(2)}, u32[]{:S(2)}) collective-permute-start(bf16[64,1280]{1,0:T(8,128)(2,1)S(1)} %get-tuple-element.90), channel_id=1, source_target_pairs={{0,2},{1,3},{2,0},{3,1},{4,6},{5,7},{6,4},{7,5},{8,10},{9,11},{10,... | collective-permute-start | bytes 491528 | tf_op jit(solution)/shard_map/ppermute | solution.py:60
  46.7 3.2 %collective-permute-done.19.refs_1_ = bf16[64,1280]{1,0:T(8,128)(2,1)S(1)} collective-permute-done((bf16[64,1280]{1,0:T(8,128)(2,1)S(1)}, bf16[64,1280]{1,0:T(8,128)(2,1)S(1)}, u32[]{:S(2)}, u32[]{:S(2)}) %collective-permute-start.19) | collective-permute-done | bytes 163872 | tf_op jit(solution)/shard_map/ppermute | solution.py:60
  49.9 1.5 %collective-permute-start.20 = (bf16[32,2560]{1,0:T(8,128)(2,1)S(1)}, bf16[32,2560]{1,0:T(8,128)(2,1)S(1)}, u32[]{:S(2)}, u32[]{:S(2)}) collective-permute-start(bf16[32,2560]{1,0:T(8,128)(2,1)S(1)} %get-tuple-element.98), channel_id=1, source_target_pairs={{0,2},{1,3},{2,0},{3,1},{4,6},{5,7},{6,4},{7,5},{8,10},{9,11},{10,... | collective-permute-start | bytes 491528 | tf_op jit(solution)/shard_map/ppermute | solution.py:60
  51.4 1.6 %collective-permute-start.17 = (bf16[32,1280]{1,0:T(8,128)(2,1)S(1)}, bf16[32,1280]{1,0:T(8,128)(2,1)S(1)}, u32[]{:S(2)}, u32[]{:S(2)}) collective-permute-start(bf16[32,1280]{1,0:T(8,128)(2,1)S(1)} %get-tuple-element.92), channel_id=1, source_target_pairs={{0,16},{1,17},{2,18},{3,19},{4,20},{5,21},{6,22},{7,23},{8,24},{9,... | collective-permute-start | bytes 245768 | tf_op jit(solution)/shard_map/ppermute | solution.py:60
  53.0 2.9 %collective-permute-done.17.got_x = bf16[32,1280]{1,0:T(8,128)(2,1)S(1)} collective-permute-done((bf16[32,1280]{1,0:T(8,128)(2,1)S(1)}, bf16[32,1280]{1,0:T(8,128)(2,1)S(1)}, u32[]{:S(2)}, u32[]{:S(2)}) %collective-permute-start.17) | collective-permute-done | bytes 81952 | tf_op jit(solution)/shard_map/ppermute | solution.py:60
  56.0 1.1 %collective-permute-start.21 = (bf16[8,5120]{1,0:T(8,128)(2,1)S(1)}, bf16[8,5120]{1,0:T(8,128)(2,1)S(1)}, u32[]{:S(2)}, u32[]{:S(2)}) collective-permute-start(bf16[8,5120]{1,0:T(8,128)(2,1)S(1)} %get-tuple-element.99), channel_id=1, source_target_pairs={{0,8},{1,9},{2,10},{3,11},{4,12},{5,13},{6,14},{7,15},{8,0},{9,1},... | collective-permute-start | bytes 245768 | tf_op jit(solution)/shard_map/ppermute | solution.py:48
  57.1 1.9 %collective-permute-start.22 = (bf16[8,5120]{1,0:T(8,128)(2,1)S(1)}, bf16[8,5120]{1,0:T(8,128)(2,1)S(1)}, u32[]{:S(2)}, u32[]{:S(2)}) collective-permute-start(bf16[8,5120]{1,0:T(8,128)(2,1)S(1)} %get-tuple-element.100.after), channel_id=1, source_target_pairs={{0,12},{1,13},{2,14},{3,15},{4,8},{5,9},{6,10},{7,11},{8,4},{9,5},... | collective-permute-start | bytes 245768 | tf_op jit(solution)/shard_map/ppermute | solution.py:48
  59.5 2.3 %attention.1 = bf16[128,2048]{1,0:T(8,128)(2,1)} custom-call(bf16[8,5120]{1,0:T(8,128)(2,1)S(1)} %get-tuple-element.100.after, bf16[288,128]{1,0:T(8,128)(2,1)S(1)} %collective-permute-done.3.earlier, bf16[288,128]{1,0:T(8,128)(2,1)S(1)} %collective-permute-done.10.earlier_other, bf16[128,2304]{1,0:T(8,128)(2,1)S(1)} %get-tuple-element.102.queries, ...), custom_call_target="tpu_custom_call" | custom-call | tf_op jit(solution)/shard_map/attention/pallas_call | solution.py:92
  61.8 2.1 %collective-permute-done.21.refs_2_ = bf16[8,5120]{1,0:T(8,128)(2,1)S(1)} collective-permute-done((bf16[8,5120]{1,0:T(8,128)(2,1)S(1)}, bf16[8,5120]{1,0:T(8,128)(2,1)S(1)}, u32[]{:S(2)}, u32[]{:S(2)}) %collective-permute-start.21) | collective-permute-done | bytes 81952 | tf_op jit(solution)/shard_map/ppermute | solution.py:48
  63.9 0.7 %collective-permute-done.23.refs_1_ = bf16[8,5120]{1,0:T(8,128)(2,1)S(1)} collective-permute-done((bf16[8,5120]{1,0:T(8,128)(2,1)S(1)}, bf16[8,5120]{1,0:T(8,128)(2,1)S(1)}, u32[]{:S(2)}, u32[]{:S(2)}) %collective-permute-start.23) | collective-permute-done | bytes 81952 | tf_op jit(solution)/shard_map/ppermute | solution.py:48
  64.6 0.7 %sum.1 = bf16[8,5120]{1,0:T(8,128)(2,1)} custom-call(f32[8,5120]{1,0:T(8,128)S(1)} %get-tuple-element.105.first, bf16[8,5120]{1,0:T(8,128)(2,1)S(1)} %collective-permute-done.22.refs_0_, bf16[8,5120]{1,0:T(8,128)(2,1)S(1)} %collective-permute-done.23.refs_1_, bf16[8,5120]{1,0:T(8,128)(2,1)S(1)} %collective-permute-done.21.refs_2_), custom_call_target="tpu_custom_call" | custom-call | tf_op jit(solution)/shard_map/sum/pallas_call | solution.py:92
  (35 shorter events, 4.9 us)
Async XLA Ops:
  1.7 10.9 %collective-permute-start = (bf16[8,5248]{1,0:T(8,128)(2,1)S(1)}, bf16[8,5248]{1,0:T(8,128)(2,1)S(1)}, u32[]{:S(2)}, u32[]{:S(2)}) collective-permute-start(bf16[8,5248]{1,0:T(8,128)(2,1)S(1)} %get-tuple-element.59.refs_0_), channel_id=1, source_target_pairs={{0,12},{1,13},{2,14},{3,15},{4,8},{5,9},{6,10},{7,11},{8,4},{9,5},... | collective-permute-start | bytes 251912 | tf_op jit(solution)/shard_map/ppermute | solution.py:48
  6.8 7.0 %collective-permute-start.1 = (bf16[8,5248]{1,0:T(8,128)(2,1)S(1)}, bf16[8,5248]{1,0:T(8,128)(2,1)S(1)}, u32[]{:S(2)}, u32[]{:S(2)}) collective-permute-start(bf16[8,5248]{1,0:T(8,128)(2,1)S(1)} %get-tuple-element.59.refs_0_), channel_id=1, source_target_pairs={{0,8},{1,9},{2,10},{3,11},{4,12},{5,13},{6,14},{7,15},{8,0},{9,1},... | collective-permute-start | bytes 251912 | tf_op jit(solution)/shard_map/ppermute | solution.py:48
  6.8 7.0 %collective-permute-start.2 = (bf16[8,5248]{1,0:T(8,128)(2,1)S(1)}, bf16[8,5248]{1,0:T(8,128)(2,1)S(1)}, u32[]{:S(2)}, u32[]{:S(2)}) collective-permute-start(bf16[8,5248]{1,0:T(8,128)(2,1)S(1)} %get-tuple-element.59.refs_0_), channel_id=1, source_target_pairs={{0,4},{1,5},{2,6},{3,7},{4,0},{5,1},{6,2},{7,3},{8,12},{9,13},{10,... | collective-permute-start | bytes 251912 | tf_op jit(solution)/shard_map/ppermute | solution.py:48
  7.5 5.1 %collective-permute-start.3 = (bf16[288,128]{1,0:T(8,128)(2,1)S(1)}, bf16[288,128]{1,0:T(8,128)(2,1)S(1)}, u32[]{:S(2)}, u32[]{:S(2)}) collective-permute-start(bf16[288,128]{1,0:T(8,128)(2,1)S(1)} %get-tuple-element.56), channel_id=1, source_target_pairs={{0,16},{16,0},{1,17},{17,1},{2,18},{18,2},{3,19},{19,3},{4,20},{20... | collective-permute-start | bytes 221192 | tf_op jit(solution)/shard_map/ppermute | solution.py:44
  13.9 5.6 %collective-permute-start.8 = (bf16[32,2688]{1,0:T(8,128)(2,1)S(1)}, bf16[32,2688]{1,0:T(8,128)(2,1)S(1)}, u32[]{:S(2)}, u32[]{:S(2)}) collective-permute-start(bf16[32,2688]{1,0:T(8,128)(2,1)S(1)} %get-tuple-element.64.refs_0_), channel_id=1, source_target_pairs={{0,2},{1,3},{2,0},{3,1},{4,6},{5,7},{6,4},{7,5},{8,10},{9,11},{10,... | collective-permute-start | bytes 516104 | tf_op jit(solution)/shard_map/ppermute | solution.py:60
  15.5 5.7 %collective-permute-start.4 = (bf16[32,2560]{1,0:T(8,128)(2,1)S(1)}, bf16[32,2560]{1,0:T(8,128)(2,1)S(1)}, u32[]{:S(2)}, u32[]{:S(2)}) collective-permute-start(bf16[32,2560]{1,0:T(8,128)(2,1)S(1)} %get-tuple-element.63.refs_0_), channel_id=1, source_target_pairs={{0,16},{1,17},{2,18},{3,19},{4,20},{5,21},{6,22},{7,23},{8,24},{9,... | collective-permute-start | bytes 491528 | tf_op jit(solution)/shard_map/ppermute | solution.py:60
  19.5 8.6 %collective-permute-start.9 = (bf16[64,2688]{1,0:T(8,128)(2,1)S(1)}, bf16[64,2688]{1,0:T(8,128)(2,1)S(1)}, u32[]{:S(2)}, u32[]{:S(2)}) collective-permute-start(bf16[64,2688]{1,0:T(8,128)(2,1)S(1)} %stack_two.3.refs_0_), channel_id=1, source_target_pairs={{0,16},{1,17},{2,18},{3,19},{4,20},{5,21},{6,22},{7,23},{8,24},{9,... | collective-permute-start | bytes 1032200 | tf_op jit(solution)/shard_map/ppermute | solution.py:60
  21.3 7.9 %collective-permute-start.5 = (bf16[64,2560]{1,0:T(8,128)(2,1)S(1)}, bf16[64,2560]{1,0:T(8,128)(2,1)S(1)}, u32[]{:S(2)}, u32[]{:S(2)}) collective-permute-start(bf16[64,2560]{1,0:T(8,128)(2,1)S(1)} %stack_two.2.refs_0_), channel_id=1, source_target_pairs={{0,2},{1,3},{2,0},{3,1},{4,6},{5,7},{6,4},{7,5},{8,10},{9,11},{10,... | collective-permute-start | bytes 983048 | tf_op jit(solution)/shard_map/ppermute | solution.py:60
  22.8 5.1 %collective-permute-start.10 = (bf16[288,128]{1,0:T(8,128)(2,1)S(1)}, bf16[288,128]{1,0:T(8,128)(2,1)S(1)}, u32[]{:S(2)}, u32[]{:S(2)}) collective-permute-start(bf16[288,128]{1,0:T(8,128)(2,1)S(1)} %collective-permute-done.3.earlier), channel_id=1, source_target_pairs={{0,1},{1,0},{2,3},{3,2},{4,5},{5,4},{6,7},{7,6},{8,9},{9,8},{10,11... | collective-permute-start | bytes 221192 | tf_op jit(solution)/shard_map/ppermute | solution.py:44
  27.3 1.9 %collective-permute-start.11 = (bf16[64,2688]{1,0:T(8,128)(2,1)S(1)}, bf16[64,2688]{1,0:T(8,128)(2,1)S(1)}, u32[]{:S(2)}, u32[]{:S(2)}) collective-permute-start(bf16[64,2688]{1,0:T(8,128)(2,1)S(1)} %stack_two.3.refs_0_), channel_id=1, source_target_pairs={{0,1},{1,0},{2,3},{3,2},{4,5},{5,4},{6,7},{7,6},{8,9},{9,8},{10,11... | collective-permute-start | bytes 1032200 | tf_op jit(solution)/shard_map/ppermute | solution.py:44
  28.2 1.7 %collective-permute-start.12 = (bf16[64,2688]{1,0:T(8,128)(2,1)S(1)}, bf16[64,2688]{1,0:T(8,128)(2,1)S(1)}, u32[]{:S(2)}, u32[]{:S(2)}) collective-permute-start(bf16[64,2688]{1,0:T(8,128)(2,1)S(1)} %collective-permute-done.9.refs_1_), channel_id=1, source_target_pairs={{0,1},{1,0},{2,3},{3,2},{4,5},{5,4},{6,7},{7,6},{8,9},{9,8},{10,11... | collective-permute-start | bytes 1032200 | tf_op jit(solution)/shard_map/ppermute | solution.py:44
  28.2 3.9 %collective-permute-start.6 = (bf16[64,2560]{1,0:T(8,128)(2,1)S(1)}, bf16[64,2560]{1,0:T(8,128)(2,1)S(1)}, u32[]{:S(2)}, u32[]{:S(2)}) collective-permute-start(bf16[64,2560]{1,0:T(8,128)(2,1)S(1)} %stack_two.2.refs_0_), channel_id=1, source_target_pairs={{0,1},{1,0},{2,3},{3,2},{4,5},{5,4},{6,7},{7,6},{8,9},{9,8},{10,11... | collective-permute-start | bytes 983048 | tf_op jit(solution)/shard_map/ppermute | solution.py:44
  29.1 3.0 %collective-permute-start.7 = (bf16[64,2560]{1,0:T(8,128)(2,1)S(1)}, bf16[64,2560]{1,0:T(8,128)(2,1)S(1)}, u32[]{:S(2)}, u32[]{:S(2)}) collective-permute-start(bf16[64,2560]{1,0:T(8,128)(2,1)S(1)} %collective-permute-done.5.refs_1_), channel_id=1, source_target_pairs={{0,1},{1,0},{2,3},{3,2},{4,5},{5,4},{6,7},{7,6},{8,9},{9,8},{10,11... | collective-permute-start | bytes 983048 | tf_op jit(solution)/shard_map/ppermute | solution.py:44
  33.9 7.1 %collective-permute-start.13 = (bf16[128,512]{1,0:T(8,128)(2,1)S(1)}, bf16[128,512]{1,0:T(8,128)(2,1)S(1)}, u32[]{:S(2)}, u32[]{:S(2)}) collective-permute-start(bf16[128,512]{1,0:T(8,128)(2,1)S(1)} %get-tuple-element.77), channel_id=1, source_target_pairs={{0,16},{16,0},{1,17},{17,1},{2,18},{18,2},{3,19},{19,3},{4,20},{20... | collective-permute-start | bytes 393224 | tf_op jit(solution)/shard_map/ppermute | solution.py:44
  36.5 4.5 %collective-permute-start.14 = (bf16[128,256]{1,0:T(8,128)(2,1)S(1)}, bf16[128,256]{1,0:T(8,128)(2,1)S(1)}, u32[]{:S(2)}, u32[]{:S(2)}) collective-permute-start(bf16[128,256]{1,0:T(8,128)(2,1)S(1)} %get-tuple-element.79), channel_id=1, source_target_pairs={{0,16},{16,0},{1,17},{17,1},{2,18},{18,2},{3,19},{19,3},{4,20},{20... | collective-permute-start | bytes 196616 | tf_op jit(solution)/shard_map/ppermute | solution.py:44
  41.8 1.7 %collective-permute-start.18 = (bf16[128,1280]{1,0:T(8,128)(2,1)S(1)}, bf16[128,1280]{1,0:T(8,128)(2,1)S(1)}, u32[]{:S(2)}, u32[]{:S(2)}) collective-permute-start(bf16[128,1280]{1,0:T(8,128)(2,1)S(1)} %get-tuple-element.94), channel_id=1, source_target_pairs={{0,1},{1,0},{2,3},{3,2},{4,5},{5,4},{6,7},{7,6},{8,9},{9,8},{10,11... | collective-permute-start | bytes 983048 | tf_op jit(solution)/shard_map/ppermute | solution.py:44
  42.7 2.4 %collective-permute-start.15 = (bf16[128,1280]{1,0:T(8,128)(2,1)S(1)}, bf16[128,1280]{1,0:T(8,128)(2,1)S(1)}, u32[]{:S(2)}, u32[]{:S(2)}) collective-permute-start(bf16[128,1280]{1,0:T(8,128)(2,1)S(1)} %get-tuple-element.88), channel_id=1, source_target_pairs={{0,1},{1,0},{2,3},{3,2},{4,5},{5,4},{6,7},{7,6},{8,9},{9,8},{10,11... | collective-permute-start | bytes 983048 | tf_op jit(solution)/shard_map/ppermute | solution.py:44
  43.6 6.3 %collective-permute-start.19 = (bf16[64,1280]{1,0:T(8,128)(2,1)S(1)}, bf16[64,1280]{1,0:T(8,128)(2,1)S(1)}, u32[]{:S(2)}, u32[]{:S(2)}) collective-permute-start(bf16[64,1280]{1,0:T(8,128)(2,1)S(1)} %get-tuple-element.96), channel_id=1, source_target_pairs={{0,16},{1,17},{2,18},{3,19},{4,20},{5,21},{6,22},{7,23},{8,24},{9,... | collective-permute-start | bytes 491528 | tf_op jit(solution)/shard_map/ppermute | solution.py:60
  45.1 6.3 %collective-permute-start.16 = (bf16[64,1280]{1,0:T(8,128)(2,1)S(1)}, bf16[64,1280]{1,0:T(8,128)(2,1)S(1)}, u32[]{:S(2)}, u32[]{:S(2)}) collective-permute-start(bf16[64,1280]{1,0:T(8,128)(2,1)S(1)} %get-tuple-element.90), channel_id=1, source_target_pairs={{0,2},{1,3},{2,0},{3,1},{4,6},{5,7},{6,4},{7,5},{8,10},{9,11},{10,... | collective-permute-start | bytes 491528 | tf_op jit(solution)/shard_map/ppermute | solution.py:60
  49.9 6.0 %collective-permute-start.20 = (bf16[32,2560]{1,0:T(8,128)(2,1)S(1)}, bf16[32,2560]{1,0:T(8,128)(2,1)S(1)}, u32[]{:S(2)}, u32[]{:S(2)}) collective-permute-start(bf16[32,2560]{1,0:T(8,128)(2,1)S(1)} %get-tuple-element.98), channel_id=1, source_target_pairs={{0,2},{1,3},{2,0},{3,1},{4,6},{5,7},{6,4},{7,5},{8,10},{9,11},{10,... | collective-permute-start | bytes 491528 | tf_op jit(solution)/shard_map/ppermute | solution.py:60
  51.4 4.5 %collective-permute-start.17 = (bf16[32,1280]{1,0:T(8,128)(2,1)S(1)}, bf16[32,1280]{1,0:T(8,128)(2,1)S(1)}, u32[]{:S(2)}, u32[]{:S(2)}) collective-permute-start(bf16[32,1280]{1,0:T(8,128)(2,1)S(1)} %get-tuple-element.92), channel_id=1, source_target_pairs={{0,16},{1,17},{2,18},{3,19},{4,20},{5,21},{6,22},{7,23},{8,24},{9,... | collective-permute-start | bytes 245768 | tf_op jit(solution)/shard_map/ppermute | solution.py:60
  56.0 7.9 %collective-permute-start.21 = (bf16[8,5120]{1,0:T(8,128)(2,1)S(1)}, bf16[8,5120]{1,0:T(8,128)(2,1)S(1)}, u32[]{:S(2)}, u32[]{:S(2)}) collective-permute-start(bf16[8,5120]{1,0:T(8,128)(2,1)S(1)} %get-tuple-element.99), channel_id=1, source_target_pairs={{0,8},{1,9},{2,10},{3,11},{4,12},{5,13},{6,14},{7,15},{8,0},{9,1},... | collective-permute-start | bytes 245768 | tf_op jit(solution)/shard_map/ppermute | solution.py:48
  57.1 6.8 %collective-permute-start.22 = (bf16[8,5120]{1,0:T(8,128)(2,1)S(1)}, bf16[8,5120]{1,0:T(8,128)(2,1)S(1)}, u32[]{:S(2)}, u32[]{:S(2)}) collective-permute-start(bf16[8,5120]{1,0:T(8,128)(2,1)S(1)} %get-tuple-element.100.after), channel_id=1, source_target_pairs={{0,12},{1,13},{2,14},{3,15},{4,8},{5,9},{6,10},{7,11},{8,4},{9,5},... | collective-permute-start | bytes 245768 | tf_op jit(solution)/shard_map/ppermute | solution.py:48
  59.0 5.6 %collective-permute-start.23 = (bf16[8,5120]{1,0:T(8,128)(2,1)S(1)}, bf16[8,5120]{1,0:T(8,128)(2,1)S(1)}, u32[]{:S(2)}, u32[]{:S(2)}) collective-permute-start(bf16[8,5120]{1,0:T(8,128)(2,1)S(1)} %get-tuple-element.106), channel_id=1, source_target_pairs={{0,4},{1,5},{2,6},{3,7},{4,0},{5,1},{6,2},{7,3},{8,12},{9,13},{10,... | collective-permute-start | bytes 245768 | tf_op jit(solution)/shard_map/ppermute | solution.py:48

commit v6 on v5

--- a/solution.py
+++ b/solution.py
@@ -329,7 +329,7 @@
         span = slice(start + n, start + n + tall)
         projected = own[:, span] + times_rows_in(act[...], down_w[span, :])
         projected = projected * coef[:, :1]
-        keep[:, n : n + tall] = projected[:half].astype(jnp.bfloat16)
+        keep[:, n : n + tall] = projected[:half]
         give[:, n : n + tall] = projected[half:].astype(jnp.bfloat16)
 
 
@@ -339,7 +339,7 @@
     for out, blocks in ((stay, stays), (send, sends)):
         for number, block in enumerate(blocks):
             span = slice(block * unit, (block + 1) * unit)
-            total = keep[span, :].astype(jnp.float32) + got[span, :].astype(jnp.float32)
+            total = keep[span, :] + got[span, :].astype(jnp.float32)
             out[number * unit : (number + 1) * unit, :] = total.astype(out.dtype)
 
 
@@ -513,7 +513,7 @@
                 (other_a, "vmem"), (other_b, "vmem"), (pick_far, "vmem"), (coef, "vmem"),
                 (down_other, "vmem"), (own, "vmem"),
             ],
-            [((count // 2, part), bf16, "vmem")] * 2,
+            [((count // 2, part), f32, "vmem"), ((count // 2, part), bf16, "vmem")],
             [pltpu.VMEM((count, units), bf16)],
             "down_other",
         )

time: 65.4 us -> 65.4 us (level)
  no operation moved by 1% of the time
where the time goes in v6:
time: 65.4 us; the launch traced here: 65.2 us
  starting transfers between devices  27.2 us (42%)
  Pallas kernels  22.1 us (34%)
  waiting for transfers between devices  15.1 us (23%)
  between operations  0.8 us (1%)
    pallas_call x19, Pallas kernels, local_kernel(): pl.pallas_call(body, in_specs=[pl.BlockSpec(memory_space=kinds[kind]) for...  22.1 us
    ppermute x8, starting transfers between devices, paired(): return lax.ppermute(block, ('ctx', 'exp'), route)  12.4 us
    ppermute x8, waiting for transfers between devices, paired(): return lax.ppermute(block, ('ctx', 'exp'), route)  9.38 us
    ppermute x6, starting transfers between devices, along_line(): lax.ppermute(block, 'exp', [(i, i ^ 4 * steps) for i in range(lax.axis_si...  9.31 us
    ppermute x10, starting transfers between devices, swapped(): lax.ppermute(block, axis, [(i, i ^ bit) for i in range(lax.axis_size(axis...  5.51 us
    ppermute x6, waiting for transfers between devices, along_line(): lax.ppermute(block, 'exp', [(i, i ^ 4 * steps) for i in range(lax.axis_si...  4 us
    ppermute x10, waiting for transfers between devices, swapped(): lax.ppermute(block, axis, [(i, i ^ bit) for i in range(lax.axis_size(axis...  1.71 us
  transfers between devices with their start and end apart: 24, of which 12 were waited for; matrix products, arithmetic and copies ran while one was open for 0% of the time, Pallas kernels for 27%

profile of v6, /device:TPU:0, one launch (start us, length us, event | category | flops | bytes accessed | tf_op | source)
XLA Modules:
  0.0 65.2 jit_solution(12762126536770446410)
XLA Ops:
  0.6 1.1 %rows.1 = (bf16[8,5248]{1,0:T(8,128)(2,1)S(1)}, bf16[288,128]{1,0:T(8,128)(2,1)S(1)}) custom-call(bf16[8,5120]{1,0:T(8,128)(2,1)} %bitcast.16, s32[6,1,8]{2,1,0:T(1,128)} %bitcast.18, f32[6,1,8]{2,1,0:T(1,128)} %bitcast.19, bf16[576,128]{1,0:T(8,128)(2,1)} %bitcast.14), custom_call_target="tpu_custom_call" | custom-call | tf_op jit(solution)/shard_map/rows/pallas_call | solution.py:92
  1.7 5.1 %collective-permute-start = (bf16[8,5248]{1,0:T(8,128)(2,1)S(1)}, bf16[8,5248]{1,0:T(8,128)(2,1)S(1)}, u32[]{:S(2)}, u32[]{:S(2)}) collective-permute-start(bf16[8,5248]{1,0:T(8,128)(2,1)S(1)} %get-tuple-element.59.refs_0_), channel_id=1, source_target_pairs={{0,12},{1,13},{2,14},{3,15},{4,8},{5,9},{6,10},{7,11},{8,4},{9,5},... | collective-permute-start | bytes 251912 | tf_op jit(solution)/shard_map/ppermute | solution.py:48
  7.5 1.6 %collective-permute-start.3 = (bf16[288,128]{1,0:T(8,128)(2,1)S(1)}, bf16[288,128]{1,0:T(8,128)(2,1)S(1)}, u32[]{:S(2)}, u32[]{:S(2)}) collective-permute-start(bf16[288,128]{1,0:T(8,128)(2,1)S(1)} %get-tuple-element.56), channel_id=1, source_target_pairs={{0,16},{16,0},{1,17},{17,1},{2,18},{18,2},{3,19},{19,3},{4,20},{20... | collective-permute-start | bytes 221192 | tf_op jit(solution)/shard_map/ppermute | solution.py:44
  9.1 3.5 %fetch.2 = (bf16[768,2560]{1,0:T(8,128)(2,1)S(1)}, bf16[768,2560]{1,0:T(8,128)(2,1)S(1)}, bf16[128,2304]{1,0:T(8,128)(2,1)S(1)}, bf16[576,128]{1,0:T(8,128)(2,1)S(1)}) custom-call(bf16[8,5248]{1,0:T(8,128)(2,1)S(1)} %get-tuple-element.59.refs_0_, bf16[768,5120]{1,0:T(8,128)(2,1)} %bitcast.8, bf16[768,5120]{1,0:T(8,128)(2,1)} %bitcast.10, ...), custom_call_target="tpu_custom_call" | custom-call | tf_op jit(solution)/shard_map/fetch/pallas_call | solution.py:92
  12.7 1.2 %collective-permute-done.1.refs_2_ = bf16[8,5248]{1,0:T(8,128)(2,1)S(1)} collective-permute-done((bf16[8,5248]{1,0:T(8,128)(2,1)S(1)}, bf16[8,5248]{1,0:T(8,128)(2,1)S(1)}, u32[]{:S(2)}, u32[]{:S(2)}) %collective-permute-start.1) | collective-permute-done | bytes 84000 | tf_op jit(solution)/shard_map/ppermute | solution.py:48
  13.9 1.6 %collective-permute-start.8 = (bf16[32,2688]{1,0:T(8,128)(2,1)S(1)}, bf16[32,2688]{1,0:T(8,128)(2,1)S(1)}, u32[]{:S(2)}, u32[]{:S(2)}) collective-permute-start(bf16[32,2688]{1,0:T(8,128)(2,1)S(1)} %get-tuple-element.64.refs_0_), channel_id=1, source_target_pairs={{0,2},{1,3},{2,0},{3,1},{4,6},{5,7},{6,4},{7,5},{8,10},{9,11},{10,... | collective-permute-start | bytes 516104 | tf_op jit(solution)/shard_map/ppermute | solution.py:60
  15.5 1.5 %collective-permute-start.4 = (bf16[32,2560]{1,0:T(8,128)(2,1)S(1)}, bf16[32,2560]{1,0:T(8,128)(2,1)S(1)}, u32[]{:S(2)}, u32[]{:S(2)}) collective-permute-start(bf16[32,2560]{1,0:T(8,128)(2,1)S(1)} %get-tuple-element.63.refs_0_), channel_id=1, source_target_pairs={{0,16},{1,17},{2,18},{3,19},{4,20},{5,21},{6,22},{7,23},{8,24},{9,... | collective-permute-start | bytes 491528 | tf_op jit(solution)/shard_map/ppermute | solution.py:60
  17.0 2.5 %collective-permute-done.8.refs_1_ = bf16[32,2688]{1,0:T(8,128)(2,1)S(1)} collective-permute-done((bf16[32,2688]{1,0:T(8,128)(2,1)S(1)}, bf16[32,2688]{1,0:T(8,128)(2,1)S(1)}, u32[]{:S(2)}, u32[]{:S(2)}) %collective-permute-start.8) | collective-permute-done | bytes 172064 | tf_op jit(solution)/shard_map/ppermute | solution.py:60
  19.5 1.7 %collective-permute-start.9 = (bf16[64,2688]{1,0:T(8,128)(2,1)S(1)}, bf16[64,2688]{1,0:T(8,128)(2,1)S(1)}, u32[]{:S(2)}, u32[]{:S(2)}) collective-permute-start(bf16[64,2688]{1,0:T(8,128)(2,1)S(1)} %stack_two.3.refs_0_), channel_id=1, source_target_pairs={{0,16},{1,17},{2,18},{3,19},{4,20},{5,21},{6,22},{7,23},{8,24},{9,... | collective-permute-start | bytes 1032200 | tf_op jit(solution)/shard_map/ppermute | solution.py:60
  21.3 1.6 %collective-permute-start.5 = (bf16[64,2560]{1,0:T(8,128)(2,1)S(1)}, bf16[64,2560]{1,0:T(8,128)(2,1)S(1)}, u32[]{:S(2)}, u32[]{:S(2)}) collective-permute-start(bf16[64,2560]{1,0:T(8,128)(2,1)S(1)} %stack_two.2.refs_0_), channel_id=1, source_target_pairs={{0,2},{1,3},{2,0},{3,1},{4,6},{5,7},{6,4},{7,5},{8,10},{9,11},{10,... | collective-permute-start | bytes 983048 | tf_op jit(solution)/shard_map/ppermute | solution.py:60
  22.8 4.5 %fetch.3 = (bf16[768,2560]{1,0:T(8,128)(2,1)S(1)}, bf16[768,2560]{1,0:T(8,128)(2,1)S(1)}, bf16[2560,768]{1,0:T(8,128)(2,1)S(1)}) custom-call(bf16[64,2560]{1,0:T(8,128)(2,1)S(1)} %stack_two.2.refs_0_, bf16[768,5120]{1,0:T(8,128)(2,1)} %bitcast.9, bf16[768,5120]{1,0:T(8,128)(2,1)} %bitcast.11, bf16[2560,1536]{1,0:T(8,128)(2,1)} %bitcast.12), custom_call_target="tpu_custom_call" | custom-call | tf_op jit(solution)/shard_map/fetch/pallas_call | solution.py:92
  29.2 0.6 collective-permute-done.12.refs_3_
  29.8 2.3 %gate_up_first.1 = (f32[256,768]{1,0:T(8,128)S(1)}, f32[256,768]{1,0:T(8,128)S(1)}, bf16[256,128]{1,0:T(8,128)(2,1)S(1)}, bf16[256,128]{1,0:T(8,128)(2,1)S(1)}, f32[256,128]{1,0:T(8,128)S(1)}) custom-call(bf16[64,2688]{1,0:T(8,128)(2,1)S(1)} %stack_two.3.refs_0_, bf16[64,2688]{1,0:T(8,128)(2,1)S(1)} %collective-permute-done.9.refs_1_, ...), custom_call_target="tpu_custom_call" | custom-call | tf_op jit(solution)/shard_map/gate_up_first/pallas_call | solution.py:92
  32.2 1.7 %gate_up_second.1 = (bf16[256,512]{1,0:T(8,128)(2,1)S(1)}, bf16[128,512]{1,0:T(8,128)(2,1)S(1)}, bf16[256,2560]{1,0:T(8,128)(2,1)S(1)}) custom-call(bf16[64,2560]{1,0:T(8,128)(2,1)S(1)} %stack_two.2.refs_0_, bf16[64,2560]{1,0:T(8,128)(2,1)S(1)} %collective-permute-done.5.refs_1_, bf16[64,2560]{1,0:T(8,128)(2,1)S(1)} %collective-permute-done.6.refs_2_, ...), custom_call_target="tpu_custom_call" | custom-call | tf_op jit(solution)/shard_map/gate_up_second/pallas_call | solution.py:92
  33.9 1.6 %collective-permute-start.13 = (bf16[128,512]{1,0:T(8,128)(2,1)S(1)}, bf16[128,512]{1,0:T(8,128)(2,1)S(1)}, u32[]{:S(2)}, u32[]{:S(2)}) collective-permute-start(bf16[128,512]{1,0:T(8,128)(2,1)S(1)} %get-tuple-element.77), channel_id=1, source_target_pairs={{0,16},{16,0},{1,17},{17,1},{2,18},{18,2},{3,19},{19,3},{4,20},{20... | collective-permute-start | bytes 393224 | tf_op jit(solution)/shard_map/ppermute | solution.py:44
  35.4 1.0 %gate_up_third.1 = (bf16[256,256]{1,0:T(8,128)(2,1)S(1)}, bf16[128,256]{1,0:T(8,128)(2,1)S(1)}) custom-call(bf16[256,2560]{1,0:T(8,128)(2,1)S(1)} %get-tuple-element.78.refs_0_, bf16[768,2560]{1,0:T(8,128)(2,1)S(1)} %get-tuple-element.69.refs_4_.refs_1_, bf16[768,2560]{1,0:T(8,128)(2,1)S(1)} %get-tuple-element.70.refs_5_.refs_2_, ...), custom_call_target="tpu_custom_call" | custom-call | tf_op jit(solution)/shard_map/gate_up_third/pallas_call | solution.py:92
  37.1 3.1 %down_own.1 = (f32[256,2560]{1,0:T(8,128)S(1)}, bf16[2560,768]{1,0:T(8,128)(2,1)S(1)}) custom-call(bf16[256,512]{1,0:T(8,128)(2,1)S(1)} %get-tuple-element.82.act_a, bf16[256,256]{1,0:T(8,128)(2,1)S(1)} %get-tuple-element.83.act_b, bf16[2560,768]{1,0:T(8,128)(2,1)S(1)} %get-tuple-element.84.down_own, bf16[2560,1536]{1,0:T(8,128)(2,1)} %bitcast.13), custom_call_target="tpu_custom_call" | custom-call | tf_op jit(solution)/shard_map/down_own/pallas_call | solution.py:92
  40.2 0.7 %collective-permute-done.14.refs_1_ = bf16[128,256]{1,0:T(8,128)(2,1)S(1)} collective-permute-done((bf16[128,256]{1,0:T(8,128)(2,1)S(1)}, bf16[128,256]{1,0:T(8,128)(2,1)S(1)}, u32[]{:S(2)}, u32[]{:S(2)}) %collective-permute-start.14) | collective-permute-done | bytes 65568 | tf_op jit(solution)/shard_map/ppermute | solution.py:44
  41.0 0.8 %down_other.3 = (f32[128,1280]{1,0:T(8,128)S(1)}, bf16[128,1280]{1,0:T(8,128)(2,1)S(1)}) custom-call(bf16[128,512]{1,0:T(8,128)(2,1)S(1)} %collective-permute-done.13.refs_0_, bf16[128,256]{1,0:T(8,128)(2,1)S(1)} %collective-permute-done.14.refs_1_, bf16[256,128]{1,0:T(8,128)(2,1)S(1)} %get-tuple-element.80.refs_2_, ...), custom_call_target="tpu_custom_call" | custom-call | tf_op jit(solution)/shard_map/down_other/pallas_call | solution.py:92
  41.9 0.8 %down_other.2 = (f32[128,1280]{1,0:T(8,128)S(1)}, bf16[128,1280]{1,0:T(8,128)(2,1)S(1)}) custom-call(bf16[128,512]{1,0:T(8,128)(2,1)S(1)} %collective-permute-done.13.refs_0_, bf16[128,256]{1,0:T(8,128)(2,1)S(1)} %collective-permute-done.14.refs_1_, bf16[256,128]{1,0:T(8,128)(2,1)S(1)} %get-tuple-element.80.refs_2_, ...), custom_call_target="tpu_custom_call" | custom-call | tf_op jit(solution)/shard_map/down_other/pallas_call | solution.py:92
  43.5 1.5 %collective-permute-start.19 = (bf16[64,1280]{1,0:T(8,128)(2,1)S(1)}, bf16[64,1280]{1,0:T(8,128)(2,1)S(1)}, u32[]{:S(2)}, u32[]{:S(2)}) collective-permute-start(bf16[64,1280]{1,0:T(8,128)(2,1)S(1)} %get-tuple-element.96), channel_id=1, source_target_pairs={{0,16},{1,17},{2,18},{3,19},{4,20},{5,21},{6,22},{7,23},{8,24},{9,... | collective-permute-start | bytes 491528 | tf_op jit(solution)/shard_map/ppermute | solution.py:60
  45.1 1.6 %collective-permute-start.16 = (bf16[64,1280]{1,0:T(8,128)(2,1)S(1)}, bf16[64,1280]{1,0:T(8,128)(2,1)S(1)}, u32[]{:S(2)}, u32[]{:S(2)}) collective-permute-start(bf16[64,1280]{1,0:T(8,128)(2,1)S(1)} %get-tuple-element.90), channel_id=1, source_target_pairs={{0,2},{1,3},{2,0},{3,1},{4,6},{5,7},{6,4},{7,5},{8,10},{9,11},{10,... | collective-permute-start | bytes 491528 | tf_op jit(solution)/shard_map/ppermute | solution.py:60
  46.7 3.2 %collective-permute-done.19.refs_1_ = bf16[64,1280]{1,0:T(8,128)(2,1)S(1)} collective-permute-done((bf16[64,1280]{1,0:T(8,128)(2,1)S(1)}, bf16[64,1280]{1,0:T(8,128)(2,1)S(1)}, u32[]{:S(2)}, u32[]{:S(2)}) %collective-permute-start.19) | collective-permute-done | bytes 163872 | tf_op jit(solution)/shard_map/ppermute | solution.py:60
  49.9 1.5 %collective-permute-start.20 = (bf16[32,2560]{1,0:T(8,128)(2,1)S(1)}, bf16[32,2560]{1,0:T(8,128)(2,1)S(1)}, u32[]{:S(2)}, u32[]{:S(2)}) collective-permute-start(bf16[32,2560]{1,0:T(8,128)(2,1)S(1)} %get-tuple-element.98), channel_id=1, source_target_pairs={{0,2},{1,3},{2,0},{3,1},{4,6},{5,7},{6,4},{7,5},{8,10},{9,11},{10,... | collective-permute-start | bytes 491528 | tf_op jit(solution)/shard_map/ppermute | solution.py:60
  51.4 1.6 %collective-permute-start.17 = (bf16[32,1280]{1,0:T(8,128)(2,1)S(1)}, bf16[32,1280]{1,0:T(8,128)(2,1)S(1)}, u32[]{:S(2)}, u32[]{:S(2)}) collective-permute-start(bf16[32,1280]{1,0:T(8,128)(2,1)S(1)} %get-tuple-element.92), channel_id=1, source_target_pairs={{0,16},{1,17},{2,18},{3,19},{4,20},{5,21},{6,22},{7,23},{8,24},{9,... | collective-permute-start | bytes 245768 | tf_op jit(solution)/shard_map/ppermute | solution.py:60
  53.0 2.9 %collective-permute-done.17.got_x = bf16[32,1280]{1,0:T(8,128)(2,1)S(1)} collective-permute-done((bf16[32,1280]{1,0:T(8,128)(2,1)S(1)}, bf16[32,1280]{1,0:T(8,128)(2,1)S(1)}, u32[]{:S(2)}, u32[]{:S(2)}) %collective-permute-start.17) | collective-permute-done | bytes 81952 | tf_op jit(solution)/shard_map/ppermute | solution.py:60
  56.0 1.1 %collective-permute-start.21 = (bf16[8,5120]{1,0:T(8,128)(2,1)S(1)}, bf16[8,5120]{1,0:T(8,128)(2,1)S(1)}, u32[]{:S(2)}, u32[]{:S(2)}) collective-permute-start(bf16[8,5120]{1,0:T(8,128)(2,1)S(1)} %get-tuple-element.99), channel_id=1, source_target_pairs={{0,8},{1,9},{2,10},{3,11},{4,12},{5,13},{6,14},{7,15},{8,0},{9,1},... | collective-permute-start | bytes 245768 | tf_op jit(solution)/shard_map/ppermute | solution.py:48
  57.1 1.9 %collective-permute-start.22 = (bf16[8,5120]{1,0:T(8,128)(2,1)S(1)}, bf16[8,5120]{1,0:T(8,128)(2,1)S(1)}, u32[]{:S(2)}, u32[]{:S(2)}) collective-permute-start(bf16[8,5120]{1,0:T(8,128)(2,1)S(1)} %get-tuple-element.100.after), channel_id=1, source_target_pairs={{0,12},{1,13},{2,14},{3,15},{4,8},{5,9},{6,10},{7,11},{8,4},{9,5},... | collective-permute-start | bytes 245768 | tf_op jit(solution)/shard_map/ppermute | solution.py:48
  59.5 2.3 %attention.1 = bf16[128,2048]{1,0:T(8,128)(2,1)} custom-call(bf16[8,5120]{1,0:T(8,128)(2,1)S(1)} %get-tuple-element.100.after, bf16[288,128]{1,0:T(8,128)(2,1)S(1)} %collective-permute-done.3.earlier, bf16[288,128]{1,0:T(8,128)(2,1)S(1)} %collective-permute-done.10.earlier_other, bf16[128,2304]{1,0:T(8,128)(2,1)S(1)} %get-tuple-element.102.queries, ...), custom_call_target="tpu_custom_call" | custom-call | tf_op jit(solution)/shard_map/attention/pallas_call | solution.py:92
  61.8 2.1 %collective-permute-done.21.refs_2_ = bf16[8,5120]{1,0:T(8,128)(2,1)S(1)} collective-permute-done((bf16[8,5120]{1,0:T(8,128)(2,1)S(1)}, bf16[8,5120]{1,0:T(8,128)(2,1)S(1)}, u32[]{:S(2)}, u32[]{:S(2)}) %collective-permute-start.21) | collective-permute-done | bytes 81952 | tf_op jit(solution)/shard_map/ppermute | solution.py:48
  63.9 0.7 %collective-permute-done.23.refs_1_ = bf16[8,5120]{1,0:T(8,128)(2,1)S(1)} collective-permute-done((bf16[8,5120]{1,0:T(8,128)(2,1)S(1)}, bf16[8,5120]{1,0:T(8,128)(2,1)S(1)}, u32[]{:S(2)}, u32[]{:S(2)}) %collective-permute-start.23) | collective-permute-done | bytes 81952 | tf_op jit(solution)/shard_map/ppermute | solution.py:48
  64.6 0.7 %sum.1 = bf16[8,5120]{1,0:T(8,128)(2,1)} custom-call(f32[8,5120]{1,0:T(8,128)S(1)} %get-tuple-element.105.first, bf16[8,5120]{1,0:T(8,128)(2,1)S(1)} %collective-permute-done.22.refs_0_, bf16[8,5120]{1,0:T(8,128)(2,1)S(1)} %collective-permute-done.23.refs_1_, bf16[8,5120]{1,0:T(8,128)(2,1)S(1)} %collective-permute-done.21.refs_2_), custom_call_target="tpu_custom_call" | custom-call | tf_op jit(solution)/shard_map/sum/pallas_call | solution.py:92
  (35 shorter events, 4.8 us)
Async XLA Ops:
  1.7 10.9 %collective-permute-start = (bf16[8,5248]{1,0:T(8,128)(2,1)S(1)}, bf16[8,5248]{1,0:T(8,128)(2,1)S(1)}, u32[]{:S(2)}, u32[]{:S(2)}) collective-permute-start(bf16[8,5248]{1,0:T(8,128)(2,1)S(1)} %get-tuple-element.59.refs_0_), channel_id=1, source_target_pairs={{0,12},{1,13},{2,14},{3,15},{4,8},{5,9},{6,10},{7,11},{8,4},{9,5},... | collective-permute-start | bytes 251912 | tf_op jit(solution)/shard_map/ppermute | solution.py:48
  6.8 7.0 %collective-permute-start.1 = (bf16[8,5248]{1,0:T(8,128)(2,1)S(1)}, bf16[8,5248]{1,0:T(8,128)(2,1)S(1)}, u32[]{:S(2)}, u32[]{:S(2)}) collective-permute-start(bf16[8,5248]{1,0:T(8,128)(2,1)S(1)} %get-tuple-element.59.refs_0_), channel_id=1, source_target_pairs={{0,8},{1,9},{2,10},{3,11},{4,12},{5,13},{6,14},{7,15},{8,0},{9,1},... | collective-permute-start | bytes 251912 | tf_op jit(solution)/shard_map/ppermute | solution.py:48
  6.8 7.0 %collective-permute-start.2 = (bf16[8,5248]{1,0:T(8,128)(2,1)S(1)}, bf16[8,5248]{1,0:T(8,128)(2,1)S(1)}, u32[]{:S(2)}, u32[]{:S(2)}) collective-permute-start(bf16[8,5248]{1,0:T(8,128)(2,1)S(1)} %get-tuple-element.59.refs_0_), channel_id=1, source_target_pairs={{0,4},{1,5},{2,6},{3,7},{4,0},{5,1},{6,2},{7,3},{8,12},{9,13},{10,... | collective-permute-start | bytes 251912 | tf_op jit(solution)/shard_map/ppermute | solution.py:48
  7.5 5.1 %collective-permute-start.3 = (bf16[288,128]{1,0:T(8,128)(2,1)S(1)}, bf16[288,128]{1,0:T(8,128)(2,1)S(1)}, u32[]{:S(2)}, u32[]{:S(2)}) collective-permute-start(bf16[288,128]{1,0:T(8,128)(2,1)S(1)} %get-tuple-element.56), channel_id=1, source_target_pairs={{0,16},{16,0},{1,17},{17,1},{2,18},{18,2},{3,19},{19,3},{4,20},{20... | collective-permute-start | bytes 221192 | tf_op jit(solution)/shard_map/ppermute | solution.py:44
  13.9 5.6 %collective-permute-start.8 = (bf16[32,2688]{1,0:T(8,128)(2,1)S(1)}, bf16[32,2688]{1,0:T(8,128)(2,1)S(1)}, u32[]{:S(2)}, u32[]{:S(2)}) collective-permute-start(bf16[32,2688]{1,0:T(8,128)(2,1)S(1)} %get-tuple-element.64.refs_0_), channel_id=1, source_target_pairs={{0,2},{1,3},{2,0},{3,1},{4,6},{5,7},{6,4},{7,5},{8,10},{9,11},{10,... | collective-permute-start | bytes 516104 | tf_op jit(solution)/shard_map/ppermute | solution.py:60
  15.5 5.7 %collective-permute-start.4 = (bf16[32,2560]{1,0:T(8,128)(2,1)S(1)}, bf16[32,2560]{1,0:T(8,128)(2,1)S(1)}, u32[]{:S(2)}, u32[]{:S(2)}) collective-permute-start(bf16[32,2560]{1,0:T(8,128)(2,1)S(1)} %get-tuple-element.63.refs_0_), channel_id=1, source_target_pairs={{0,16},{1,17},{2,18},{3,19},{4,20},{5,21},{6,22},{7,23},{8,24},{9,... | collective-permute-start | bytes 491528 | tf_op jit(solution)/shard_map/ppermute | solution.py:60
  19.5 8.6 %collective-permute-start.9 = (bf16[64,2688]{1,0:T(8,128)(2,1)S(1)}, bf16[64,2688]{1,0:T(8,128)(2,1)S(1)}, u32[]{:S(2)}, u32[]{:S(2)}) collective-permute-start(bf16[64,2688]{1,0:T(8,128)(2,1)S(1)} %stack_two.3.refs_0_), channel_id=1, source_target_pairs={{0,16},{1,17},{2,18},{3,19},{4,20},{5,21},{6,22},{7,23},{8,24},{9,... | collective-permute-start | bytes 1032200 | tf_op jit(solution)/shard_map/ppermute | solution.py:60
  21.3 7.9 %collective-permute-start.5 = (bf16[64,2560]{1,0:T(8,128)(2,1)S(1)}, bf16[64,2560]{1,0:T(8,128)(2,1)S(1)}, u32[]{:S(2)}, u32[]{:S(2)}) collective-permute-start(bf16[64,2560]{1,0:T(8,128)(2,1)S(1)} %stack_two.2.refs_0_), channel_id=1, source_target_pairs={{0,2},{1,3},{2,0},{3,1},{4,6},{5,7},{6,4},{7,5},{8,10},{9,11},{10,... | collective-permute-start | bytes 983048 | tf_op jit(solution)/shard_map/ppermute | solution.py:60
  22.8 5.1 %collective-permute-start.10 = (bf16[288,128]{1,0:T(8,128)(2,1)S(1)}, bf16[288,128]{1,0:T(8,128)(2,1)S(1)}, u32[]{:S(2)}, u32[]{:S(2)}) collective-permute-start(bf16[288,128]{1,0:T(8,128)(2,1)S(1)} %collective-permute-done.3.earlier), channel_id=1, source_target_pairs={{0,1},{1,0},{2,3},{3,2},{4,5},{5,4},{6,7},{7,6},{8,9},{9,8},{10,11... | collective-permute-start | bytes 221192 | tf_op jit(solution)/shard_map/ppermute | solution.py:44
  27.3 1.9 %collective-permute-start.11 = (bf16[64,2688]{1,0:T(8,128)(2,1)S(1)}, bf16[64,2688]{1,0:T(8,128)(2,1)S(1)}, u32[]{:S(2)}, u32[]{:S(2)}) collective-permute-start(bf16[64,2688]{1,0:T(8,128)(2,1)S(1)} %stack_two.3.refs_0_), channel_id=1, source_target_pairs={{0,1},{1,0},{2,3},{3,2},{4,5},{5,4},{6,7},{7,6},{8,9},{9,8},{10,11... | collective-permute-start | bytes 1032200 | tf_op jit(solution)/shard_map/ppermute | solution.py:44
  28.2 1.7 %collective-permute-start.12 = (bf16[64,2688]{1,0:T(8,128)(2,1)S(1)}, bf16[64,2688]{1,0:T(8,128)(2,1)S(1)}, u32[]{:S(2)}, u32[]{:S(2)}) collective-permute-start(bf16[64,2688]{1,0:T(8,128)(2,1)S(1)} %collective-permute-done.9.refs_1_), channel_id=1, source_target_pairs={{0,1},{1,0},{2,3},{3,2},{4,5},{5,4},{6,7},{7,6},{8,9},{9,8},{10,11... | collective-permute-start | bytes 1032200 | tf_op jit(solution)/shard_map/ppermute | solution.py:44
  28.2 3.9 %collective-permute-start.6 = (bf16[64,2560]{1,0:T(8,128)(2,1)S(1)}, bf16[64,2560]{1,0:T(8,128)(2,1)S(1)}, u32[]{:S(2)}, u32[]{:S(2)}) collective-permute-start(bf16[64,2560]{1,0:T(8,128)(2,1)S(1)} %stack_two.2.refs_0_), channel_id=1, source_target_pairs={{0,1},{1,0},{2,3},{3,2},{4,5},{5,4},{6,7},{7,6},{8,9},{9,8},{10,11... | collective-permute-start | bytes 983048 | tf_op jit(solution)/shard_map/ppermute | solution.py:44
  29.1 3.0 %collective-permute-start.7 = (bf16[64,2560]{1,0:T(8,128)(2,1)S(1)}, bf16[64,2560]{1,0:T(8,128)(2,1)S(1)}, u32[]{:S(2)}, u32[]{:S(2)}) collective-permute-start(bf16[64,2560]{1,0:T(8,128)(2,1)S(1)} %collective-permute-done.5.refs_1_), channel_id=1, source_target_pairs={{0,1},{1,0},{2,3},{3,2},{4,5},{5,4},{6,7},{7,6},{8,9},{9,8},{10,11... | collective-permute-start | bytes 983048 | tf_op jit(solution)/shard_map/ppermute | solution.py:44
  33.9 7.1 %collective-permute-start.13 = (bf16[128,512]{1,0:T(8,128)(2,1)S(1)}, bf16[128,512]{1,0:T(8,128)(2,1)S(1)}, u32[]{:S(2)}, u32[]{:S(2)}) collective-permute-start(bf16[128,512]{1,0:T(8,128)(2,1)S(1)} %get-tuple-element.77), channel_id=1, source_target_pairs={{0,16},{16,0},{1,17},{17,1},{2,18},{18,2},{3,19},{19,3},{4,20},{20... | collective-permute-start | bytes 393224 | tf_op jit(solution)/shard_map/ppermute | solution.py:44
  36.5 4.5 %collective-permute-start.14 = (bf16[128,256]{1,0:T(8,128)(2,1)S(1)}, bf16[128,256]{1,0:T(8,128)(2,1)S(1)}, u32[]{:S(2)}, u32[]{:S(2)}) collective-permute-start(bf16[128,256]{1,0:T(8,128)(2,1)S(1)} %get-tuple-element.79), channel_id=1, source_target_pairs={{0,16},{16,0},{1,17},{17,1},{2,18},{18,2},{3,19},{19,3},{4,20},{20... | collective-permute-start | bytes 196616 | tf_op jit(solution)/shard_map/ppermute | solution.py:44
  41.8 1.7 %collective-permute-start.18 = (bf16[128,1280]{1,0:T(8,128)(2,1)S(1)}, bf16[128,1280]{1,0:T(8,128)(2,1)S(1)}, u32[]{:S(2)}, u32[]{:S(2)}) collective-permute-start(bf16[128,1280]{1,0:T(8,128)(2,1)S(1)} %get-tuple-element.94), channel_id=1, source_target_pairs={{0,1},{1,0},{2,3},{3,2},{4,5},{5,4},{6,7},{7,6},{8,9},{9,8},{10,11... | collective-permute-start | bytes 983048 | tf_op jit(solution)/shard_map/ppermute | solution.py:44
  42.7 2.3 %collective-permute-start.15 = (bf16[128,1280]{1,0:T(8,128)(2,1)S(1)}, bf16[128,1280]{1,0:T(8,128)(2,1)S(1)}, u32[]{:S(2)}, u32[]{:S(2)}) collective-permute-start(bf16[128,1280]{1,0:T(8,128)(2,1)S(1)} %get-tuple-element.88), channel_id=1, source_target_pairs={{0,1},{1,0},{2,3},{3,2},{4,5},{5,4},{6,7},{7,6},{8,9},{9,8},{10,11... | collective-permute-start | bytes 983048 | tf_op jit(solution)/shard_map/ppermute | solution.py:44
  43.5 6.3 %collective-permute-start.19 = (bf16[64,1280]{1,0:T(8,128)(2,1)S(1)}, bf16[64,1280]{1,0:T(8,128)(2,1)S(1)}, u32[]{:S(2)}, u32[]{:S(2)}) collective-permute-start(bf16[64,1280]{1,0:T(8,128)(2,1)S(1)} %get-tuple-element.96), channel_id=1, source_target_pairs={{0,16},{1,17},{2,18},{3,19},{4,20},{5,21},{6,22},{7,23},{8,24},{9,... | collective-permute-start | bytes 491528 | tf_op jit(solution)/shard_map/ppermute | solution.py:60
  45.1 6.3 %collective-permute-start.16 = (bf16[64,1280]{1,0:T(8,128)(2,1)S(1)}, bf16[64,1280]{1,0:T(8,128)(2,1)S(1)}, u32[]{:S(2)}, u32[]{:S(2)}) collective-permute-start(bf16[64,1280]{1,0:T(8,128)(2,1)S(1)} %get-tuple-element.90), channel_id=1, source_target_pairs={{0,2},{1,3},{2,0},{3,1},{4,6},{5,7},{6,4},{7,5},{8,10},{9,11},{10,... | collective-permute-start | bytes 491528 | tf_op jit(solution)/shard_map/ppermute | solution.py:60
  49.9 6.0 %collective-permute-start.20 = (bf16[32,2560]{1,0:T(8,128)(2,1)S(1)}, bf16[32,2560]{1,0:T(8,128)(2,1)S(1)}, u32[]{:S(2)}, u32[]{:S(2)}) collective-permute-start(bf16[32,2560]{1,0:T(8,128)(2,1)S(1)} %get-tuple-element.98), channel_id=1, source_target_pairs={{0,2},{1,3},{2,0},{3,1},{4,6},{5,7},{6,4},{7,5},{8,10},{9,11},{10,... | collective-permute-start | bytes 491528 | tf_op jit(solution)/shard_map/ppermute | solution.py:60
  51.4 4.5 %collective-permute-start.17 = (bf16[32,1280]{1,0:T(8,128)(2,1)S(1)}, bf16[32,1280]{1,0:T(8,128)(2,1)S(1)}, u32[]{:S(2)}, u32[]{:S(2)}) collective-permute-start(bf16[32,1280]{1,0:T(8,128)(2,1)S(1)} %get-tuple-element.92), channel_id=1, source_target_pairs={{0,16},{1,17},{2,18},{3,19},{4,20},{5,21},{6,22},{7,23},{8,24},{9,... | collective-permute-start | bytes 245768 | tf_op jit(solution)/shard_map/ppermute | solution.py:60
  56.0 7.9 %collective-permute-start.21 = (bf16[8,5120]{1,0:T(8,128)(2,1)S(1)}, bf16[8,5120]{1,0:T(8,128)(2,1)S(1)}, u32[]{:S(2)}, u32[]{:S(2)}) collective-permute-start(bf16[8,5120]{1,0:T(8,128)(2,1)S(1)} %get-tuple-element.99), channel_id=1, source_target_pairs={{0,8},{1,9},{2,10},{3,11},{4,12},{5,13},{6,14},{7,15},{8,0},{9,1},... | collective-permute-start | bytes 245768 | tf_op jit(solution)/shard_map/ppermute | solution.py:48
  57.1 6.8 %collective-permute-start.22 = (bf16[8,5120]{1,0:T(8,128)(2,1)S(1)}, bf16[8,5120]{1,0:T(8,128)(2,1)S(1)}, u32[]{:S(2)}, u32[]{:S(2)}) collective-permute-start(bf16[8,5120]{1,0:T(8,128)(2,1)S(1)} %get-tuple-element.100.after), channel_id=1, source_target_pairs={{0,12},{1,13},{2,14},{3,15},{4,8},{5,9},{6,10},{7,11},{8,4},{9,5},... | collective-permute-start | bytes 245768 | tf_op jit(solution)/shard_map/ppermute | solution.py:48
  59.0 5.6 %collective-permute-start.23 = (bf16[8,5120]{1,0:T(8,128)(2,1)S(1)}, bf16[8,5120]{1,0:T(8,128)(2,1)S(1)}, u32[]{:S(2)}, u32[]{:S(2)}) collective-permute-start(bf16[8,5120]{1,0:T(8,128)(2,1)S(1)} %get-tuple-element.106), channel_id=1, source_target_pairs={{0,4},{1,5},{2,6},{3,7},{4,0},{5,1},{6,2},{7,3},{8,12},{9,13},{10,... | collective-permute-start | bytes 245768 | tf_op jit(solution)/shard_map/ppermute | solution.py:48

commit v7 on v6

--- a/solution.py
+++ b/solution.py
@@ -127,21 +127,17 @@
         pltpu.make_async_copy(source, target, sems.at[number])
         for number, (source, target) in enumerate(
             (
-                (tokens_in, tokens),
                 (names_in, names),
                 (weights_in, weights),
+                (tokens_in, tokens),
                 (latents_in.at[pl.ds(at, share), :], latents),
             )
         )
     ]
     for copy in copies:
         copy.start()
-    for copy in copies:
-        copy.wait()
     count = tokens.shape[0]
     width = tokens.shape[1]
-    out[:, :half] = tokens[:, :half]
-    out[:, half + 128 :] = tokens[:, half:width]
     lane = lax.broadcasted_iota(jnp.int32, (count, 128), 1)
     same = lax.broadcasted_iota(jnp.int32, (count, count), 0) == lax.broadcasted_iota(
         jnp.int32, (count, count), 1
@@ -152,6 +148,8 @@
             jnp.where(same, jnp.broadcast_to(row, same.shape), 0.0), axis=1, keepdims=True
         )
 
+    for copy in copies[:2]:
+        copy.wait()
     note = jnp.zeros((count, 128), jnp.float32)
     for k in range(topk):
         name = column(names[k].astype(jnp.float32))
@@ -160,6 +158,10 @@
         for value, at in ((name, k), (weight, topk + k), (low, 2 * topk + k)):
             note = jnp.where(lane == at, value, note)
     out[:, half : half + 128] = note.astype(jnp.bfloat16)
+    for copy in copies[2:]:
+        copy.wait()
+    out[:, :half] = tokens[:, :half]
+    out[:, half + 128 :] = tokens[:, half:width]
 
 
 def fetch_kernel(after, *refs, start):
@@ -247,11 +249,11 @@
     rows = tokens.shape[0]
     slots = pick_out.shape[1]
     expert = lax.axis_index("exp")
-    assemble(tokens, two, far, two_other, far_other, unit, True)
+    assemble(tokens, two, far, two_other, far_other, unit, False)
     gate_out[...] = times_rows_in(tokens[...], gate_w[...])
     up_out[...] = times_rows_in(tokens[...], up_w[...])
 
-    assemble(notes, two, far, two_other, far_other, unit, True, width)
+    assemble(notes, two, far, two_other, far_other, unit, False, width)
     note = notes[...].astype(jnp.float32)
     lane = lax.broadcasted_iota(jnp.int32, note.shape, 1)
     mine = (note == expert.astype(jnp.float32)) & (lane < topk)
@@ -294,7 +296,7 @@
     two, far, two_other, far_other, gate_w, up_w, gate_in, up_in, pick,
     act_out, packed_out, tokens, *, unit,
 ):
-    assemble(tokens, two, far, two_other, far_other, unit, False)
+    assemble(tokens, two, far, two_other, far_other, unit, True)
     finish_units(tokens, gate_w, up_w, gate_in, up_in, pick, act_out, packed_out, 0)
 
 
@@ -355,7 +357,7 @@
         send[:, part:] = got[unit:, :]
 
 
-def line_kernel(left_y, got_x, left_x, got_y, *outs):
+def line_kernel(left_x, got_y, left_y, got_x, *outs):
     ctx = lax.axis_index("ctx")
     count, part = outs[0].shape[0], left_y.shape[1]
     whole = left_x[...] + got_y[...].astype(jnp.float32)
@@ -439,7 +441,7 @@
         "stack_line",
     )
     pieces = []
-    for near, first, then in zip(nears, (over_y, over_x), (over_x, over_y)):
+    for near, first, then in zip(nears, (over_x, over_y), (over_y, over_x)):
         got = paired(near, first)
         (two,) = local_kernel(
             lambda *refs, cut=near.shape[1]: stack_kernel(*refs, cuts=((0, cut),)),
@@ -506,7 +508,7 @@
     )
     part = columns // 2
     crossing = []
-    for start, y_first in ((0, True), (part, False)):
+    for start, y_first in ((part, False), (0, True)):
         keep, give = local_kernel(
             lambda *refs, start=start: other_kernel(*refs, start=start),
             [

time: 65.4 us -> 65.3 us (level)
  transfers between devices with their start and end apart: 24 -> 24, of which waited for: 12 -> 11; matrix products, arithmetic and copies ran while one was open for 0% -> 0% of each run, Pallas kernels for 27% -> 27%
where the time goes in v7:
time: 65.3 us; the launch traced here: 65.1 us
  starting transfers between devices  27.2 us (42%)
  Pallas kernels  22 us (34%)
  waiting for transfers between devices  15 us (23%)
  between operations  0.8 us (1%)
    pallas_call x19, Pallas kernels, local_kernel(): pl.pallas_call(body, in_specs=[pl.BlockSpec(memory_space=kinds[kind]) for...  22 us
    ppermute x8, starting transfers between devices, paired(): return lax.ppermute(block, ('ctx', 'exp'), route)  12.4 us
    ppermute x8, waiting for transfers between devices, paired(): return lax.ppermute(block, ('ctx', 'exp'), route)  9.42 us
    ppermute x6, starting transfers between devices, along_line(): lax.ppermute(block, 'exp', [(i, i ^ 4 * steps) for i in range(lax.axis_si...  9.31 us
    ppermute x10, starting transfers between devices, swapped(): lax.ppermute(block, axis, [(i, i ^ bit) for i in range(lax.axis_size(axis...  5.51 us
    ppermute x6, waiting for transfers between devices, along_line(): lax.ppermute(block, 'exp', [(i, i ^ 4 * steps) for i in range(lax.axis_si...  3.91 us
    ppermute x10, waiting for transfers between devices, swapped(): lax.ppermute(block, axis, [(i, i ^ bit) for i in range(lax.axis_size(axis...  1.69 us
  transfers between devices with their start and end apart: 24, of which 11 were waited for; matrix products, arithmetic and copies ran while one was open for 0% of the time, Pallas kernels for 27%

profile of v7, /device:TPU:0, one launch (start us, length us, event | category | flops | bytes accessed | tf_op | source)
XLA Modules:
  0.0 65.1 jit_solution(10098690865566547440)
XLA Ops:
  0.6 1.0 %rows.1 = (bf16[8,5248]{1,0:T(8,128)(2,1)S(1)}, bf16[288,128]{1,0:T(8,128)(2,1)S(1)}) custom-call(bf16[8,5120]{1,0:T(8,128)(2,1)} %bitcast.16, s32[6,1,8]{2,1,0:T(1,128)} %bitcast.18, f32[6,1,8]{2,1,0:T(1,128)} %bitcast.19, bf16[576,128]{1,0:T(8,128)(2,1)} %bitcast.14), custom_call_target="tpu_custom_call" | custom-call | tf_op jit(solution)/shard_map/rows/pallas_call | solution.py:92
  1.6 5.1 %collective-permute-start = (bf16[8,5248]{1,0:T(8,128)(2,1)S(1)}, bf16[8,5248]{1,0:T(8,128)(2,1)S(1)}, u32[]{:S(2)}, u32[]{:S(2)}) collective-permute-start(bf16[8,5248]{1,0:T(8,128)(2,1)S(1)} %get-tuple-element.59.refs_0_), channel_id=1, source_target_pairs={{0,12},{1,13},{2,14},{3,15},{4,8},{5,9},{6,10},{7,11},{8,4},{9,5},... | collective-permute-start | bytes 251912 | tf_op jit(solution)/shard_map/ppermute | solution.py:48
  6.8 0.6 collective-permute-start.2
  7.4 1.6 %collective-permute-start.3 = (bf16[288,128]{1,0:T(8,128)(2,1)S(1)}, bf16[288,128]{1,0:T(8,128)(2,1)S(1)}, u32[]{:S(2)}, u32[]{:S(2)}) collective-permute-start(bf16[288,128]{1,0:T(8,128)(2,1)S(1)} %get-tuple-element.56), channel_id=1, source_target_pairs={{0,16},{16,0},{1,17},{17,1},{2,18},{18,2},{3,19},{19,3},{4,20},{20... | collective-permute-start | bytes 221192 | tf_op jit(solution)/shard_map/ppermute | solution.py:44
  9.0 3.5 %fetch.2 = (bf16[768,2560]{1,0:T(8,128)(2,1)S(1)}, bf16[768,2560]{1,0:T(8,128)(2,1)S(1)}, bf16[128,2304]{1,0:T(8,128)(2,1)S(1)}, bf16[576,128]{1,0:T(8,128)(2,1)S(1)}) custom-call(bf16[8,5248]{1,0:T(8,128)(2,1)S(1)} %get-tuple-element.59.refs_0_, bf16[768,5120]{1,0:T(8,128)(2,1)} %bitcast.8, bf16[768,5120]{1,0:T(8,128)(2,1)} %bitcast.10, ...), custom_call_target="tpu_custom_call" | custom-call | tf_op jit(solution)/shard_map/fetch/pallas_call | solution.py:92
  12.6 1.2 %collective-permute-done.1.refs_2_ = bf16[8,5248]{1,0:T(8,128)(2,1)S(1)} collective-permute-done((bf16[8,5248]{1,0:T(8,128)(2,1)S(1)}, bf16[8,5248]{1,0:T(8,128)(2,1)S(1)}, u32[]{:S(2)}, u32[]{:S(2)}) %collective-permute-start.1) | collective-permute-done | bytes 84000 | tf_op jit(solution)/shard_map/ppermute | solution.py:48
  13.8 1.6 %collective-permute-start.8 = (bf16[32,2688]{1,0:T(8,128)(2,1)S(1)}, bf16[32,2688]{1,0:T(8,128)(2,1)S(1)}, u32[]{:S(2)}, u32[]{:S(2)}) collective-permute-start(bf16[32,2688]{1,0:T(8,128)(2,1)S(1)} %get-tuple-element.64.refs_0_), channel_id=1, source_target_pairs={{0,16},{1,17},{2,18},{3,19},{4,20},{5,21},{6,22},{7,23},{8,24},{9,... | collective-permute-start | bytes 516104 | tf_op jit(solution)/shard_map/ppermute | solution.py:60
  15.4 1.5 %collective-permute-start.4 = (bf16[32,2560]{1,0:T(8,128)(2,1)S(1)}, bf16[32,2560]{1,0:T(8,128)(2,1)S(1)}, u32[]{:S(2)}, u32[]{:S(2)}) collective-permute-start(bf16[32,2560]{1,0:T(8,128)(2,1)S(1)} %get-tuple-element.63.refs_0_), channel_id=1, source_target_pairs={{0,2},{1,3},{2,0},{3,1},{4,6},{5,7},{6,4},{7,5},{8,10},{9,11},{10,... | collective-permute-start | bytes 491528 | tf_op jit(solution)/shard_map/ppermute | solution.py:60
  16.9 2.5 %collective-permute-done.8.refs_1_ = bf16[32,2688]{1,0:T(8,128)(2,1)S(1)} collective-permute-done((bf16[32,2688]{1,0:T(8,128)(2,1)S(1)}, bf16[32,2688]{1,0:T(8,128)(2,1)S(1)}, u32[]{:S(2)}, u32[]{:S(2)}) %collective-permute-start.8) | collective-permute-done | bytes 172064 | tf_op jit(solution)/shard_map/ppermute | solution.py:60
  19.4 1.7 %collective-permute-start.9 = (bf16[64,2688]{1,0:T(8,128)(2,1)S(1)}, bf16[64,2688]{1,0:T(8,128)(2,1)S(1)}, u32[]{:S(2)}, u32[]{:S(2)}) collective-permute-start(bf16[64,2688]{1,0:T(8,128)(2,1)S(1)} %stack_two.3.refs_0_), channel_id=1, source_target_pairs={{0,2},{1,3},{2,0},{3,1},{4,6},{5,7},{6,4},{7,5},{8,10},{9,11},{10,... | collective-permute-start | bytes 1032200 | tf_op jit(solution)/shard_map/ppermute | solution.py:60
  21.2 1.6 %collective-permute-start.5 = (bf16[64,2560]{1,0:T(8,128)(2,1)S(1)}, bf16[64,2560]{1,0:T(8,128)(2,1)S(1)}, u32[]{:S(2)}, u32[]{:S(2)}) collective-permute-start(bf16[64,2560]{1,0:T(8,128)(2,1)S(1)} %stack_two.2.refs_0_), channel_id=1, source_target_pairs={{0,16},{1,17},{2,18},{3,19},{4,20},{5,21},{6,22},{7,23},{8,24},{9,... | collective-permute-start | bytes 983048 | tf_op jit(solution)/shard_map/ppermute | solution.py:60
  22.8 4.5 %fetch.3 = (bf16[768,2560]{1,0:T(8,128)(2,1)S(1)}, bf16[768,2560]{1,0:T(8,128)(2,1)S(1)}, bf16[2560,768]{1,0:T(8,128)(2,1)S(1)}) custom-call(bf16[64,2560]{1,0:T(8,128)(2,1)S(1)} %stack_two.2.refs_0_, bf16[768,5120]{1,0:T(8,128)(2,1)} %bitcast.9, bf16[768,5120]{1,0:T(8,128)(2,1)} %bitcast.11, bf16[2560,1536]{1,0:T(8,128)(2,1)} %bitcast.12), custom_call_target="tpu_custom_call" | custom-call | tf_op jit(solution)/shard_map/fetch/pallas_call | solution.py:92
  29.1 0.6 collective-permute-done.12.refs_3_
  29.7 2.3 %gate_up_first.1 = (f32[256,768]{1,0:T(8,128)S(1)}, f32[256,768]{1,0:T(8,128)S(1)}, bf16[256,128]{1,0:T(8,128)(2,1)S(1)}, bf16[256,128]{1,0:T(8,128)(2,1)S(1)}, f32[256,128]{1,0:T(8,128)S(1)}) custom-call(bf16[64,2688]{1,0:T(8,128)(2,1)S(1)} %stack_two.3.refs_0_, bf16[64,2688]{1,0:T(8,128)(2,1)S(1)} %collective-permute-done.9.refs_1_, ...), custom_call_target="tpu_custom_call" | custom-call | tf_op jit(solution)/shard_map/gate_up_first/pallas_call | solution.py:92
  32.0 1.7 %gate_up_second.1 = (bf16[256,512]{1,0:T(8,128)(2,1)S(1)}, bf16[128,512]{1,0:T(8,128)(2,1)S(1)}, bf16[256,2560]{1,0:T(8,128)(2,1)S(1)}) custom-call(bf16[64,2560]{1,0:T(8,128)(2,1)S(1)} %stack_two.2.refs_0_, bf16[64,2560]{1,0:T(8,128)(2,1)S(1)} %collective-permute-done.5.refs_1_, bf16[64,2560]{1,0:T(8,128)(2,1)S(1)} %collective-permute-done.6.refs_2_, ...), custom_call_target="tpu_custom_call" | custom-call | tf_op jit(solution)/shard_map/gate_up_second/pallas_call | solution.py:92
  33.8 1.6 %collective-permute-start.13 = (bf16[128,512]{1,0:T(8,128)(2,1)S(1)}, bf16[128,512]{1,0:T(8,128)(2,1)S(1)}, u32[]{:S(2)}, u32[]{:S(2)}) collective-permute-start(bf16[128,512]{1,0:T(8,128)(2,1)S(1)} %get-tuple-element.77), channel_id=1, source_target_pairs={{0,16},{16,0},{1,17},{17,1},{2,18},{18,2},{3,19},{19,3},{4,20},{20... | collective-permute-start | bytes 393224 | tf_op jit(solution)/shard_map/ppermute | solution.py:44
  35.3 1.0 %gate_up_third.1 = (bf16[256,256]{1,0:T(8,128)(2,1)S(1)}, bf16[128,256]{1,0:T(8,128)(2,1)S(1)}) custom-call(bf16[256,2560]{1,0:T(8,128)(2,1)S(1)} %get-tuple-element.78.refs_0_, bf16[768,2560]{1,0:T(8,128)(2,1)S(1)} %get-tuple-element.69.refs_4_.refs_1_, bf16[768,2560]{1,0:T(8,128)(2,1)S(1)} %get-tuple-element.70.refs_5_.refs_2_, ...), custom_call_target="tpu_custom_call" | custom-call | tf_op jit(solution)/shard_map/gate_up_third/pallas_call | solution.py:92
  37.0 3.1 %down_own.1 = (f32[256,2560]{1,0:T(8,128)S(1)}, bf16[2560,768]{1,0:T(8,128)(2,1)S(1)}) custom-call(bf16[256,512]{1,0:T(8,128)(2,1)S(1)} %get-tuple-element.82.act_a, bf16[256,256]{1,0:T(8,128)(2,1)S(1)} %get-tuple-element.83.act_b, bf16[2560,768]{1,0:T(8,128)(2,1)S(1)} %get-tuple-element.84.down_own, bf16[2560,1536]{1,0:T(8,128)(2,1)} %bitcast.13), custom_call_target="tpu_custom_call" | custom-call | tf_op jit(solution)/shard_map/down_own/pallas_call | solution.py:92
  40.1 0.8 %collective-permute-done.14.refs_1_ = bf16[128,256]{1,0:T(8,128)(2,1)S(1)} collective-permute-done((bf16[128,256]{1,0:T(8,128)(2,1)S(1)}, bf16[128,256]{1,0:T(8,128)(2,1)S(1)}, u32[]{:S(2)}, u32[]{:S(2)}) %collective-permute-start.14) | collective-permute-done | bytes 65568 | tf_op jit(solution)/shard_map/ppermute | solution.py:44
  40.9 0.8 %down_other.2 = (f32[128,1280]{1,0:T(8,128)S(1)}, bf16[128,1280]{1,0:T(8,128)(2,1)S(1)}) custom-call(bf16[128,512]{1,0:T(8,128)(2,1)S(1)} %collective-permute-done.13.refs_0_, bf16[128,256]{1,0:T(8,128)(2,1)S(1)} %collective-permute-done.14.refs_1_, bf16[256,128]{1,0:T(8,128)(2,1)S(1)} %get-tuple-element.80.refs_2_, ...), custom_call_target="tpu_custom_call" | custom-call | tf_op jit(solution)/shard_map/down_other/pallas_call | solution.py:92
  41.8 0.8 %down_other.3 = (f32[128,1280]{1,0:T(8,128)S(1)}, bf16[128,1280]{1,0:T(8,128)(2,1)S(1)}) custom-call(bf16[128,512]{1,0:T(8,128)(2,1)S(1)} %collective-permute-done.13.refs_0_, bf16[128,256]{1,0:T(8,128)(2,1)S(1)} %collective-permute-done.14.refs_1_, bf16[256,128]{1,0:T(8,128)(2,1)S(1)} %get-tuple-element.80.refs_2_, ...), custom_call_target="tpu_custom_call" | custom-call | tf_op jit(solution)/shard_map/down_other/pallas_call | solution.py:92
  43.5 1.5 %collective-permute-start.16 = (bf16[64,1280]{1,0:T(8,128)(2,1)S(1)}, bf16[64,1280]{1,0:T(8,128)(2,1)S(1)}, u32[]{:S(2)}, u32[]{:S(2)}) collective-permute-start(bf16[64,1280]{1,0:T(8,128)(2,1)S(1)} %get-tuple-element.90), channel_id=1, source_target_pairs={{0,16},{1,17},{2,18},{3,19},{4,20},{5,21},{6,22},{7,23},{8,24},{9,... | collective-permute-start | bytes 491528 | tf_op jit(solution)/shard_map/ppermute | solution.py:60
  45.0 1.6 %collective-permute-start.19 = (bf16[64,1280]{1,0:T(8,128)(2,1)S(1)}, bf16[64,1280]{1,0:T(8,128)(2,1)S(1)}, u32[]{:S(2)}, u32[]{:S(2)}) collective-permute-start(bf16[64,1280]{1,0:T(8,128)(2,1)S(1)} %get-tuple-element.96), channel_id=1, source_target_pairs={{0,2},{1,3},{2,0},{3,1},{4,6},{5,7},{6,4},{7,5},{8,10},{9,11},{10,... | collective-permute-start | bytes 491528 | tf_op jit(solution)/shard_map/ppermute | solution.py:60
  46.6 3.2 %collective-permute-done.16.refs_1_ = bf16[64,1280]{1,0:T(8,128)(2,1)S(1)} collective-permute-done((bf16[64,1280]{1,0:T(8,128)(2,1)S(1)}, bf16[64,1280]{1,0:T(8,128)(2,1)S(1)}, u32[]{:S(2)}, u32[]{:S(2)}) %collective-permute-start.16) | collective-permute-done | bytes 163872 | tf_op jit(solution)/shard_map/ppermute | solution.py:60
  49.8 1.5 %collective-permute-start.17 = (bf16[32,2560]{1,0:T(8,128)(2,1)S(1)}, bf16[32,2560]{1,0:T(8,128)(2,1)S(1)}, u32[]{:S(2)}, u32[]{:S(2)}) collective-permute-start(bf16[32,2560]{1,0:T(8,128)(2,1)S(1)} %get-tuple-element.92), channel_id=1, source_target_pairs={{0,2},{1,3},{2,0},{3,1},{4,6},{5,7},{6,4},{7,5},{8,10},{9,11},{10,... | collective-permute-start | bytes 491528 | tf_op jit(solution)/shard_map/ppermute | solution.py:60
  51.3 1.6 %collective-permute-start.20 = (bf16[32,1280]{1,0:T(8,128)(2,1)S(1)}, bf16[32,1280]{1,0:T(8,128)(2,1)S(1)}, u32[]{:S(2)}, u32[]{:S(2)}) collective-permute-start(bf16[32,1280]{1,0:T(8,128)(2,1)S(1)} %get-tuple-element.98), channel_id=1, source_target_pairs={{0,16},{1,17},{2,18},{3,19},{4,20},{5,21},{6,22},{7,23},{8,24},{9,... | collective-permute-start | bytes 245768 | tf_op jit(solution)/shard_map/ppermute | solution.py:60
  52.9 3.0 %collective-permute-done.20.got_x = bf16[32,1280]{1,0:T(8,128)(2,1)S(1)} collective-permute-done((bf16[32,1280]{1,0:T(8,128)(2,1)S(1)}, bf16[32,1280]{1,0:T(8,128)(2,1)S(1)}, u32[]{:S(2)}, u32[]{:S(2)}) %collective-permute-start.20) | collective-permute-done | bytes 81952 | tf_op jit(solution)/shard_map/ppermute | solution.py:60
  55.9 0.9 %collective-permute-start.21 = (bf16[8,5120]{1,0:T(8,128)(2,1)S(1)}, bf16[8,5120]{1,0:T(8,128)(2,1)S(1)}, u32[]{:S(2)}, u32[]{:S(2)}) collective-permute-start(bf16[8,5120]{1,0:T(8,128)(2,1)S(1)} %get-tuple-element.99), channel_id=1, source_target_pairs={{0,8},{1,9},{2,10},{3,11},{4,12},{5,13},{6,14},{7,15},{8,0},{9,1},... | collective-permute-start | bytes 245768 | tf_op jit(solution)/shard_map/ppermute | solution.py:48
  56.8 2.3 %collective-permute-start.22 = (bf16[8,5120]{1,0:T(8,128)(2,1)S(1)}, bf16[8,5120]{1,0:T(8,128)(2,1)S(1)}, u32[]{:S(2)}, u32[]{:S(2)}) collective-permute-start(bf16[8,5120]{1,0:T(8,128)(2,1)S(1)} %get-tuple-element.100.after), channel_id=1, source_target_pairs={{0,12},{1,13},{2,14},{3,15},{4,8},{5,9},{6,10},{7,11},{8,4},{9,5},... | collective-permute-start | bytes 245768 | tf_op jit(solution)/shard_map/ppermute | solution.py:48
  59.4 2.3 %attention.1 = bf16[128,2048]{1,0:T(8,128)(2,1)} custom-call(bf16[8,5120]{1,0:T(8,128)(2,1)S(1)} %get-tuple-element.100.after, bf16[288,128]{1,0:T(8,128)(2,1)S(1)} %collective-permute-done.3.earlier, bf16[288,128]{1,0:T(8,128)(2,1)S(1)} %collective-permute-done.10.earlier_other, bf16[128,2304]{1,0:T(8,128)(2,1)S(1)} %get-tuple-element.102.queries, ...), custom_call_target="tpu_custom_call" | custom-call | tf_op jit(solution)/shard_map/attention/pallas_call | solution.py:92
  61.7 2.1 %collective-permute-done.21.refs_2_ = bf16[8,5120]{1,0:T(8,128)(2,1)S(1)} collective-permute-done((bf16[8,5120]{1,0:T(8,128)(2,1)S(1)}, bf16[8,5120]{1,0:T(8,128)(2,1)S(1)}, u32[]{:S(2)}, u32[]{:S(2)}) %collective-permute-start.21) | collective-permute-done | bytes 81952 | tf_op jit(solution)/shard_map/ppermute | solution.py:48
  64.4 0.7 %sum.1 = bf16[8,5120]{1,0:T(8,128)(2,1)} custom-call(f32[8,5120]{1,0:T(8,128)S(1)} %get-tuple-element.105.first, bf16[8,5120]{1,0:T(8,128)(2,1)S(1)} %collective-permute-done.22.refs_0_, bf16[8,5120]{1,0:T(8,128)(2,1)S(1)} %collective-permute-done.23.refs_1_, bf16[8,5120]{1,0:T(8,128)(2,1)S(1)} %collective-permute-done.21.refs_2_), custom_call_target="tpu_custom_call" | custom-call | tf_op jit(solution)/shard_map/sum/pallas_call | solution.py:92
  (35 shorter events, 4.6 us)
Async XLA Ops:
  1.6 10.9 %collective-permute-start = (bf16[8,5248]{1,0:T(8,128)(2,1)S(1)}, bf16[8,5248]{1,0:T(8,128)(2,1)S(1)}, u32[]{:S(2)}, u32[]{:S(2)}) collective-permute-start(bf16[8,5248]{1,0:T(8,128)(2,1)S(1)} %get-tuple-element.59.refs_0_), channel_id=1, source_target_pairs={{0,12},{1,13},{2,14},{3,15},{4,8},{5,9},{6,10},{7,11},{8,4},{9,5},... | collective-permute-start | bytes 251912 | tf_op jit(solution)/shard_map/ppermute | solution.py:48
  6.7 7.0 %collective-permute-start.1 = (bf16[8,5248]{1,0:T(8,128)(2,1)S(1)}, bf16[8,5248]{1,0:T(8,128)(2,1)S(1)}, u32[]{:S(2)}, u32[]{:S(2)}) collective-permute-start(bf16[8,5248]{1,0:T(8,128)(2,1)S(1)} %get-tuple-element.59.refs_0_), channel_id=1, source_target_pairs={{0,8},{1,9},{2,10},{3,11},{4,12},{5,13},{6,14},{7,15},{8,0},{9,1},... | collective-permute-start | bytes 251912 | tf_op jit(solution)/shard_map/ppermute | solution.py:48
  6.8 7.0 %collective-permute-start.2 = (bf16[8,5248]{1,0:T(8,128)(2,1)S(1)}, bf16[8,5248]{1,0:T(8,128)(2,1)S(1)}, u32[]{:S(2)}, u32[]{:S(2)}) collective-permute-start(bf16[8,5248]{1,0:T(8,128)(2,1)S(1)} %get-tuple-element.59.refs_0_), channel_id=1, source_target_pairs={{0,4},{1,5},{2,6},{3,7},{4,0},{5,1},{6,2},{7,3},{8,12},{9,13},{10,... | collective-permute-start | bytes 251912 | tf_op jit(solution)/shard_map/ppermute | solution.py:48
  7.4 5.1 %collective-permute-start.3 = (bf16[288,128]{1,0:T(8,128)(2,1)S(1)}, bf16[288,128]{1,0:T(8,128)(2,1)S(1)}, u32[]{:S(2)}, u32[]{:S(2)}) collective-permute-start(bf16[288,128]{1,0:T(8,128)(2,1)S(1)} %get-tuple-element.56), channel_id=1, source_target_pairs={{0,16},{16,0},{1,17},{17,1},{2,18},{18,2},{3,19},{19,3},{4,20},{20... | collective-permute-start | bytes 221192 | tf_op jit(solution)/shard_map/ppermute | solution.py:44
  13.8 5.6 %collective-permute-start.8 = (bf16[32,2688]{1,0:T(8,128)(2,1)S(1)}, bf16[32,2688]{1,0:T(8,128)(2,1)S(1)}, u32[]{:S(2)}, u32[]{:S(2)}) collective-permute-start(bf16[32,2688]{1,0:T(8,128)(2,1)S(1)} %get-tuple-element.64.refs_0_), channel_id=1, source_target_pairs={{0,16},{1,17},{2,18},{3,19},{4,20},{5,21},{6,22},{7,23},{8,24},{9,... | collective-permute-start | bytes 516104 | tf_op jit(solution)/shard_map/ppermute | solution.py:60
  15.4 5.8 %collective-permute-start.4 = (bf16[32,2560]{1,0:T(8,128)(2,1)S(1)}, bf16[32,2560]{1,0:T(8,128)(2,1)S(1)}, u32[]{:S(2)}, u32[]{:S(2)}) collective-permute-start(bf16[32,2560]{1,0:T(8,128)(2,1)S(1)} %get-tuple-element.63.refs_0_), channel_id=1, source_target_pairs={{0,2},{1,3},{2,0},{3,1},{4,6},{5,7},{6,4},{7,5},{8,10},{9,11},{10,... | collective-permute-start | bytes 491528 | tf_op jit(solution)/shard_map/ppermute | solution.py:60
  19.4 8.6 %collective-permute-start.9 = (bf16[64,2688]{1,0:T(8,128)(2,1)S(1)}, bf16[64,2688]{1,0:T(8,128)(2,1)S(1)}, u32[]{:S(2)}, u32[]{:S(2)}) collective-permute-start(bf16[64,2688]{1,0:T(8,128)(2,1)S(1)} %stack_two.3.refs_0_), channel_id=1, source_target_pairs={{0,2},{1,3},{2,0},{3,1},{4,6},{5,7},{6,4},{7,5},{8,10},{9,11},{10,... | collective-permute-start | bytes 1032200 | tf_op jit(solution)/shard_map/ppermute | solution.py:60
  21.2 7.9 %collective-permute-start.5 = (bf16[64,2560]{1,0:T(8,128)(2,1)S(1)}, bf16[64,2560]{1,0:T(8,128)(2,1)S(1)}, u32[]{:S(2)}, u32[]{:S(2)}) collective-permute-start(bf16[64,2560]{1,0:T(8,128)(2,1)S(1)} %stack_two.2.refs_0_), channel_id=1, source_target_pairs={{0,16},{1,17},{2,18},{3,19},{4,20},{5,21},{6,22},{7,23},{8,24},{9,... | collective-permute-start | bytes 983048 | tf_op jit(solution)/shard_map/ppermute | solution.py:60
  22.7 5.1 %collective-permute-start.10 = (bf16[288,128]{1,0:T(8,128)(2,1)S(1)}, bf16[288,128]{1,0:T(8,128)(2,1)S(1)}, u32[]{:S(2)}, u32[]{:S(2)}) collective-permute-start(bf16[288,128]{1,0:T(8,128)(2,1)S(1)} %collective-permute-done.3.earlier), channel_id=1, source_target_pairs={{0,1},{1,0},{2,3},{3,2},{4,5},{5,4},{6,7},{7,6},{8,9},{9,8},{10,11... | collective-permute-start | bytes 221192 | tf_op jit(solution)/shard_map/ppermute | solution.py:44
  27.2 1.9 %collective-permute-start.11 = (bf16[64,2688]{1,0:T(8,128)(2,1)S(1)}, bf16[64,2688]{1,0:T(8,128)(2,1)S(1)}, u32[]{:S(2)}, u32[]{:S(2)}) collective-permute-start(bf16[64,2688]{1,0:T(8,128)(2,1)S(1)} %stack_two.3.refs_0_), channel_id=1, source_target_pairs={{0,1},{1,0},{2,3},{3,2},{4,5},{5,4},{6,7},{7,6},{8,9},{9,8},{10,11... | collective-permute-start | bytes 1032200 | tf_op jit(solution)/shard_map/ppermute | solution.py:44
  28.1 1.7 %collective-permute-start.12 = (bf16[64,2688]{1,0:T(8,128)(2,1)S(1)}, bf16[64,2688]{1,0:T(8,128)(2,1)S(1)}, u32[]{:S(2)}, u32[]{:S(2)}) collective-permute-start(bf16[64,2688]{1,0:T(8,128)(2,1)S(1)} %collective-permute-done.9.refs_1_), channel_id=1, source_target_pairs={{0,1},{1,0},{2,3},{3,2},{4,5},{5,4},{6,7},{7,6},{8,9},{9,8},{10,11... | collective-permute-start | bytes 1032200 | tf_op jit(solution)/shard_map/ppermute | solution.py:44
  28.1 3.9 %collective-permute-start.6 = (bf16[64,2560]{1,0:T(8,128)(2,1)S(1)}, bf16[64,2560]{1,0:T(8,128)(2,1)S(1)}, u32[]{:S(2)}, u32[]{:S(2)}) collective-permute-start(bf16[64,2560]{1,0:T(8,128)(2,1)S(1)} %stack_two.2.refs_0_), channel_id=1, source_target_pairs={{0,1},{1,0},{2,3},{3,2},{4,5},{5,4},{6,7},{7,6},{8,9},{9,8},{10,11... | collective-permute-start | bytes 983048 | tf_op jit(solution)/shard_map/ppermute | solution.py:44
  29.1 3.0 %collective-permute-start.7 = (bf16[64,2560]{1,0:T(8,128)(2,1)S(1)}, bf16[64,2560]{1,0:T(8,128)(2,1)S(1)}, u32[]{:S(2)}, u32[]{:S(2)}) collective-permute-start(bf16[64,2560]{1,0:T(8,128)(2,1)S(1)} %collective-permute-done.5.refs_1_), channel_id=1, source_target_pairs={{0,1},{1,0},{2,3},{3,2},{4,5},{5,4},{6,7},{7,6},{8,9},{9,8},{10,11... | collective-permute-start | bytes 983048 | tf_op jit(solution)/shard_map/ppermute | solution.py:44
  33.8 7.1 %collective-permute-start.13 = (bf16[128,512]{1,0:T(8,128)(2,1)S(1)}, bf16[128,512]{1,0:T(8,128)(2,1)S(1)}, u32[]{:S(2)}, u32[]{:S(2)}) collective-permute-start(bf16[128,512]{1,0:T(8,128)(2,1)S(1)} %get-tuple-element.77), channel_id=1, source_target_pairs={{0,16},{16,0},{1,17},{17,1},{2,18},{18,2},{3,19},{19,3},{4,20},{20... | collective-permute-start | bytes 393224 | tf_op jit(solution)/shard_map/ppermute | solution.py:44
  36.4 4.5 %collective-permute-start.14 = (bf16[128,256]{1,0:T(8,128)(2,1)S(1)}, bf16[128,256]{1,0:T(8,128)(2,1)S(1)}, u32[]{:S(2)}, u32[]{:S(2)}) collective-permute-start(bf16[128,256]{1,0:T(8,128)(2,1)S(1)} %get-tuple-element.79), channel_id=1, source_target_pairs={{0,16},{16,0},{1,17},{17,1},{2,18},{18,2},{3,19},{19,3},{4,20},{20... | collective-permute-start | bytes 196616 | tf_op jit(solution)/shard_map/ppermute | solution.py:44
  41.7 1.7 %collective-permute-start.15 = (bf16[128,1280]{1,0:T(8,128)(2,1)S(1)}, bf16[128,1280]{1,0:T(8,128)(2,1)S(1)}, u32[]{:S(2)}, u32[]{:S(2)}) collective-permute-start(bf16[128,1280]{1,0:T(8,128)(2,1)S(1)} %get-tuple-element.88), channel_id=1, source_target_pairs={{0,1},{1,0},{2,3},{3,2},{4,5},{5,4},{6,7},{7,6},{8,9},{9,8},{10,11... | collective-permute-start | bytes 983048 | tf_op jit(solution)/shard_map/ppermute | solution.py:44
  42.6 2.3 %collective-permute-start.18 = (bf16[128,1280]{1,0:T(8,128)(2,1)S(1)}, bf16[128,1280]{1,0:T(8,128)(2,1)S(1)}, u32[]{:S(2)}, u32[]{:S(2)}) collective-permute-start(bf16[128,1280]{1,0:T(8,128)(2,1)S(1)} %get-tuple-element.94), channel_id=1, source_target_pairs={{0,1},{1,0},{2,3},{3,2},{4,5},{5,4},{6,7},{7,6},{8,9},{9,8},{10,11... | collective-permute-start | bytes 983048 | tf_op jit(solution)/shard_map/ppermute | solution.py:44
  43.5 6.3 %collective-permute-start.16 = (bf16[64,1280]{1,0:T(8,128)(2,1)S(1)}, bf16[64,1280]{1,0:T(8,128)(2,1)S(1)}, u32[]{:S(2)}, u32[]{:S(2)}) collective-permute-start(bf16[64,1280]{1,0:T(8,128)(2,1)S(1)} %get-tuple-element.90), channel_id=1, source_target_pairs={{0,16},{1,17},{2,18},{3,19},{4,20},{5,21},{6,22},{7,23},{8,24},{9,... | collective-permute-start | bytes 491528 | tf_op jit(solution)/shard_map/ppermute | solution.py:60
  45.0 6.3 %collective-permute-start.19 = (bf16[64,1280]{1,0:T(8,128)(2,1)S(1)}, bf16[64,1280]{1,0:T(8,128)(2,1)S(1)}, u32[]{:S(2)}, u32[]{:S(2)}) collective-permute-start(bf16[64,1280]{1,0:T(8,128)(2,1)S(1)} %get-tuple-element.96), channel_id=1, source_target_pairs={{0,2},{1,3},{2,0},{3,1},{4,6},{5,7},{6,4},{7,5},{8,10},{9,11},{10,... | collective-permute-start | bytes 491528 | tf_op jit(solution)/shard_map/ppermute | solution.py:60
  49.8 6.0 %collective-permute-start.17 = (bf16[32,2560]{1,0:T(8,128)(2,1)S(1)}, bf16[32,2560]{1,0:T(8,128)(2,1)S(1)}, u32[]{:S(2)}, u32[]{:S(2)}) collective-permute-start(bf16[32,2560]{1,0:T(8,128)(2,1)S(1)} %get-tuple-element.92), channel_id=1, source_target_pairs={{0,2},{1,3},{2,0},{3,1},{4,6},{5,7},{6,4},{7,5},{8,10},{9,11},{10,... | collective-permute-start | bytes 491528 | tf_op jit(solution)/shard_map/ppermute | solution.py:60
  51.3 4.5 %collective-permute-start.20 = (bf16[32,1280]{1,0:T(8,128)(2,1)S(1)}, bf16[32,1280]{1,0:T(8,128)(2,1)S(1)}, u32[]{:S(2)}, u32[]{:S(2)}) collective-permute-start(bf16[32,1280]{1,0:T(8,128)(2,1)S(1)} %get-tuple-element.98), channel_id=1, source_target_pairs={{0,16},{1,17},{2,18},{3,19},{4,20},{5,21},{6,22},{7,23},{8,24},{9,... | collective-permute-start | bytes 245768 | tf_op jit(solution)/shard_map/ppermute | solution.py:60
  55.9 7.9 %collective-permute-start.21 = (bf16[8,5120]{1,0:T(8,128)(2,1)S(1)}, bf16[8,5120]{1,0:T(8,128)(2,1)S(1)}, u32[]{:S(2)}, u32[]{:S(2)}) collective-permute-start(bf16[8,5120]{1,0:T(8,128)(2,1)S(1)} %get-tuple-element.99), channel_id=1, source_target_pairs={{0,8},{1,9},{2,10},{3,11},{4,12},{5,13},{6,14},{7,15},{8,0},{9,1},... | collective-permute-start | bytes 245768 | tf_op jit(solution)/shard_map/ppermute | solution.py:48
  56.8 7.0 %collective-permute-start.22 = (bf16[8,5120]{1,0:T(8,128)(2,1)S(1)}, bf16[8,5120]{1,0:T(8,128)(2,1)S(1)}, u32[]{:S(2)}, u32[]{:S(2)}) collective-permute-start(bf16[8,5120]{1,0:T(8,128)(2,1)S(1)} %get-tuple-element.100.after), channel_id=1, source_target_pairs={{0,12},{1,13},{2,14},{3,15},{4,8},{5,9},{6,10},{7,11},{8,4},{9,5},... | collective-permute-start | bytes 245768 | tf_op jit(solution)/shard_map/ppermute | solution.py:48
  59.1 5.3 %collective-permute-start.23 = (bf16[8,5120]{1,0:T(8,128)(2,1)S(1)}, bf16[8,5120]{1,0:T(8,128)(2,1)S(1)}, u32[]{:S(2)}, u32[]{:S(2)}) collective-permute-start(bf16[8,5120]{1,0:T(8,128)(2,1)S(1)} %get-tuple-element.106), channel_id=1, source_target_pairs={{0,4},{1,5},{2,6},{3,7},{4,0},{5,1},{6,2},{7,3},{8,12},{9,13},{10,... | collective-permute-start | bytes 245768 | tf_op jit(solution)/shard_map/ppermute | solution.py:48

commit v8 on v7

--- a/solution.py
+++ b/solution.py
@@ -175,6 +175,13 @@
             source = source.at[:, pl.ds(own_at, width)]
         pairs.append((source, target))
     for copy in start_copies(pairs, sems, PIECES):
+        copy.wait()
+
+
+def fetch_other_kernel(after, source, target, sems):
+    width = target.shape[1]
+    at = pl.multiple_of((1 - lax.axis_index("ctx")) * width, 128)
+    for copy in start_copies([(source.at[:, pl.ds(at, width)], target)], sems, PIECES):
         copy.wait()
 
 
@@ -304,32 +311,37 @@
     finish_units(tokens, gate_w, up_w, gate_in, up_in, pick, act_out, packed_out, start)
 
 
-def own_kernel(act_a, act_b, down_own, down_w, out, down_other, sems):
-    units = down_own.shape[1]
+def own_kernel(act_a, act_b, down_own, out):
     few = act_a.shape[1]
-    other_at = pl.multiple_of((1 - lax.axis_index("ctx")) * units, 128)
-    copies = start_copies([(down_w.at[:, pl.ds(other_at, units)], down_other)], sems, PIECES)
-    tall = out.shape[1] // 5 if out.shape[1] % 640 == 0 else out.shape[1]
+    tall = 512 if out.shape[1] % 512 == 0 else out.shape[1]
     for n in range(0, out.shape[1], tall):
         span = slice(n, n + tall)
         out[:, span] = times_rows_in(act_a[...], down_own[span, :few]) + times_rows_in(
             act_b[...], down_own[span, few:]
         )
-    for copy in copies:
-        copy.wait()
-
-
-def other_kernel(packed_a, packed_b, pick, coef, down_w, own, keep, give, act, *, start):
-    few = packed_a.shape[1]
-    for packed, span in ((packed_a, slice(0, few)), (packed_b, slice(few, act.shape[1]))):
-        act[:, span] = jnp.dot(
-            pick[...], packed[...], preferred_element_type=jnp.float32
-        ).astype(jnp.bfloat16)
+
+
+def more_kernel(packed, pick, down_w, own, out, act):
+    few = act.shape[1]
+    act[...] = jnp.dot(pick[...], packed[...], preferred_element_type=jnp.float32).astype(
+        jnp.bfloat16
+    )
+    tall = 512 if out.shape[1] % 512 == 0 else out.shape[1]
+    for n in range(0, out.shape[1], tall):
+        span = slice(n, n + tall)
+        out[:, span] = own[:, span] + times_rows_in(act[...], down_w[span, :few])
+
+
+def other_kernel(packed, pick, coef, down_w, own, keep, give, act, *, start):
+    act[...] = jnp.dot(pick[...], packed[...], preferred_element_type=jnp.float32).astype(
+        jnp.bfloat16
+    )
+    few = down_w.shape[1] - act.shape[1]
     half, part = keep.shape
     tall = part // 5 if part % 5 == 0 else part
     for n in range(0, part, tall):
         span = slice(start + n, start + n + tall)
-        projected = own[:, span] + times_rows_in(act[...], down_w[span, :])
+        projected = own[:, span] + times_rows_in(act[...], down_w[span, few:])
         projected = projected * coef[:, :1]
         keep[:, n : n + tall] = projected[:half]
         give[:, n : n + tall] = projected[half:].astype(jnp.bfloat16)
@@ -440,9 +452,18 @@
         [],
         "stack_line",
     )
+    (down_other,) = local_kernel(
+        fetch_other_kernel,
+        [(nears[1], "vmem"), (w_down[0], "hbm")],
+        [((columns, units), bf16, "vmem")],
+        [pltpu.SemaphoreType.DMA((PIECES,))],
+        "fetch",
+    )
     pieces = []
     for near, first, then in zip(nears, (over_x, over_y), (over_y, over_x)):
         got = paired(near, first)
+        if first is over_x:
+            got, down_other = lax.optimization_barrier((got, down_other))
         (two,) = local_kernel(
             lambda *refs, cut=near.shape[1]: stack_kernel(*refs, cuts=((0, cut),)),
             [(near, "vmem"), (got, "vmem")],
@@ -499,12 +520,19 @@
         "gate_up_third",
     )
     other_b = swapped(packed_b, "ctx", 1)
-    own, down_other = local_kernel(
+    (own,) = local_kernel(
         own_kernel,
-        [(act_a, "vmem"), (act_b, "vmem"), (down_mine, "vmem"), (w_down[0], "hbm")],
-        [((count, columns), f32, "vmem"), ((columns, units), bf16, "vmem")],
-        [pltpu.SemaphoreType.DMA((PIECES,))],
+        [(act_a, "vmem"), (act_b, "vmem"), (down_mine, "vmem")],
+        [((count, columns), f32, "vmem")],
+        [],
         "down_own",
+    )
+    (own,) = local_kernel(
+        more_kernel,
+        [(other_a, "vmem"), (pick_far, "vmem"), (down_other, "vmem"), (own, "vmem")],
+        [((count, columns), f32, "vmem")],
+        [pltpu.VMEM((count, few), bf16)],
+        "down_more",
     )
     part = columns // 2
     crossing = []
@@ -512,11 +540,11 @@
         keep, give = local_kernel(
             lambda *refs, start=start: other_kernel(*refs, start=start),
             [
-                (other_a, "vmem"), (other_b, "vmem"), (pick_far, "vmem"), (coef, "vmem"),
+                (other_b, "vmem"), (pick_far, "vmem"), (coef, "vmem"),
                 (down_other, "vmem"), (own, "vmem"),
             ],
             [((count // 2, part), f32, "vmem"), ((count // 2, part), bf16, "vmem")],
-            [pltpu.VMEM((count, units), bf16)],
+            [pltpu.VMEM((count, units - few), bf16)],
             "down_other",
         )
         send, stay = local_kernel(

time: 65.3 us -> 65 us (level)
  waiting for transfers between devices: 15 us -> 14 us
    ppermute x8, waiting for transfers between devices: 9.42 us -> 6.86 us  [paired(): return lax.ppermute(block, ('ctx', 'exp'), route)]
    ppermute x10, waiting for transfers between devices: 1.69 us -> 3.1 us  [swapped(): lax.ppermute(block, axis, [(i, i ^ bit) for i in range(lax.axis_size(axis...]
    pallas_call x19 -> x21, Pallas kernels: 22 us -> 22.5 us  [local_kernel(): pl.pallas_call(body, in_specs=[pl.BlockSpec(memory_space=kinds[kind]) for...]
  transfers between devices with their start and end apart: 24 -> 24, of which waited for: 11 -> 11; matrix products, arithmetic and copies ran while one was open for 0% -> 0% of each run, Pallas kernels for 27% -> 29%
where the time goes in v8:
time: 65 us; the launch traced here: 64.9 us
  starting transfers between devices  27.6 us (42%)
  Pallas kernels  22.5 us (35%)
  waiting for transfers between devices  14 us (22%)
  between operations  0.82 us (1%)
    pallas_call x21, Pallas kernels, local_kernel(): pl.pallas_call(body, in_specs=[pl.BlockSpec(memory_space=kinds[kind]) for...  22.5 us
    ppermute x8, starting transfers between devices, paired(): return lax.ppermute(block, ('ctx', 'exp'), route)  12.8 us
    ppermute x6, starting transfers between devices, along_line(): lax.ppermute(block, 'exp', [(i, i ^ 4 * steps) for i in range(lax.axis_si...  9.31 us
    ppermute x8, waiting for transfers between devices, paired(): return lax.ppermute(block, ('ctx', 'exp'), route)  6.86 us
    ppermute x10, starting transfers between devices, swapped(): lax.ppermute(block, axis, [(i, i ^ bit) for i in range(lax.axis_size(axis...  5.51 us
    ppermute x6, waiting for transfers between devices, along_line(): lax.ppermute(block, 'exp', [(i, i ^ 4 * steps) for i in range(lax.axis_si...  4.04 us
    ppermute x10, waiting for transfers between devices, swapped(): lax.ppermute(block, axis, [(i, i ^ bit) for i in range(lax.axis_size(axis...  3.1 us
  transfers between devices with their start and end apart: 24, of which 11 were waited for; matrix products, arithmetic and copies ran while one was open for 0% of the time, Pallas kernels for 29%

profile of v8, /device:TPU:0, one launch (start us, length us, event | category | flops | bytes accessed | tf_op | source)
XLA Modules:
  0.0 64.9 jit_solution(12888458018197013762)
XLA Ops:
  0.6 1.0 %rows.1 = (bf16[8,5248]{1,0:T(8,128)(2,1)S(1)}, bf16[288,128]{1,0:T(8,128)(2,1)S(1)}) custom-call(bf16[8,5120]{1,0:T(8,128)(2,1)} %bitcast.16, s32[6,1,8]{2,1,0:T(1,128)} %bitcast.18, f32[6,1,8]{2,1,0:T(1,128)} %bitcast.19, bf16[576,128]{1,0:T(8,128)(2,1)} %bitcast.14), custom_call_target="tpu_custom_call" | custom-call | tf_op jit(solution)/shard_map/rows/pallas_call | solution.py:92
  1.6 5.1 %collective-permute-start = (bf16[8,5248]{1,0:T(8,128)(2,1)S(1)}, bf16[8,5248]{1,0:T(8,128)(2,1)S(1)}, u32[]{:S(2)}, u32[]{:S(2)}) collective-permute-start(bf16[8,5248]{1,0:T(8,128)(2,1)S(1)} %get-tuple-element.59.refs_0_), channel_id=1, source_target_pairs={{0,12},{1,13},{2,14},{3,15},{4,8},{5,9},{6,10},{7,11},{8,4},{9,5},... | collective-permute-start | bytes 251912 | tf_op jit(solution)/shard_map/ppermute | solution.py:48
  6.8 0.6 collective-permute-start.2
  7.4 1.6 %collective-permute-start.3 = (bf16[288,128]{1,0:T(8,128)(2,1)S(1)}, bf16[288,128]{1,0:T(8,128)(2,1)S(1)}, u32[]{:S(2)}, u32[]{:S(2)}) collective-permute-start(bf16[288,128]{1,0:T(8,128)(2,1)S(1)} %get-tuple-element.56), channel_id=1, source_target_pairs={{0,16},{16,0},{1,17},{17,1},{2,18},{18,2},{3,19},{19,3},{4,20},{20... | collective-permute-start | bytes 221192 | tf_op jit(solution)/shard_map/ppermute | solution.py:44
  9.0 3.5 %fetch.3 = (bf16[768,2560]{1,0:T(8,128)(2,1)S(1)}, bf16[768,2560]{1,0:T(8,128)(2,1)S(1)}, bf16[128,2304]{1,0:T(8,128)(2,1)S(1)}, bf16[576,128]{1,0:T(8,128)(2,1)S(1)}) custom-call(bf16[8,5248]{1,0:T(8,128)(2,1)S(1)} %get-tuple-element.59.refs_0_, bf16[768,5120]{1,0:T(8,128)(2,1)} %bitcast.8, bf16[768,5120]{1,0:T(8,128)(2,1)} %bitcast.10, ...), custom_call_target="tpu_custom_call" | custom-call | tf_op jit(solution)/shard_map/fetch/pallas_call | solution.py:92
  12.6 1.2 %collective-permute-done.1.refs_2_ = bf16[8,5248]{1,0:T(8,128)(2,1)S(1)} collective-permute-done((bf16[8,5248]{1,0:T(8,128)(2,1)S(1)}, bf16[8,5248]{1,0:T(8,128)(2,1)S(1)}, u32[]{:S(2)}, u32[]{:S(2)}) %collective-permute-start.1) | collective-permute-done | bytes 84000 | tf_op jit(solution)/shard_map/ppermute | solution.py:48
  13.8 1.6 %collective-permute-start.8 = (bf16[32,2688]{1,0:T(8,128)(2,1)S(1)}, bf16[32,2688]{1,0:T(8,128)(2,1)S(1)}, u32[]{:S(2)}, u32[]{:S(2)}) collective-permute-start(bf16[32,2688]{1,0:T(8,128)(2,1)S(1)} %get-tuple-element.64.refs_0_), channel_id=1, source_target_pairs={{0,16},{1,17},{2,18},{3,19},{4,20},{5,21},{6,22},{7,23},{8,24},{9,... | collective-permute-start | bytes 516104 | tf_op jit(solution)/shard_map/ppermute | solution.py:60
  15.4 1.5 %collective-permute-start.4 = (bf16[32,2560]{1,0:T(8,128)(2,1)S(1)}, bf16[32,2560]{1,0:T(8,128)(2,1)S(1)}, u32[]{:S(2)}, u32[]{:S(2)}) collective-permute-start(bf16[32,2560]{1,0:T(8,128)(2,1)S(1)} %get-tuple-element.63.refs_0_.after), channel_id=1, source_target_pairs={{0,2},{1,3},{2,0},{3,1},{4,6},{5,7},{6,4},{7,5},{8,10},{9,11},{10,... | collective-permute-start | bytes 491528 | tf_op jit(solution)/shard_map/ppermute | solution.py:60
  16.9 2.1 %fetch.4.down_w.refs_3_ = bf16[2560,768]{1,0:T(8,128)(2,1)S(1)} custom-call(bf16[32,2560]{1,0:T(8,128)(2,1)S(1)} %get-tuple-element.63.refs_0_.after, bf16[2560,1536]{1,0:T(8,128)(2,1)} %bitcast.12), custom_call_target="tpu_custom_call" | custom-call | tf_op jit(solution)/shard_map/fetch/pallas_call | solution.py:92
  19.4 1.7 %collective-permute-start.9 = (bf16[64,2688]{1,0:T(8,128)(2,1)S(1)}, bf16[64,2688]{1,0:T(8,128)(2,1)S(1)}, u32[]{:S(2)}, u32[]{:S(2)}) collective-permute-start(bf16[64,2688]{1,0:T(8,128)(2,1)S(1)} %stack_two.3.refs_0_), channel_id=1, source_target_pairs={{0,2},{1,3},{2,0},{3,1},{4,6},{5,7},{6,4},{7,5},{8,10},{9,11},{10,... | collective-permute-start | bytes 1032200 | tf_op jit(solution)/shard_map/ppermute | solution.py:60
  21.2 1.6 %collective-permute-start.5 = (bf16[64,2560]{1,0:T(8,128)(2,1)S(1)}, bf16[64,2560]{1,0:T(8,128)(2,1)S(1)}, u32[]{:S(2)}, u32[]{:S(2)}) collective-permute-start(bf16[64,2560]{1,0:T(8,128)(2,1)S(1)} %stack_two.2.refs_0_), channel_id=1, source_target_pairs={{0,16},{1,17},{2,18},{3,19},{4,20},{5,21},{6,22},{7,23},{8,24},{9,... | collective-permute-start | bytes 983048 | tf_op jit(solution)/shard_map/ppermute | solution.py:60
  22.8 4.5 %fetch.5 = (bf16[768,2560]{1,0:T(8,128)(2,1)S(1)}, bf16[768,2560]{1,0:T(8,128)(2,1)S(1)}, bf16[2560,768]{1,0:T(8,128)(2,1)S(1)}) custom-call(bf16[64,2560]{1,0:T(8,128)(2,1)S(1)} %stack_two.2.refs_0_, bf16[768,5120]{1,0:T(8,128)(2,1)} %bitcast.9, bf16[768,5120]{1,0:T(8,128)(2,1)} %bitcast.11, bf16[2560,1536]{1,0:T(8,128)(2,1)} %bitcast.13), custom_call_target="tpu_custom_call" | custom-call | tf_op jit(solution)/shard_map/fetch/pallas_call | solution.py:92
  29.1 0.6 collective-permute-done.12.refs_3_
  29.7 2.3 %gate_up_first.1 = (f32[256,768]{1,0:T(8,128)S(1)}, f32[256,768]{1,0:T(8,128)S(1)}, bf16[256,128]{1,0:T(8,128)(2,1)S(1)}, bf16[256,128]{1,0:T(8,128)(2,1)S(1)}, f32[256,128]{1,0:T(8,128)S(1)}) custom-call(bf16[64,2688]{1,0:T(8,128)(2,1)S(1)} %stack_two.3.refs_0_, bf16[64,2688]{1,0:T(8,128)(2,1)S(1)} %collective-permute-done.9.refs_1_, ...), custom_call_target="tpu_custom_call" | custom-call | tf_op jit(solution)/shard_map/gate_up_first/pallas_call | solution.py:92
  32.0 1.7 %gate_up_second.1 = (bf16[256,512]{1,0:T(8,128)(2,1)S(1)}, bf16[128,512]{1,0:T(8,128)(2,1)S(1)}, bf16[256,2560]{1,0:T(8,128)(2,1)S(1)}) custom-call(bf16[64,2560]{1,0:T(8,128)(2,1)S(1)} %stack_two.2.refs_0_, bf16[64,2560]{1,0:T(8,128)(2,1)S(1)} %collective-permute-done.5.refs_1_, bf16[64,2560]{1,0:T(8,128)(2,1)S(1)} %collective-permute-done.6.refs_2_, ...), custom_call_target="tpu_custom_call" | custom-call | tf_op jit(solution)/shard_map/gate_up_second/pallas_call | solution.py:92
  33.8 1.6 %collective-permute-start.14 = (bf16[128,512]{1,0:T(8,128)(2,1)S(1)}, bf16[128,512]{1,0:T(8,128)(2,1)S(1)}, u32[]{:S(2)}, u32[]{:S(2)}) collective-permute-start(bf16[128,512]{1,0:T(8,128)(2,1)S(1)} %get-tuple-element.83), channel_id=1, source_target_pairs={{0,16},{16,0},{1,17},{17,1},{2,18},{18,2},{3,19},{19,3},{4,20},{20... | collective-permute-start | bytes 393224 | tf_op jit(solution)/shard_map/ppermute | solution.py:44
  35.3 1.0 %gate_up_third.1 = (bf16[256,256]{1,0:T(8,128)(2,1)S(1)}, bf16[128,256]{1,0:T(8,128)(2,1)S(1)}) custom-call(bf16[256,2560]{1,0:T(8,128)(2,1)S(1)} %get-tuple-element.78.refs_0_, bf16[768,2560]{1,0:T(8,128)(2,1)S(1)} %get-tuple-element.70.refs_4_.refs_1_, bf16[768,2560]{1,0:T(8,128)(2,1)S(1)} %get-tuple-element.71.refs_5_.refs_2_, ...), custom_call_target="tpu_custom_call" | custom-call | tf_op jit(solution)/shard_map/gate_up_third/pallas_call | solution.py:92
  37.0 1.2 %down_own.1.own = f32[256,2560]{1,0:T(8,128)S(1)} custom-call(bf16[256,512]{1,0:T(8,128)(2,1)S(1)} %get-tuple-element.84.act_a, bf16[256,256]{1,0:T(8,128)(2,1)S(1)} %get-tuple-element.85.act_b, bf16[2560,768]{1,0:T(8,128)(2,1)S(1)} %get-tuple-element.86.down_own), custom_call_target="tpu_custom_call" | custom-call | tf_op jit(solution)/shard_map/down_own/pallas_call | solution.py:92
  38.2 1.8 %collective-permute-done.14.packed = bf16[128,512]{1,0:T(8,128)(2,1)S(1)} collective-permute-done((bf16[128,512]{1,0:T(8,128)(2,1)S(1)}, bf16[128,512]{1,0:T(8,128)(2,1)S(1)}, u32[]{:S(2)}, u32[]{:S(2)}) %collective-permute-start.14) | collective-permute-done | bytes 131104 | tf_op jit(solution)/shard_map/ppermute | solution.py:44
  40.0 1.0 %down_more.1.refs_4_ = f32[256,2560]{1,0:T(8,128)S(1)} custom-call(bf16[128,512]{1,0:T(8,128)(2,1)S(1)} %collective-permute-done.14.packed, bf16[256,128]{1,0:T(8,128)(2,1)S(1)} %get-tuple-element.80.pick.refs_1_, bf16[2560,768]{1,0:T(8,128)(2,1)S(1)} %fetch.4.down_w.refs_3_, f32[256,2560]{1,0:T(8,128)S(1)} %down_own.1.own), custom_call_target="tpu_custom_call" | custom-call | tf_op jit(solution)/shard_map/down_more/pallas_call | solution.py:92
  43.2 1.6 %collective-permute-start.16 = (bf16[64,1280]{1,0:T(8,128)(2,1)S(1)}, bf16[64,1280]{1,0:T(8,128)(2,1)S(1)}, u32[]{:S(2)}, u32[]{:S(2)}) collective-permute-start(bf16[64,1280]{1,0:T(8,128)(2,1)S(1)} %get-tuple-element.90), channel_id=1, source_target_pairs={{0,16},{1,17},{2,18},{3,19},{4,20},{5,21},{6,22},{7,23},{8,24},{9,... | collective-permute-start | bytes 491528 | tf_op jit(solution)/shard_map/ppermute | solution.py:60
  44.9 1.6 %collective-permute-start.19 = (bf16[64,1280]{1,0:T(8,128)(2,1)S(1)}, bf16[64,1280]{1,0:T(8,128)(2,1)S(1)}, u32[]{:S(2)}, u32[]{:S(2)}) collective-permute-start(bf16[64,1280]{1,0:T(8,128)(2,1)S(1)} %get-tuple-element.96), channel_id=1, source_target_pairs={{0,2},{1,3},{2,0},{3,1},{4,6},{5,7},{6,4},{7,5},{8,10},{9,11},{10,... | collective-permute-start | bytes 491528 | tf_op jit(solution)/shard_map/ppermute | solution.py:60
  46.5 3.0 %collective-permute-done.16.refs_1_ = bf16[64,1280]{1,0:T(8,128)(2,1)S(1)} collective-permute-done((bf16[64,1280]{1,0:T(8,128)(2,1)S(1)}, bf16[64,1280]{1,0:T(8,128)(2,1)S(1)}, u32[]{:S(2)}, u32[]{:S(2)}) %collective-permute-start.16) | collective-permute-done | bytes 163872 | tf_op jit(solution)/shard_map/ppermute | solution.py:60
  49.5 1.4 %collective-permute-start.17 = (bf16[32,2560]{1,0:T(8,128)(2,1)S(1)}, bf16[32,2560]{1,0:T(8,128)(2,1)S(1)}, u32[]{:S(2)}, u32[]{:S(2)}) collective-permute-start(bf16[32,2560]{1,0:T(8,128)(2,1)S(1)} %get-tuple-element.92), channel_id=1, source_target_pairs={{0,2},{1,3},{2,0},{3,1},{4,6},{5,7},{6,4},{7,5},{8,10},{9,11},{10,... | collective-permute-start | bytes 491528 | tf_op jit(solution)/shard_map/ppermute | solution.py:60
  51.0 1.8 %collective-permute-start.20 = (bf16[32,1280]{1,0:T(8,128)(2,1)S(1)}, bf16[32,1280]{1,0:T(8,128)(2,1)S(1)}, u32[]{:S(2)}, u32[]{:S(2)}) collective-permute-start(bf16[32,1280]{1,0:T(8,128)(2,1)S(1)} %get-tuple-element.98), channel_id=1, source_target_pairs={{0,16},{1,17},{2,18},{3,19},{4,20},{5,21},{6,22},{7,23},{8,24},{9,... | collective-permute-start | bytes 245768 | tf_op jit(solution)/shard_map/ppermute | solution.py:60
  52.8 2.7 %collective-permute-done.20.got_x = bf16[32,1280]{1,0:T(8,128)(2,1)S(1)} collective-permute-done((bf16[32,1280]{1,0:T(8,128)(2,1)S(1)}, bf16[32,1280]{1,0:T(8,128)(2,1)S(1)}, u32[]{:S(2)}, u32[]{:S(2)}) %collective-permute-start.20) | collective-permute-done | bytes 81952 | tf_op jit(solution)/shard_map/ppermute | solution.py:60
  55.5 1.2 %collective-permute-start.21 = (bf16[8,5120]{1,0:T(8,128)(2,1)S(1)}, bf16[8,5120]{1,0:T(8,128)(2,1)S(1)}, u32[]{:S(2)}, u32[]{:S(2)}) collective-permute-start(bf16[8,5120]{1,0:T(8,128)(2,1)S(1)} %get-tuple-element.99), channel_id=1, source_target_pairs={{0,8},{1,9},{2,10},{3,11},{4,12},{5,13},{6,14},{7,15},{8,0},{9,1},... | collective-permute-start | bytes 245768 | tf_op jit(solution)/shard_map/ppermute | solution.py:48
  56.7 2.3 %collective-permute-start.22 = (bf16[8,5120]{1,0:T(8,128)(2,1)S(1)}, bf16[8,5120]{1,0:T(8,128)(2,1)S(1)}, u32[]{:S(2)}, u32[]{:S(2)}) collective-permute-start(bf16[8,5120]{1,0:T(8,128)(2,1)S(1)} %get-tuple-element.100.after), channel_id=1, source_target_pairs={{0,12},{1,13},{2,14},{3,15},{4,8},{5,9},{6,10},{7,11},{8,4},{9,5},... | collective-permute-start | bytes 245768 | tf_op jit(solution)/shard_map/ppermute | solution.py:48
  59.1 2.3 %attention.1 = bf16[128,2048]{1,0:T(8,128)(2,1)} custom-call(bf16[8,5120]{1,0:T(8,128)(2,1)S(1)} %get-tuple-element.100.after, bf16[288,128]{1,0:T(8,128)(2,1)S(1)} %collective-permute-done.3.earlier, bf16[288,128]{1,0:T(8,128)(2,1)S(1)} %collective-permute-done.10.earlier_other, bf16[128,2304]{1,0:T(8,128)(2,1)S(1)} %get-tuple-element.102.queries, ...), custom_call_target="tpu_custom_call" | custom-call | tf_op jit(solution)/shard_map/attention/pallas_call | solution.py:92
  61.4 2.1 %collective-permute-done.21.refs_2_ = bf16[8,5120]{1,0:T(8,128)(2,1)S(1)} collective-permute-done((bf16[8,5120]{1,0:T(8,128)(2,1)S(1)}, bf16[8,5120]{1,0:T(8,128)(2,1)S(1)}, u32[]{:S(2)}, u32[]{:S(2)}) %collective-permute-start.21) | collective-permute-done | bytes 81952 | tf_op jit(solution)/shard_map/ppermute | solution.py:48
  63.5 0.7 %collective-permute-done.23.refs_1_ = bf16[8,5120]{1,0:T(8,128)(2,1)S(1)} collective-permute-done((bf16[8,5120]{1,0:T(8,128)(2,1)S(1)}, bf16[8,5120]{1,0:T(8,128)(2,1)S(1)}, u32[]{:S(2)}, u32[]{:S(2)}) %collective-permute-start.23) | collective-permute-done | bytes 81952 | tf_op jit(solution)/shard_map/ppermute | solution.py:48
  64.2 0.7 %sum.1 = bf16[8,5120]{1,0:T(8,128)(2,1)} custom-call(f32[8,5120]{1,0:T(8,128)S(1)} %get-tuple-element.105.first, bf16[8,5120]{1,0:T(8,128)(2,1)S(1)} %collective-permute-done.22.refs_0_, bf16[8,5120]{1,0:T(8,128)(2,1)S(1)} %collective-permute-done.23.refs_1_, bf16[8,5120]{1,0:T(8,128)(2,1)S(1)} %collective-permute-done.21.refs_2_), custom_call_target="tpu_custom_call" | custom-call | tf_op jit(solution)/shard_map/sum/pallas_call | solution.py:92
  (37 shorter events, 5.4 us)
Async XLA Ops:
  1.6 10.9 %collective-permute-start = (bf16[8,5248]{1,0:T(8,128)(2,1)S(1)}, bf16[8,5248]{1,0:T(8,128)(2,1)S(1)}, u32[]{:S(2)}, u32[]{:S(2)}) collective-permute-start(bf16[8,5248]{1,0:T(8,128)(2,1)S(1)} %get-tuple-element.59.refs_0_), channel_id=1, source_target_pairs={{0,12},{1,13},{2,14},{3,15},{4,8},{5,9},{6,10},{7,11},{8,4},{9,5},... | collective-permute-start | bytes 251912 | tf_op jit(solution)/shard_map/ppermute | solution.py:48
  6.7 7.0 %collective-permute-start.1 = (bf16[8,5248]{1,0:T(8,128)(2,1)S(1)}, bf16[8,5248]{1,0:T(8,128)(2,1)S(1)}, u32[]{:S(2)}, u32[]{:S(2)}) collective-permute-start(bf16[8,5248]{1,0:T(8,128)(2,1)S(1)} %get-tuple-element.59.refs_0_), channel_id=1, source_target_pairs={{0,8},{1,9},{2,10},{3,11},{4,12},{5,13},{6,14},{7,15},{8,0},{9,1},... | collective-permute-start | bytes 251912 | tf_op jit(solution)/shard_map/ppermute | solution.py:48
  6.8 7.0 %collective-permute-start.2 = (bf16[8,5248]{1,0:T(8,128)(2,1)S(1)}, bf16[8,5248]{1,0:T(8,128)(2,1)S(1)}, u32[]{:S(2)}, u32[]{:S(2)}) collective-permute-start(bf16[8,5248]{1,0:T(8,128)(2,1)S(1)} %get-tuple-element.59.refs_0_), channel_id=1, source_target_pairs={{0,4},{1,5},{2,6},{3,7},{4,0},{5,1},{6,2},{7,3},{8,12},{9,13},{10,... | collective-permute-start | bytes 251912 | tf_op jit(solution)/shard_map/ppermute | solution.py:48
  7.4 5.1 %collective-permute-start.3 = (bf16[288,128]{1,0:T(8,128)(2,1)S(1)}, bf16[288,128]{1,0:T(8,128)(2,1)S(1)}, u32[]{:S(2)}, u32[]{:S(2)}) collective-permute-start(bf16[288,128]{1,0:T(8,128)(2,1)S(1)} %get-tuple-element.56), channel_id=1, source_target_pairs={{0,16},{16,0},{1,17},{17,1},{2,18},{18,2},{3,19},{19,3},{4,20},{20... | collective-permute-start | bytes 221192 | tf_op jit(solution)/shard_map/ppermute | solution.py:44
  13.8 5.6 %collective-permute-start.8 = (bf16[32,2688]{1,0:T(8,128)(2,1)S(1)}, bf16[32,2688]{1,0:T(8,128)(2,1)S(1)}, u32[]{:S(2)}, u32[]{:S(2)}) collective-permute-start(bf16[32,2688]{1,0:T(8,128)(2,1)S(1)} %get-tuple-element.64.refs_0_), channel_id=1, source_target_pairs={{0,16},{1,17},{2,18},{3,19},{4,20},{5,21},{6,22},{7,23},{8,24},{9,... | collective-permute-start | bytes 516104 | tf_op jit(solution)/shard_map/ppermute | solution.py:60
  15.4 5.8 %collective-permute-start.4 = (bf16[32,2560]{1,0:T(8,128)(2,1)S(1)}, bf16[32,2560]{1,0:T(8,128)(2,1)S(1)}, u32[]{:S(2)}, u32[]{:S(2)}) collective-permute-start(bf16[32,2560]{1,0:T(8,128)(2,1)S(1)} %get-tuple-element.63.refs_0_.after), channel_id=1, source_target_pairs={{0,2},{1,3},{2,0},{3,1},{4,6},{5,7},{6,4},{7,5},{8,10},{9,11},{10,... | collective-permute-start | bytes 491528 | tf_op jit(solution)/shard_map/ppermute | solution.py:60
  19.4 8.6 %collective-permute-start.9 = (bf16[64,2688]{1,0:T(8,128)(2,1)S(1)}, bf16[64,2688]{1,0:T(8,128)(2,1)S(1)}, u32[]{:S(2)}, u32[]{:S(2)}) collective-permute-start(bf16[64,2688]{1,0:T(8,128)(2,1)S(1)} %stack_two.3.refs_0_), channel_id=1, source_target_pairs={{0,2},{1,3},{2,0},{3,1},{4,6},{5,7},{6,4},{7,5},{8,10},{9,11},{10,... | collective-permute-start | bytes 1032200 | tf_op jit(solution)/shard_map/ppermute | solution.py:60
  21.2 7.9 %collective-permute-start.5 = (bf16[64,2560]{1,0:T(8,128)(2,1)S(1)}, bf16[64,2560]{1,0:T(8,128)(2,1)S(1)}, u32[]{:S(2)}, u32[]{:S(2)}) collective-permute-start(bf16[64,2560]{1,0:T(8,128)(2,1)S(1)} %stack_two.2.refs_0_), channel_id=1, source_target_pairs={{0,16},{1,17},{2,18},{3,19},{4,20},{5,21},{6,22},{7,23},{8,24},{9,... | collective-permute-start | bytes 983048 | tf_op jit(solution)/shard_map/ppermute | solution.py:60
  22.7 5.1 %collective-permute-start.10 = (bf16[288,128]{1,0:T(8,128)(2,1)S(1)}, bf16[288,128]{1,0:T(8,128)(2,1)S(1)}, u32[]{:S(2)}, u32[]{:S(2)}) collective-permute-start(bf16[288,128]{1,0:T(8,128)(2,1)S(1)} %collective-permute-done.3.earlier), channel_id=1, source_target_pairs={{0,1},{1,0},{2,3},{3,2},{4,5},{5,4},{6,7},{7,6},{8,9},{9,8},{10,11... | collective-permute-start | bytes 221192 | tf_op jit(solution)/shard_map/ppermute | solution.py:44
  27.2 1.9 %collective-permute-start.11 = (bf16[64,2688]{1,0:T(8,128)(2,1)S(1)}, bf16[64,2688]{1,0:T(8,128)(2,1)S(1)}, u32[]{:S(2)}, u32[]{:S(2)}) collective-permute-start(bf16[64,2688]{1,0:T(8,128)(2,1)S(1)} %stack_two.3.refs_0_), channel_id=1, source_target_pairs={{0,1},{1,0},{2,3},{3,2},{4,5},{5,4},{6,7},{7,6},{8,9},{9,8},{10,11... | collective-permute-start | bytes 1032200 | tf_op jit(solution)/shard_map/ppermute | solution.py:44
  28.1 1.7 %collective-permute-start.12 = (bf16[64,2688]{1,0:T(8,128)(2,1)S(1)}, bf16[64,2688]{1,0:T(8,128)(2,1)S(1)}, u32[]{:S(2)}, u32[]{:S(2)}) collective-permute-start(bf16[64,2688]{1,0:T(8,128)(2,1)S(1)} %collective-permute-done.9.refs_1_), channel_id=1, source_target_pairs={{0,1},{1,0},{2,3},{3,2},{4,5},{5,4},{6,7},{7,6},{8,9},{9,8},{10,11... | collective-permute-start | bytes 1032200 | tf_op jit(solution)/shard_map/ppermute | solution.py:44
  28.1 3.9 %collective-permute-start.6 = (bf16[64,2560]{1,0:T(8,128)(2,1)S(1)}, bf16[64,2560]{1,0:T(8,128)(2,1)S(1)}, u32[]{:S(2)}, u32[]{:S(2)}) collective-permute-start(bf16[64,2560]{1,0:T(8,128)(2,1)S(1)} %stack_two.2.refs_0_), channel_id=1, source_target_pairs={{0,1},{1,0},{2,3},{3,2},{4,5},{5,4},{6,7},{7,6},{8,9},{9,8},{10,11... | collective-permute-start | bytes 983048 | tf_op jit(solution)/shard_map/ppermute | solution.py:44
  29.1 3.0 %collective-permute-start.7 = (bf16[64,2560]{1,0:T(8,128)(2,1)S(1)}, bf16[64,2560]{1,0:T(8,128)(2,1)S(1)}, u32[]{:S(2)}, u32[]{:S(2)}) collective-permute-start(bf16[64,2560]{1,0:T(8,128)(2,1)S(1)} %collective-permute-done.5.refs_1_), channel_id=1, source_target_pairs={{0,1},{1,0},{2,3},{3,2},{4,5},{5,4},{6,7},{7,6},{8,9},{9,8},{10,11... | collective-permute-start | bytes 983048 | tf_op jit(solution)/shard_map/ppermute | solution.py:44
  33.8 6.2 %collective-permute-start.14 = (bf16[128,512]{1,0:T(8,128)(2,1)S(1)}, bf16[128,512]{1,0:T(8,128)(2,1)S(1)}, u32[]{:S(2)}, u32[]{:S(2)}) collective-permute-start(bf16[128,512]{1,0:T(8,128)(2,1)S(1)} %get-tuple-element.83), channel_id=1, source_target_pairs={{0,16},{16,0},{1,17},{17,1},{2,18},{18,2},{3,19},{19,3},{4,20},{20... | collective-permute-start | bytes 393224 | tf_op jit(solution)/shard_map/ppermute | solution.py:44
  36.4 4.6 %collective-permute-start.13 = (bf16[128,256]{1,0:T(8,128)(2,1)S(1)}, bf16[128,256]{1,0:T(8,128)(2,1)S(1)}, u32[]{:S(2)}, u32[]{:S(2)}) collective-permute-start(bf16[128,256]{1,0:T(8,128)(2,1)S(1)} %get-tuple-element.79), channel_id=1, source_target_pairs={{0,16},{16,0},{1,17},{17,1},{2,18},{18,2},{3,19},{19,3},{4,20},{20... | collective-permute-start | bytes 196616 | tf_op jit(solution)/shard_map/ppermute | solution.py:44
  41.4 1.7 %collective-permute-start.15 = (bf16[128,1280]{1,0:T(8,128)(2,1)S(1)}, bf16[128,1280]{1,0:T(8,128)(2,1)S(1)}, u32[]{:S(2)}, u32[]{:S(2)}) collective-permute-start(bf16[128,1280]{1,0:T(8,128)(2,1)S(1)} %get-tuple-element.88), channel_id=1, source_target_pairs={{0,1},{1,0},{2,3},{3,2},{4,5},{5,4},{6,7},{7,6},{8,9},{9,8},{10,11... | collective-permute-start | bytes 983048 | tf_op jit(solution)/shard_map/ppermute | solution.py:44
  42.0 2.8 %collective-permute-start.18 = (bf16[128,1280]{1,0:T(8,128)(2,1)S(1)}, bf16[128,1280]{1,0:T(8,128)(2,1)S(1)}, u32[]{:S(2)}, u32[]{:S(2)}) collective-permute-start(bf16[128,1280]{1,0:T(8,128)(2,1)S(1)} %get-tuple-element.94), channel_id=1, source_target_pairs={{0,1},{1,0},{2,3},{3,2},{4,5},{5,4},{6,7},{7,6},{8,9},{9,8},{10,11... | collective-permute-start | bytes 983048 | tf_op jit(solution)/shard_map/ppermute | solution.py:44
  43.2 6.3 %collective-permute-start.16 = (bf16[64,1280]{1,0:T(8,128)(2,1)S(1)}, bf16[64,1280]{1,0:T(8,128)(2,1)S(1)}, u32[]{:S(2)}, u32[]{:S(2)}) collective-permute-start(bf16[64,1280]{1,0:T(8,128)(2,1)S(1)} %get-tuple-element.90), channel_id=1, source_target_pairs={{0,16},{1,17},{2,18},{3,19},{4,20},{5,21},{6,22},{7,23},{8,24},{9,... | collective-permute-start | bytes 491528 | tf_op jit(solution)/shard_map/ppermute | solution.py:60
  44.9 6.1 %collective-permute-start.19 = (bf16[64,1280]{1,0:T(8,128)(2,1)S(1)}, bf16[64,1280]{1,0:T(8,128)(2,1)S(1)}, u32[]{:S(2)}, u32[]{:S(2)}) collective-permute-start(bf16[64,1280]{1,0:T(8,128)(2,1)S(1)} %get-tuple-element.96), channel_id=1, source_target_pairs={{0,2},{1,3},{2,0},{3,1},{4,6},{5,7},{6,4},{7,5},{8,10},{9,11},{10,... | collective-permute-start | bytes 491528 | tf_op jit(solution)/shard_map/ppermute | solution.py:60
  49.5 6.0 %collective-permute-start.17 = (bf16[32,2560]{1,0:T(8,128)(2,1)S(1)}, bf16[32,2560]{1,0:T(8,128)(2,1)S(1)}, u32[]{:S(2)}, u32[]{:S(2)}) collective-permute-start(bf16[32,2560]{1,0:T(8,128)(2,1)S(1)} %get-tuple-element.92), channel_id=1, source_target_pairs={{0,2},{1,3},{2,0},{3,1},{4,6},{5,7},{6,4},{7,5},{8,10},{9,11},{10,... | collective-permute-start | bytes 491528 | tf_op jit(solution)/shard_map/ppermute | solution.py:60
  51.0 4.5 %collective-permute-start.20 = (bf16[32,1280]{1,0:T(8,128)(2,1)S(1)}, bf16[32,1280]{1,0:T(8,128)(2,1)S(1)}, u32[]{:S(2)}, u32[]{:S(2)}) collective-permute-start(bf16[32,1280]{1,0:T(8,128)(2,1)S(1)} %get-tuple-element.98), channel_id=1, source_target_pairs={{0,16},{1,17},{2,18},{3,19},{4,20},{5,21},{6,22},{7,23},{8,24},{9,... | collective-permute-start | bytes 245768 | tf_op jit(solution)/shard_map/ppermute | solution.py:60
  55.5 7.9 %collective-permute-start.21 = (bf16[8,5120]{1,0:T(8,128)(2,1)S(1)}, bf16[8,5120]{1,0:T(8,128)(2,1)S(1)}, u32[]{:S(2)}, u32[]{:S(2)}) collective-permute-start(bf16[8,5120]{1,0:T(8,128)(2,1)S(1)} %get-tuple-element.99), channel_id=1, source_target_pairs={{0,8},{1,9},{2,10},{3,11},{4,12},{5,13},{6,14},{7,15},{8,0},{9,1},... | collective-permute-start | bytes 245768 | tf_op jit(solution)/shard_map/ppermute | solution.py:48
  56.7 6.7 %collective-permute-start.22 = (bf16[8,5120]{1,0:T(8,128)(2,1)S(1)}, bf16[8,5120]{1,0:T(8,128)(2,1)S(1)}, u32[]{:S(2)}, u32[]{:S(2)}) collective-permute-start(bf16[8,5120]{1,0:T(8,128)(2,1)S(1)} %get-tuple-element.100.after), channel_id=1, source_target_pairs={{0,12},{1,13},{2,14},{3,15},{4,8},{5,9},{6,10},{7,11},{8,4},{9,5},... | collective-permute-start | bytes 245768 | tf_op jit(solution)/shard_map/ppermute | solution.py:48
  59.0 5.2 %collective-permute-start.23 = (bf16[8,5120]{1,0:T(8,128)(2,1)S(1)}, bf16[8,5120]{1,0:T(8,128)(2,1)S(1)}, u32[]{:S(2)}, u32[]{:S(2)}) collective-permute-start(bf16[8,5120]{1,0:T(8,128)(2,1)S(1)} %get-tuple-element.106), channel_id=1, source_target_pairs={{0,4},{1,5},{2,6},{3,7},{4,0},{5,1},{6,2},{7,3},{8,12},{9,13},{10,... | collective-permute-start | bytes 245768 | tf_op jit(solution)/shard_map/ppermute | solution.py:48

commit v9 on v8

--- a/solution.py
+++ b/solution.py
@@ -249,16 +249,17 @@
 
 def first_kernel(
     two, far, two_other, far_other, gate_w, up_w,
-    gate_out, up_out, pick_out, pick_far_out, coef_out,
-    tokens, notes, *, unit, tok_dev, capacity, topk,
+    gate_out, up_out, pick_out, pick_far_out, coef_out, tokens,
+    notes, *, unit, tok_dev, capacity, topk,
 ):
     width = tokens.shape[1]
     rows = tokens.shape[0]
     slots = pick_out.shape[1]
     expert = lax.axis_index("exp")
     assemble(tokens, two, far, two_other, far_other, unit, False)
-    gate_out[...] = times_rows_in(tokens[...], gate_w[...])
-    up_out[...] = times_rows_in(tokens[...], up_w[...])
+    few = gate_out.shape[1]
+    gate_out[...] = times_rows_in(tokens[...], gate_w[:few, :])
+    up_out[...] = times_rows_in(tokens[...], up_w[:few, :])
 
     assemble(notes, two, far, two_other, far_other, unit, False, width)
     note = notes[...].astype(jnp.float32)
@@ -288,10 +289,7 @@
     coef_out[...] = jnp.broadcast_to(coef, coef_out.shape)
 
 
-def finish_units(tokens, gate_w, up_w, gate_in, up_in, pick, act_out, packed_out, start):
-    span = slice(start, start + act_out.shape[1])
-    gate = gate_in[:, span] + times_rows_in(tokens[...], gate_w[span, :])
-    upper = up_in[:, span] + times_rows_in(tokens[...], up_w[span, :])
+def finish_units(gate, upper, pick, act_out, packed_out):
     act = (gate / (1.0 + jnp.exp(-gate)) * upper).astype(jnp.bfloat16)
     act_out[...] = act
     packed_out[...] = lax.dot_general(
@@ -304,11 +302,18 @@
     act_out, packed_out, tokens, *, unit,
 ):
     assemble(tokens, two, far, two_other, far_other, unit, True)
-    finish_units(tokens, gate_w, up_w, gate_in, up_in, pick, act_out, packed_out, 0)
-
-
-def third_kernel(tokens, gate_w, up_w, gate_in, up_in, pick, act_out, packed_out, *, start):
-    finish_units(tokens, gate_w, up_w, gate_in, up_in, pick, act_out, packed_out, start)
+    few = act_out.shape[1]
+    gate = gate_in[...] + times_rows_in(tokens[...], gate_w[:few, :])
+    upper = up_in[...] + times_rows_in(tokens[...], up_w[:few, :])
+    finish_units(gate, upper, pick, act_out, packed_out)
+
+
+def third_kernel(first, gate_1, up_1, second, gate_2, up_2, pick, act_out, packed_out, *, start):
+    gate = times_rows_in(first[...], gate_1[start:, :]) + times_rows_in(
+        second[...], gate_2[start:, :]
+    )
+    upper = times_rows_in(first[...], up_1[start:, :]) + times_rows_in(second[...], up_2[start:, :])
+    finish_units(gate, upper, pick, act_out, packed_out)
 
 
 def own_kernel(act_a, act_b, down_own, out):
@@ -487,20 +492,20 @@
         group = (two, far, swapped(two, "exp", 1), swapped(far, "exp", 1))
         pieces[number] = [(piece, "vmem") for piece in group]
 
-    gate, up, pick, pick_far, coef = local_kernel(
+    few = 2 * units // 3 if units % 384 == 0 else units // 2
+    gate, up, pick, pick_far, coef, tokens_1 = local_kernel(
         lambda *refs: first_kernel(
             *refs, unit=unit, tok_dev=tok_dev, capacity=capacity, topk=topk
         ),
         [*pieces[0], (gate_1, "vmem"), (up_1, "vmem")],
-        [((count, units), f32, "vmem")] * 2
+        [((count, few), f32, "vmem")] * 2
         + [((count, slots), bf16, "vmem")] * 2
-        + [((count, 128), f32, "vmem")],
-        [pltpu.VMEM((count, half), bf16), pltpu.VMEM((count, 128), bf16)],
+        + [((count, 128), f32, "vmem"), ((count, half), bf16, "vmem")],
+        [pltpu.VMEM((count, 128), bf16)],
         "gate_up_first",
     )
-    few = 2 * units // 3 if units % 384 == 0 else units // 2
     sums_in = [(gate_2, "vmem"), (up_2, "vmem"), (gate, "vmem"), (up, "vmem"), (pick, "vmem")]
-    act_a, packed_a, tokens = local_kernel(
+    act_a, packed_a, tokens_2 = local_kernel(
         lambda *refs: second_kernel(*refs, unit=unit),
         [*pieces[1], *sums_in],
         [
@@ -514,7 +519,10 @@
     other_a = swapped(packed_a, "ctx", 1)
     act_b, packed_b = local_kernel(
         lambda *refs: third_kernel(*refs, start=few),
-        [(tokens, "vmem"), *sums_in],
+        [
+            (tokens_1, "vmem"), (gate_1, "vmem"), (up_1, "vmem"),
+            (tokens_2, "vmem"), (gate_2, "vmem"), (up_2, "vmem"), (pick, "vmem"),
+        ],
         [((count, units - few), bf16, "vmem"), ((slots, units - few), bf16, "vmem")],
         [],
         "gate_up_third",
@@ -588,7 +596,7 @@
         "attention",
     )
     sends = dict(zip(places, sends))
-    got = [along_line(sends[d], d) for d in (3, 1, 2)]
+    got = [along_line(sends[d], d) for d in (1, 2, 3)]
     got[-1], attended = lax.optimization_barrier((got[-1], attended))
     (mixed,) = local_kernel(
         sum_kernel,

time: 65 us -> 65.2 us (level)
  waiting for transfers between devices: 14 us -> 15.1 us
  starting transfers between devices: 27.6 us -> 26.7 us
    ppermute x8, waiting for transfers between devices: 6.86 us -> 9.42 us  [paired(): return lax.ppermute(block, ('ctx', 'exp'), route)]
    ppermute x8, starting transfers between devices: 12.8 us -> 10.9 us  [paired(): return lax.ppermute(block, ('ctx', 'exp'), route)]
    ppermute x6, starting transfers between devices: 9.31 us -> 10.1 us  [along_line(): lax.ppermute(block, 'exp', [(i, i ^ 4 * steps) for i in range(lax.axis_si...]
    ppermute x6, waiting for transfers between devices: 4.04 us -> 3.27 us  [along_line(): lax.ppermute(block, 'exp', [(i, i ^ 4 * steps) for i in range(lax.axis_si...]
    ppermute x10, waiting for transfers between devices: 3.1 us -> 2.45 us  [swapped(): lax.ppermute(block, axis, [(i, i ^ bit) for i in range(lax.axis_size(axis...]
  transfers between devices with their start and end apart: 24 -> 24, of which waited for: 11 -> 13; matrix products, arithmetic and copies ran while one was open for 0% -> 0% of each run, Pallas kernels for 29% -> 28%
where the time goes in v9:
time: 65.2 us; the launch traced here: 65.1 us
  starting transfers between devices  26.7 us (41%)
  Pallas kernels  22.4 us (34%)
  waiting for transfers between devices  15.1 us (23%)
  between operations  0.81 us (1%)
    pallas_call x21, Pallas kernels, local_kernel(): pl.pallas_call(body, in_specs=[pl.BlockSpec(memory_space=kinds[kind]) for...  22.4 us
    ppermute x8, starting transfers between devices, paired(): return lax.ppermute(block, ('ctx', 'exp'), route)  10.9 us
    ppermute x6, starting transfers between devices, along_line(): lax.ppermute(block, 'exp', [(i, i ^ 4 * steps) for i in range(lax.axis_si...  10.1 us
    ppermute x8, waiting for transfers between devices, paired(): return lax.ppermute(block, ('ctx', 'exp'), route)  9.42 us
    ppermute x10, starting transfers between devices, swapped(): lax.ppermute(block, axis, [(i, i ^ bit) for i in range(lax.axis_size(axis...  5.59 us
    ppermute x6, waiting for transfers between devices, along_line(): lax.ppermute(block, 'exp', [(i, i ^ 4 * steps) for i in range(lax.axis_si...  3.27 us
    ppermute x10, waiting for transfers between devices, swapped(): lax.ppermute(block, axis, [(i, i ^ bit) for i in range(lax.axis_size(axis...  2.45 us
  transfers between devices with their start and end apart: 24, of which 13 were waited for; matrix products, arithmetic and copies ran while one was open for 0% of the time, Pallas kernels for 28%

profile of v9, /device:TPU:0, one launch (start us, length us, event | category | flops | bytes accessed | tf_op | source)
XLA Modules:
  0.0 65.1 jit_solution(14852016721510572250)
XLA Ops:
  0.6 1.0 %rows.1 = (bf16[8,5248]{1,0:T(8,128)(2,1)S(1)}, bf16[288,128]{1,0:T(8,128)(2,1)S(1)}) custom-call(bf16[8,5120]{1,0:T(8,128)(2,1)} %bitcast.16, s32[6,1,8]{2,1,0:T(1,128)} %bitcast.18, f32[6,1,8]{2,1,0:T(1,128)} %bitcast.19, bf16[576,128]{1,0:T(8,128)(2,1)} %bitcast.14), custom_call_target="tpu_custom_call" | custom-call | tf_op jit(solution)/shard_map/rows/pallas_call | solution.py:92
  1.6 3.1 %collective-permute-start.2 = (bf16[8,5248]{1,0:T(8,128)(2,1)S(1)}, bf16[8,5248]{1,0:T(8,128)(2,1)S(1)}, u32[]{:S(2)}, u32[]{:S(2)}) collective-permute-start(bf16[8,5248]{1,0:T(8,128)(2,1)S(1)} %get-tuple-element.60.refs_0_), channel_id=1, source_target_pairs={{0,4},{1,5},{2,6},{3,7},{4,0},{5,1},{6,2},{7,3},{8,12},{9,13},{10,... | collective-permute-start | bytes 251912 | tf_op jit(solution)/shard_map/ppermute | solution.py:48
  4.7 2.6 %collective-permute-start.1 = (bf16[8,5248]{1,0:T(8,128)(2,1)S(1)}, bf16[8,5248]{1,0:T(8,128)(2,1)S(1)}, u32[]{:S(2)}, u32[]{:S(2)}) collective-permute-start(bf16[8,5248]{1,0:T(8,128)(2,1)S(1)} %get-tuple-element.60.refs_0_), channel_id=1, source_target_pairs={{0,8},{1,9},{2,10},{3,11},{4,12},{5,13},{6,14},{7,15},{8,0},{9,1},... | collective-permute-start | bytes 251912 | tf_op jit(solution)/shard_map/ppermute | solution.py:48
  7.3 1.7 %collective-permute-start.3 = (bf16[288,128]{1,0:T(8,128)(2,1)S(1)}, bf16[288,128]{1,0:T(8,128)(2,1)S(1)}, u32[]{:S(2)}, u32[]{:S(2)}) collective-permute-start(bf16[288,128]{1,0:T(8,128)(2,1)S(1)} %get-tuple-element.57), channel_id=1, source_target_pairs={{0,16},{16,0},{1,17},{17,1},{2,18},{18,2},{3,19},{19,3},{4,20},{20... | collective-permute-start | bytes 221192 | tf_op jit(solution)/shard_map/ppermute | solution.py:44
  9.0 3.5 %fetch.3 = (bf16[768,2560]{1,0:T(8,128)(2,1)S(1)}, bf16[768,2560]{1,0:T(8,128)(2,1)S(1)}, bf16[128,2304]{1,0:T(8,128)(2,1)S(1)}, bf16[576,128]{1,0:T(8,128)(2,1)S(1)}) custom-call(bf16[8,5248]{1,0:T(8,128)(2,1)S(1)} %get-tuple-element.60.refs_0_, bf16[768,5120]{1,0:T(8,128)(2,1)} %bitcast.8, bf16[768,5120]{1,0:T(8,128)(2,1)} %bitcast.10, ...), custom_call_target="tpu_custom_call" | custom-call | tf_op jit(solution)/shard_map/fetch/pallas_call | solution.py:92
  12.6 1.5 %collective-permute-done.1.refs_2_ = bf16[8,5248]{1,0:T(8,128)(2,1)S(1)} collective-permute-done((bf16[8,5248]{1,0:T(8,128)(2,1)S(1)}, bf16[8,5248]{1,0:T(8,128)(2,1)S(1)}, u32[]{:S(2)}, u32[]{:S(2)}) %collective-permute-start.1) | collective-permute-done | bytes 84000 | tf_op jit(solution)/shard_map/ppermute | solution.py:48
  14.1 1.6 %collective-permute-start.4 = (bf16[32,2688]{1,0:T(8,128)(2,1)S(1)}, bf16[32,2688]{1,0:T(8,128)(2,1)S(1)}, u32[]{:S(2)}, u32[]{:S(2)}) collective-permute-start(bf16[32,2688]{1,0:T(8,128)(2,1)S(1)} %get-tuple-element.64.refs_0_), channel_id=1, source_target_pairs={{0,16},{1,17},{2,18},{3,19},{4,20},{5,21},{6,22},{7,23},{8,24},{9,... | collective-permute-start | bytes 516104 | tf_op jit(solution)/shard_map/ppermute | solution.py:60
  15.7 1.5 %collective-permute-start.6 = (bf16[32,2560]{1,0:T(8,128)(2,1)S(1)}, bf16[32,2560]{1,0:T(8,128)(2,1)S(1)}, u32[]{:S(2)}, u32[]{:S(2)}) collective-permute-start(bf16[32,2560]{1,0:T(8,128)(2,1)S(1)} %get-tuple-element.65.after.refs_0_), channel_id=1, source_target_pairs={{0,2},{1,3},{2,0},{3,1},{4,6},{5,7},{6,4},{7,5},{8,10},{9,11},{10,... | collective-permute-start | bytes 491528 | tf_op jit(solution)/shard_map/ppermute | solution.py:60
  17.2 2.1 %fetch.4.down_w.refs_3_ = bf16[2560,768]{1,0:T(8,128)(2,1)S(1)} custom-call(bf16[32,2560]{1,0:T(8,128)(2,1)S(1)} %get-tuple-element.65.after.refs_0_, bf16[2560,1536]{1,0:T(8,128)(2,1)} %bitcast.12), custom_call_target="tpu_custom_call" | custom-call | tf_op jit(solution)/shard_map/fetch/pallas_call | solution.py:92
  19.6 1.6 %collective-permute-start.5 = (bf16[64,2688]{1,0:T(8,128)(2,1)S(1)}, bf16[64,2688]{1,0:T(8,128)(2,1)S(1)}, u32[]{:S(2)}, u32[]{:S(2)}) collective-permute-start(bf16[64,2688]{1,0:T(8,128)(2,1)S(1)} %stack_two.2.refs_0_), channel_id=1, source_target_pairs={{0,2},{1,3},{2,0},{3,1},{4,6},{5,7},{6,4},{7,5},{8,10},{9,11},{10,... | collective-permute-start | bytes 1032200 | tf_op jit(solution)/shard_map/ppermute | solution.py:60
  21.2 1.5 %collective-permute-done.6.refs_1_ = bf16[32,2560]{1,0:T(8,128)(2,1)S(1)} collective-permute-done((bf16[32,2560]{1,0:T(8,128)(2,1)S(1)}, bf16[32,2560]{1,0:T(8,128)(2,1)S(1)}, u32[]{:S(2)}, u32[]{:S(2)}) %collective-permute-start.6) | collective-permute-done | bytes 163872 | tf_op jit(solution)/shard_map/ppermute | solution.py:60
  23.0 4.5 %fetch.5 = (bf16[768,2560]{1,0:T(8,128)(2,1)S(1)}, bf16[768,2560]{1,0:T(8,128)(2,1)S(1)}, bf16[2560,768]{1,0:T(8,128)(2,1)S(1)}) custom-call(bf16[64,2560]{1,0:T(8,128)(2,1)S(1)} %stack_two.3.refs_0_, bf16[768,5120]{1,0:T(8,128)(2,1)} %bitcast.9, bf16[768,5120]{1,0:T(8,128)(2,1)} %bitcast.11, bf16[2560,1536]{1,0:T(8,128)(2,1)} %bitcast.13), custom_call_target="tpu_custom_call" | custom-call | tf_op jit(solution)/shard_map/fetch/pallas_call | solution.py:92
  28.9 1.0 %collective-permute-done.10.refs_1_ = bf16[64,2560]{1,0:T(8,128)(2,1)S(1)} collective-permute-done((bf16[64,2560]{1,0:T(8,128)(2,1)S(1)}, bf16[64,2560]{1,0:T(8,128)(2,1)S(1)}, u32[]{:S(2)}, u32[]{:S(2)}) %collective-permute-start.10) | collective-permute-done | bytes 327712 | tf_op jit(solution)/shard_map/ppermute | solution.py:60
  30.0 1.6 %gate_up_first.1 = (f32[256,512]{1,0:T(8,128)S(1)}, f32[256,512]{1,0:T(8,128)S(1)}, bf16[256,128]{1,0:T(8,128)(2,1)S(1)}, bf16[256,128]{1,0:T(8,128)(2,1)S(1)}, ...) custom-call(bf16[64,2688]{1,0:T(8,128)(2,1)S(1)} %stack_two.2.refs_0_, ...), custom_call_target="tpu_custom_call" | custom-call | tf_op jit(solution)/shard_map/gate_up_first/pallas_call | solution.py:92
  31.6 1.7 %gate_up_second.1 = (bf16[256,512]{1,0:T(8,128)(2,1)S(1)}, bf16[128,512]{1,0:T(8,128)(2,1)S(1)}, bf16[256,2560]{1,0:T(8,128)(2,1)S(1)}) custom-call(bf16[64,2560]{1,0:T(8,128)(2,1)S(1)} %stack_two.3.refs_0_, bf16[64,2560]{1,0:T(8,128)(2,1)S(1)} %collective-permute-done.10.refs_1_, bf16[64,2560]{1,0:T(8,128)(2,1)S(1)} %collective-permute-done.11.refs_2_, ...), custom_call_target="tpu_custom_call" | custom-call | tf_op jit(solution)/shard_map/gate_up_second/pallas_call | solution.py:92
  33.4 1.7 %collective-permute-start.14 = (bf16[128,512]{1,0:T(8,128)(2,1)S(1)}, bf16[128,512]{1,0:T(8,128)(2,1)S(1)}, u32[]{:S(2)}, u32[]{:S(2)}) collective-permute-start(bf16[128,512]{1,0:T(8,128)(2,1)S(1)} %get-tuple-element.85), channel_id=1, source_target_pairs={{0,16},{16,0},{1,17},{17,1},{2,18},{18,2},{3,19},{19,3},{4,20},{20... | collective-permute-start | bytes 393224 | tf_op jit(solution)/shard_map/ppermute | solution.py:44
  35.0 1.7 %gate_up_third.1 = (bf16[256,256]{1,0:T(8,128)(2,1)S(1)}, bf16[128,256]{1,0:T(8,128)(2,1)S(1)}) custom-call(bf16[256,2560]{1,0:T(8,128)(2,1)S(1)} %get-tuple-element.74.refs_0_, bf16[768,2560]{1,0:T(8,128)(2,1)S(1)} %get-tuple-element.72.refs_4_.refs_1_, bf16[768,2560]{1,0:T(8,128)(2,1)S(1)} %get-tuple-element.73.refs_5_.refs_2_, ...), custom_call_target="tpu_custom_call" | custom-call | tf_op jit(solution)/shard_map/gate_up_third/pallas_call | solution.py:92
  37.2 1.2 %down_own.1.own = f32[256,2560]{1,0:T(8,128)S(1)} custom-call(bf16[256,512]{1,0:T(8,128)(2,1)S(1)} %get-tuple-element.86.act_a, bf16[256,256]{1,0:T(8,128)(2,1)S(1)} %get-tuple-element.87.act_b, bf16[2560,768]{1,0:T(8,128)(2,1)S(1)} %get-tuple-element.88.down_own), custom_call_target="tpu_custom_call" | custom-call | tf_op jit(solution)/shard_map/down_own/pallas_call | solution.py:92
  38.4 0.7 %collective-permute-done.14.packed = bf16[128,512]{1,0:T(8,128)(2,1)S(1)} collective-permute-done((bf16[128,512]{1,0:T(8,128)(2,1)S(1)}, bf16[128,512]{1,0:T(8,128)(2,1)S(1)}, u32[]{:S(2)}, u32[]{:S(2)}) %collective-permute-start.14) | collective-permute-done | bytes 131104 | tf_op jit(solution)/shard_map/ppermute | solution.py:44
  39.2 1.0 %down_more.1.refs_4_ = f32[256,2560]{1,0:T(8,128)S(1)} custom-call(bf16[128,512]{1,0:T(8,128)(2,1)S(1)} %collective-permute-done.14.packed, bf16[256,128]{1,0:T(8,128)(2,1)S(1)} %get-tuple-element.82.pick.refs_1_, bf16[2560,768]{1,0:T(8,128)(2,1)S(1)} %fetch.4.down_w.refs_3_, f32[256,2560]{1,0:T(8,128)S(1)} %down_own.1.own), custom_call_target="tpu_custom_call" | custom-call | tf_op jit(solution)/shard_map/down_more/pallas_call | solution.py:92
  40.2 0.9 %collective-permute-done.13.refs_0_ = bf16[128,256]{1,0:T(8,128)(2,1)S(1)} collective-permute-done((bf16[128,256]{1,0:T(8,128)(2,1)S(1)}, bf16[128,256]{1,0:T(8,128)(2,1)S(1)}, u32[]{:S(2)}, u32[]{:S(2)}) %collective-permute-start.13) | collective-permute-done | bytes 65568 | tf_op jit(solution)/shard_map/ppermute | solution.py:44
  43.3 1.3 %collective-permute-start.16 = (bf16[64,1280]{1,0:T(8,128)(2,1)S(1)}, bf16[64,1280]{1,0:T(8,128)(2,1)S(1)}, u32[]{:S(2)}, u32[]{:S(2)}) collective-permute-start(bf16[64,1280]{1,0:T(8,128)(2,1)S(1)} %get-tuple-element.92), channel_id=1, source_target_pairs={{0,16},{1,17},{2,18},{3,19},{4,20},{5,21},{6,22},{7,23},{8,24},{9,... | collective-permute-start | bytes 491528 | tf_op jit(solution)/shard_map/ppermute | solution.py:60
  44.7 1.7 %collective-permute-start.19 = (bf16[64,1280]{1,0:T(8,128)(2,1)S(1)}, bf16[64,1280]{1,0:T(8,128)(2,1)S(1)}, u32[]{:S(2)}, u32[]{:S(2)}) collective-permute-start(bf16[64,1280]{1,0:T(8,128)(2,1)S(1)} %get-tuple-element.98), channel_id=1, source_target_pairs={{0,2},{1,3},{2,0},{3,1},{4,6},{5,7},{6,4},{7,5},{8,10},{9,11},{10,... | collective-permute-start | bytes 491528 | tf_op jit(solution)/shard_map/ppermute | solution.py:60
  46.3 3.3 %collective-permute-done.16.refs_1_ = bf16[64,1280]{1,0:T(8,128)(2,1)S(1)} collective-permute-done((bf16[64,1280]{1,0:T(8,128)(2,1)S(1)}, bf16[64,1280]{1,0:T(8,128)(2,1)S(1)}, u32[]{:S(2)}, u32[]{:S(2)}) %collective-permute-start.16) | collective-permute-done | bytes 163872 | tf_op jit(solution)/shard_map/ppermute | solution.py:60
  49.6 1.7 %collective-permute-start.17 = (bf16[32,2560]{1,0:T(8,128)(2,1)S(1)}, bf16[32,2560]{1,0:T(8,128)(2,1)S(1)}, u32[]{:S(2)}, u32[]{:S(2)}) collective-permute-start(bf16[32,2560]{1,0:T(8,128)(2,1)S(1)} %get-tuple-element.94), channel_id=1, source_target_pairs={{0,2},{1,3},{2,0},{3,1},{4,6},{5,7},{6,4},{7,5},{8,10},{9,11},{10,... | collective-permute-start | bytes 491528 | tf_op jit(solution)/shard_map/ppermute | solution.py:60
  51.3 1.3 %collective-permute-start.20 = (bf16[32,1280]{1,0:T(8,128)(2,1)S(1)}, bf16[32,1280]{1,0:T(8,128)(2,1)S(1)}, u32[]{:S(2)}, u32[]{:S(2)}) collective-permute-start(bf16[32,1280]{1,0:T(8,128)(2,1)S(1)} %get-tuple-element.100), channel_id=1, source_target_pairs={{0,16},{1,17},{2,18},{3,19},{4,20},{5,21},{6,22},{7,23},{8,24},{9,... | collective-permute-start | bytes 245768 | tf_op jit(solution)/shard_map/ppermute | solution.py:60
  52.7 3.2 %collective-permute-done.20.got_x = bf16[32,1280]{1,0:T(8,128)(2,1)S(1)} collective-permute-done((bf16[32,1280]{1,0:T(8,128)(2,1)S(1)}, bf16[32,1280]{1,0:T(8,128)(2,1)S(1)}, u32[]{:S(2)}, u32[]{:S(2)}) %collective-permute-start.20) | collective-permute-done | bytes 81952 | tf_op jit(solution)/shard_map/ppermute | solution.py:60
  55.9 2.3 %collective-permute-start.21 = (bf16[8,5120]{1,0:T(8,128)(2,1)S(1)}, bf16[8,5120]{1,0:T(8,128)(2,1)S(1)}, u32[]{:S(2)}, u32[]{:S(2)}) collective-permute-start(bf16[8,5120]{1,0:T(8,128)(2,1)S(1)} %get-tuple-element.101.after), channel_id=1, source_target_pairs={{0,12},{1,13},{2,14},{3,15},{4,8},{5,9},{6,10},{7,11},{8,4},{9,5},... | collective-permute-start | bytes 245768 | tf_op jit(solution)/shard_map/ppermute | solution.py:48
  58.5 1.8 %collective-permute-start.23 = (bf16[8,5120]{1,0:T(8,128)(2,1)S(1)}, bf16[8,5120]{1,0:T(8,128)(2,1)S(1)}, u32[]{:S(2)}, u32[]{:S(2)}) collective-permute-start(bf16[8,5120]{1,0:T(8,128)(2,1)S(1)} %get-tuple-element.108), channel_id=1, source_target_pairs={{0,8},{1,9},{2,10},{3,11},{4,12},{5,13},{6,14},{7,15},{8,0},{9,1},... | collective-permute-start | bytes 245768 | tf_op jit(solution)/shard_map/ppermute | solution.py:48
  60.3 2.3 %attention.1 = bf16[128,2048]{1,0:T(8,128)(2,1)} custom-call(bf16[8,5120]{1,0:T(8,128)(2,1)S(1)} %get-tuple-element.101.after, bf16[288,128]{1,0:T(8,128)(2,1)S(1)} %collective-permute-done.3.earlier, bf16[288,128]{1,0:T(8,128)(2,1)S(1)} %collective-permute-done.7.earlier_other, bf16[128,2304]{1,0:T(8,128)(2,1)S(1)} %get-tuple-element.103.queries, ...), custom_call_target="tpu_custom_call" | custom-call | tf_op jit(solution)/shard_map/attention/pallas_call | solution.py:92
  62.7 1.7 %collective-permute-done.22.refs_0_ = bf16[8,5120]{1,0:T(8,128)(2,1)S(1)} collective-permute-done((bf16[8,5120]{1,0:T(8,128)(2,1)S(1)}, bf16[8,5120]{1,0:T(8,128)(2,1)S(1)}, u32[]{:S(2)}, u32[]{:S(2)}) %collective-permute-start.22) | collective-permute-done | bytes 81952 | tf_op jit(solution)/shard_map/ppermute | solution.py:48
  64.4 0.7 %sum.1 = bf16[8,5120]{1,0:T(8,128)(2,1)} custom-call(f32[8,5120]{1,0:T(8,128)S(1)} %get-tuple-element.106.first, bf16[8,5120]{1,0:T(8,128)(2,1)S(1)} %collective-permute-done.22.refs_0_, bf16[8,5120]{1,0:T(8,128)(2,1)S(1)} %collective-permute-done.23.refs_1_, bf16[8,5120]{1,0:T(8,128)(2,1)S(1)} %collective-permute-done.21.refs_2_), custom_call_target="tpu_custom_call" | custom-call | tf_op jit(solution)/shard_map/sum/pallas_call | solution.py:92
  (37 shorter events, 5.5 us)
Async XLA Ops:
  1.6 10.9 %collective-permute-start.2 = (bf16[8,5248]{1,0:T(8,128)(2,1)S(1)}, bf16[8,5248]{1,0:T(8,128)(2,1)S(1)}, u32[]{:S(2)}, u32[]{:S(2)}) collective-permute-start(bf16[8,5248]{1,0:T(8,128)(2,1)S(1)} %get-tuple-element.60.refs_0_), channel_id=1, source_target_pairs={{0,4},{1,5},{2,6},{3,7},{4,0},{5,1},{6,2},{7,3},{8,12},{9,13},{10,... | collective-permute-start | bytes 251912 | tf_op jit(solution)/shard_map/ppermute | solution.py:48
  4.7 9.3 %collective-permute-start.1 = (bf16[8,5248]{1,0:T(8,128)(2,1)S(1)}, bf16[8,5248]{1,0:T(8,128)(2,1)S(1)}, u32[]{:S(2)}, u32[]{:S(2)}) collective-permute-start(bf16[8,5248]{1,0:T(8,128)(2,1)S(1)} %get-tuple-element.60.refs_0_), channel_id=1, source_target_pairs={{0,8},{1,9},{2,10},{3,11},{4,12},{5,13},{6,14},{7,15},{8,0},{9,1},... | collective-permute-start | bytes 251912 | tf_op jit(solution)/shard_map/ppermute | solution.py:48
  7.3 6.8 %collective-permute-start = (bf16[8,5248]{1,0:T(8,128)(2,1)S(1)}, bf16[8,5248]{1,0:T(8,128)(2,1)S(1)}, u32[]{:S(2)}, u32[]{:S(2)}) collective-permute-start(bf16[8,5248]{1,0:T(8,128)(2,1)S(1)} %get-tuple-element.60.refs_0_), channel_id=1, source_target_pairs={{0,12},{1,13},{2,14},{3,15},{4,8},{5,9},{6,10},{7,11},{8,4},{9,5},... | collective-permute-start | bytes 251912 | tf_op jit(solution)/shard_map/ppermute | solution.py:48
  7.3 5.2 %collective-permute-start.3 = (bf16[288,128]{1,0:T(8,128)(2,1)S(1)}, bf16[288,128]{1,0:T(8,128)(2,1)S(1)}, u32[]{:S(2)}, u32[]{:S(2)}) collective-permute-start(bf16[288,128]{1,0:T(8,128)(2,1)S(1)} %get-tuple-element.57), channel_id=1, source_target_pairs={{0,16},{16,0},{1,17},{17,1},{2,18},{18,2},{3,19},{19,3},{4,20},{20... | collective-permute-start | bytes 221192 | tf_op jit(solution)/shard_map/ppermute | solution.py:44
  14.1 5.5 %collective-permute-start.4 = (bf16[32,2688]{1,0:T(8,128)(2,1)S(1)}, bf16[32,2688]{1,0:T(8,128)(2,1)S(1)}, u32[]{:S(2)}, u32[]{:S(2)}) collective-permute-start(bf16[32,2688]{1,0:T(8,128)(2,1)S(1)} %get-tuple-element.64.refs_0_), channel_id=1, source_target_pairs={{0,16},{1,17},{2,18},{3,19},{4,20},{5,21},{6,22},{7,23},{8,24},{9,... | collective-permute-start | bytes 516104 | tf_op jit(solution)/shard_map/ppermute | solution.py:60
  15.7 7.0 %collective-permute-start.6 = (bf16[32,2560]{1,0:T(8,128)(2,1)S(1)}, bf16[32,2560]{1,0:T(8,128)(2,1)S(1)}, u32[]{:S(2)}, u32[]{:S(2)}) collective-permute-start(bf16[32,2560]{1,0:T(8,128)(2,1)S(1)} %get-tuple-element.65.after.refs_0_), channel_id=1, source_target_pairs={{0,2},{1,3},{2,0},{3,1},{4,6},{5,7},{6,4},{7,5},{8,10},{9,11},{10,... | collective-permute-start | bytes 491528 | tf_op jit(solution)/shard_map/ppermute | solution.py:60
  19.6 8.7 %collective-permute-start.5 = (bf16[64,2688]{1,0:T(8,128)(2,1)S(1)}, bf16[64,2688]{1,0:T(8,128)(2,1)S(1)}, u32[]{:S(2)}, u32[]{:S(2)}) collective-permute-start(bf16[64,2688]{1,0:T(8,128)(2,1)S(1)} %stack_two.2.refs_0_), channel_id=1, source_target_pairs={{0,2},{1,3},{2,0},{3,1},{4,6},{5,7},{6,4},{7,5},{8,10},{9,11},{10,... | collective-permute-start | bytes 1032200 | tf_op jit(solution)/shard_map/ppermute | solution.py:60
  22.7 7.1 %collective-permute-start.10 = (bf16[64,2560]{1,0:T(8,128)(2,1)S(1)}, bf16[64,2560]{1,0:T(8,128)(2,1)S(1)}, u32[]{:S(2)}, u32[]{:S(2)}) collective-permute-start(bf16[64,2560]{1,0:T(8,128)(2,1)S(1)} %stack_two.3.refs_0_), channel_id=1, source_target_pairs={{0,16},{1,17},{2,18},{3,19},{4,20},{5,21},{6,22},{7,23},{8,24},{9,... | collective-permute-start | bytes 983048 | tf_op jit(solution)/shard_map/ppermute | solution.py:60
  23.0 5.1 %collective-permute-start.7 = (bf16[288,128]{1,0:T(8,128)(2,1)S(1)}, bf16[288,128]{1,0:T(8,128)(2,1)S(1)}, u32[]{:S(2)}, u32[]{:S(2)}) collective-permute-start(bf16[288,128]{1,0:T(8,128)(2,1)S(1)} %collective-permute-done.3.earlier), channel_id=1, source_target_pairs={{0,1},{1,0},{2,3},{3,2},{4,5},{5,4},{6,7},{7,6},{8,9},{9,8},{10,11... | collective-permute-start | bytes 221192 | tf_op jit(solution)/shard_map/ppermute | solution.py:44
  27.5 2.3 %collective-permute-start.8 = (bf16[64,2688]{1,0:T(8,128)(2,1)S(1)}, bf16[64,2688]{1,0:T(8,128)(2,1)S(1)}, u32[]{:S(2)}, u32[]{:S(2)}) collective-permute-start(bf16[64,2688]{1,0:T(8,128)(2,1)S(1)} %stack_two.2.refs_0_), channel_id=1, source_target_pairs={{0,1},{1,0},{2,3},{3,2},{4,5},{5,4},{6,7},{7,6},{8,9},{9,8},{10,11... | collective-permute-start | bytes 1032200 | tf_op jit(solution)/shard_map/ppermute | solution.py:44
  28.4 1.7 %collective-permute-start.9 = (bf16[64,2688]{1,0:T(8,128)(2,1)S(1)}, bf16[64,2688]{1,0:T(8,128)(2,1)S(1)}, u32[]{:S(2)}, u32[]{:S(2)}) collective-permute-start(bf16[64,2688]{1,0:T(8,128)(2,1)S(1)} %collective-permute-done.5.refs_1_), channel_id=1, source_target_pairs={{0,1},{1,0},{2,3},{3,2},{4,5},{5,4},{6,7},{7,6},{8,9},{9,8},{10,11... | collective-permute-start | bytes 1032200 | tf_op jit(solution)/shard_map/ppermute | solution.py:44
  28.4 3.3 %collective-permute-start.11 = (bf16[64,2560]{1,0:T(8,128)(2,1)S(1)}, bf16[64,2560]{1,0:T(8,128)(2,1)S(1)}, u32[]{:S(2)}, u32[]{:S(2)}) collective-permute-start(bf16[64,2560]{1,0:T(8,128)(2,1)S(1)} %stack_two.3.refs_0_), channel_id=1, source_target_pairs={{0,1},{1,0},{2,3},{3,2},{4,5},{5,4},{6,7},{7,6},{8,9},{9,8},{10,11... | collective-permute-start | bytes 983048 | tf_op jit(solution)/shard_map/ppermute | solution.py:44
  29.8 1.8 %collective-permute-start.12 = (bf16[64,2560]{1,0:T(8,128)(2,1)S(1)}, bf16[64,2560]{1,0:T(8,128)(2,1)S(1)}, u32[]{:S(2)}, u32[]{:S(2)}) collective-permute-start(bf16[64,2560]{1,0:T(8,128)(2,1)S(1)} %collective-permute-done.10.refs_1_), channel_id=1, source_target_pairs={{0,1},{1,0},{2,3},{3,2},{4,5},{5,4},{6,7},{7,6},{8,9},{9,8},{10,11... | collective-permute-start | bytes 983048 | tf_op jit(solution)/shard_map/ppermute | solution.py:44
  33.4 5.8 %collective-permute-start.14 = (bf16[128,512]{1,0:T(8,128)(2,1)S(1)}, bf16[128,512]{1,0:T(8,128)(2,1)S(1)}, u32[]{:S(2)}, u32[]{:S(2)}) collective-permute-start(bf16[128,512]{1,0:T(8,128)(2,1)S(1)} %get-tuple-element.85), channel_id=1, source_target_pairs={{0,16},{16,0},{1,17},{17,1},{2,18},{18,2},{3,19},{19,3},{4,20},{20... | collective-permute-start | bytes 393224 | tf_op jit(solution)/shard_map/ppermute | solution.py:44
  36.7 4.3 %collective-permute-start.13 = (bf16[128,256]{1,0:T(8,128)(2,1)S(1)}, bf16[128,256]{1,0:T(8,128)(2,1)S(1)}, u32[]{:S(2)}, u32[]{:S(2)}) collective-permute-start(bf16[128,256]{1,0:T(8,128)(2,1)S(1)} %get-tuple-element.81), channel_id=1, source_target_pairs={{0,16},{16,0},{1,17},{17,1},{2,18},{18,2},{3,19},{19,3},{4,20},{20... | collective-permute-start | bytes 196616 | tf_op jit(solution)/shard_map/ppermute | solution.py:44
  41.5 1.7 %collective-permute-start.15 = (bf16[128,1280]{1,0:T(8,128)(2,1)S(1)}, bf16[128,1280]{1,0:T(8,128)(2,1)S(1)}, u32[]{:S(2)}, u32[]{:S(2)}) collective-permute-start(bf16[128,1280]{1,0:T(8,128)(2,1)S(1)} %get-tuple-element.90), channel_id=1, source_target_pairs={{0,1},{1,0},{2,3},{3,2},{4,5},{5,4},{6,7},{7,6},{8,9},{9,8},{10,11... | collective-permute-start | bytes 983048 | tf_op jit(solution)/shard_map/ppermute | solution.py:44
  42.1 2.5 %collective-permute-start.18 = (bf16[128,1280]{1,0:T(8,128)(2,1)S(1)}, bf16[128,1280]{1,0:T(8,128)(2,1)S(1)}, u32[]{:S(2)}, u32[]{:S(2)}) collective-permute-start(bf16[128,1280]{1,0:T(8,128)(2,1)S(1)} %get-tuple-element.96), channel_id=1, source_target_pairs={{0,1},{1,0},{2,3},{3,2},{4,5},{5,4},{6,7},{7,6},{8,9},{9,8},{10,11... | collective-permute-start | bytes 983048 | tf_op jit(solution)/shard_map/ppermute | solution.py:44
  43.3 6.3 %collective-permute-start.16 = (bf16[64,1280]{1,0:T(8,128)(2,1)S(1)}, bf16[64,1280]{1,0:T(8,128)(2,1)S(1)}, u32[]{:S(2)}, u32[]{:S(2)}) collective-permute-start(bf16[64,1280]{1,0:T(8,128)(2,1)S(1)} %get-tuple-element.92), channel_id=1, source_target_pairs={{0,16},{1,17},{2,18},{3,19},{4,20},{5,21},{6,22},{7,23},{8,24},{9,... | collective-permute-start | bytes 491528 | tf_op jit(solution)/shard_map/ppermute | solution.py:60
  44.7 6.6 %collective-permute-start.19 = (bf16[64,1280]{1,0:T(8,128)(2,1)S(1)}, bf16[64,1280]{1,0:T(8,128)(2,1)S(1)}, u32[]{:S(2)}, u32[]{:S(2)}) collective-permute-start(bf16[64,1280]{1,0:T(8,128)(2,1)S(1)} %get-tuple-element.98), channel_id=1, source_target_pairs={{0,2},{1,3},{2,0},{3,1},{4,6},{5,7},{6,4},{7,5},{8,10},{9,11},{10,... | collective-permute-start | bytes 491528 | tf_op jit(solution)/shard_map/ppermute | solution.py:60
  49.6 6.2 %collective-permute-start.17 = (bf16[32,2560]{1,0:T(8,128)(2,1)S(1)}, bf16[32,2560]{1,0:T(8,128)(2,1)S(1)}, u32[]{:S(2)}, u32[]{:S(2)}) collective-permute-start(bf16[32,2560]{1,0:T(8,128)(2,1)S(1)} %get-tuple-element.94), channel_id=1, source_target_pairs={{0,2},{1,3},{2,0},{3,1},{4,6},{5,7},{6,4},{7,5},{8,10},{9,11},{10,... | collective-permute-start | bytes 491528 | tf_op jit(solution)/shard_map/ppermute | solution.py:60
  51.3 4.5 %collective-permute-start.20 = (bf16[32,1280]{1,0:T(8,128)(2,1)S(1)}, bf16[32,1280]{1,0:T(8,128)(2,1)S(1)}, u32[]{:S(2)}, u32[]{:S(2)}) collective-permute-start(bf16[32,1280]{1,0:T(8,128)(2,1)S(1)} %get-tuple-element.100), channel_id=1, source_target_pairs={{0,16},{1,17},{2,18},{3,19},{4,20},{5,21},{6,22},{7,23},{8,24},{9,... | collective-permute-start | bytes 245768 | tf_op jit(solution)/shard_map/ppermute | solution.py:60
  55.9 6.8 %collective-permute-start.21 = (bf16[8,5120]{1,0:T(8,128)(2,1)S(1)}, bf16[8,5120]{1,0:T(8,128)(2,1)S(1)}, u32[]{:S(2)}, u32[]{:S(2)}) collective-permute-start(bf16[8,5120]{1,0:T(8,128)(2,1)S(1)} %get-tuple-element.101.after), channel_id=1, source_target_pairs={{0,12},{1,13},{2,14},{3,15},{4,8},{5,9},{6,10},{7,11},{8,4},{9,5},... | collective-permute-start | bytes 245768 | tf_op jit(solution)/shard_map/ppermute | solution.py:48
  58.2 6.2 %collective-permute-start.22 = (bf16[8,5120]{1,0:T(8,128)(2,1)S(1)}, bf16[8,5120]{1,0:T(8,128)(2,1)S(1)}, u32[]{:S(2)}, u32[]{:S(2)}) collective-permute-start(bf16[8,5120]{1,0:T(8,128)(2,1)S(1)} %get-tuple-element.107), channel_id=1, source_target_pairs={{0,4},{1,5},{2,6},{3,7},{4,0},{5,1},{6,2},{7,3},{8,12},{9,13},{10,... | collective-permute-start | bytes 245768 | tf_op jit(solution)/shard_map/ppermute | solution.py:48
  58.5 5.9 %collective-permute-start.23 = (bf16[8,5120]{1,0:T(8,128)(2,1)S(1)}, bf16[8,5120]{1,0:T(8,128)(2,1)S(1)}, u32[]{:S(2)}, u32[]{:S(2)}) collective-permute-start(bf16[8,5120]{1,0:T(8,128)(2,1)S(1)} %get-tuple-element.108), channel_id=1, source_target_pairs={{0,8},{1,9},{2,10},{3,11},{4,12},{5,13},{6,14},{7,15},{8,0},{9,1},... | collective-permute-start | bytes 245768 | tf_op jit(solution)/shard_map/ppermute | solution.py:48
